TPU v7x, 32 devices: a whole 2x2x4 slice. The times are simulated.
32 devices in a mesh: groups: 2 (over x), band: 16 (over z, y, core).
Axes of the slice: x: 2, y: 2, z: 4, core: 2. Of those that a mesh axis runs over, the one named last changes fastest.
Arguments:
- grid_latent: bfloat16 [32768, 512], P(('groups', 'band')), parts along dimension 0, may hold values from -6 to 6
- mesh_latent: bfloat16 [8192, 512], P(('groups', 'band')), parts along dimension 0, may hold values from -6 to 6
- edge_latent: bfloat16 [49152, 512], P(('groups', 'band')), parts along dimension 0, may hold values from -6 to 6
- mesh_cot: bfloat16 [8192, 512], P(('groups', 'band')), parts along dimension 0, may hold values from -6 to 6
- send_rows: int32 [16, 128], P('band'), may hold values from 0 to 1023
- edge_slot: int32 [24576], P('band'), may hold values from 0 to 127, as said below
- edge_dst: int32 [24576], P('band'), may hold values from 0 to 255
- w_edge1: bfloat16 [1536, 512], replicated, may hold values from -0.15625 to 0.15625
- w_edge2: bfloat16 [512, 512], replicated, may hold values from -0.25 to 0.25
- w_node1: bfloat16 [1024, 512], replicated, may hold values from -0.1875 to 0.1875
- w_node2: bfloat16 [512, 512], replicated, may hold values from -0.25 to 0.25
Outputs:
- mesh_out: bfloat16 [8192, 512], P(('groups', 'band')), parts along dimension 0
- grid_grad: float32 [32768, 512], P(('groups', 'band')), parts along dimension 0
- grad_edge1: float32 [3072, 512], P('groups'), parts along dimension 0
- grad_edge2: float32 [1024, 512], P('groups'), parts along dimension 0
There are 2 independent parts, one for each index of `groups`. A program takes and returns all parts, laid end to end along the dimension named above; an argument that names none is the same for every part. Nothing has to cross between parts.
Inputs may be any that keep to these rules, and one draw needn't show every extreme that they name: `edge_slot`: for edge e of owner o with slot q = b * 8 + s, slot s holds one of the rows that band b sends to owner o. Owners in the first and last eighth (the polar faces) may read any slot of any band; every other owner reads only from the bands within 16 // 4 of a band drawn for it, counted round the axis.
All inputs are finite; a program needn't handle non-finite values.
Results may differ from a plain program's by a relative error of at most 0.0066.
Values may be sent and summed in bfloat16 or wider, within the bound.
No kernel may reach another device: no remote copies, remote signals or barrier semaphores. Data moves between devices by JAX's collectives and lax.ppermute only.
A program may use at most 64 MiB of HBM per device.

v0:
```python
import jax
import jax.numpy as jnp
from jax import lax
from jax.sharding import PartitionSpec as P


def silu_slope(value):
    sigma = jax.nn.sigmoid(value)
    return sigma * (1.0 + value * (1.0 - sigma))


def shards(
    grid_latent,
    mesh_latent,
    edge_latent,
    mesh_cot,
    send_rows,
    edge_slot,
    edge_dst,
    w_edge1,
    w_edge2,
    w_node1,
    w_node2,
):
    band_count = lax.axis_size("band")
    feature_width = grid_latent.shape[1]
    mesh_rows = mesh_latent.shape[0]
    outgoing = jnp.take(grid_latent, send_rows[0], axis=0).reshape(band_count, -1, feature_width)
    arrived = lax.all_to_all(outgoing, "band", split_axis=0, concat_axis=0, tiled=True)
    slot_rows = arrived.reshape(-1, feature_width)
    inputs = jnp.concatenate(
        [
            jnp.take(slot_rows, edge_slot, axis=0),
            jnp.take(mesh_latent, edge_dst, axis=0),
            edge_latent,
        ],
        axis=1,
    )
    pre_edge = jnp.dot(inputs, w_edge1, preferred_element_type=jnp.float32)
    hidden = jax.nn.silu(pre_edge).astype(jnp.bfloat16)
    message = jnp.dot(hidden, w_edge2, preferred_element_type=jnp.float32).astype(jnp.bfloat16)
    received = jax.ops.segment_sum(
        message.astype(jnp.float32), edge_dst, num_segments=mesh_rows
    ).astype(jnp.bfloat16)
    node_in = jnp.concatenate([mesh_latent, received], axis=1)
    pre_node = jnp.dot(node_in, w_node1, preferred_element_type=jnp.float32)
    node_hidden = jax.nn.silu(pre_node).astype(jnp.bfloat16)
    mesh_out = (
        mesh_latent.astype(jnp.float32)
        + jnp.dot(node_hidden, w_node2, preferred_element_type=jnp.float32)
    ).astype(jnp.bfloat16)
    d_pre_node = (
        jnp.dot(mesh_cot, w_node2.T, preferred_element_type=jnp.float32) * silu_slope(pre_node)
    ).astype(jnp.bfloat16)
    d_received = jnp.dot(d_pre_node, w_node1[feature_width:].T, preferred_element_type=jnp.float32)
    d_message = jnp.take(d_received, edge_dst, axis=0).astype(jnp.bfloat16)
    d_pre_edge = (
        jnp.dot(d_message, w_edge2.T, preferred_element_type=jnp.float32) * silu_slope(pre_edge)
    ).astype(jnp.bfloat16)
    d_gathered = jnp.dot(d_pre_edge, w_edge1[:feature_width].T, preferred_element_type=jnp.float32)
    d_slots = jax.ops.segment_sum(d_gathered, edge_slot, num_segments=slot_rows.shape[0]).reshape(
        band_count, -1, feature_width
    )
    returned = lax.all_to_all(d_slots, "band", split_axis=0, concat_axis=0, tiled=True)
    grid_grad = jax.ops.segment_sum(
        returned.reshape(-1, feature_width), send_rows[0], num_segments=grid_latent.shape[0]
    )
    local_first = jnp.dot(inputs.T, d_pre_edge, preferred_element_type=jnp.float32)
    local_second = jnp.dot(hidden.T, d_message, preferred_element_type=jnp.float32)
    summed_first, summed_second = lax.psum((local_first, local_second), "band")
    return (mesh_out, grid_grad, summed_first, summed_second)


def solution(mesh):
    in_specs = (
        P(("groups", "band"), None),
        P(("groups", "band"), None),
        P(("groups", "band"), None),
        P(("groups", "band"), None),
        P("band", None),
        P("band"),
        P("band"),
        P(),
        P(),
        P(),
        P(),
    )
    out_specs = (
        P(("groups", "band"), None),
        P(("groups", "band"), None),
        P("groups", None),
        P("groups", None),
    )
    return jax.shard_map(shards, mesh=mesh, in_specs=in_specs, out_specs=out_specs, check_vma=False)
```

profile of v0, /device:TPU:0, one launch (start us, length us, event | category | flops | bytes accessed | tf_op | source)
XLA Modules:
  0.0 199.3 jit_solution(14527276296612553282)
XLA Ops:
  8.5 1.3 reduce.3
  11.5 7.4 %all-to-all-start = ((bf16[16,8,512]{2,1,0:T(8,128)(2,1)}), bf16[16,8,512]{2,1,0:T(8,128)(2,1)S(1)}, u32[]{:S(2)}, u32[]{:S(2)}) async-start(bf16[16,8,512]{2,1,0:T(8,128)(2,1)} %bitcast_select_fusion), calls=%async_computation | async-start | bytes 262144 | tf_op jit(solution)/shard_map/all_to_all | solution.py:29
  19.0 4.8 %gather_fusion.2 = bf16[1536,512]{1,0:T(8,128)(2,1)S(1)} fusion(bf16[256,512]{1,0:T(8,128)(2,1)S(1)} %copy-done.1, s32[2048]{0:T(1024)S(1)} %pad_clamp_fusion), kind=kCustom, calls=%fused_computation.2 | custom fusion | bytes 3151872 | tf_op jit(solution)/shard_map/jit(_take)/gather | solution.py:34
  23.9 3.0 %all-to-all-done = bf16[16,8,512]{2,1,0:T(8,128)(2,1)S(1)} async-done(((bf16[16,8,512]{2,1,0:T(8,128)(2,1)}), bf16[16,8,512]{2,1,0:T(8,128)(2,1)S(1)}, u32[]{:S(2)}, u32[]{:S(2)}) %all-to-all-start) | async-done | bytes 131104 | tf_op jit(solution)/shard_map/all_to_all | solution.py:29
  26.8 5.4 %gather_fusion.1 = bf16[1536,512]{1,0:T(8,128)(2,1)} fusion(bf16[128,512]{1,0:T(8,128)(2,1)S(1)} %bitcast.23, s32[2048]{0:T(1024)S(1)} %pad_clamp_fusion.1), kind=kCustom, calls=%fused_computation.1 | custom fusion | bytes 3151872 | tf_op jit(solution)/shard_map/jit(_take)/gather | solution.py:33
  32.2 2.3 %broadcast_select_fusion = (bf16[1536,512]{1,0:T(8,128)(2,1)S(1)}, bf16[1536,512]{1,0:T(8,128)(2,1)S(1)}) fusion(bf16[1536,512]{1,0:T(8,128)(2,1)S(1)} %gather_fusion.2, pred[1536]{0:T(1024)(128)(4,1)S(1)} %compare_and_fusion, bf16[1536,512]{1,0:T(8,128)(2,1)} %gather_fusion.1, pred[1536]{0:T(1024)(128)(4,1)S(1)} %compare_and_fusion.2), kind=kLoop, calls=%fused_computation.18 | loop fusion | flops 1572864 | bytes 6294528 | tf_op jit(solution)/shard_map/jit(_take)/select_n | solution.py:34
  34.6 4.3 %multiply_convert_fusion = (bf16[1536,512]{1,0:T(8,128)(2,1)S(1)}, f32[1536,512]{1,0:T(8,128)}) fusion(bf16[1536,512]{1,0:T(8,128)(2,1)S(1)} %copy-done.8, bf16[1536,512]{1,0:T(8,128)(2,1)S(1)} %copy-done.11, bf16[1536,512]{1,0:T(8,128)(2,1)S(1)} %get-tuple-element.8, bf16[1536,512]{1,0:T(8,128)(2,1)S(1)} %get-tuple-element.9), kind=kOutput, calls=%fused_computation.12 | convolution fusion | flops 2434007040 | bytes 11010048 | tf_op jit(solution)/shard_map/dot_general | solution.py:39
  38.9 1.2 copy-done.19
  40.1 1.0 convolution_convert_fusion
  41.1 10.1 %scatter_custom_fusion = f32[256,512]{1,0:T(8,128)S(1)} fusion(s32[1536]{0:T(1024)S(1)} %copy-done.9, bf16[1536,512]{1,0:T(8,128)(2,1)S(1)} %convolution_convert_fusion, f32[]{:T(128)} %constant.46.clone.1), kind=kCustom, calls=%fused_computation.10 | custom fusion | flops 1572864 | bytes 2097156 | tf_op jit(solution)/shard_map/scatter-add | solution.py:42
  51.2 2.6 %fusion.10 = f32[256,512]{1,0:T(8,128)} fusion(bf16[1024,512]{1,0:T(8,128)(2,1)} %param.20, bf16[256,512]{1,0:T(8,128)(2,1)S(1)} %convert_element_type.34, bf16[256,512]{1,0:T(8,128)(2,1)S(1)} %copy-done.1), kind=kOutput, calls=%fused_computation.27 | convolution fusion | flops 269484032 | bytes 2097152 | tf_op jit(solution)/shard_map/dot_general | solution.py:46
  53.8 1.6 fusion.7
  55.5 4.8 %gather_fusion.3 = bf16[1536,512]{1,0:T(8,128)(2,1)S(1)} fusion(bf16[256,512]{1,0:T(8,128)(2,1)S(1)} %fusion.7, s32[2048]{0:T(1024)S(1)} %pad_clamp_fusion), kind=kCustom, calls=%fused_computation.3 | custom fusion | bytes 3151872 | tf_op jit(solution)/shard_map/jit(_take)/gather | solution.py:56
  60.3 4.1 %fusion.33 = f32[512,512]{1,0:T(8,128)} fusion(bf16[1536,512]{1,0:T(8,128)(2,1)} %copy-done.19, bf16[1536,512]{1,0:T(8,128)(2,1)S(1)} %gather_fusion.3, pred[1536]{0:T(1024)(128)(4,1)S(1)} %compare_and_fusion), kind=kOutput, calls=%fused_computation.63 | convolution fusion | flops 806092800 | bytes 4195840 | tf_op jit(solution)/shard_map/dot_general | solution.py:69
  64.4 3.4 %fusion.2 = bf16[1536,512]{1,0:T(8,128)(2,1)S(1)} fusion(f32[1536,512]{1,0:T(8,128)S(1)} %copy-done.20, bf16[512,512]{1,0:T(8,128)(2,1)S(1)} %copy-done.15, bf16[1536,512]{1,0:T(8,128)(2,1)} %copy-done.2, pred[1536]{0:T(1024)(128)(4,1)S(1)} %compare_and_fusion), kind=kOutput, calls=%fused_computation.15 | convolution fusion | flops 813170688 | bytes 6817280 | tf_op jit(solution)/shard_map/dot_general | solution.py:58
  67.8 4.1 %fusion.3 = f32[1536,512]{1,0:T(8,128)} fusion(bf16[1536,512]{1,0:T(8,128)(2,1)S(1)} %fusion.2, bf16[1536,512]{1,0:T(8,128)(2,1)S(1)} %copy-done.12, bf16[1536,512]{1,0:T(8,128)(2,1)S(1)} %copy-done.4, bf16[1536,512]{1,0:T(8,128)(2,1)S(1)} %copy-done.6), kind=kOutput, calls=%fused_computation.16 | convolution fusion | flops 2430074880 | bytes 9437184 | tf_op jit(solution)/shard_map/dot_general | solution.py:68
  72.0 3.8 %fusion.14 = f32[1536,512]{1,0:T(8,128)} fusion(bf16[1536,512]{1,0:T(8,128)(2,1)S(1)} %fusion.2, bf16[1536,512]{1,0:T(8,128)(2,1)} %param.18), kind=kOutput, calls=%fused_computation.31 | convolution fusion | flops 805306368 | bytes 5242880 | tf_op jit(solution)/shard_map/dot_general | solution.py:60
  75.8 11.0 %scatter_custom_fusion.1 = f32[128,512]{1,0:T(8,128)} fusion(s32[1536]{0:T(1024)S(1)} %copy-done.10, f32[1536,512]{1,0:T(8,128)} %fusion.14, f32[]{:T(128)} %constant.46.clone.1), kind=kCustom, calls=%fused_computation.45 | custom fusion | flops 786432 | bytes 262656 | tf_op jit(solution)/shard_map/scatter-add | solution.py:61
  86.8 3.5 %all-to-all-start.1 = ((f32[16,8,512]{2,1,0:T(8,128)}), f32[16,8,512]{2,1,0:T(8,128)S(1)}, u32[]{:S(2)}, u32[]{:S(2)}) async-start(f32[16,8,512]{2,1,0:T(8,128)} %bitcast.5), calls=%async_computation.1 | async-start | bytes 524288 | tf_op jit(solution)/shard_map/all_to_all | solution.py:64
  90.3 2.1 %fusion.5 = bf16[256,512]{1,0:T(8,128)(2,1)} fusion(bf16[512,512]{1,0:T(8,128)(2,1)S(1)} %copy-done.17, bf16[256,512]{1,0:T(8,128)(2,1)S(1)} %copy-done.1, f32[256,512]{1,0:T(8,128)} %fusion.10), kind=kOutput, calls=%fused_computation.22 | convolution fusion | flops 135266304 | bytes 1572864 | tf_op jit(solution)/shard_map/dot_general | solution.py:50
  92.4 12.5 %all-to-all-done.1 = f32[16,8,512]{2,1,0:T(8,128)S(1)} async-done(((f32[16,8,512]{2,1,0:T(8,128)}), f32[16,8,512]{2,1,0:T(8,128)S(1)}, u32[]{:S(2)}, u32[]{:S(2)}) %all-to-all-start.1) | async-done | bytes 262176 | tf_op jit(solution)/shard_map/all_to_all | solution.py:64
  104.9 2.9 %scatter_custom_fusion.2 = f32[1024,512]{1,0:T(8,128)} fusion(s32[128]{0:T(128)} %bitcast.24, f32[]{:T(128)} %constant.46.clone.1, f32[16,8,512]{2,1,0:T(8,128)S(1)} %all-to-all-done.1), kind=kCustom, calls=%fused_computation.25 | custom fusion | flops 65536 | bytes 2359808 | tf_op jit(solution)/shard_map/scatter-add | solution.py:65
  107.8 79.7 %all-reduce.3.cloned.1.call-done = (f32[1536,512]{1,0:T(8,128)}, f32[512,512]{1,0:T(8,128)}) async-done(((f32[1536,512]{1,0:T(8,128)}, f32[512,512]{1,0:T(8,128)}), (f32[1536,512]{1,0:T(8,128)}, f32[512,512]{1,0:T(8,128)})) %all-reduce.3.cloned.1.call-update) | async-done | bytes 4194320 | tf_op jit(solution)/shard_map/psum | solution.py:70
  187.5 3.9 %copy.17 = f32[1536,512]{1,0:T(8,128)} copy(f32[1536,512]{1,0:T(8,128)} %get-tuple-element.12) | data formatting | bytes 6291456
  (58 shorter events, 4.2 us)
Async XLA Ops:
  7.2 2.7 %copy-start = (bf16[1024,512]{1,0:T(8,128)(2,1)S(1)}, bf16[1024,512]{1,0:T(8,128)(2,1)}, u32[]{:S(2)}) copy-start(bf16[1024,512]{1,0:T(8,128)(2,1)} %param.11) | copy-start | bytes 3145732
  7.2 11.8 %copy-start.9 = (s32[1536]{0:T(1024)S(1)}, s32[1536]{0:T(1024)}, u32[]{:S(2)}) copy-start(s32[1536]{0:T(1024)} %param.17) | copy-start | bytes 18436
  7.2 11.8 %copy-start.10 = (s32[1536]{0:T(1024)S(1)}, s32[1536]{0:T(1024)}, u32[]{:S(2)}) copy-start(s32[1536]{0:T(1024)} %param.16) | copy-start | bytes 18436
  7.2 11.8 %copy-start.1 = (bf16[256,512]{1,0:T(8,128)(2,1)S(1)}, bf16[256,512]{1,0:T(8,128)(2,1)}, u32[]{:S(2)}) copy-start(bf16[256,512]{1,0:T(8,128)(2,1)} %param.12) | copy-start | bytes 786436
  11.5 15.3 %all-to-all-start = ((bf16[16,8,512]{2,1,0:T(8,128)(2,1)}), bf16[16,8,512]{2,1,0:T(8,128)(2,1)S(1)}, u32[]{:S(2)}, u32[]{:S(2)}) async-start(bf16[16,8,512]{2,1,0:T(8,128)(2,1)} %bitcast_select_fusion), calls=%async_computation | async-start | bytes 262144 | tf_op jit(solution)/shard_map/all_to_all | solution.py:29
  18.9 168.6 %all-reduce.3.cloned.1.call-start = ((), (), s32[]{:S(2)}) async-start(), calls=%async_computation.2 | async-start | bytes 8388608 | tf_op jit(solution)/shard_map/psum | solution.py:70
  32.2 2.3 %copy-start.8 = (bf16[1536,512]{1,0:T(8,128)(2,1)S(1)}, bf16[1536,512]{1,0:T(8,128)(2,1)}, u32[]{:S(2)}) copy-start(bf16[1536,512]{1,0:T(8,128)(2,1)} %param.18) | copy-start | bytes 4718596
  32.2 2.4 %copy-start.11 = (bf16[1536,512]{1,0:T(8,128)(2,1)S(1)}, bf16[1536,512]{1,0:T(8,128)(2,1)}, u32[]{:S(2)}) copy-start(bf16[1536,512]{1,0:T(8,128)(2,1)} %param.13) | copy-start | bytes 4718596
  34.5 4.4 %copy-start.3 = (bf16[1536,512]{1,0:T(8,128)(2,1)}, bf16[1536,512]{1,0:T(8,128)(2,1)S(1)}, u32[]{:S(2)}) copy-start(bf16[1536,512]{1,0:T(8,128)(2,1)S(1)} %get-tuple-element.8) | copy-start | bytes 4718596
  34.6 4.4 %copy-start.5 = (bf16[1536,512]{1,0:T(8,128)(2,1)}, bf16[1536,512]{1,0:T(8,128)(2,1)S(1)}, u32[]{:S(2)}) copy-start(bf16[1536,512]{1,0:T(8,128)(2,1)S(1)} %get-tuple-element.9) | copy-start | bytes 4718596
  34.6 5.5 %copy-start.14 = (bf16[512,512]{1,0:T(8,128)(2,1)S(1)}, bf16[512,512]{1,0:T(8,128)(2,1)}, u32[]{:S(2)}) copy-start(bf16[512,512]{1,0:T(8,128)(2,1)} %param.19) | copy-start | bytes 1572868
  38.9 1.2 copy-start.19
  51.2 2.7 %copy-start.13 = (bf16[1024,512]{1,0:T(8,128)(2,1)S(1)}, bf16[1024,512]{1,0:T(8,128)(2,1)}, u32[]{:S(2)}) copy-start(bf16[1024,512]{1,0:T(8,128)(2,1)} %param.20) | copy-start | bytes 3145732
  51.2 2.6 %copy-start.16 = (bf16[512,512]{1,0:T(8,128)(2,1)S(1)}, bf16[512,512]{1,0:T(8,128)(2,1)}, u32[]{:S(2)}) copy-start(bf16[512,512]{1,0:T(8,128)(2,1)} %param.21) | copy-start | bytes 1572868
  51.2 2.6 %copy-start.18 = (bf16[256,512]{1,0:T(8,128)(2,1)S(1)}, bf16[256,512]{1,0:T(8,128)(2,1)}, u32[]{:S(2)}) copy-start(bf16[256,512]{1,0:T(8,128)(2,1)} %param.14) | copy-start | bytes 786436
  60.3 4.1 %copy-start.2 = (bf16[1536,512]{1,0:T(8,128)(2,1)}, bf16[1536,512]{1,0:T(8,128)(2,1)S(1)}, u32[]{:S(2)}) copy-start(bf16[1536,512]{1,0:T(8,128)(2,1)S(1)} %gather_fusion.3) | copy-start | bytes 4718596
  60.3 4.1 %copy-start.15 = (bf16[512,512]{1,0:T(8,128)(2,1)S(1)}, bf16[512,512]{1,0:T(8,128)(2,1)}, u32[]{:S(2)}) copy-start(bf16[512,512]{1,0:T(8,128)(2,1)} %param.19) | copy-start | bytes 1572868
  60.3 4.1 %copy-start.20 = (f32[1536,512]{1,0:T(8,128)S(1)}, f32[1536,512]{1,0:T(8,128)}, u32[]{:S(2)}) copy-start(f32[1536,512]{1,0:T(8,128)} %get-tuple-element.7) | copy-start | bytes 9437188
  64.4 3.4 %copy-start.4 = (bf16[1536,512]{1,0:T(8,128)(2,1)S(1)}, bf16[1536,512]{1,0:T(8,128)(2,1)}, u32[]{:S(2)}) copy-start(bf16[1536,512]{1,0:T(8,128)(2,1)} %copy-done.3) | copy-start | bytes 4718596
  64.4 3.4 %copy-start.6 = (bf16[1536,512]{1,0:T(8,128)(2,1)S(1)}, bf16[1536,512]{1,0:T(8,128)(2,1)}, u32[]{:S(2)}) copy-start(bf16[1536,512]{1,0:T(8,128)(2,1)} %copy-done.5) | copy-start | bytes 4718596
  64.4 3.4 %copy-start.12 = (bf16[1536,512]{1,0:T(8,128)(2,1)S(1)}, bf16[1536,512]{1,0:T(8,128)(2,1)}, u32[]{:S(2)}) copy-start(bf16[1536,512]{1,0:T(8,128)(2,1)} %param.13) | copy-start | bytes 4718596
  72.0 18.3 %copy-start.17 = (bf16[512,512]{1,0:T(8,128)(2,1)S(1)}, bf16[512,512]{1,0:T(8,128)(2,1)}, u32[]{:S(2)}) copy-start(bf16[512,512]{1,0:T(8,128)(2,1)} %param.21) | copy-start | bytes 1572868
  86.8 18.2 %all-to-all-start.1 = ((f32[16,8,512]{2,1,0:T(8,128)}), f32[16,8,512]{2,1,0:T(8,128)S(1)}, u32[]{:S(2)}, u32[]{:S(2)}) async-start(f32[16,8,512]{2,1,0:T(8,128)} %bitcast.5), calls=%async_computation.1 | async-start | bytes 524288 | tf_op jit(solution)/shard_map/all_to_all | solution.py:64
  187.5 4.0 %copy-start.7 = (f32[512,512]{1,0:T(8,128)S(1)}, f32[512,512]{1,0:T(8,128)}, u32[]{:S(2)}) copy-start(f32[512,512]{1,0:T(8,128)} %get-tuple-element.13) | copy-start | bytes 3145732
Sparse Core Ops, SparseCore 0:
  72.1 115.3 all-reduce.2
where the time goes:
time: 200 us; the launch traced here: 199 us
  waiting for transfers between devices  95.2 us (48%)
  other arithmetic  29.1 us (15%)
  matrix products  26.9 us (13%)
  local copies, waits for them, and re-layouts  22.7 us (11%)
  between operations  14.4 us (7%)
  starting transfers between devices  11 us (6%)
    psum x1, waiting for transfers between devices, shards(): summed_first, summed_second = lax.psum((local_first, local_second), 'band')  79.7 us
    all_to_all x1, waiting for transfers between devices, shards(): lax.all_to_all(d_slots, 'band', split_axis=0, concat_axis=0, tiled=True)  12.5 us
    scatter-add x1, other arithmetic, shards(): jax.ops.segment_sum(d_gathered, edge_slot, num_segments=slot_rows.shape[0])  11 us
    scatter-add x1, other arithmetic, shards(): jax.ops.segment_sum(message.astype(jnp.float32), edge_dst, num_segments=m...  10.1 us
    all_to_all x1, starting transfers between devices, shards(): lax.all_to_all(outgoing, 'band', split_axis=0, concat_axis=0, tiled=True)  7.39 us
    unnamed x45, local copies, waits for them, and re-layouts  6.7 us
    gather x1, local copies, waits for them, and re-layouts, shards(): jnp.take(slot_rows, edge_slot, axis=0)  5.4 us
    gather x1, local copies, waits for them, and re-layouts, shards(): d_message = jnp.take(d_received, edge_dst, axis=0).astype(jnp.bfloat16)  4.81 us
  transfers between devices with their start and end apart: 3, of which 3 were waited for; matrix products, arithmetic and copies ran while one was open for 12% of the time, Pallas kernels for 0%

commit v1 on v0

v1 whole, which is shorter than its diff:
```python
import functools

import jax
import jax.numpy as jnp
from jax import lax
from jax.experimental import pallas as pl
from jax.experimental.pallas import tpu as pltpu
from jax.sharding import PartitionSpec as P

BF16 = jnp.bfloat16
F32 = jnp.float32
VMEM_LIMIT = 50 * 1024 * 1024


def dot_nn(a, b):
    return jnp.dot(a, b, preferred_element_type=F32)


def dot_tn(a, b):
    return lax.dot_general(a, b, (((0,), (0,)), ((), ())), preferred_element_type=F32)


def dot_nt(a, b):
    return lax.dot_general(a, b, (((1,), (1,)), ((), ())), preferred_element_type=F32)


def split(value):
    high = value.astype(BF16)
    low = (value - high.astype(F32)).astype(BF16)
    return high, low


def one_hot_rows(index_row, rows):
    shape = (rows, index_row.shape[1])
    hit = lax.broadcasted_iota(jnp.int32, shape, 0) == index_row
    return jnp.where(hit, 1.0, 0.0).astype(BF16)


def params():
    return pltpu.CompilerParams(vmem_limit_bytes=VMEM_LIMIT)


def cost(flops, nbytes):
    return pl.CostEstimate(flops=flops, bytes_accessed=nbytes, transcendentals=0)


def pick_kernel(rows_ref, grid_ref, out_ref):
    chosen = one_hot_rows(rows_ref[...], grid_ref.shape[0])
    out_ref[...] = dot_tn(chosen, grid_ref[...]).astype(BF16)


def put_kernel(rows_ref, back_ref, out_ref):
    chosen = one_hot_rows(rows_ref[...], out_ref.shape[0])
    out_ref[...] = dot_nn(chosen, back_ref[...])


def base_kernel(tile, dst_ref, mesh_ref, edge_ref, w1_ref, out_ref):
    width = mesh_ref.shape[1]
    mesh_rows = mesh_ref.shape[0]
    high, low = split(dot_nn(mesh_ref[...], w1_ref[width : 2 * width, :]))
    pair = jnp.concatenate([high, low], axis=0)

    def step(at, carry):
        rows = pl.ds(pl.multiple_of(at * tile, tile), tile)
        to_mesh = one_hot_rows(dst_ref[:, rows], mesh_rows)
        twice = jnp.concatenate([to_mesh, to_mesh], axis=0)
        out_ref[rows, :] = dot_nn(edge_ref[rows, :], w1_ref[2 * width :, :]) + dot_tn(twice, pair)
        return carry

    lax.fori_loop(0, edge_ref.shape[0] // tile, step, 0)


def main_kernel(
    tile,
    sizes,
    a_cols,
    slot_ref,
    dst_ref,
    slots_ref,
    base_ref,
    mesh_ref,
    edge_ref,
    cot_ref,
    w1_ref,
    w2_ref,
    wn1_ref,
    wn2_ref,
    mesh_out_ref,
    d_slots_ref,
    a_keep_ref,
    a_send_ref,
    b_keep_ref,
    b_send_ref,
    slope_ref,
    sums_ref,
    grads_ref,
):
    outer, inner = sizes
    width = mesh_ref.shape[1]
    mesh_rows = mesh_ref.shape[0]
    slot_rows = slots_ref.shape[0]
    tiles = edge_ref.shape[0] // tile
    me = lax.axis_index("band")
    my_core = me % 2
    my_inner = (me // 2) % inner
    my_outer = me // (2 * inner)

    high, low = split(dot_nn(slots_ref[...], w1_ref[:width, :]))
    slot_pair = jnp.concatenate([high, low], axis=0)
    sums_ref[...] = jnp.zeros_like(sums_ref)

    def forward(at, carry):
        rows = pl.ds(pl.multiple_of(at * tile, tile), tile)
        from_slot = one_hot_rows(slot_ref[:, rows], slot_rows)
        twice = jnp.concatenate([from_slot, from_slot], axis=0)
        pre = base_ref[rows, :] + dot_tn(twice, slot_pair)
        sigma = 0.5 + 0.5 * jnp.tanh(0.5 * pre)
        hidden = pre * sigma
        slope_ref[rows, :] = sigma + hidden * (1.0 - sigma)
        to_mesh = one_hot_rows(dst_ref[:, rows], mesh_rows)
        sums_ref[slot_rows:, :] += dot_nn(to_mesh, hidden.astype(BF16))
        return carry

    lax.fori_loop(0, tiles, forward, 0)

    hidden_high, hidden_low = split(sums_ref[slot_rows:, :])
    received = (dot_nn(hidden_high, w2_ref[...]) + dot_nn(hidden_low, w2_ref[...])).astype(BF16)
    mesh = mesh_ref[...]
    pre_node = dot_nn(mesh, wn1_ref[:width, :]) + dot_nn(received, wn1_ref[width:, :])
    sigma = 0.5 + 0.5 * jnp.tanh(0.5 * pre_node)
    node = pre_node * sigma
    mesh_out_ref[...] = (mesh.astype(F32) + dot_nn(node.astype(BF16), wn2_ref[...])).astype(BF16)
    slope = sigma + node * (1.0 - sigma)
    d_pre_node = (dot_nt(cot_ref[...], wn2_ref[...]) * slope).astype(BF16)
    d_received = dot_nt(d_pre_node, wn1_ref[width:, :]).astype(BF16)
    grads_ref[3 * width :, :] = dot_tn(hidden_high, d_received) + dot_tn(hidden_low, d_received)
    high, low = split(dot_nt(d_received, w2_ref[...]))
    back_pair = jnp.concatenate([high, low], axis=0)
    sums_ref[...] = jnp.zeros_like(sums_ref)
    grads_ref[2 * width : 3 * width, :] = jnp.zeros((width, grads_ref.shape[1]), F32)

    def backward(at, carry):
        rows = pl.ds(pl.multiple_of(at * tile, tile), tile)
        from_slot = one_hot_rows(slot_ref[:, rows], slot_rows)
        to_mesh = one_hot_rows(dst_ref[:, rows], mesh_rows)
        twice = jnp.concatenate([to_mesh, to_mesh], axis=0)
        d_pre = (dot_tn(twice, back_pair) * slope_ref[rows, :]).astype(BF16)
        both = jnp.concatenate([from_slot, to_mesh], axis=0)
        sums_ref[...] += dot_nn(both, d_pre)
        grads_ref[2 * width : 3 * width, :] += dot_tn(edge_ref[rows, :], d_pre)
        return carry

    lax.fori_loop(0, tiles, backward, 0)

    slot_high, slot_low = split(sums_ref[:slot_rows, :])
    d_slots = dot_nt(slot_high, w1_ref[:width, :]) + dot_nt(slot_low, w1_ref[:width, :])
    d_slots_ref[...] = d_slots.astype(BF16)
    slots = slots_ref[...]
    grads_ref[:width, :] = dot_tn(slots, slot_high) + dot_tn(slots, slot_low)
    mesh_high, mesh_low = split(sums_ref[slot_rows:, :])
    grads_ref[width : 2 * width, :] = dot_tn(mesh, mesh_high) + dot_tn(mesh, mesh_low)

    chunk = grads_ref.shape[0] // (2 * outer * inner)

    def spread(far_core, a_ref, b_ref):
        core = my_core ^ far_core

        def step(at, carry):
            far_inner, far_outer = at // outer, at % outer
            owner = ((my_outer ^ far_outer) * inner + (my_inner ^ far_inner)) * 2 + core
            rows = grads_ref[pl.ds(pl.multiple_of(owner * chunk, chunk), chunk), :].astype(BF16)
            a_ref[pl.ds(pl.multiple_of(at * chunk, chunk), chunk), :] = rows[:, :a_cols]
            other = far_outer * inner + far_inner
            b_ref[pl.ds(pl.multiple_of(other * chunk, chunk), chunk), :] = rows[:, a_cols:]
            return carry

        lax.fori_loop(0, outer * inner, step, 0)

    spread(1, a_send_ref, b_send_ref)
    spread(0, a_keep_ref, b_keep_ref)


def order_kernel(sizes, a_cols, a_ref, b_ref, first_ref, second_ref):
    outer, inner = sizes
    chunk = a_ref.shape[0] // (2 * outer * inner)
    me = lax.axis_index("band")
    my_core = me % 2
    my_inner = (me // 2) % inner
    my_outer = me // (2 * inner)
    first_chunks = first_ref.shape[0] // chunk

    def place(out_ref, start):
        def step(at, carry):
            owner = at + start
            far_core = my_core ^ (owner % 2)
            far_inner = my_inner ^ ((owner // 2) % inner)
            far_outer = my_outer ^ (owner // (2 * inner))
            a_at = (far_core * inner + far_inner) * outer + far_outer
            b_at = (far_core * outer + far_outer) * inner + far_inner
            rows = pl.ds(pl.multiple_of(at * chunk, chunk), chunk)
            a_rows = pl.ds(pl.multiple_of(a_at * chunk, chunk), chunk)
            b_rows = pl.ds(pl.multiple_of(b_at * chunk, chunk), chunk)
            out_ref[rows, :a_cols] = a_ref[a_rows, :].astype(F32)
            out_ref[rows, a_cols:] = b_ref[b_rows, :].astype(F32)
            return carry

        lax.fori_loop(0, out_ref.shape[0] // chunk, step, 0)

    place(first_ref, 0)
    place(second_ref, first_chunks)


def shards(
    sizes,
    grid_latent,
    mesh_latent,
    edge_latent,
    mesh_cot,
    send_rows,
    edge_slot,
    edge_dst,
    w_edge1,
    w_edge2,
    w_node1,
    w_node2,
):
    outer, inner = sizes
    band_count = lax.axis_size("band")
    width = grid_latent.shape[1]
    hidden_width = w_edge1.shape[1]
    edges = edge_latent.shape[0]
    mesh_rows = mesh_latent.shape[0]
    slot_rows = send_rows.shape[1]
    tile = 256
    a_cols = hidden_width * 3 // 4
    b_cols = hidden_width - a_cols
    slot_row = edge_slot.reshape(1, edges)
    dst_row = edge_dst.reshape(1, edges)

    def permute(value, stride, size, shift):
        pairs = []
        for source in range(band_count):
            place = (source // stride) % size
            pairs.append((source, source + ((place ^ shift) - place) * stride))
        return lax.ppermute(value, "band", pairs)

    outgoing = pl.pallas_call(
        pick_kernel,
        out_shape=jax.ShapeDtypeStruct((slot_rows, width), BF16),
        compiler_params=params(),
        name="pick",
    )(send_rows, grid_latent)
    slots = lax.all_to_all(
        outgoing.reshape(band_count, -1, width), "band", split_axis=0, concat_axis=0, tiled=True
    ).reshape(slot_rows, width)

    base = pl.pallas_call(
        functools.partial(base_kernel, tile),
        out_shape=jax.ShapeDtypeStruct((edges, hidden_width), F32),
        compiler_params=params(),
        cost_estimate=cost(2 * edges * width * hidden_width * 2, edges * width * 8),
        name="base",
    )(dst_row, mesh_latent, edge_latent, w_edge1)

    grad_rows = 3 * width + hidden_width
    half = grad_rows // 2
    mesh_out, d_slots, a_keep, a_send, b_keep, b_send = pl.pallas_call(
        functools.partial(main_kernel, tile, sizes, a_cols),
        out_shape=[
            jax.ShapeDtypeStruct((mesh_rows, width), BF16),
            jax.ShapeDtypeStruct((slot_rows, width), BF16),
            jax.ShapeDtypeStruct((half, a_cols), BF16),
            jax.ShapeDtypeStruct((half, a_cols), BF16),
            jax.ShapeDtypeStruct((half, b_cols), BF16),
            jax.ShapeDtypeStruct((half, b_cols), BF16),
        ],
        scratch_shapes=[
            pltpu.VMEM((edges, hidden_width), F32),
            pltpu.VMEM((slot_rows + mesh_rows, hidden_width), F32),
            pltpu.VMEM((grad_rows, hidden_width), F32),
        ],
        compiler_params=params(),
        name="edges",
    )(
        slot_row,
        dst_row,
        slots,
        base,
        mesh_latent,
        edge_latent,
        mesh_cot,
        w_edge1,
        w_edge2,
        w_node1,
        w_node2,
    )

    returned = lax.all_to_all(
        d_slots.reshape(band_count, -1, width), "band", split_axis=0, concat_axis=0, tiled=True
    ).reshape(slot_rows, width)
    grid_grad = pl.pallas_call(
        put_kernel,
        out_shape=jax.ShapeDtypeStruct(grid_latent.shape, F32),
        compiler_params=params(),
        name="put",
    )(send_rows, returned)

    def fold(value, stride, size):
        rows = value.shape[0] // size
        total = value[:rows].astype(F32)
        for shift in range(1, size):
            piece = value[shift * rows : (shift + 1) * rows]
            total = total + permute(piece, stride, size, shift).astype(F32)
        return total.astype(BF16)

    def unfold(value, stride, size):
        pieces = [value] + [permute(value, stride, size, shift) for shift in range(1, size)]
        return jnp.concatenate(pieces, axis=0)

    inner_at, outer_at = (2, inner), (2 * inner, outer)
    a_sum = (a_keep.astype(F32) + permute(a_send, 1, 2, 1).astype(F32)).astype(BF16)
    b_sum = (b_keep.astype(F32) + permute(b_send, 1, 2, 1).astype(F32)).astype(BF16)
    a_own = fold(fold(a_sum, *inner_at), *outer_at)
    b_own = fold(fold(b_sum, *outer_at), *inner_at)
    a_all = unfold(unfold(unfold(a_own, *outer_at), *inner_at), 1, 2)
    b_all = unfold(unfold(unfold(b_own, *inner_at), *outer_at), 1, 2)

    grad_edge1, grad_edge2 = pl.pallas_call(
        functools.partial(order_kernel, sizes, a_cols),
        out_shape=[
            jax.ShapeDtypeStruct((3 * width, hidden_width), F32),
            jax.ShapeDtypeStruct((hidden_width, width), F32),
        ],
        compiler_params=params(),
        name="order",
    )(a_all, b_all)
    return (mesh_out, grid_grad, grad_edge1, grad_edge2)


def solution(mesh):
    chips = mesh.shape["band"] // 2
    inner = 1
    while inner * inner * 4 <= chips:
        inner *= 2
    sizes = (chips // inner, inner)
    in_specs = (
        P(("groups", "band"), None),
        P(("groups", "band"), None),
        P(("groups", "band"), None),
        P(("groups", "band"), None),
        P("band", None),
        P("band"),
        P("band"),
        P(),
        P(),
        P(),
        P(),
    )
    out_specs = (
        P(("groups", "band"), None),
        P(("groups", "band"), None),
        P("groups", None),
        P("groups", None),
    )
    return jax.shard_map(
        functools.partial(shards, sizes), mesh=mesh, in_specs=in_specs, out_specs=out_specs, check_vma=False
    )
```

time: 200 us -> 105 us (0.53)
  waiting for transfers between devices: 95.2 us -> 25.5 us
  other arithmetic: 29.1 us -> 0.52 us
  matrix products: 26.9 us -> 0 us
  Pallas kernels: 0 us -> 25.2 us
  starting transfers between devices: 11 us -> 32.8 us
  local copies, waits for them, and re-layouts: 22.7 us -> 6.74 us
  between operations: 14.4 us -> 0.84 us
  blocking collectives: 0 us -> 13.3 us
    psum x1 -> x0, waiting for transfers between devices: 79.7 us -> none  [shards(): summed_first, summed_second = lax.psum((local_first, local_second), 'band')]
    dot_general x9 -> x0, matrix products: 26.9 us -> none  [the longest x1 4.3 us: shards(): pre_edge = jnp.dot(inputs, w_edge1, preferred_element_type=jnp.float32)]
    ppermute x0 -> x20, waiting for transfers between devices: none -> 25.5 us  [permute(): return lax.ppermute(value, 'band', pairs)]
    ppermute x0 -> x20, starting transfers between devices: none -> 25.4 us  [permute(): return lax.ppermute(value, 'band', pairs)]
    pallas_call x0 -> x5, Pallas kernels: none -> 25.2 us  [the longest x1 15.2 us: shards(): pl.pallas_call(functools.partial(main_kernel, tile, sizes, a_cols), out_s...]
    scatter-add x3 -> x0, other arithmetic: 23.9 us -> none  [the longest x1 11 us: shards(): jax.ops.segment_sum(d_gathered, edge_slot, num_segments=slot_rows.shape[0])]
    gather x4 -> x0, local copies, waits for them, and re-layouts: 15.9 us -> none  [the longest x1 5.4 us: shards(): jnp.take(slot_rows, edge_slot, axis=0)]
    all_to_all x2 -> x1, waiting for transfers between devices: 15.5 us -> 0.01 us  [shards(): lax.all_to_all(outgoing.reshape(band_count, -1, width), 'band', split_axi...]
  transfers between devices with their start and end apart: 3 -> 21, of which waited for: 3 -> 9; matrix products, arithmetic and copies ran while one was open for 12% -> 2% of each run, Pallas kernels for 0% -> 6%
where the time goes in v1:
time: 105 us
  starting transfers between devices  32.8 us (31%)
  waiting for transfers between devices  25.5 us (24%)
  Pallas kernels  25.2 us (24%)
  blocking collectives  13.3 us (13%)
  local copies, waits for them, and re-layouts  6.74 us (6%)
    ppermute x20, waiting for transfers between devices, permute(): return lax.ppermute(value, 'band', pairs)  25.5 us
    ppermute x20, starting transfers between devices, permute(): return lax.ppermute(value, 'band', pairs)  25.4 us
    pallas_call x1, Pallas kernels, shards(): pl.pallas_call(functools.partial(main_kernel, tile, sizes, a_cols), out_s...  15.2 us
    all_to_all x1, blocking collectives, shards(): lax.all_to_all(d_slots.reshape(band_count, -1, width), 'band', split_axis...  13.3 us
    all_to_all x1, starting transfers between devices, shards(): lax.all_to_all(outgoing.reshape(band_count, -1, width), 'band', split_axi...  7.39 us
    unnamed x26, local copies, waits for them, and re-layouts  4.89 us
    pallas_call x1, Pallas kernels, shards(): pl.pallas_call(functools.partial(base_kernel, tile), out_shape=jax.ShapeD...  4.74 us
    pallas_call x1, Pallas kernels, shards(): pl.pallas_call(functools.partial(order_kernel, sizes, a_cols), out_shape=...  2.58 us
  transfers between devices with their start and end apart: 21, of which 9 were waited for; matrix products, arithmetic and copies ran while one was open for 2% of the time, Pallas kernels for 6%

profile of v1, /device:TPU:0, one launch (start us, length us, event | category | flops | bytes accessed | tf_op | source)
XLA Modules:
  0.0 105.0 jit_solution(10979895332932926709)
XLA Ops:
  3.5 7.4 %all-to-all-start = ((bf16[16,8,512]{2,1,0:T(8,128)(2,1)}), bf16[16,8,512]{2,1,0:T(8,128)(2,1)S(1)}, u32[]{:S(2)}, u32[]{:S(2)}) async-start(bf16[16,8,512]{2,1,0:T(8,128)(2,1)} %bitcast), calls=%async_computation | async-start | bytes 262144 | tf_op jit(solution)/shard_map/all_to_all | solution.py:253
  13.7 1.4 %copy-done.1 = bf16[1536,512]{1,0:T(8,128)(2,1)S(1)} copy-done((bf16[1536,512]{1,0:T(8,128)(2,1)S(1)}, bf16[1536,512]{1,0:T(8,128)(2,1)}, u32[]{:S(2)}) %copy-start.1) | copy-done | bytes 1572888
  15.1 4.7 %base.1.base_ref = f32[1536,512]{1,0:T(8,128)} custom-call(s32[1,1536]{1,0:T(1,128)S(1)} %reshape.27.dst_ref, bf16[256,512]{1,0:T(8,128)(2,1)S(1)} %copy-done.3, bf16[1536,512]{1,0:T(8,128)(2,1)S(1)} %copy-done, bf16[1536,512]{1,0:T(8,128)(2,1)S(1)} %copy-done.1), custom_call_target="tpu_custom_call" | custom-call | flops 1610612736 | bytes 6291456 | tf_op jit(solution)/shard_map/base/pallas_call | solution.py:257
  19.9 15.2 %edges.1 = (bf16[256,512]{1,0:T(8,128)(2,1)}, bf16[128,512]{1,0:T(8,128)(2,1)S(1)}, bf16[1024,384]{1,0:T(8,128)(2,1)S(1)}, bf16[1024,384]{1,0:T(8,128)(2,1)S(1)}...) custom-call(s32[1,1536]{1,0:T(1,128)S(1)} %reshape.26.slot_ref, s32[1,1536]{1,0:T(1,128)S(1)} %reshape.27.dst_ref, ...), custom_call_target="tpu_custom_call" | custom-call | tf_op jit(solution)/shard_map/edges/pallas_call | solution.py:267
  35.6 2.2 %collective-permute-done.10 = bf16[1024,128]{1,0:T(8,128)(2,1)S(1)} collective-permute-done((bf16[1024,128]{1,0:T(8,128)(2,1)S(1)}, bf16[1024,128]{1,0:T(8,128)(2,1)S(1)}, u32[]{:S(2)}, u32[]{:S(2)}) %collective-permute-start.10) | collective-permute-done | bytes 262176 | tf_op jit(solution)/shard_map/ppermute | solution.py:245
  37.9 2.0 %collective-permute-start.11 = (bf16[256,128]{1,0:T(8,128)(2,1)S(1)}, bf16[256,128]{1,0:T(8,128)(2,1)S(1)}, u32[]{:S(2)}, u32[]{:S(2)}) collective-permute-start(bf16[256,128]{1,0:T(8,128)(2,1)S(1)} %get-tuple-element.29), channel_id=1, source_target_pairs={{0,4},{1,5},{2,6},{3,7},{4,0},{5,1},{6,2},{7,3},{8,12},{9,13},{10,... | collective-permute-start | bytes 196616 | tf_op jit(solution)/shard_map/ppermute | solution.py:245
  39.8 2.4 %collective-permute-start.12 = (bf16[256,128]{1,0:T(8,128)(2,1)S(1)}, bf16[256,128]{1,0:T(8,128)(2,1)S(1)}, u32[]{:S(2)}, u32[]{:S(2)}) collective-permute-start(bf16[256,128]{1,0:T(8,128)(2,1)S(1)} %get-tuple-element.31), channel_id=1, source_target_pairs={{0,8},{1,9},{2,10},{3,11},{4,12},{5,13},{6,14},{7,15},{8,0},{9,1},... | collective-permute-start | bytes 196616 | tf_op jit(solution)/shard_map/ppermute | solution.py:245
  42.6 1.9 %collective-permute-start.1 = (bf16[512,384]{1,0:T(8,128)(2,1)S(1)}, bf16[512,384]{1,0:T(8,128)(2,1)S(1)}, u32[]{:S(2)}, u32[]{:S(2)}) collective-permute-start(bf16[512,384]{1,0:T(8,128)(2,1)S(1)} %slice.49), channel_id=1, source_target_pairs={{0,2},{1,3},{2,0},{3,1},{4,6},{5,7},{6,4},{7,5},{8,10},{9,11},{10,... | collective-permute-start | bytes 1179656 | tf_op jit(solution)/shard_map/ppermute | solution.py:245
  44.5 2.8 %collective-permute-done.12 = bf16[256,128]{1,0:T(8,128)(2,1)S(1)} collective-permute-done((bf16[256,128]{1,0:T(8,128)(2,1)S(1)}, bf16[256,128]{1,0:T(8,128)(2,1)S(1)}, u32[]{:S(2)}, u32[]{:S(2)}) %collective-permute-start.12) | collective-permute-done | bytes 65568 | tf_op jit(solution)/shard_map/ppermute | solution.py:245
  48.4 1.5 %collective-permute-start.14 = (bf16[128,128]{1,0:T(8,128)(2,1)S(1)}, bf16[128,128]{1,0:T(8,128)(2,1)S(1)}, u32[]{:S(2)}, u32[]{:S(2)}) collective-permute-start(bf16[128,128]{1,0:T(8,128)(2,1)S(1)} %slice.59), channel_id=1, source_target_pairs={{0,2},{1,3},{2,0},{3,1},{4,6},{5,7},{6,4},{7,5},{8,10},{9,11},{10,... | collective-permute-start | bytes 98312 | tf_op jit(solution)/shard_map/ppermute | solution.py:245
  49.9 4.0 %collective-permute-done.14 = bf16[128,128]{1,0:T(8,128)(2,1)S(1)} collective-permute-done((bf16[128,128]{1,0:T(8,128)(2,1)S(1)}, bf16[128,128]{1,0:T(8,128)(2,1)S(1)}, u32[]{:S(2)}, u32[]{:S(2)}) %collective-permute-start.14) | collective-permute-done | bytes 32800 | tf_op jit(solution)/shard_map/ppermute | solution.py:245
  53.9 1.7 %collective-permute-start.15 = (bf16[128,128]{1,0:T(8,128)(2,1)S(1)}, bf16[128,128]{1,0:T(8,128)(2,1)S(1)}, u32[]{:S(2)}, u32[]{:S(2)}) collective-permute-start(bf16[128,128]{1,0:T(8,128)(2,1)S(1)} %get-tuple-element.21), channel_id=1, source_target_pairs={{0,2},{1,3},{2,0},{3,1},{4,6},{5,7},{6,4},{7,5},{8,10},{9,11},{10,... | collective-permute-start | bytes 98312 | tf_op jit(solution)/shard_map/ppermute | solution.py:245
  56.4 3.3 %collective-permute-start.3 = (bf16[128,384]{1,0:T(8,128)(2,1)S(1)}, bf16[128,384]{1,0:T(8,128)(2,1)S(1)}, u32[]{:S(2)}, u32[]{:S(2)}) collective-permute-start(bf16[128,384]{1,0:T(8,128)(2,1)S(1)} %get-tuple-element.28), channel_id=1, source_target_pairs={{0,8},{1,9},{2,10},{3,11},{4,12},{5,13},{6,14},{7,15},{8,0},{9,1},... | collective-permute-start | bytes 294920 | tf_op jit(solution)/shard_map/ppermute | solution.py:245
  60.7 4.0 %collective-permute-done.3 = bf16[128,384]{1,0:T(8,128)(2,1)S(1)} collective-permute-done((bf16[128,384]{1,0:T(8,128)(2,1)S(1)}, bf16[128,384]{1,0:T(8,128)(2,1)S(1)}, u32[]{:S(2)}, u32[]{:S(2)}) %collective-permute-start.3) | collective-permute-done | bytes 98336 | tf_op jit(solution)/shard_map/ppermute | solution.py:245
  64.7 1.5 %collective-permute-done.4 = bf16[128,384]{1,0:T(8,128)(2,1)S(1)} collective-permute-done((bf16[128,384]{1,0:T(8,128)(2,1)S(1)}, bf16[128,384]{1,0:T(8,128)(2,1)S(1)}, u32[]{:S(2)}, u32[]{:S(2)}) %collective-permute-start.4) | collective-permute-done | bytes 98336 | tf_op jit(solution)/shard_map/ppermute | solution.py:245
  67.5 1.4 %collective-permute-start.6 = (bf16[128,384]{1,0:T(8,128)(2,1)S(1)}, bf16[128,384]{1,0:T(8,128)(2,1)S(1)}, u32[]{:S(2)}, u32[]{:S(2)}) collective-permute-start(bf16[128,384]{1,0:T(8,128)(2,1)S(1)} %get-tuple-element.23), channel_id=1, source_target_pairs={{0,8},{1,9},{2,10},{3,11},{4,12},{5,13},{6,14},{7,15},{8,0},{9,1},... | collective-permute-start | bytes 294920 | tf_op jit(solution)/shard_map/ppermute | solution.py:245
  68.9 1.8 %collective-permute-start.7 = (bf16[128,384]{1,0:T(8,128)(2,1)S(1)}, bf16[128,384]{1,0:T(8,128)(2,1)S(1)}, u32[]{:S(2)}, u32[]{:S(2)}) collective-permute-start(bf16[128,384]{1,0:T(8,128)(2,1)S(1)} %get-tuple-element.23), channel_id=1, source_target_pairs={{0,12},{1,13},{2,14},{3,15},{4,8},{5,9},{6,10},{7,11},{8,4},{9,5},... | collective-permute-start | bytes 294920 | tf_op jit(solution)/shard_map/ppermute | solution.py:245
  71.1 2.3 %collective-permute-start.17 = (bf16[256,128]{1,0:T(8,128)(2,1)S(1)}, bf16[256,128]{1,0:T(8,128)(2,1)S(1)}, u32[]{:S(2)}, u32[]{:S(2)}) collective-permute-start(bf16[256,128]{1,0:T(8,128)(2,1)S(1)} %pad_maximum_fusion.1), channel_id=1, source_target_pairs={{0,8},{1,9},{2,10},{3,11},{4,12},{5,13},{6,14},{7,15},{8,0},{9,1},... | collective-permute-start | bytes 196616 | tf_op jit(solution)/shard_map/ppermute | solution.py:245
  73.4 2.5 %collective-permute-start.18 = (bf16[256,128]{1,0:T(8,128)(2,1)S(1)}, bf16[256,128]{1,0:T(8,128)(2,1)S(1)}, u32[]{:S(2)}, u32[]{:S(2)}) collective-permute-start(bf16[256,128]{1,0:T(8,128)(2,1)S(1)} %pad_maximum_fusion.1), channel_id=1, source_target_pairs={{0,12},{1,13},{2,14},{3,15},{4,8},{5,9},{6,10},{7,11},{8,4},{9,5},... | collective-permute-start | bytes 196616 | tf_op jit(solution)/shard_map/ppermute | solution.py:245
  75.8 2.5 %collective-permute-done.6 = bf16[128,384]{1,0:T(8,128)(2,1)S(1)} collective-permute-done((bf16[128,384]{1,0:T(8,128)(2,1)S(1)}, bf16[128,384]{1,0:T(8,128)(2,1)S(1)}, u32[]{:S(2)}, u32[]{:S(2)}) %collective-permute-start.6) | collective-permute-done | bytes 98336 | tf_op jit(solution)/shard_map/ppermute | solution.py:245
  79.1 7.1 %collective-permute-done.8 = bf16[512,384]{1,0:T(8,128)(2,1)S(1)} collective-permute-done((bf16[512,384]{1,0:T(8,128)(2,1)S(1)}, bf16[512,384]{1,0:T(8,128)(2,1)S(1)}, u32[]{:S(2)}, u32[]{:S(2)}) %collective-permute-start.8) | collective-permute-done | bytes 393248 | tf_op jit(solution)/shard_map/ppermute | solution.py:245
  87.1 13.3 %all_to_all.10 = bf16[16,8,512]{2,1,0:T(8,128)(2,1)S(1)} all-to-all(bf16[16,8,512]{2,1,0:T(8,128)(2,1)S(1)} %bitcast.6), channel_id=1, replica_groups=mesh['groups'=2,'band'=16] {'band'}, dimensions={0} | all-to-all | bytes 262144 | tf_op jit(solution)/shard_map/all_to_all | solution.py:298
  100.5 1.7 %put.1 = f32[1024,512]{1,0:T(8,128)} custom-call(s32[1,128]{1,0:T(1,128)S(1)} %copy-done.8, bf16[128,512]{1,0:T(8,128)(2,1)S(1)} %bitcast.5), custom_call_target="tpu_custom_call" | custom-call | tf_op jit(solution)/shard_map/put/pallas_call | solution.py:301
  102.4 2.6 %order.1 = (f32[1536,512]{1,0:T(8,128)}, f32[512,512]{1,0:T(8,128)}) custom-call(bf16[2048,384]{1,0:T(8,128)(2,1)S(1)} %constant_dynamic-update-slice_fusion.5.a_ref, bf16[2048,128]{1,0:T(8,128)(2,1)S(1)} %constant_dynamic-update-slice_fusion.16.b_ref), custom_call_target="tpu_custom_call" | custom-call | tf_op jit(solution)/shard_map/order/pallas_call | solution.py:328
  (68 shorter events, 12.9 us)
Async XLA Ops:
  2.5 9.8 %copy-start.3 = (bf16[256,512]{1,0:T(8,128)(2,1)S(1)}, bf16[256,512]{1,0:T(8,128)(2,1)}, u32[]{:S(2)}) copy-start(bf16[256,512]{1,0:T(8,128)(2,1)} %mesh_ref.3) | copy-start | bytes 786436
  3.5 16.4 %all-to-all-start = ((bf16[16,8,512]{2,1,0:T(8,128)(2,1)}), bf16[16,8,512]{2,1,0:T(8,128)(2,1)S(1)}, u32[]{:S(2)}, u32[]{:S(2)}) async-start(bf16[16,8,512]{2,1,0:T(8,128)(2,1)} %bitcast), calls=%async_computation | async-start | bytes 262144 | tf_op jit(solution)/shard_map/all_to_all | solution.py:253
  15.1 4.8 %copy-start.6 = (bf16[256,512]{1,0:T(8,128)(2,1)S(1)}, bf16[256,512]{1,0:T(8,128)(2,1)}, u32[]{:S(2)}) copy-start(bf16[256,512]{1,0:T(8,128)(2,1)} %cot_ref.1) | copy-start | bytes 786436
  35.1 7.3 %collective-permute-start = (bf16[1024,384]{1,0:T(8,128)(2,1)S(1)}, bf16[1024,384]{1,0:T(8,128)(2,1)S(1)}, u32[]{:S(2)}, u32[]{:S(2)}) collective-permute-start(bf16[1024,384]{1,0:T(8,128)(2,1)S(1)} %get-tuple-element.15), channel_id=1, source_target_pairs={{0,1},{1,0},{2,3},{3,2},{4,5},{5,4},{6,7},{7,6},{8,9},{9,8},{10,11... | collective-permute-start | bytes 2359304 | tf_op jit(solution)/shard_map/ppermute | solution.py:245
  35.5 2.3 %collective-permute-start.10 = (bf16[1024,128]{1,0:T(8,128)(2,1)S(1)}, bf16[1024,128]{1,0:T(8,128)(2,1)S(1)}, u32[]{:S(2)}, u32[]{:S(2)}) collective-permute-start(bf16[1024,128]{1,0:T(8,128)(2,1)S(1)} %get-tuple-element.17), channel_id=1, source_target_pairs={{0,1},{1,0},{2,3},{3,2},{4,5},{5,4},{6,7},{7,6},{8,9},{9,8},{10,11... | collective-permute-start | bytes 786440 | tf_op jit(solution)/shard_map/ppermute | solution.py:245
  37.9 6.7 %collective-permute-start.11 = (bf16[256,128]{1,0:T(8,128)(2,1)S(1)}, bf16[256,128]{1,0:T(8,128)(2,1)S(1)}, u32[]{:S(2)}, u32[]{:S(2)}) collective-permute-start(bf16[256,128]{1,0:T(8,128)(2,1)S(1)} %get-tuple-element.29), channel_id=1, source_target_pairs={{0,4},{1,5},{2,6},{3,7},{4,0},{5,1},{6,2},{7,3},{8,12},{9,13},{10,... | collective-permute-start | bytes 196616 | tf_op jit(solution)/shard_map/ppermute | solution.py:245
  39.8 7.5 %collective-permute-start.12 = (bf16[256,128]{1,0:T(8,128)(2,1)S(1)}, bf16[256,128]{1,0:T(8,128)(2,1)S(1)}, u32[]{:S(2)}, u32[]{:S(2)}) collective-permute-start(bf16[256,128]{1,0:T(8,128)(2,1)S(1)} %get-tuple-element.31), channel_id=1, source_target_pairs={{0,8},{1,9},{2,10},{3,11},{4,12},{5,13},{6,14},{7,15},{8,0},{9,1},... | collective-permute-start | bytes 196616 | tf_op jit(solution)/shard_map/ppermute | solution.py:245
  42.2 6.2 %collective-permute-start.13 = (bf16[256,128]{1,0:T(8,128)(2,1)S(1)}, bf16[256,128]{1,0:T(8,128)(2,1)S(1)}, u32[]{:S(2)}, u32[]{:S(2)}) collective-permute-start(bf16[256,128]{1,0:T(8,128)(2,1)S(1)} %get-tuple-element.30), channel_id=1, source_target_pairs={{0,12},{1,13},{2,14},{3,15},{4,8},{5,9},{6,10},{7,11},{8,4},{9,5},... | collective-permute-start | bytes 196616 | tf_op jit(solution)/shard_map/ppermute | solution.py:245
  42.6 13.1 %collective-permute-start.1 = (bf16[512,384]{1,0:T(8,128)(2,1)S(1)}, bf16[512,384]{1,0:T(8,128)(2,1)S(1)}, u32[]{:S(2)}, u32[]{:S(2)}) collective-permute-start(bf16[512,384]{1,0:T(8,128)(2,1)S(1)} %slice.49), channel_id=1, source_target_pairs={{0,2},{1,3},{2,0},{3,1},{4,6},{5,7},{6,4},{7,5},{8,10},{9,11},{10,... | collective-permute-start | bytes 1179656 | tf_op jit(solution)/shard_map/ppermute | solution.py:245
  48.4 5.5 %collective-permute-start.14 = (bf16[128,128]{1,0:T(8,128)(2,1)S(1)}, bf16[128,128]{1,0:T(8,128)(2,1)S(1)}, u32[]{:S(2)}, u32[]{:S(2)}) collective-permute-start(bf16[128,128]{1,0:T(8,128)(2,1)S(1)} %slice.59), channel_id=1, source_target_pairs={{0,2},{1,3},{2,0},{3,1},{4,6},{5,7},{6,4},{7,5},{8,10},{9,11},{10,... | collective-permute-start | bytes 98312 | tf_op jit(solution)/shard_map/ppermute | solution.py:245
  53.9 16.8 %collective-permute-start.15 = (bf16[128,128]{1,0:T(8,128)(2,1)S(1)}, bf16[128,128]{1,0:T(8,128)(2,1)S(1)}, u32[]{:S(2)}, u32[]{:S(2)}) collective-permute-start(bf16[128,128]{1,0:T(8,128)(2,1)S(1)} %get-tuple-element.21), channel_id=1, source_target_pairs={{0,2},{1,3},{2,0},{3,1},{4,6},{5,7},{6,4},{7,5},{8,10},{9,11},{10,... | collective-permute-start | bytes 98312 | tf_op jit(solution)/shard_map/ppermute | solution.py:245
  55.8 4.9 %collective-permute-start.2 = (bf16[128,384]{1,0:T(8,128)(2,1)S(1)}, bf16[128,384]{1,0:T(8,128)(2,1)S(1)}, u32[]{:S(2)}, u32[]{:S(2)}) collective-permute-start(bf16[128,384]{1,0:T(8,128)(2,1)S(1)} %get-tuple-element.26), channel_id=1, source_target_pairs={{0,4},{1,5},{2,6},{3,7},{4,0},{5,1},{6,2},{7,3},{8,12},{9,13},{10,... | collective-permute-start | bytes 294920 | tf_op jit(solution)/shard_map/ppermute | solution.py:245
  56.4 8.3 %collective-permute-start.3 = (bf16[128,384]{1,0:T(8,128)(2,1)S(1)}, bf16[128,384]{1,0:T(8,128)(2,1)S(1)}, u32[]{:S(2)}, u32[]{:S(2)}) collective-permute-start(bf16[128,384]{1,0:T(8,128)(2,1)S(1)} %get-tuple-element.28), channel_id=1, source_target_pairs={{0,8},{1,9},{2,10},{3,11},{4,12},{5,13},{6,14},{7,15},{8,0},{9,1},... | collective-permute-start | bytes 294920 | tf_op jit(solution)/shard_map/ppermute | solution.py:245
  59.7 6.5 %collective-permute-start.4 = (bf16[128,384]{1,0:T(8,128)(2,1)S(1)}, bf16[128,384]{1,0:T(8,128)(2,1)S(1)}, u32[]{:S(2)}, u32[]{:S(2)}) collective-permute-start(bf16[128,384]{1,0:T(8,128)(2,1)S(1)} %get-tuple-element.27), channel_id=1, source_target_pairs={{0,12},{1,13},{2,14},{3,15},{4,8},{5,9},{6,10},{7,11},{8,4},{9,5},... | collective-permute-start | bytes 294920 | tf_op jit(solution)/shard_map/ppermute | solution.py:245
  66.3 7.1 %collective-permute-start.5 = (bf16[128,384]{1,0:T(8,128)(2,1)S(1)}, bf16[128,384]{1,0:T(8,128)(2,1)S(1)}, u32[]{:S(2)}, u32[]{:S(2)}) collective-permute-start(bf16[128,384]{1,0:T(8,128)(2,1)S(1)} %get-tuple-element.23), channel_id=1, source_target_pairs={{0,4},{1,5},{2,6},{3,7},{4,0},{5,1},{6,2},{7,3},{8,12},{9,13},{10,... | collective-permute-start | bytes 294920 | tf_op jit(solution)/shard_map/ppermute | solution.py:245
  67.5 10.8 %collective-permute-start.6 = (bf16[128,384]{1,0:T(8,128)(2,1)S(1)}, bf16[128,384]{1,0:T(8,128)(2,1)S(1)}, u32[]{:S(2)}, u32[]{:S(2)}) collective-permute-start(bf16[128,384]{1,0:T(8,128)(2,1)S(1)} %get-tuple-element.23), channel_id=1, source_target_pairs={{0,8},{1,9},{2,10},{3,11},{4,12},{5,13},{6,14},{7,15},{8,0},{9,1},... | collective-permute-start | bytes 294920 | tf_op jit(solution)/shard_map/ppermute | solution.py:245
  68.9 9.4 %collective-permute-start.7 = (bf16[128,384]{1,0:T(8,128)(2,1)S(1)}, bf16[128,384]{1,0:T(8,128)(2,1)S(1)}, u32[]{:S(2)}, u32[]{:S(2)}) collective-permute-start(bf16[128,384]{1,0:T(8,128)(2,1)S(1)} %get-tuple-element.23), channel_id=1, source_target_pairs={{0,12},{1,13},{2,14},{3,15},{4,8},{5,9},{6,10},{7,11},{8,4},{9,5},... | collective-permute-start | bytes 294920 | tf_op jit(solution)/shard_map/ppermute | solution.py:245
  70.7 15.7 %collective-permute-start.16 = (bf16[256,128]{1,0:T(8,128)(2,1)S(1)}, bf16[256,128]{1,0:T(8,128)(2,1)S(1)}, u32[]{:S(2)}, u32[]{:S(2)}) collective-permute-start(bf16[256,128]{1,0:T(8,128)(2,1)S(1)} %pad_maximum_fusion.1), channel_id=1, source_target_pairs={{0,4},{1,5},{2,6},{3,7},{4,0},{5,1},{6,2},{7,3},{8,12},{9,13},{10,... | collective-permute-start | bytes 196616 | tf_op jit(solution)/shard_map/ppermute | solution.py:245
  71.1 15.5 %collective-permute-start.17 = (bf16[256,128]{1,0:T(8,128)(2,1)S(1)}, bf16[256,128]{1,0:T(8,128)(2,1)S(1)}, u32[]{:S(2)}, u32[]{:S(2)}) collective-permute-start(bf16[256,128]{1,0:T(8,128)(2,1)S(1)} %pad_maximum_fusion.1), channel_id=1, source_target_pairs={{0,8},{1,9},{2,10},{3,11},{4,12},{5,13},{6,14},{7,15},{8,0},{9,1},... | collective-permute-start | bytes 196616 | tf_op jit(solution)/shard_map/ppermute | solution.py:245
  73.4 13.2 %collective-permute-start.18 = (bf16[256,128]{1,0:T(8,128)(2,1)S(1)}, bf16[256,128]{1,0:T(8,128)(2,1)S(1)}, u32[]{:S(2)}, u32[]{:S(2)}) collective-permute-start(bf16[256,128]{1,0:T(8,128)(2,1)S(1)} %pad_maximum_fusion.1), channel_id=1, source_target_pairs={{0,12},{1,13},{2,14},{3,15},{4,8},{5,9},{6,10},{7,11},{8,4},{9,5},... | collective-permute-start | bytes 196616 | tf_op jit(solution)/shard_map/ppermute | solution.py:245
  78.4 7.8 %collective-permute-start.8 = (bf16[512,384]{1,0:T(8,128)(2,1)S(1)}, bf16[512,384]{1,0:T(8,128)(2,1)S(1)}, u32[]{:S(2)}, u32[]{:S(2)}) collective-permute-start(bf16[512,384]{1,0:T(8,128)(2,1)S(1)} %pad_maximum_fusion), channel_id=1, source_target_pairs={{0,2},{1,3},{2,0},{3,1},{4,6},{5,7},{6,4},{7,5},{8,10},{9,11},{10,... | collective-permute-start | bytes 1179656 | tf_op jit(solution)/shard_map/ppermute | solution.py:245
  79.0 21.5 %copy-start.8 = (s32[1,128]{1,0:T(1,128)S(1)}, s32[1,128]{1,0:T(1,128)}, u32[]{:S(2)}) copy-start(s32[1,128]{1,0:T(1,128)} %rows_ref.3) | copy-start | bytes 1540
  86.4 15.9 %collective-permute-start.9 = (bf16[1024,384]{1,0:T(8,128)(2,1)S(1)}, bf16[1024,384]{1,0:T(8,128)(2,1)S(1)}, u32[]{:S(2)}, u32[]{:S(2)}) collective-permute-start(bf16[1024,384]{1,0:T(8,128)(2,1)S(1)} %get-tuple-element.24), channel_id=1, source_target_pairs={{0,1},{1,0},{2,3},{3,2},{4,5},{5,4},{6,7},{7,6},{8,9},{9,8},{10,11... | collective-permute-start | bytes 2359304 | tf_op jit(solution)/shard_map/ppermute | solution.py:245
  86.6 15.6 %collective-permute-start.19 = (bf16[1024,128]{1,0:T(8,128)(2,1)S(1)}, bf16[1024,128]{1,0:T(8,128)(2,1)S(1)}, u32[]{:S(2)}, u32[]{:S(2)}) collective-permute-start(bf16[1024,128]{1,0:T(8,128)(2,1)S(1)} %get-tuple-element.38), channel_id=1, source_target_pairs={{0,1},{1,0},{2,3},{3,2},{4,5},{5,4},{6,7},{7,6},{8,9},{9,8},{10,11... | collective-permute-start | bytes 786440 | tf_op jit(solution)/shard_map/ppermute | solution.py:245
  (6 other events, 14.2 us)

commit v2 on v1

v2 whole, which is shorter than its diff:
```python
import functools

import jax
import jax.numpy as jnp
from jax import lax
from jax.experimental import pallas as pl
from jax.experimental.pallas import tpu as pltpu
from jax.sharding import PartitionSpec as P

BF16 = jnp.bfloat16
F32 = jnp.float32
VMEM_LIMIT = 50 * 1024 * 1024


def dot_nn(a, b):
    return jnp.dot(a, b, preferred_element_type=F32)


def dot_tn(a, b):
    return lax.dot_general(a, b, (((0,), (0,)), ((), ())), preferred_element_type=F32)


def dot_nt(a, b):
    return lax.dot_general(a, b, (((1,), (1,)), ((), ())), preferred_element_type=F32)


def split(value):
    high = value.astype(BF16)
    low = (value - high.astype(F32)).astype(BF16)
    return high, low


def one_hot_rows(index_row, rows):
    shape = (rows, index_row.shape[1])
    hit = lax.broadcasted_iota(jnp.int32, shape, 0) == index_row
    return jnp.where(hit, 1.0, 0.0).astype(BF16)


def one_hot_columns(index_row, columns):
    lanes = index_row.shape[1]
    index = jnp.transpose(jnp.broadcast_to(index_row, (lanes, lanes)))
    pieces = []
    for start in range(0, columns, lanes):
        hit = lax.broadcasted_iota(jnp.int32, (lanes, lanes), 1) + start == index
        pieces.append(jnp.where(hit, 1.0, 0.0).astype(BF16))
    return pieces[0] if len(pieces) == 1 else jnp.concatenate(pieces, axis=1)


def tile_rows(index_ref, at, lines, rows):
    found = [one_hot_rows(index_ref[pl.ds(at * lines + k, 1), :], rows) for k in range(lines)]
    return jnp.concatenate(found, axis=1)


def tile_columns(index_ref, at, lines, columns):
    found = [one_hot_columns(index_ref[pl.ds(at * lines + k, 1), :], columns) for k in range(lines)]
    return jnp.concatenate(found, axis=0)


def place_of(sizes):
    outer, inner = sizes
    me = lax.axis_index("band")
    return me // (2 * inner), (me // 2) % inner, me % 2


def owner_at(sizes, far_outer, far_inner, far_core):
    my_outer, my_inner, my_core = place_of(sizes)
    return ((my_outer ^ far_outer) * sizes[1] + (my_inner ^ far_inner)) * 2 + (my_core ^ far_core)


def params():
    return pltpu.CompilerParams(vmem_limit_bytes=VMEM_LIMIT)


def cost(flops, nbytes):
    return pl.CostEstimate(flops=flops, bytes_accessed=nbytes, transcendentals=0)


def pick_kernel(rows_ref, grid_ref, out_ref):
    chosen = one_hot_rows(rows_ref[...], grid_ref.shape[0])
    out_ref[...] = dot_tn(chosen, grid_ref[...]).astype(BF16)


def put_kernel(sizes, rows_ref, back_ref, out_ref, ordered_ref):
    outer, inner = sizes
    cap = back_ref.shape[0] // (2 * outer * inner)
    back = back_ref[...].astype(F32)
    for at in range(2 * outer * inner):
        far_core, far_inner, far_outer = at % 2, at // 2 % inner, at // (2 * inner)
        owner = owner_at(sizes, far_outer, far_inner, far_core)
        ordered_ref[pl.ds(pl.multiple_of(owner * cap, cap), cap), :] = back[at * cap : (at + 1) * cap]
    chosen = one_hot_rows(rows_ref[...], out_ref.shape[0])
    out_ref[...] = dot_nn(chosen, ordered_ref[...].astype(BF16))


def base_kernel(
    lines,
    dst_ref,
    mesh_ref,
    edge_ref,
    cot_ref,
    w1_ref,
    wn1_ref,
    wn2_ref,
    base_ref,
    turned_ref,
    node_ref,
    cot_out_ref,
):
    width = mesh_ref.shape[1]
    mesh_rows = mesh_ref.shape[0]
    tile = lines * 128
    high, low = split(dot_nn(mesh_ref[...], w1_ref[width : 2 * width, :]))
    pair = jnp.concatenate([high, low], axis=0)

    def step(at, carry):
        rows = pl.ds(pl.multiple_of(at * tile, tile), tile)
        to_mesh = tile_columns(dst_ref, at, lines, mesh_rows)
        twice = jnp.concatenate([to_mesh, to_mesh], axis=1)
        edge = edge_ref[rows, :]
        base_ref[rows, :] = dot_nn(edge, w1_ref[2 * width :, :]) + dot_nn(twice, pair)
        turned_ref[:, rows] = jnp.transpose(edge)
        return carry

    lax.fori_loop(0, edge_ref.shape[0] // tile, step, 0)
    node_ref[...] = dot_nn(mesh_ref[...], wn1_ref[:width, :])
    cot_out_ref[...] = dot_nt(cot_ref[...], wn2_ref[...])


def main_kernel(
    lines,
    sizes,
    slot_ref,
    dst_ref,
    slots_ref,
    base_ref,
    turned_ref,
    mesh_ref,
    node_ref,
    cot_ref,
    w1_ref,
    w2_ref,
    wn1_ref,
    wn2_ref,
    *rest,
):
    outer, inner = sizes
    mesh_out_ref, d_slots_ref = rest[:2]
    send_refs, keep_refs = rest[2 : 2 + outer], rest[2 + outer : 2 + 2 * outer]
    slope_ref, value_ref, both_ref, grads_ref, slot_grads_ref, ordered_ref = rest[2 + 2 * outer :]
    width = mesh_ref.shape[1]
    mesh_rows = mesh_ref.shape[0]
    slot_rows = slots_ref.shape[0]
    tile = lines * 128
    tiles = base_ref.shape[0] // tile

    high, low = split(dot_nn(slots_ref[...], w1_ref[:width, :]))
    slot_pair = jnp.concatenate([high, low], axis=0)

    def forward(at, carry):
        rows = pl.ds(pl.multiple_of(at * tile, tile), tile)
        from_slot = tile_columns(slot_ref, at, lines, slot_rows)
        twice = jnp.concatenate([from_slot, from_slot], axis=1)
        pre = base_ref[rows, :] + dot_nn(twice, slot_pair)
        sigma = 0.5 + 0.5 * jnp.tanh(0.5 * pre)
        hidden = pre * sigma
        slope_ref[rows, :] = sigma + hidden * (1.0 - sigma)
        value_ref[rows, :] = hidden.astype(BF16)
        both_ref[:slot_rows, rows] = tile_rows(slot_ref, at, lines, slot_rows)
        both_ref[slot_rows:, rows] = tile_rows(dst_ref, at, lines, mesh_rows)
        return carry

    lax.fori_loop(0, tiles, forward, 0)

    hidden_high, hidden_low = split(dot_nn(both_ref[slot_rows:, :], value_ref[...]))
    received = (dot_nn(hidden_high, w2_ref[...]) + dot_nn(hidden_low, w2_ref[...])).astype(BF16)
    mesh = mesh_ref[...]
    pre_node = node_ref[...] + dot_nn(received, wn1_ref[width:, :])
    sigma = 0.5 + 0.5 * jnp.tanh(0.5 * pre_node)
    node = pre_node * sigma
    slope = sigma + node * (1.0 - sigma)
    d_pre_node = (cot_ref[...] * slope).astype(BF16)
    d_received = dot_nt(d_pre_node, wn1_ref[width:, :]).astype(BF16)
    high, low = split(dot_nt(d_received, w2_ref[...]))
    back_pair = jnp.concatenate([high, low], axis=0)

    def backward(at, carry):
        rows = pl.ds(pl.multiple_of(at * tile, tile), tile)
        to_mesh = tile_columns(dst_ref, at, lines, mesh_rows)
        twice = jnp.concatenate([to_mesh, to_mesh], axis=1)
        value_ref[rows, :] = (dot_nn(twice, back_pair) * slope_ref[rows, :]).astype(BF16)
        return carry

    lax.fori_loop(0, tiles, backward, 0)

    grads_ref[3 * width :, :] = dot_tn(hidden_high, d_received) + dot_tn(hidden_low, d_received)
    mesh_out_ref[...] = (mesh.astype(F32) + dot_nn(node.astype(BF16), wn2_ref[...])).astype(BF16)
    sums = dot_nn(both_ref[...], value_ref[...])
    slot_high, slot_low = split(sums[:slot_rows])
    slot_grads_ref[...] = dot_nt(slot_high, w1_ref[:width, :]) + dot_nt(slot_low, w1_ref[:width, :])
    slots = slots_ref[...]
    grads_ref[:width, :] = dot_tn(slots, slot_high) + dot_tn(slots, slot_low)
    mesh_high, mesh_low = split(sums[slot_rows:])
    grads_ref[width : 2 * width, :] = dot_tn(mesh, mesh_high) + dot_tn(mesh, mesh_low)
    grads_ref[2 * width : 3 * width, :] = dot_nn(turned_ref[...], value_ref[...])

    chunk = grads_ref.shape[0] // (2 * outer * inner)
    cap = slot_rows // (2 * outer * inner)
    for far_core in range(2):
        for far_inner in range(inner):
            for far_outer in range(outer):
                owner = owner_at(sizes, far_outer, far_inner, far_core)
                at = (far_core * inner + far_inner) * outer + far_outer
                from_rows = pl.ds(pl.multiple_of(owner * cap, cap), cap)
                ordered_ref[at * cap : (at + 1) * cap, :] = slot_grads_ref[from_rows, :]
                value = grads_ref[pl.ds(pl.multiple_of(owner * chunk, chunk), chunk), :]
                rows = slice(far_inner * chunk, (far_inner + 1) * chunk)
                if far_core:
                    send_refs[far_outer][rows, :] = value.astype(BF16)
                else:
                    keep_refs[far_outer][rows, :] = value
    d_slots_ref[...] = ordered_ref[...].astype(BF16)


def order_kernel(sizes, *refs):
    outer, inner = sizes
    first_ref, second_ref = refs[-2:]
    pieces = refs[:-2]
    chunk = pieces[0].shape[0]
    first_chunks = first_ref.shape[0] // chunk

    for at, piece in enumerate(pieces):
        far_outer, far_inner, far_core = at % outer, at // outer % inner, at // (outer * inner)
        owner = owner_at(sizes, far_outer, far_inner, far_core)
        value = piece[...].astype(F32)

        @pl.when(owner < first_chunks)
        def _():
            first_ref[pl.ds(pl.multiple_of(owner * chunk, chunk), chunk), :] = value

        @pl.when(owner >= first_chunks)
        def _():
            start = (owner - first_chunks) * chunk
            second_ref[pl.ds(pl.multiple_of(start, chunk), chunk), :] = value


def shards(
    sizes,
    grid_latent,
    mesh_latent,
    edge_latent,
    mesh_cot,
    send_rows,
    edge_slot,
    edge_dst,
    w_edge1,
    w_edge2,
    w_node1,
    w_node2,
):
    outer, inner = sizes
    band_count = lax.axis_size("band")
    width = grid_latent.shape[1]
    hidden_width = w_edge1.shape[1]
    edges = edge_latent.shape[0]
    mesh_rows = mesh_latent.shape[0]
    slot_rows = send_rows.shape[1]
    lines = 2
    slot_index = edge_slot.reshape(edges // 128, 128)
    dst_index = edge_dst.reshape(edges // 128, 128)

    def permute(value, stride, size, shift):
        pairs = []
        for source in range(band_count):
            place = (source // stride) % size
            pairs.append((source, source + ((place ^ shift) - place) * stride))
        return lax.ppermute(value, "band", pairs)

    def to_core(value):
        return permute(value, 1, 2, 1)

    def to_inner(value, shift):
        return permute(value, 2, inner, shift)

    def to_outer(value, shift):
        return permute(value, 2 * inner, outer, shift)

    outgoing = pl.pallas_call(
        pick_kernel,
        out_shape=jax.ShapeDtypeStruct((slot_rows, width), BF16),
        compiler_params=params(),
        name="pick",
    )(send_rows, grid_latent)
    slots = lax.all_to_all(
        outgoing.reshape(band_count, -1, width), "band", split_axis=0, concat_axis=0, tiled=True
    ).reshape(slot_rows, width)

    base, turned, node, cot = pl.pallas_call(
        functools.partial(base_kernel, lines),
        out_shape=[
            jax.ShapeDtypeStruct((edges, hidden_width), F32),
            jax.ShapeDtypeStruct((width, edges), BF16),
            jax.ShapeDtypeStruct((mesh_rows, hidden_width), F32),
            jax.ShapeDtypeStruct((mesh_rows, hidden_width), F32),
        ],
        compiler_params=params(),
        cost_estimate=cost(2 * edges * width * hidden_width * 2, edges * width * 8),
        name="base",
    )(dst_index, mesh_latent, edge_latent, mesh_cot, w_edge1, w_node1, w_node2)

    grad_rows = 3 * width + hidden_width
    chunk = grad_rows // band_count
    group = (inner * chunk, hidden_width)
    mesh_out, d_slots, *sides = pl.pallas_call(
        functools.partial(main_kernel, lines, sizes),
        out_shape=[
            jax.ShapeDtypeStruct((mesh_rows, width), BF16),
            jax.ShapeDtypeStruct((slot_rows, width), BF16),
        ]
        + [jax.ShapeDtypeStruct(group, BF16)] * outer
        + [jax.ShapeDtypeStruct(group, F32)] * outer,
        scratch_shapes=[
            pltpu.VMEM((edges, hidden_width), F32),
            pltpu.VMEM((edges, hidden_width), BF16),
            pltpu.VMEM((slot_rows + mesh_rows, edges), BF16),
            pltpu.VMEM((grad_rows, hidden_width), F32),
            pltpu.VMEM((slot_rows, width), F32),
            pltpu.VMEM((slot_rows, width), F32),
        ],
        compiler_params=params(),
        name="edges",
    )(
        slot_index,
        dst_index,
        slots,
        base,
        turned,
        mesh_latent,
        node,
        cot,
        w_edge1,
        w_edge2,
        w_node1,
        w_node2,
    )
    sends, keeps = sides[:outer], sides[outer:]

    own_sums = None
    arrived = []
    for far_outer in range(outer - 1, -1, -1):
        half = keeps[far_outer] + to_core(sends[far_outer]).astype(F32)
        total = half[:chunk]
        for far_inner in range(1, inner):
            part = half[far_inner * chunk : (far_inner + 1) * chunk].astype(BF16)
            total = total + to_inner(part, far_inner).astype(F32)
        if far_outer:
            arrived.append(to_outer(total.astype(BF16), far_outer))
        else:
            own_sums = total
    for value in arrived:
        own_sums = own_sums + value.astype(F32)
    own = own_sums.astype(BF16)

    pieces = [own] + [to_outer(own, far_outer) for far_outer in range(1, outer)]
    for far_inner in range(1, inner):
        pieces += [to_inner(value, far_inner) for value in pieces[:outer]]
    pieces += [to_core(value) for value in pieces]

    cap = slot_rows // band_count
    back = d_slots.reshape(2, inner, outer, cap, width)
    back = jnp.stack([back[0], to_core(back[1])], axis=2)
    back = jnp.stack([back[0]] + [to_inner(back[k], k) for k in range(1, inner)], axis=1)
    back = jnp.stack([back[0]] + [to_outer(back[k], k) for k in range(1, outer)], axis=0)
    grid_grad = pl.pallas_call(
        functools.partial(put_kernel, sizes),
        out_shape=jax.ShapeDtypeStruct(grid_latent.shape, F32),
        scratch_shapes=[pltpu.VMEM((slot_rows, width), F32)],
        compiler_params=params(),
        name="put",
    )(send_rows, back.reshape(slot_rows, width))

    grad_edge1, grad_edge2 = pl.pallas_call(
        functools.partial(order_kernel, sizes),
        out_shape=[
            jax.ShapeDtypeStruct((3 * width, hidden_width), F32),
            jax.ShapeDtypeStruct((hidden_width, width), F32),
        ],
        compiler_params=params(),
        name="order",
    )(*pieces)
    return (mesh_out, grid_grad, grad_edge1, grad_edge2)


def solution(mesh):
    chips = mesh.shape["band"] // 2
    inner = 1
    while inner * inner * 4 <= chips:
        inner *= 2
    sizes = (chips // inner, inner)
    in_specs = (
        P(("groups", "band"), None),
        P(("groups", "band"), None),
        P(("groups", "band"), None),
        P(("groups", "band"), None),
        P("band", None),
        P("band"),
        P("band"),
        P(),
        P(),
        P(),
        P(),
    )
    out_specs = (
        P(("groups", "band"), None),
        P(("groups", "band"), None),
        P("groups", None),
        P("groups", None),
    )
    return jax.shard_map(
        functools.partial(shards, sizes), mesh=mesh, in_specs=in_specs, out_specs=out_specs, check_vma=False
    )
```

time: 105 us -> 93.4 us (0.89)
  blocking collectives: 13.3 us -> 0 us
  waiting for transfers between devices: 25.5 us -> 20.5 us
  starting transfers between devices: 32.8 us -> 36.3 us
  local copies, waits for them, and re-layouts: 6.74 us -> 8.42 us
  Pallas kernels: 25.2 us -> 26.4 us
    all_to_all x1 -> x0, blocking collectives: 13.3 us -> none  [shards(): lax.all_to_all(d_slots.reshape(band_count, -1, width), 'band', split_axis...]
    ppermute x20 -> x31, waiting for transfers between devices: 25.5 us -> 20.5 us  [permute(): return lax.ppermute(value, 'band', pairs)]
    ppermute x20 -> x31, starting transfers between devices: 25.4 us -> 28.9 us  [permute(): return lax.ppermute(value, 'band', pairs)]
    unnamed x26, local copies, waits for them, and re-layouts: 4.89 us -> 8.33 us
    reshape x2 -> x0, local copies, waits for them, and re-layouts: 1.41 us -> none  [the longest x1 0.7 us: shards(): dst_row = edge_dst.reshape(1, edges)]
    pallas_call x4, Pallas kernels: 24.2 us -> 25.4 us  [the longest x1 13.8 us: shards(): pl.pallas_call(functools.partial(main_kernel, lines, sizes), out_shape=[j...]
  transfers between devices with their start and end apart: 21 -> 32, of which waited for: 9 -> 8; matrix products, arithmetic and copies ran while one was open for 2% -> 1% of each run, Pallas kernels for 6% -> 10%
where the time goes in v2:
time: 93.4 us; the launch traced here: 92.9 us
  starting transfers between devices  36.3 us (39%)
  Pallas kernels  26.4 us (28%)
  waiting for transfers between devices  20.5 us (22%)
  local copies, waits for them, and re-layouts  8.42 us (9%)
    ppermute x31, starting transfers between devices, permute(): return lax.ppermute(value, 'band', pairs)  28.9 us
    ppermute x31, waiting for transfers between devices, permute(): return lax.ppermute(value, 'band', pairs)  20.5 us
    pallas_call x1, Pallas kernels, shards(): pl.pallas_call(functools.partial(main_kernel, lines, sizes), out_shape=[j...  13.8 us
    unnamed x26, local copies, waits for them, and re-layouts  8.33 us
    all_to_all x1, starting transfers between devices, shards(): lax.all_to_all(outgoing.reshape(band_count, -1, width), 'band', split_axi...  7.38 us
    pallas_call x1, Pallas kernels, shards(): pl.pallas_call(functools.partial(base_kernel, lines), out_shape=[jax.Shap...  7.32 us
    pallas_call x1, Pallas kernels, shards(): pl.pallas_call(functools.partial(order_kernel, sizes), out_shape=[jax.Sha...  2.5 us
  transfers between devices with their start and end apart: 32, of which 8 were waited for; matrix products, arithmetic and copies ran while one was open for 1% of the time, Pallas kernels for 10%

profile of v2, /device:TPU:0, one launch (start us, length us, event | category | flops | bytes accessed | tf_op | source)
XLA Modules:
  0.0 92.9 jit_solution(1927443763320080940)
XLA Ops:
  3.5 7.4 %all-to-all-start = ((bf16[16,8,512]{2,1,0:T(8,128)(2,1)}), bf16[16,8,512]{2,1,0:T(8,128)(2,1)S(1)}, u32[]{:S(2)}, u32[]{:S(2)}) async-start(bf16[16,8,512]{2,1,0:T(8,128)(2,1)} %bitcast.2), calls=%async_computation | async-start | bytes 262144 | tf_op jit(solution)/shard_map/all_to_all | solution.py:293
  10.9 1.2 %copy-done = bf16[1024,512]{1,0:T(8,128)(2,1)S(1)} copy-done((bf16[1024,512]{1,0:T(8,128)(2,1)S(1)}, bf16[1024,512]{1,0:T(8,128)(2,1)}, u32[]{:S(2)}) %copy-start) | copy-done | bytes 1048600
  15.8 7.3 %base.1 = (f32[1536,512]{1,0:T(8,128)}, bf16[512,1536]{1,0:T(8,128)(2,1)}, f32[256,512]{1,0:T(8,128)S(1)}, f32[256,512]{1,0:T(8,128)S(1)}) custom-call(s32[12,128]{1,0:T(8,128)S(1)} %bitcast.29, bf16[256,512]{1,0:T(8,128)(2,1)S(1)} %copy-done.5, bf16[1536,512]{1,0:T(8,128)(2,1)} %edge_ref.1, bf16[256,512]{1,0:T(8,128)(2,1)S(1)} %copy-done.12, ...), custom_call_target="tpu_custom_call" | custom-call | flops 1610612736 | bytes 6291456 | tf_op jit(solution)/shard_map/base/pallas_call | solution.py:297
  24.7 13.8 %edges.1 = (bf16[256,512]{1,0:T(8,128)(2,1)}, bf16[128,512]{1,0:T(8,128)(2,1)S(1)}, bf16[256,512]{1,0:T(8,128)(2,1)S(1)}, bf16[256,512]{1,0:T(8,128)(2,1)S(1)}, ...) custom-call(s32[12,128]{1,0:T(8,128)S(1)} %bitcast.28, ...), custom_call_target="tpu_custom_call" | custom-call | tf_op jit(solution)/shard_map/edges/pallas_call | solution.py:313
  40.2 1.9 %collective-permute-start.1 = (bf16[4,2,8,512]{3,2,1,0:T(8,128)(2,1)S(1)}, bf16[4,2,8,512]{3,2,1,0:T(8,128)(2,1)S(1)}, u32[]{:S(2)}, u32[]{:S(2)}) collective-permute-start(bf16[4,2,8,512]{3,2,1,0:T(8,128)(2,1)S(1)} %get-tuple-element.41), channel_id=1, source_target_pairs={{0,2},{1,3},{2,0},{3,1},{4,6},{5,7},{6,4},{7,5},{8,10},{9,11},{10,... | collective-permute-start | bytes 196616 | tf_op jit(solution)/shard_map/ppermute | solution.py:276
  42.6 1.9 %collective-permute-start.8 = (bf16[128,512]{1,0:T(8,128)(2,1)S(1)}, bf16[128,512]{1,0:T(8,128)(2,1)S(1)}, u32[]{:S(2)}, u32[]{:S(2)}) collective-permute-start(bf16[128,512]{1,0:T(8,128)(2,1)S(1)} %slice.140), channel_id=1, source_target_pairs={{0,2},{1,3},{2,0},{3,1},{4,6},{5,7},{6,4},{7,5},{8,10},{9,11},{10,... | collective-permute-start | bytes 393224 | tf_op jit(solution)/shard_map/ppermute | solution.py:276
  45.0 1.9 %collective-permute-start.14 = (bf16[128,512]{1,0:T(8,128)(2,1)S(1)}, bf16[128,512]{1,0:T(8,128)(2,1)S(1)}, u32[]{:S(2)}, u32[]{:S(2)}) collective-permute-start(bf16[128,512]{1,0:T(8,128)(2,1)S(1)} %slice.138), channel_id=1, source_target_pairs={{0,2},{1,3},{2,0},{3,1},{4,6},{5,7},{6,4},{7,5},{8,10},{9,11},{10,... | collective-permute-start | bytes 393224 | tf_op jit(solution)/shard_map/ppermute | solution.py:276
  46.9 4.6 %collective-permute-done.8 = bf16[128,512]{1,0:T(8,128)(2,1)S(1)} collective-permute-done((bf16[128,512]{1,0:T(8,128)(2,1)S(1)}, bf16[128,512]{1,0:T(8,128)(2,1)S(1)}, u32[]{:S(2)}, u32[]{:S(2)}) %collective-permute-start.8) | collective-permute-done | bytes 131104 | tf_op jit(solution)/shard_map/ppermute | solution.py:276
  51.5 3.4 %collective-permute-start.9 = (bf16[128,512]{1,0:T(8,128)(2,1)S(1)}, bf16[128,512]{1,0:T(8,128)(2,1)S(1)}, u32[]{:S(2)}, u32[]{:S(2)}) collective-permute-start(bf16[128,512]{1,0:T(8,128)(2,1)S(1)} %fusion.2), channel_id=1, source_target_pairs={{0,12},{1,13},{2,14},{3,15},{4,8},{5,9},{6,10},{7,11},{8,4},{9,5},... | collective-permute-start | bytes 393224 | tf_op jit(solution)/shard_map/ppermute | solution.py:276
  54.9 1.8 %collective-permute-start.12 = (bf16[128,512]{1,0:T(8,128)(2,1)S(1)}, bf16[128,512]{1,0:T(8,128)(2,1)S(1)}, u32[]{:S(2)}, u32[]{:S(2)}) collective-permute-start(bf16[128,512]{1,0:T(8,128)(2,1)S(1)} %fusion.1), channel_id=1, source_target_pairs={{0,8},{1,9},{2,10},{3,11},{4,12},{5,13},{6,14},{7,15},{8,0},{9,1},... | collective-permute-start | bytes 393224 | tf_op jit(solution)/shard_map/ppermute | solution.py:276
  56.7 1.6 %collective-permute-start.15 = (bf16[128,512]{1,0:T(8,128)(2,1)S(1)}, bf16[128,512]{1,0:T(8,128)(2,1)S(1)}, u32[]{:S(2)}, u32[]{:S(2)}) collective-permute-start(bf16[128,512]{1,0:T(8,128)(2,1)S(1)} %fusion), channel_id=1, source_target_pairs={{0,4},{1,5},{2,6},{3,7},{4,0},{5,1},{6,2},{7,3},{8,12},{9,13},{10,... | collective-permute-start | bytes 393224 | tf_op jit(solution)/shard_map/ppermute | solution.py:276
  58.9 2.7 %collective-permute-start.4 = (bf16[2,2,8,512]{3,2,1,0:T(8,128)(2,1)S(1)}, bf16[2,2,8,512]{3,2,1,0:T(8,128)(2,1)S(1)}, u32[]{:S(2)}, u32[]{:S(2)}) collective-permute-start(bf16[2,2,8,512]{3,2,1,0:T(8,128)(2,1)S(1)} %get-tuple-element.38), channel_id=1, source_target_pairs={{0,12},{1,13},{2,14},{3,15},{4,8},{5,9},{6,10},{7,11},{8,4},{9,5},... | collective-permute-start | bytes 98312 | tf_op jit(solution)/shard_map/ppermute | solution.py:276
  61.6 2.3 %collective-permute-start.3 = (bf16[2,2,8,512]{3,2,1,0:T(8,128)(2,1)S(1)}, bf16[2,2,8,512]{3,2,1,0:T(8,128)(2,1)S(1)}, u32[]{:S(2)}, u32[]{:S(2)}) collective-permute-start(bf16[2,2,8,512]{3,2,1,0:T(8,128)(2,1)S(1)} %get-tuple-element.39), channel_id=1, source_target_pairs={{0,8},{1,9},{2,10},{3,11},{4,12},{5,13},{6,14},{7,15},{8,0},{9,1},... | collective-permute-start | bytes 98312 | tf_op jit(solution)/shard_map/ppermute | solution.py:276
  63.9 2.3 %collective-permute-done.12 = bf16[128,512]{1,0:T(8,128)(2,1)S(1)} collective-permute-done((bf16[128,512]{1,0:T(8,128)(2,1)S(1)}, bf16[128,512]{1,0:T(8,128)(2,1)S(1)}, u32[]{:S(2)}, u32[]{:S(2)}) %collective-permute-start.12) | collective-permute-done | bytes 131104 | tf_op jit(solution)/shard_map/ppermute | solution.py:276
  66.3 1.8 %collective-permute-start.19 = (bf16[128,512]{1,0:T(8,128)(2,1)S(1)}, bf16[128,512]{1,0:T(8,128)(2,1)S(1)}, u32[]{:S(2)}, u32[]{:S(2)}) collective-permute-start(bf16[128,512]{1,0:T(8,128)(2,1)S(1)} %fusion.6.refs_0_), channel_id=1, source_target_pairs={{0,2},{1,3},{2,0},{3,1},{4,6},{5,7},{6,4},{7,5},{8,10},{9,11},{10,... | collective-permute-start | bytes 393224 | tf_op jit(solution)/shard_map/ppermute | solution.py:276
  68.1 2.9 %collective-permute-start.18 = (bf16[128,512]{1,0:T(8,128)(2,1)S(1)}, bf16[128,512]{1,0:T(8,128)(2,1)S(1)}, u32[]{:S(2)}, u32[]{:S(2)}) collective-permute-start(bf16[128,512]{1,0:T(8,128)(2,1)S(1)} %fusion.6.refs_0_), channel_id=1, source_target_pairs={{0,12},{1,13},{2,14},{3,15},{4,8},{5,9},{6,10},{7,11},{8,4},{9,5},... | collective-permute-start | bytes 393224 | tf_op jit(solution)/shard_map/ppermute | solution.py:276
  71.1 1.4 %collective-permute-start.16 = (bf16[128,512]{1,0:T(8,128)(2,1)S(1)}, bf16[128,512]{1,0:T(8,128)(2,1)S(1)}, u32[]{:S(2)}, u32[]{:S(2)}) collective-permute-start(bf16[128,512]{1,0:T(8,128)(2,1)S(1)} %fusion.6.refs_0_), channel_id=1, source_target_pairs={{0,4},{1,5},{2,6},{3,7},{4,0},{5,1},{6,2},{7,3},{8,12},{9,13},{10,... | collective-permute-start | bytes 393224 | tf_op jit(solution)/shard_map/ppermute | solution.py:276
  72.6 3.6 %collective-permute-done.18.refs_3_ = bf16[128,512]{1,0:T(8,128)(2,1)S(1)} collective-permute-done((bf16[128,512]{1,0:T(8,128)(2,1)S(1)}, bf16[128,512]{1,0:T(8,128)(2,1)S(1)}, u32[]{:S(2)}, u32[]{:S(2)}) %collective-permute-start.18) | collective-permute-done | bytes 131104 | tf_op jit(solution)/shard_map/ppermute | solution.py:276
  76.5 3.8 %collective-permute-done.17.refs_2_ = bf16[128,512]{1,0:T(8,128)(2,1)S(1)} collective-permute-done((bf16[128,512]{1,0:T(8,128)(2,1)S(1)}, bf16[128,512]{1,0:T(8,128)(2,1)S(1)}, u32[]{:S(2)}, u32[]{:S(2)}) %collective-permute-start.17) | collective-permute-done | bytes 131104 | tf_op jit(solution)/shard_map/ppermute | solution.py:276
  80.9 1.5 %collective-permute-start.20 = (bf16[128,512]{1,0:T(8,128)(2,1)S(1)}, bf16[128,512]{1,0:T(8,128)(2,1)S(1)}, u32[]{:S(2)}, u32[]{:S(2)}) collective-permute-start(bf16[128,512]{1,0:T(8,128)(2,1)S(1)} %collective-permute-done.16.refs_1_), channel_id=1, source_target_pairs={{0,2},{1,3},{2,0},{3,1},{4,6},{5,7},{6,4},{7,5},{8,10},{9,11},{10,... | collective-permute-start | bytes 393224 | tf_op jit(solution)/shard_map/ppermute | solution.py:276
  83.0 3.7 %collective-permute-done.21.refs_6_ = bf16[128,512]{1,0:T(8,128)(2,1)S(1)} collective-permute-done((bf16[128,512]{1,0:T(8,128)(2,1)S(1)}, bf16[128,512]{1,0:T(8,128)(2,1)S(1)}, u32[]{:S(2)}, u32[]{:S(2)}) %collective-permute-start.21) | collective-permute-done | bytes 131104 | tf_op jit(solution)/shard_map/ppermute | solution.py:276
  86.7 1.9 %collective-permute-done.20.refs_5_ = bf16[128,512]{1,0:T(8,128)(2,1)S(1)} collective-permute-done((bf16[128,512]{1,0:T(8,128)(2,1)S(1)}, bf16[128,512]{1,0:T(8,128)(2,1)S(1)}, u32[]{:S(2)}, u32[]{:S(2)}) %collective-permute-start.20) | collective-permute-done | bytes 131104 | tf_op jit(solution)/shard_map/ppermute | solution.py:276
  88.6 1.8 %put.1 = f32[1024,512]{1,0:T(8,128)} custom-call(s32[1,128]{1,0:T(1,128)S(1)} %copy-done.11, bf16[128,512]{1,0:T(8,128)(2,1)S(1)} %bitcast.27), custom_call_target="tpu_custom_call" | custom-call | tf_op jit(solution)/shard_map/put/pallas_call | solution.py:373
  90.4 2.5 %order.1 = (f32[1536,512]{1,0:T(8,128)}, f32[512,512]{1,0:T(8,128)}) custom-call(bf16[128,512]{1,0:T(8,128)(2,1)S(1)} %fusion.6.refs_0_, bf16[128,512]{1,0:T(8,128)(2,1)S(1)} %collective-permute-done.16.refs_1_, bf16[128,512]{1,0:T(8,128)(2,1)S(1)} %collective-permute-done.17.refs_2_, bf16[128,512]{1,0:T(8,128)(2,1)S(1)} %collective-permute-done.18.refs_3_, ...), custom_call_target="tpu_custom_call" | custom-call | tf_op jit(solution)/shard_map/order/pallas_call | solution.py:381
  (87 shorter events, 13.1 us)
Async XLA Ops:
  3.5 21.2 %all-to-all-start = ((bf16[16,8,512]{2,1,0:T(8,128)(2,1)}), bf16[16,8,512]{2,1,0:T(8,128)(2,1)S(1)}, u32[]{:S(2)}, u32[]{:S(2)}) async-start(bf16[16,8,512]{2,1,0:T(8,128)(2,1)} %bitcast.2), calls=%async_computation | async-start | bytes 262144 | tf_op jit(solution)/shard_map/all_to_all | solution.py:293
  40.2 18.1 %collective-permute-start.1 = (bf16[4,2,8,512]{3,2,1,0:T(8,128)(2,1)S(1)}, bf16[4,2,8,512]{3,2,1,0:T(8,128)(2,1)S(1)}, u32[]{:S(2)}, u32[]{:S(2)}) collective-permute-start(bf16[4,2,8,512]{3,2,1,0:T(8,128)(2,1)S(1)} %get-tuple-element.41), channel_id=1, source_target_pairs={{0,2},{1,3},{2,0},{3,1},{4,6},{5,7},{6,4},{7,5},{8,10},{9,11},{10,... | collective-permute-start | bytes 196616 | tf_op jit(solution)/shard_map/ppermute | solution.py:276
  42.2 16.7 %collective-permute-start.6 = (bf16[128,512]{1,0:T(8,128)(2,1)S(1)}, bf16[128,512]{1,0:T(8,128)(2,1)S(1)}, u32[]{:S(2)}, u32[]{:S(2)}) collective-permute-start(bf16[128,512]{1,0:T(8,128)(2,1)S(1)} %slice.141), channel_id=1, source_target_pairs={{0,2},{1,3},{2,0},{3,1},{4,6},{5,7},{6,4},{7,5},{8,10},{9,11},{10,... | collective-permute-start | bytes 393224 | tf_op jit(solution)/shard_map/ppermute | solution.py:276
  42.6 8.9 %collective-permute-start.8 = (bf16[128,512]{1,0:T(8,128)(2,1)S(1)}, bf16[128,512]{1,0:T(8,128)(2,1)S(1)}, u32[]{:S(2)}, u32[]{:S(2)}) collective-permute-start(bf16[128,512]{1,0:T(8,128)(2,1)S(1)} %slice.140), channel_id=1, source_target_pairs={{0,2},{1,3},{2,0},{3,1},{4,6},{5,7},{6,4},{7,5},{8,10},{9,11},{10,... | collective-permute-start | bytes 393224 | tf_op jit(solution)/shard_map/ppermute | solution.py:276
  44.6 10.3 %collective-permute-start.11 = (bf16[128,512]{1,0:T(8,128)(2,1)S(1)}, bf16[128,512]{1,0:T(8,128)(2,1)S(1)}, u32[]{:S(2)}, u32[]{:S(2)}) collective-permute-start(bf16[128,512]{1,0:T(8,128)(2,1)S(1)} %slice.139), channel_id=1, source_target_pairs={{0,2},{1,3},{2,0},{3,1},{4,6},{5,7},{6,4},{7,5},{8,10},{9,11},{10,... | collective-permute-start | bytes 393224 | tf_op jit(solution)/shard_map/ppermute | solution.py:276
  45.0 11.7 %collective-permute-start.14 = (bf16[128,512]{1,0:T(8,128)(2,1)S(1)}, bf16[128,512]{1,0:T(8,128)(2,1)S(1)}, u32[]{:S(2)}, u32[]{:S(2)}) collective-permute-start(bf16[128,512]{1,0:T(8,128)(2,1)S(1)} %slice.138), channel_id=1, source_target_pairs={{0,2},{1,3},{2,0},{3,1},{4,6},{5,7},{6,4},{7,5},{8,10},{9,11},{10,... | collective-permute-start | bytes 393224 | tf_op jit(solution)/shard_map/ppermute | solution.py:276
  51.5 10.1 %collective-permute-start.9 = (bf16[128,512]{1,0:T(8,128)(2,1)S(1)}, bf16[128,512]{1,0:T(8,128)(2,1)S(1)}, u32[]{:S(2)}, u32[]{:S(2)}) collective-permute-start(bf16[128,512]{1,0:T(8,128)(2,1)S(1)} %fusion.2), channel_id=1, source_target_pairs={{0,12},{1,13},{2,14},{3,15},{4,8},{5,9},{6,10},{7,11},{8,4},{9,5},... | collective-permute-start | bytes 393224 | tf_op jit(solution)/shard_map/ppermute | solution.py:276
  54.9 11.3 %collective-permute-start.12 = (bf16[128,512]{1,0:T(8,128)(2,1)S(1)}, bf16[128,512]{1,0:T(8,128)(2,1)S(1)}, u32[]{:S(2)}, u32[]{:S(2)}) collective-permute-start(bf16[128,512]{1,0:T(8,128)(2,1)S(1)} %fusion.1), channel_id=1, source_target_pairs={{0,8},{1,9},{2,10},{3,11},{4,12},{5,13},{6,14},{7,15},{8,0},{9,1},... | collective-permute-start | bytes 393224 | tf_op jit(solution)/shard_map/ppermute | solution.py:276
  56.7 9.5 %collective-permute-start.15 = (bf16[128,512]{1,0:T(8,128)(2,1)S(1)}, bf16[128,512]{1,0:T(8,128)(2,1)S(1)}, u32[]{:S(2)}, u32[]{:S(2)}) collective-permute-start(bf16[128,512]{1,0:T(8,128)(2,1)S(1)} %fusion), channel_id=1, source_target_pairs={{0,4},{1,5},{2,6},{3,7},{4,0},{5,1},{6,2},{7,3},{8,12},{9,13},{10,... | collective-permute-start | bytes 393224 | tf_op jit(solution)/shard_map/ppermute | solution.py:276
  58.3 12.7 %collective-permute-start.2 = (bf16[2,2,8,512]{3,2,1,0:T(8,128)(2,1)S(1)}, bf16[2,2,8,512]{3,2,1,0:T(8,128)(2,1)S(1)}, u32[]{:S(2)}, u32[]{:S(2)}) collective-permute-start(bf16[2,2,8,512]{3,2,1,0:T(8,128)(2,1)S(1)} %get-tuple-element.37), channel_id=1, source_target_pairs={{0,4},{1,5},{2,6},{3,7},{4,0},{5,1},{6,2},{7,3},{8,12},{9,13},{10,... | collective-permute-start | bytes 98312 | tf_op jit(solution)/shard_map/ppermute | solution.py:276
  58.9 12.1 %collective-permute-start.4 = (bf16[2,2,8,512]{3,2,1,0:T(8,128)(2,1)S(1)}, bf16[2,2,8,512]{3,2,1,0:T(8,128)(2,1)S(1)}, u32[]{:S(2)}, u32[]{:S(2)}) collective-permute-start(bf16[2,2,8,512]{3,2,1,0:T(8,128)(2,1)S(1)} %get-tuple-element.38), channel_id=1, source_target_pairs={{0,12},{1,13},{2,14},{3,15},{4,8},{5,9},{6,10},{7,11},{8,4},{9,5},... | collective-permute-start | bytes 98312 | tf_op jit(solution)/shard_map/ppermute | solution.py:276
  61.6 9.5 %collective-permute-start.3 = (bf16[2,2,8,512]{3,2,1,0:T(8,128)(2,1)S(1)}, bf16[2,2,8,512]{3,2,1,0:T(8,128)(2,1)S(1)}, u32[]{:S(2)}, u32[]{:S(2)}) collective-permute-start(bf16[2,2,8,512]{3,2,1,0:T(8,128)(2,1)S(1)} %get-tuple-element.39), channel_id=1, source_target_pairs={{0,8},{1,9},{2,10},{3,11},{4,12},{5,13},{6,14},{7,15},{8,0},{9,1},... | collective-permute-start | bytes 98312 | tf_op jit(solution)/shard_map/ppermute | solution.py:276
  66.3 6.3 %collective-permute-start.19 = (bf16[128,512]{1,0:T(8,128)(2,1)S(1)}, bf16[128,512]{1,0:T(8,128)(2,1)S(1)}, u32[]{:S(2)}, u32[]{:S(2)}) collective-permute-start(bf16[128,512]{1,0:T(8,128)(2,1)S(1)} %fusion.6.refs_0_), channel_id=1, source_target_pairs={{0,2},{1,3},{2,0},{3,1},{4,6},{5,7},{6,4},{7,5},{8,10},{9,11},{10,... | collective-permute-start | bytes 393224 | tf_op jit(solution)/shard_map/ppermute | solution.py:276
  68.1 8.1 %collective-permute-start.18 = (bf16[128,512]{1,0:T(8,128)(2,1)S(1)}, bf16[128,512]{1,0:T(8,128)(2,1)S(1)}, u32[]{:S(2)}, u32[]{:S(2)}) collective-permute-start(bf16[128,512]{1,0:T(8,128)(2,1)S(1)} %fusion.6.refs_0_), channel_id=1, source_target_pairs={{0,12},{1,13},{2,14},{3,15},{4,8},{5,9},{6,10},{7,11},{8,4},{9,5},... | collective-permute-start | bytes 393224 | tf_op jit(solution)/shard_map/ppermute | solution.py:276
  71.0 9.3 %collective-permute-start.17 = (bf16[128,512]{1,0:T(8,128)(2,1)S(1)}, bf16[128,512]{1,0:T(8,128)(2,1)S(1)}, u32[]{:S(2)}, u32[]{:S(2)}) collective-permute-start(bf16[128,512]{1,0:T(8,128)(2,1)S(1)} %fusion.6.refs_0_), channel_id=1, source_target_pairs={{0,8},{1,9},{2,10},{3,11},{4,12},{5,13},{6,14},{7,15},{8,0},{9,1},... | collective-permute-start | bytes 393224 | tf_op jit(solution)/shard_map/ppermute | solution.py:276
  71.1 9.7 %collective-permute-start.16 = (bf16[128,512]{1,0:T(8,128)(2,1)S(1)}, bf16[128,512]{1,0:T(8,128)(2,1)S(1)}, u32[]{:S(2)}, u32[]{:S(2)}) collective-permute-start(bf16[128,512]{1,0:T(8,128)(2,1)S(1)} %fusion.6.refs_0_), channel_id=1, source_target_pairs={{0,4},{1,5},{2,6},{3,7},{4,0},{5,1},{6,2},{7,3},{8,12},{9,13},{10,... | collective-permute-start | bytes 393224 | tf_op jit(solution)/shard_map/ppermute | solution.py:276
  72.6 9.8 %collective-permute-start.27 = (bf16[128,512]{1,0:T(8,128)(2,1)S(1)}, bf16[128,512]{1,0:T(8,128)(2,1)S(1)}, u32[]{:S(2)}, u32[]{:S(2)}) collective-permute-start(bf16[128,512]{1,0:T(8,128)(2,1)S(1)} %collective-permute-done.19.refs_4_), channel_id=1, source_target_pairs={{0,1},{1,0},{2,3},{3,2},{4,5},{5,4},{6,7},{7,6},{8,9},{9,8},{10,11... | collective-permute-start | bytes 393224 | tf_op jit(solution)/shard_map/ppermute | solution.py:276
  76.2 6.2 %collective-permute-start.26 = (bf16[128,512]{1,0:T(8,128)(2,1)S(1)}, bf16[128,512]{1,0:T(8,128)(2,1)S(1)}, u32[]{:S(2)}, u32[]{:S(2)}) collective-permute-start(bf16[128,512]{1,0:T(8,128)(2,1)S(1)} %collective-permute-done.18.refs_3_), channel_id=1, source_target_pairs={{0,1},{1,0},{2,3},{3,2},{4,5},{5,4},{6,7},{7,6},{8,9},{9,8},{10,11... | collective-permute-start | bytes 393224 | tf_op jit(solution)/shard_map/ppermute | solution.py:276
  76.2 6.7 %collective-permute-start.22 = (bf16[128,512]{1,0:T(8,128)(2,1)S(1)}, bf16[128,512]{1,0:T(8,128)(2,1)S(1)}, u32[]{:S(2)}, u32[]{:S(2)}) collective-permute-start(bf16[128,512]{1,0:T(8,128)(2,1)S(1)} %collective-permute-done.18.refs_3_), channel_id=1, source_target_pairs={{0,2},{1,3},{2,0},{3,1},{4,6},{5,7},{6,4},{7,5},{8,10},{9,11},{10,... | collective-permute-start | bytes 393224 | tf_op jit(solution)/shard_map/ppermute | solution.py:276
  80.4 6.4 %collective-permute-start.21 = (bf16[128,512]{1,0:T(8,128)(2,1)S(1)}, bf16[128,512]{1,0:T(8,128)(2,1)S(1)}, u32[]{:S(2)}, u32[]{:S(2)}) collective-permute-start(bf16[128,512]{1,0:T(8,128)(2,1)S(1)} %collective-permute-done.17.refs_2_), channel_id=1, source_target_pairs={{0,2},{1,3},{2,0},{3,1},{4,6},{5,7},{6,4},{7,5},{8,10},{9,11},{10,... | collective-permute-start | bytes 393224 | tf_op jit(solution)/shard_map/ppermute | solution.py:276
  80.9 7.7 %collective-permute-start.20 = (bf16[128,512]{1,0:T(8,128)(2,1)S(1)}, bf16[128,512]{1,0:T(8,128)(2,1)S(1)}, u32[]{:S(2)}, u32[]{:S(2)}) collective-permute-start(bf16[128,512]{1,0:T(8,128)(2,1)S(1)} %collective-permute-done.16.refs_1_), channel_id=1, source_target_pairs={{0,2},{1,3},{2,0},{3,1},{4,6},{5,7},{6,4},{7,5},{8,10},{9,11},{10,... | collective-permute-start | bytes 393224 | tf_op jit(solution)/shard_map/ppermute | solution.py:276
  82.4 8.0 %collective-permute-start.25 = (bf16[128,512]{1,0:T(8,128)(2,1)S(1)}, bf16[128,512]{1,0:T(8,128)(2,1)S(1)}, u32[]{:S(2)}, u32[]{:S(2)}) collective-permute-start(bf16[128,512]{1,0:T(8,128)(2,1)S(1)} %collective-permute-done.17.refs_2_), channel_id=1, source_target_pairs={{0,1},{1,0},{2,3},{3,2},{4,5},{5,4},{6,7},{7,6},{8,9},{9,8},{10,11... | collective-permute-start | bytes 393224 | tf_op jit(solution)/shard_map/ppermute | solution.py:276
  82.4 8.0 %collective-permute-start.24 = (bf16[128,512]{1,0:T(8,128)(2,1)S(1)}, bf16[128,512]{1,0:T(8,128)(2,1)S(1)}, u32[]{:S(2)}, u32[]{:S(2)}) collective-permute-start(bf16[128,512]{1,0:T(8,128)(2,1)S(1)} %collective-permute-done.16.refs_1_), channel_id=1, source_target_pairs={{0,1},{1,0},{2,3},{3,2},{4,5},{5,4},{6,7},{7,6},{8,9},{9,8},{10,11... | collective-permute-start | bytes 393224 | tf_op jit(solution)/shard_map/ppermute | solution.py:276
  82.9 7.5 %collective-permute-start.30 = (bf16[128,512]{1,0:T(8,128)(2,1)S(1)}, bf16[128,512]{1,0:T(8,128)(2,1)S(1)}, u32[]{:S(2)}, u32[]{:S(2)}) collective-permute-start(bf16[128,512]{1,0:T(8,128)(2,1)S(1)} %collective-permute-done.22.refs_7_), channel_id=1, source_target_pairs={{0,1},{1,0},{2,3},{3,2},{4,5},{5,4},{6,7},{7,6},{8,9},{9,8},{10,11... | collective-permute-start | bytes 393224 | tf_op jit(solution)/shard_map/ppermute | solution.py:276
  (21 other events, 108.3 us)

commit v3 on v2

--- a/solution.py
+++ b/solution.py
@@ -9,7 +9,7 @@
 
 BF16 = jnp.bfloat16
 F32 = jnp.float32
-VMEM_LIMIT = 50 * 1024 * 1024
+MIB = 1024 * 1024
 
 
 def dot_nn(a, b):
@@ -67,17 +67,33 @@
     return ((my_outer ^ far_outer) * sizes[1] + (my_inner ^ far_inner)) * 2 + (my_core ^ far_core)
 
 
-def params():
-    return pltpu.CompilerParams(vmem_limit_bytes=VMEM_LIMIT)
+def params(mib):
+    return pltpu.CompilerParams(vmem_limit_bytes=mib * MIB)
+
+
+def specs(space, count):
+    return [pl.BlockSpec(memory_space=space)] * count
 
 
 def cost(flops, nbytes):
     return pl.CostEstimate(flops=flops, bytes_accessed=nbytes, transcendentals=0)
 
 
-def pick_kernel(rows_ref, grid_ref, out_ref):
-    chosen = one_hot_rows(rows_ref[...], grid_ref.shape[0])
-    out_ref[...] = dot_tn(chosen, grid_ref[...]).astype(BF16)
+def load(pairs, sems):
+    copies = [pltpu.make_async_copy(source, target, sems.at[at]) for at, (source, target) in enumerate(pairs)]
+    for copy in copies:
+        copy.start()
+    return copies
+
+
+def pick_kernel(rows_hbm, grid_hbm, out_ref, rows_ref, grid_ref, sems):
+    rows_copy, grid_copy = load([(rows_hbm, rows_ref), (grid_hbm, grid_ref)], sems)
+    rows_copy.wait()
+    picked = out_ref.shape[0]
+    chosen = [one_hot_columns(rows_ref[:, at : at + 128], grid_ref.shape[0]) for at in range(0, picked, 128)]
+    grid_copy.wait()
+    for at, some in enumerate(chosen):
+        out_ref[at * 128 : (at + 1) * 128, :] = dot_nn(some, grid_ref[...]).astype(BF16)
 
 
 def put_kernel(sizes, rows_ref, back_ref, out_ref, ordered_ref):
@@ -94,6 +110,18 @@
 
 def base_kernel(
     lines,
+    dst_hbm,
+    mesh_hbm,
+    edge_hbm,
+    cot_hbm,
+    w1_hbm,
+    wn1_hbm,
+    wn2_hbm,
+    base_ref,
+    turned_ref,
+    hot_ref,
+    node_ref,
+    cot_out_ref,
     dst_ref,
     mesh_ref,
     edge_ref,
@@ -101,63 +129,85 @@
     w1_ref,
     wn1_ref,
     wn2_ref,
-    base_ref,
-    turned_ref,
-    node_ref,
-    cot_out_ref,
+    sems,
 ):
     width = mesh_ref.shape[1]
     mesh_rows = mesh_ref.shape[0]
     tile = lines * 128
-    high, low = split(dot_nn(mesh_ref[...], w1_ref[width : 2 * width, :]))
-    pair = jnp.concatenate([high, low], axis=0)
-
-    def step(at, carry):
-        rows = pl.ds(pl.multiple_of(at * tile, tile), tile)
+    tiles = edge_ref.shape[0] // tile
+    pairs = [
+        (dst_hbm, dst_ref),
+        (mesh_hbm, mesh_ref),
+        (w1_hbm.at[pl.ds(width, width), :], w1_ref.at[pl.ds(0, width), :]),
+        (w1_hbm.at[pl.ds(2 * width, width), :], w1_ref.at[pl.ds(width, width), :]),
+    ]
+    pairs += [(edge_hbm.at[pl.ds(at * tile, tile), :], edge_ref.at[pl.ds(at * tile, tile), :]) for at in range(tiles)]
+    pairs += [(wn1_hbm.at[pl.ds(0, width), :], wn1_ref), (cot_hbm, cot_ref), (wn2_hbm, wn2_ref)]
+    copies = load(pairs, sems)
+    same = lax.broadcasted_iota(jnp.int32, (256, 256), 0) == lax.broadcasted_iota(jnp.int32, (256, 256), 1)
+    eye = jnp.where(same, 1.0, 0.0).astype(BF16)
+    for copy in copies[:4]:
+        copy.wait()
+    moved = dot_nn(mesh_ref[...], w1_ref[:width, :]).astype(BF16)
+    for at in range(tiles):
+        rows = slice(at * tile, (at + 1) * tile)
         to_mesh = tile_columns(dst_ref, at, lines, mesh_rows)
-        twice = jnp.concatenate([to_mesh, to_mesh], axis=1)
+        hot_ref[rows, :] = to_mesh
+        copies[4 + at].wait()
         edge = edge_ref[rows, :]
-        base_ref[rows, :] = dot_nn(edge, w1_ref[2 * width :, :]) + dot_nn(twice, pair)
-        turned_ref[:, rows] = jnp.transpose(edge)
-        return carry
-
-    lax.fori_loop(0, edge_ref.shape[0] // tile, step, 0)
-    node_ref[...] = dot_nn(mesh_ref[...], wn1_ref[:width, :])
+        base_ref[rows, :] = dot_nn(edge, w1_ref[width:, :]) + dot_nn(to_mesh, moved)
+        for start in range(0, width, 256):
+            turned_ref[start : start + 256, rows] = dot_nt(eye, edge[:, start : start + 256]).astype(BF16)
+    for copy in copies[4 + tiles :]:
+        copy.wait()
+    node_ref[...] = dot_nn(mesh_ref[...], wn1_ref[...])
     cot_out_ref[...] = dot_nt(cot_ref[...], wn2_ref[...])
 
 
 def main_kernel(
     lines,
     sizes,
-    slot_ref,
-    dst_ref,
+    slot_hbm,
+    dst_hbm,
+    mesh_hbm,
+    w1_hbm,
+    w2_hbm,
+    wn1_hbm,
+    wn2_hbm,
     slots_ref,
     base_ref,
     turned_ref,
-    mesh_ref,
+    hot_ref,
     node_ref,
     cot_ref,
-    w1_ref,
-    w2_ref,
-    wn1_ref,
-    wn2_ref,
     *rest,
 ):
     outer, inner = sizes
     mesh_out_ref, d_slots_ref = rest[:2]
     send_refs, keep_refs = rest[2 : 2 + outer], rest[2 + outer : 2 + 2 * outer]
-    slope_ref, value_ref, both_ref, grads_ref, slot_grads_ref, ordered_ref = rest[2 + 2 * outer :]
+    slope_ref, value_ref, both_ref, grads_ref, slot_grads_ref, ordered_ref = rest[2 + 2 * outer : 8 + 2 * outer]
+    slot_ref, dst_ref, mesh_ref, w1_ref, w2_ref, wn1_ref, wn2_ref, sems = rest[8 + 2 * outer :]
     width = mesh_ref.shape[1]
     mesh_rows = mesh_ref.shape[0]
     slot_rows = slots_ref.shape[0]
     tile = lines * 128
     tiles = base_ref.shape[0] // tile
-
-    high, low = split(dot_nn(slots_ref[...], w1_ref[:width, :]))
-    slot_pair = jnp.concatenate([high, low], axis=0)
-
-    def forward(at, carry):
-        rows = pl.ds(pl.multiple_of(at * tile, tile), tile)
+    pairs = [
+        (slot_hbm, slot_ref),
+        (w1_hbm.at[pl.ds(0, width), :], w1_ref),
+        (dst_hbm, dst_ref),
+        (w2_hbm, w2_ref),
+        (wn1_hbm.at[pl.ds(width, wn1_ref.shape[0]), :], wn1_ref),
+        (mesh_hbm, mesh_ref),
+        (wn2_hbm, wn2_ref),
+    ]
+    copies = load(pairs, sems)
+    for copy in copies[:3]:
+        copy.wait()
+
+    slot_pair = jnp.concatenate(split(dot_nn(slots_ref[...], w1_ref[...])), axis=0)
+    for at in range(tiles):
+        rows = slice(at * tile, (at + 1) * tile)
         from_slot = tile_columns(slot_ref, at, lines, slot_rows)
         twice = jnp.concatenate([from_slot, from_slot], axis=1)
         pre = base_ref[rows, :] + dot_nn(twice, slot_pair)
@@ -167,40 +217,30 @@
         value_ref[rows, :] = hidden.astype(BF16)
         both_ref[:slot_rows, rows] = tile_rows(slot_ref, at, lines, slot_rows)
         both_ref[slot_rows:, rows] = tile_rows(dst_ref, at, lines, mesh_rows)
-        return carry
-
-    lax.fori_loop(0, tiles, forward, 0)
-
-    hidden_high, hidden_low = split(dot_nn(both_ref[slot_rows:, :], value_ref[...]))
-    received = (dot_nn(hidden_high, w2_ref[...]) + dot_nn(hidden_low, w2_ref[...])).astype(BF16)
+
+    for copy in copies[3:]:
+        copy.wait()
+    hidden_sums = dot_nn(both_ref[slot_rows:, :], value_ref[...]).astype(BF16)
+    received = dot_nn(hidden_sums, w2_ref[...]).astype(BF16)
     mesh = mesh_ref[...]
-    pre_node = node_ref[...] + dot_nn(received, wn1_ref[width:, :])
+    pre_node = node_ref[...] + dot_nn(received, wn1_ref[...])
     sigma = 0.5 + 0.5 * jnp.tanh(0.5 * pre_node)
     node = pre_node * sigma
     slope = sigma + node * (1.0 - sigma)
     d_pre_node = (cot_ref[...] * slope).astype(BF16)
-    d_received = dot_nt(d_pre_node, wn1_ref[width:, :]).astype(BF16)
-    high, low = split(dot_nt(d_received, w2_ref[...]))
-    back_pair = jnp.concatenate([high, low], axis=0)
-
-    def backward(at, carry):
-        rows = pl.ds(pl.multiple_of(at * tile, tile), tile)
-        to_mesh = tile_columns(dst_ref, at, lines, mesh_rows)
-        twice = jnp.concatenate([to_mesh, to_mesh], axis=1)
-        value_ref[rows, :] = (dot_nn(twice, back_pair) * slope_ref[rows, :]).astype(BF16)
-        return carry
-
-    lax.fori_loop(0, tiles, backward, 0)
-
-    grads_ref[3 * width :, :] = dot_tn(hidden_high, d_received) + dot_tn(hidden_low, d_received)
+    d_received = dot_nt(d_pre_node, wn1_ref[...]).astype(BF16)
+    spread = dot_nt(d_received, w2_ref[...]).astype(BF16)
+
+    for at in range(tiles):
+        rows = slice(at * tile, (at + 1) * tile)
+        value_ref[rows, :] = (dot_nn(hot_ref[rows, :], spread) * slope_ref[rows, :]).astype(BF16)
+
+    grads_ref[3 * width :, :] = dot_tn(hidden_sums, d_received)
     mesh_out_ref[...] = (mesh.astype(F32) + dot_nn(node.astype(BF16), wn2_ref[...])).astype(BF16)
-    sums = dot_nn(both_ref[...], value_ref[...])
-    slot_high, slot_low = split(sums[:slot_rows])
-    slot_grads_ref[...] = dot_nt(slot_high, w1_ref[:width, :]) + dot_nt(slot_low, w1_ref[:width, :])
-    slots = slots_ref[...]
-    grads_ref[:width, :] = dot_tn(slots, slot_high) + dot_tn(slots, slot_low)
-    mesh_high, mesh_low = split(sums[slot_rows:])
-    grads_ref[width : 2 * width, :] = dot_tn(mesh, mesh_high) + dot_tn(mesh, mesh_low)
+    sums = dot_nn(both_ref[...], value_ref[...]).astype(BF16)
+    slot_grads_ref[...] = dot_nt(sums[:slot_rows], w1_ref[...])
+    grads_ref[:width, :] = dot_tn(slots_ref[...], sums[:slot_rows])
+    grads_ref[width : 2 * width, :] = dot_tn(mesh, sums[slot_rows:])
     grads_ref[2 * width : 3 * width, :] = dot_nn(turned_ref[...], value_ref[...])
 
     chunk = grads_ref.shape[0] // (2 * outer * inner)
@@ -221,26 +261,31 @@
     d_slots_ref[...] = ordered_ref[...].astype(BF16)
 
 
-def order_kernel(sizes, *refs):
+def order_kernel(sizes, places, aliased, *refs):
     outer, inner = sizes
-    first_ref, second_ref = refs[-2:]
-    pieces = refs[:-2]
+    pieces = refs[: len(places)]
+    first_hbm, second_hbm, stage_ref, sems = refs[len(places) + aliased :]
     chunk = pieces[0].shape[0]
-    first_chunks = first_ref.shape[0] // chunk
-
-    for at, piece in enumerate(pieces):
-        far_outer, far_inner, far_core = at % outer, at // outer % inner, at // (outer * inner)
-        owner = owner_at(sizes, far_outer, far_inner, far_core)
-        value = piece[...].astype(F32)
+    first_chunks = first_hbm.shape[0] // chunk
+
+    def send(k, target, start):
+        rows = pl.ds(pl.multiple_of(start, chunk), chunk)
+        return pltpu.make_async_copy(stage_ref.at[k], target.at[rows, :], sems.at[k])
+
+    for k, (at, piece) in enumerate(zip(places, pieces)):
+        owner = owner_at(sizes, at % outer, at // outer % inner, at // (outer * inner))
+        stage_ref[k] = piece[...].astype(F32)
 
         @pl.when(owner < first_chunks)
         def _():
-            first_ref[pl.ds(pl.multiple_of(owner * chunk, chunk), chunk), :] = value
+            send(k, first_hbm, owner * chunk).start()
 
         @pl.when(owner >= first_chunks)
         def _():
-            start = (owner - first_chunks) * chunk
-            second_ref[pl.ds(pl.multiple_of(start, chunk), chunk), :] = value
+            send(k, second_hbm, (owner - first_chunks) * chunk).start()
+
+    for k in range(len(places)):
+        send(k, first_hbm, 0).wait()
 
 
 def shards(
@@ -264,7 +309,7 @@
     edges = edge_latent.shape[0]
     mesh_rows = mesh_latent.shape[0]
     slot_rows = send_rows.shape[1]
-    lines = 2
+    lines = 4
     slot_index = edge_slot.reshape(edges // 128, 128)
     dst_index = edge_dst.reshape(edges // 128, 128)
 
@@ -287,22 +332,42 @@
     outgoing = pl.pallas_call(
         pick_kernel,
         out_shape=jax.ShapeDtypeStruct((slot_rows, width), BF16),
-        compiler_params=params(),
+        in_specs=specs(pltpu.HBM, 2),
+        out_specs=pl.BlockSpec(memory_space=pltpu.VMEM),
+        scratch_shapes=[
+            pltpu.VMEM(send_rows.shape, jnp.int32),
+            pltpu.VMEM(grid_latent.shape, BF16),
+            pltpu.SemaphoreType.DMA((2,)),
+        ],
+        compiler_params=params(16),
         name="pick",
     )(send_rows, grid_latent)
     slots = lax.all_to_all(
         outgoing.reshape(band_count, -1, width), "band", split_axis=0, concat_axis=0, tiled=True
     ).reshape(slot_rows, width)
 
-    base, turned, node, cot = pl.pallas_call(
+    base, turned, hot, node, cot = pl.pallas_call(
         functools.partial(base_kernel, lines),
         out_shape=[
             jax.ShapeDtypeStruct((edges, hidden_width), F32),
             jax.ShapeDtypeStruct((width, edges), BF16),
+            jax.ShapeDtypeStruct((edges, mesh_rows), BF16),
             jax.ShapeDtypeStruct((mesh_rows, hidden_width), F32),
             jax.ShapeDtypeStruct((mesh_rows, hidden_width), F32),
         ],
-        compiler_params=params(),
+        in_specs=specs(pltpu.HBM, 7),
+        out_specs=specs(pltpu.VMEM, 5),
+        scratch_shapes=[
+            pltpu.VMEM(dst_index.shape, jnp.int32),
+            pltpu.VMEM(mesh_latent.shape, BF16),
+            pltpu.VMEM(edge_latent.shape, BF16),
+            pltpu.VMEM(mesh_cot.shape, BF16),
+            pltpu.VMEM((2 * width, hidden_width), BF16),
+            pltpu.VMEM((width, hidden_width), BF16),
+            pltpu.VMEM(w_node2.shape, BF16),
+            pltpu.SemaphoreType.DMA((7 + edges // (128 * lines),)),
+        ],
+        compiler_params=params(20),
         cost_estimate=cost(2 * edges * width * hidden_width * 2, edges * width * 8),
         name="base",
     )(dst_index, mesh_latent, edge_latent, mesh_cot, w_edge1, w_node1, w_node2)
@@ -318,6 +383,8 @@
         ]
         + [jax.ShapeDtypeStruct(group, BF16)] * outer
         + [jax.ShapeDtypeStruct(group, F32)] * outer,
+        in_specs=specs(pltpu.HBM, 7) + specs(pltpu.VMEM, 6),
+        out_specs=specs(pltpu.VMEM, 2 + 2 * outer),
         scratch_shapes=[
             pltpu.VMEM((edges, hidden_width), F32),
             pltpu.VMEM((edges, hidden_width), BF16),
@@ -325,33 +392,56 @@
             pltpu.VMEM((grad_rows, hidden_width), F32),
             pltpu.VMEM((slot_rows, width), F32),
             pltpu.VMEM((slot_rows, width), F32),
+            pltpu.VMEM(slot_index.shape, jnp.int32),
+            pltpu.VMEM(dst_index.shape, jnp.int32),
+            pltpu.VMEM(mesh_latent.shape, BF16),
+            pltpu.VMEM((width, hidden_width), BF16),
+            pltpu.VMEM(w_edge2.shape, BF16),
+            pltpu.VMEM((w_node1.shape[0] - width, w_node1.shape[1]), BF16),
+            pltpu.VMEM(w_node2.shape, BF16),
+            pltpu.SemaphoreType.DMA((7,)),
         ],
-        compiler_params=params(),
+        compiler_params=params(36),
         name="edges",
     )(
         slot_index,
         dst_index,
-        slots,
-        base,
-        turned,
         mesh_latent,
-        node,
-        cot,
         w_edge1,
         w_edge2,
         w_node1,
         w_node2,
+        slots,
+        base,
+        turned,
+        hot,
+        node,
+        cot,
     )
     sends, keeps = sides[:outer], sides[outer:]
 
+    def after(value, *others):
+        return lax.optimization_barrier((value, *others))[0]
+
+    order = list(range(outer - 1, -1, -1))
+    crossed = {order[0]: to_core(sends[order[0]])}
+    for far_outer in order[1:]:
+        crossed[far_outer] = to_core(after(sends[far_outer], crossed[order[0]]))
     own_sums = None
     arrived = []
-    for far_outer in range(outer - 1, -1, -1):
-        half = keeps[far_outer] + to_core(sends[far_outer]).astype(F32)
+    before = None
+    for far_outer in order:
+        half = keeps[far_outer] + crossed[far_outer].astype(F32)
         total = half[:chunk]
+        received = []
         for far_inner in range(1, inner):
             part = half[far_inner * chunk : (far_inner + 1) * chunk].astype(BF16)
-            total = total + to_inner(part, far_inner).astype(F32)
+            if before is not None:
+                part = after(part, *before)
+            received.append(to_inner(part, far_inner))
+        before = received
+        for value in received:
+            total = total + value.astype(F32)
         if far_outer:
             arrived.append(to_outer(total.astype(BF16), far_outer))
         else:
@@ -360,7 +450,14 @@
         own_sums = own_sums + value.astype(F32)
     own = own_sums.astype(BF16)
 
-    pieces = [own] + [to_outer(own, far_outer) for far_outer in range(1, outer)]
+    turns = []
+    for step in range(1, outer // 2 + 1):
+        turns += [outer - step] + [step] * (step != outer - step)
+    fetched = {0: own}
+    for at, far_outer in enumerate(turns):
+        value = own if at < 2 else after(own, fetched[turns[at - 2]])
+        fetched[far_outer] = to_outer(value, far_outer)
+    pieces = [fetched[far_outer] for far_outer in range(outer)]
     for far_inner in range(1, inner):
         pieces += [to_inner(value, far_inner) for value in pieces[:outer]]
     pieces += [to_core(value) for value in pieces]
@@ -374,19 +471,31 @@
         functools.partial(put_kernel, sizes),
         out_shape=jax.ShapeDtypeStruct(grid_latent.shape, F32),
         scratch_shapes=[pltpu.VMEM((slot_rows, width), F32)],
-        compiler_params=params(),
+        compiler_params=params(16),
         name="put",
     )(send_rows, back.reshape(slot_rows, width))
 
-    grad_edge1, grad_edge2 = pl.pallas_call(
-        functools.partial(order_kernel, sizes),
-        out_shape=[
-            jax.ShapeDtypeStruct((3 * width, hidden_width), F32),
-            jax.ShapeDtypeStruct((hidden_width, width), F32),
-        ],
-        compiler_params=params(),
-        name="order",
-    )(*pieces)
+    late = [at for at in range(band_count) if at % outer == turns[-1]]
+    early = [at for at in range(band_count) if at % outer != turns[-1]]
+    grads = []
+    for places in (early, late):
+        grads = pl.pallas_call(
+            functools.partial(order_kernel, sizes, places, len(grads)),
+            out_shape=[
+                jax.ShapeDtypeStruct((3 * width, hidden_width), F32),
+                jax.ShapeDtypeStruct((hidden_width, width), F32),
+            ],
+            in_specs=specs(pltpu.VMEM, len(places)) + specs(pltpu.HBM, len(grads)),
+            out_specs=specs(pltpu.HBM, 2),
+            scratch_shapes=[
+                pltpu.VMEM((len(places), chunk, hidden_width), F32),
+                pltpu.SemaphoreType.DMA((len(places),)),
+            ],
+            input_output_aliases={len(places) + k: k for k in range(len(grads))},
+            compiler_params=params(16),
+            name="order",
+        )(*[pieces[at] for at in places], *grads)
+    grad_edge1, grad_edge2 = grads
     return (mesh_out, grid_grad, grad_edge1, grad_edge2)
 
 

time: 93.4 us -> 106 us (1.13)
  local copies, waits for them, and re-layouts: 8.42 us -> 22.6 us
  waiting for transfers between devices: 20.5 us -> 33.8 us
  Pallas kernels: 26.4 us -> 16 us
  starting transfers between devices: 36.3 us -> 30.8 us
    unnamed x26 -> x50, local copies, waits for them, and re-layouts: 8.33 us -> 22.5 us
    ppermute x31, waiting for transfers between devices: 20.5 us -> 33.8 us  [permute(): return lax.ppermute(value, 'band', pairs)]
    pallas_call x1, Pallas kernels: 13.8 us -> 7.01 us  [shards(): pl.pallas_call(functools.partial(main_kernel, lines, sizes), out_shape=[j...]
    ppermute x31, starting transfers between devices: 28.9 us -> 23.4 us  [permute(): return lax.ppermute(value, 'band', pairs)]
    pallas_call x1, Pallas kernels: 7.32 us -> 3.28 us  [shards(): pl.pallas_call(functools.partial(base_kernel, lines), out_shape=[jax.Shap...]
    pallas_call x1 -> x2, Pallas kernels: 2.5 us -> 2.8 us  [shards(): pl.pallas_call(functools.partial(order_kernel, sizes, places, len(grads))...]
  transfers between devices with their start and end apart: 32 -> 32, of which waited for: 8 -> 13; matrix products, arithmetic and copies ran while one was open for 1% -> 1% of each run, Pallas kernels for 10% -> 7%
where the time goes in v3:
time: 106 us; the launch traced here: 105 us
  waiting for transfers between devices  33.8 us (32%)
  starting transfers between devices  30.8 us (29%)
  local copies, waits for them, and re-layouts  22.6 us (21%)
  Pallas kernels  16 us (15%)
    ppermute x31, waiting for transfers between devices, permute(): return lax.ppermute(value, 'band', pairs)  33.8 us
    ppermute x31, starting transfers between devices, permute(): return lax.ppermute(value, 'band', pairs)  23.4 us
    unnamed x50, local copies, waits for them, and re-layouts  22.5 us
    all_to_all x1, starting transfers between devices, shards(): lax.all_to_all(outgoing.reshape(band_count, -1, width), 'band', split_axi...  7.4 us
    pallas_call x1, Pallas kernels, shards(): pl.pallas_call(functools.partial(main_kernel, lines, sizes), out_shape=[j...  7.01 us
    pallas_call x1, Pallas kernels, shards(): pl.pallas_call(functools.partial(base_kernel, lines), out_shape=[jax.Shap...  3.28 us
    pallas_call x2, Pallas kernels, shards(): pl.pallas_call(functools.partial(order_kernel, sizes, places, len(grads))...  2.8 us
  transfers between devices with their start and end apart: 32, of which 13 were waited for; matrix products, arithmetic and copies ran while one was open for 1% of the time, Pallas kernels for 7%

profile of v3, /device:TPU:0, one launch (start us, length us, event | category | flops | bytes accessed | tf_op | source)
XLA Modules:
  0.0 104.7 jit_solution(16230790382464678113)
XLA Ops:
  3.7 7.4 %all-to-all-start = ((bf16[16,8,512]{2,1,0:T(8,128)(2,1)}), bf16[16,8,512]{2,1,0:T(8,128)(2,1)S(1)}, u32[]{:S(2)}, u32[]{:S(2)}) async-start(bf16[16,8,512]{2,1,0:T(8,128)(2,1)} %bitcast.2), calls=%async_computation | async-start | bytes 262144 | tf_op jit(solution)/shard_map/all_to_all | solution.py:345
  18.8 3.3 %base.1 = (f32[1536,512]{1,0:T(8,128)S(1)}, bf16[512,1536]{1,0:T(8,128)(2,1)S(1)}, bf16[1536,256]{1,0:T(8,128)(2,1)S(1)}, f32[256,512]{1,0:T(8,128)S(1)}, f32[256,512]{1,0:T(8,128)S(1)}) custom-call(s32[12,128]{1,0:T(8,128)S(1)} %bitcast.29, bf16[256,512]{1,0:T(8,128)(2,1)S(1)} %copy-done.16, bf16[1536,512]{1,0:T(8,128)(2,1)S(1)} %copy-done.23, ...), custom_call_target="tpu_custom_call" | custom-call | flops 1610612736 | bytes 6291456 | tf_op jit(solution)/shard_map/base/pallas_call | solution.py:349
  35.1 7.0 %edges.1 = (bf16[256,512]{1,0:T(8,128)(2,1)}, bf16[128,512]{1,0:T(8,128)(2,1)S(1)}, bf16[256,512]{1,0:T(8,128)(2,1)S(1)}, bf16[256,512]{1,0:T(8,128)(2,1)S(1)}, ...) custom-call(s32[12,128]{1,0:T(8,128)S(1)} %bitcast.28, ...), custom_call_target="tpu_custom_call" | custom-call | tf_op jit(solution)/shard_map/edges/pallas_call | solution.py:378
  43.8 2.0 %collective-permute-start.9 = (bf16[128,512]{1,0:T(8,128)(2,1)S(1)}, bf16[128,512]{1,0:T(8,128)(2,1)S(1)}, u32[]{:S(2)}, u32[]{:S(2)}) collective-permute-start(bf16[128,512]{1,0:T(8,128)(2,1)S(1)} %slice.138), channel_id=1, source_target_pairs={{0,2},{1,3},{2,0},{3,1},{4,6},{5,7},{6,4},{7,5},{8,10},{9,11},{10,... | collective-permute-start | bytes 393224 | tf_op jit(solution)/shard_map/ppermute | solution.py:321
  46.3 3.4 %collective-permute-done.9 = bf16[128,512]{1,0:T(8,128)(2,1)S(1)} collective-permute-done((bf16[128,512]{1,0:T(8,128)(2,1)S(1)}, bf16[128,512]{1,0:T(8,128)(2,1)S(1)}, u32[]{:S(2)}, u32[]{:S(2)}) %collective-permute-start.9) | collective-permute-done | bytes 131104 | tf_op jit(solution)/shard_map/ppermute | solution.py:321
  49.7 3.5 %collective-permute-start.13 = (bf16[128,512]{1,0:T(8,128)(2,1)S(1)}, bf16[128,512]{1,0:T(8,128)(2,1)S(1)}, u32[]{:S(2)}, u32[]{:S(2)}) collective-permute-start(bf16[128,512]{1,0:T(8,128)(2,1)S(1)} %fusion.2), channel_id=1, source_target_pairs={{0,12},{1,13},{2,14},{3,15},{4,8},{5,9},{6,10},{7,11},{8,4},{9,5},... | collective-permute-start | bytes 393224 | tf_op jit(solution)/shard_map/ppermute | solution.py:321
  53.4 1.5 %collective-permute-start.10 = (bf16[128,512]{1,0:T(8,128)(2,1)S(1)}, bf16[128,512]{1,0:T(8,128)(2,1)S(1)}, u32[]{:S(2)}, u32[]{:S(2)}) collective-permute-start(bf16[128,512]{1,0:T(8,128)(2,1)S(1)} %slice.139), channel_id=1, source_target_pairs={{0,2},{1,3},{2,0},{3,1},{4,6},{5,7},{6,4},{7,5},{8,10},{9,11},{10,... | collective-permute-start | bytes 393224 | tf_op jit(solution)/shard_map/ppermute | solution.py:321
  55.1 3.3 %collective-permute-done.10 = bf16[128,512]{1,0:T(8,128)(2,1)S(1)} collective-permute-done((bf16[128,512]{1,0:T(8,128)(2,1)S(1)}, bf16[128,512]{1,0:T(8,128)(2,1)S(1)}, u32[]{:S(2)}, u32[]{:S(2)}) %collective-permute-start.10) | collective-permute-done | bytes 131104 | tf_op jit(solution)/shard_map/ppermute | solution.py:321
  58.4 1.5 %collective-permute-start.11 = (bf16[128,512]{1,0:T(8,128)(2,1)S(1)}, bf16[128,512]{1,0:T(8,128)(2,1)S(1)}, u32[]{:S(2)}, u32[]{:S(2)}) collective-permute-start(bf16[128,512]{1,0:T(8,128)(2,1)S(1)} %slice.140), channel_id=1, source_target_pairs={{0,2},{1,3},{2,0},{3,1},{4,6},{5,7},{6,4},{7,5},{8,10},{9,11},{10,... | collective-permute-start | bytes 393224 | tf_op jit(solution)/shard_map/ppermute | solution.py:321
  60.0 3.8 %collective-permute-done.11 = bf16[128,512]{1,0:T(8,128)(2,1)S(1)} collective-permute-done((bf16[128,512]{1,0:T(8,128)(2,1)S(1)}, bf16[128,512]{1,0:T(8,128)(2,1)S(1)}, u32[]{:S(2)}, u32[]{:S(2)}) %collective-permute-start.11) | collective-permute-done | bytes 131104 | tf_op jit(solution)/shard_map/ppermute | solution.py:321
  63.7 1.5 %collective-permute-start.12 = (bf16[128,512]{1,0:T(8,128)(2,1)S(1)}, bf16[128,512]{1,0:T(8,128)(2,1)S(1)}, u32[]{:S(2)}, u32[]{:S(2)}) collective-permute-start(bf16[128,512]{1,0:T(8,128)(2,1)S(1)} %slice.141), channel_id=1, source_target_pairs={{0,2},{1,3},{2,0},{3,1},{4,6},{5,7},{6,4},{7,5},{8,10},{9,11},{10,... | collective-permute-start | bytes 393224 | tf_op jit(solution)/shard_map/ppermute | solution.py:321
  66.8 1.9 %collective-permute-done.12 = bf16[128,512]{1,0:T(8,128)(2,1)S(1)} collective-permute-done((bf16[128,512]{1,0:T(8,128)(2,1)S(1)}, bf16[128,512]{1,0:T(8,128)(2,1)S(1)}, u32[]{:S(2)}, u32[]{:S(2)}) %collective-permute-start.12) | collective-permute-done | bytes 131104 | tf_op jit(solution)/shard_map/ppermute | solution.py:321
  68.7 1.7 %collective-permute-done.15 = bf16[128,512]{1,0:T(8,128)(2,1)S(1)} collective-permute-done((bf16[128,512]{1,0:T(8,128)(2,1)S(1)}, bf16[128,512]{1,0:T(8,128)(2,1)S(1)}, u32[]{:S(2)}, u32[]{:S(2)}) %collective-permute-start.15) | collective-permute-done | bytes 131104 | tf_op jit(solution)/shard_map/ppermute | solution.py:321
  71.5 1.9 %collective-permute-start.22 = (bf16[128,512]{1,0:T(8,128)(2,1)S(1)}, bf16[128,512]{1,0:T(8,128)(2,1)S(1)}, u32[]{:S(2)}, u32[]{:S(2)}) collective-permute-start(bf16[128,512]{1,0:T(8,128)(2,1)S(1)} %fusion.6.refs_0_), channel_id=1, source_target_pairs={{0,2},{1,3},{2,0},{3,1},{4,6},{5,7},{6,4},{7,5},{8,10},{9,11},{10,... | collective-permute-start | bytes 393224 | tf_op jit(solution)/shard_map/ppermute | solution.py:321
  73.4 4.0 %collective-permute-done.16.refs_2_ = bf16[128,512]{1,0:T(8,128)(2,1)S(1)} collective-permute-done((bf16[128,512]{1,0:T(8,128)(2,1)S(1)}, bf16[128,512]{1,0:T(8,128)(2,1)S(1)}, u32[]{:S(2)}, u32[]{:S(2)}) %collective-permute-start.16) | collective-permute-done | bytes 131104 | tf_op jit(solution)/shard_map/ppermute | solution.py:321
  78.7 3.0 %collective-permute-done.2 = bf16[2,2,8,512]{3,2,1,0:T(8,128)(2,1)S(1)} collective-permute-done((bf16[2,2,8,512]{3,2,1,0:T(8,128)(2,1)S(1)}, bf16[2,2,8,512]{3,2,1,0:T(8,128)(2,1)S(1)}, u32[]{:S(2)}, u32[]{:S(2)}) %collective-permute-start.2) | collective-permute-done | bytes 32800 | tf_op jit(solution)/shard_map/ppermute | solution.py:321
  81.8 2.6 %collective-permute-start.3 = (bf16[2,2,8,512]{3,2,1,0:T(8,128)(2,1)S(1)}, bf16[2,2,8,512]{3,2,1,0:T(8,128)(2,1)S(1)}, u32[]{:S(2)}, u32[]{:S(2)}) collective-permute-start(bf16[2,2,8,512]{3,2,1,0:T(8,128)(2,1)S(1)} %get-tuple-element.59), channel_id=1, source_target_pairs={{0,8},{1,9},{2,10},{3,11},{4,12},{5,13},{6,14},{7,15},{8,0},{9,1},... | collective-permute-start | bytes 98312 | tf_op jit(solution)/shard_map/ppermute | solution.py:321
  84.4 2.2 %collective-permute-done.3 = bf16[2,2,8,512]{3,2,1,0:T(8,128)(2,1)S(1)} collective-permute-done((bf16[2,2,8,512]{3,2,1,0:T(8,128)(2,1)S(1)}, bf16[2,2,8,512]{3,2,1,0:T(8,128)(2,1)S(1)}, u32[]{:S(2)}, u32[]{:S(2)}) %collective-permute-start.3) | collective-permute-done | bytes 32800 | tf_op jit(solution)/shard_map/ppermute | solution.py:321
  86.6 2.1 %collective-permute-start.4 = (bf16[2,2,8,512]{3,2,1,0:T(8,128)(2,1)S(1)}, bf16[2,2,8,512]{3,2,1,0:T(8,128)(2,1)S(1)}, u32[]{:S(2)}, u32[]{:S(2)}) collective-permute-start(bf16[2,2,8,512]{3,2,1,0:T(8,128)(2,1)S(1)} %get-tuple-element.58), channel_id=1, source_target_pairs={{0,12},{1,13},{2,14},{3,15},{4,8},{5,9},{6,10},{7,11},{8,4},{9,5},... | collective-permute-start | bytes 98312 | tf_op jit(solution)/shard_map/ppermute | solution.py:321
  89.0 3.3 %collective-permute-done.4 = bf16[2,2,8,512]{3,2,1,0:T(8,128)(2,1)S(1)} collective-permute-done((bf16[2,2,8,512]{3,2,1,0:T(8,128)(2,1)S(1)}, bf16[2,2,8,512]{3,2,1,0:T(8,128)(2,1)S(1)}, u32[]{:S(2)}, u32[]{:S(2)}) %collective-permute-start.4) | collective-permute-done | bytes 32800 | tf_op jit(solution)/shard_map/ppermute | solution.py:321
  93.2 1.7 %collective-permute-start.18 = (bf16[128,512]{1,0:T(8,128)(2,1)S(1)}, bf16[128,512]{1,0:T(8,128)(2,1)S(1)}, u32[]{:S(2)}, u32[]{:S(2)}) collective-permute-start(bf16[128,512]{1,0:T(8,128)(2,1)S(1)} %collective-permute-done.17.refs_0_), channel_id=1, source_target_pairs={{0,2},{1,3},{2,0},{3,1},{4,6},{5,7},{6,4},{7,5},{8,10},{9,11},{10,... | collective-permute-start | bytes 393224 | tf_op jit(solution)/shard_map/ppermute | solution.py:321
  94.9 3.8 %collective-permute-done.24.refs_5_ = bf16[128,512]{1,0:T(8,128)(2,1)S(1)} collective-permute-done((bf16[128,512]{1,0:T(8,128)(2,1)S(1)}, bf16[128,512]{1,0:T(8,128)(2,1)S(1)}, u32[]{:S(2)}, u32[]{:S(2)}) %collective-permute-start.24) | collective-permute-done | bytes 131104 | tf_op jit(solution)/shard_map/ppermute | solution.py:321
  100.1 1.8 %put.1 = f32[1024,512]{1,0:T(8,128)} custom-call(s32[1,128]{1,0:T(1,128)S(1)} %copy-done.22, bf16[128,512]{1,0:T(8,128)(2,1)S(1)} %bitcast.26), custom_call_target="tpu_custom_call" | custom-call | tf_op jit(solution)/shard_map/put/pallas_call | solution.py:470
  101.9 1.8 %order.2 = (f32[1536,512]{1,0:T(8,128)}, f32[512,512]{1,0:T(8,128)}) custom-call(bf16[128,512]{1,0:T(8,128)(2,1)S(1)} %fusion.6.refs_0_, bf16[128,512]{1,0:T(8,128)(2,1)S(1)} %collective-permute-done.21.refs_1_, bf16[128,512]{1,0:T(8,128)(2,1)S(1)} %collective-permute-done.16.refs_2_, bf16[128,512]{1,0:T(8,128)(2,1)S(1)} %collective-permute-done.22.refs_3_, ...), custom_call_target="tpu_custom_call" | custom-call | tf_op jit(solution)/shard_map/order/pallas_call | solution.py:482
  (112 shorter events, 33.9 us)
Async XLA Ops:
  3.7 22.0 %all-to-all-start = ((bf16[16,8,512]{2,1,0:T(8,128)(2,1)}), bf16[16,8,512]{2,1,0:T(8,128)(2,1)S(1)}, u32[]{:S(2)}, u32[]{:S(2)}) async-start(bf16[16,8,512]{2,1,0:T(8,128)(2,1)} %bitcast.2), calls=%async_computation | async-start | bytes 262144 | tf_op jit(solution)/shard_map/all_to_all | solution.py:345
  43.8 5.8 %collective-permute-start.9 = (bf16[128,512]{1,0:T(8,128)(2,1)S(1)}, bf16[128,512]{1,0:T(8,128)(2,1)S(1)}, u32[]{:S(2)}, u32[]{:S(2)}) collective-permute-start(bf16[128,512]{1,0:T(8,128)(2,1)S(1)} %slice.138), channel_id=1, source_target_pairs={{0,2},{1,3},{2,0},{3,1},{4,6},{5,7},{6,4},{7,5},{8,10},{9,11},{10,... | collective-permute-start | bytes 393224 | tf_op jit(solution)/shard_map/ppermute | solution.py:321
  45.8 7.5 %collective-permute-start.8 = (bf16[256,512]{1,0:T(8,128)(2,1)S(1)}, bf16[256,512]{1,0:T(8,128)(2,1)S(1)}, u32[]{:S(2)}, u32[]{:S(2)}) collective-permute-start(bf16[256,512]{1,0:T(8,128)(2,1)S(1)} %get-tuple-element.46), channel_id=1, source_target_pairs={{0,1},{1,0},{2,3},{3,2},{4,5},{5,4},{6,7},{7,6},{8,9},{9,8},{10,11... | collective-permute-start | bytes 786440 | tf_op jit(solution)/shard_map/ppermute | solution.py:321
  45.8 9.1 %collective-permute-start.7 = (bf16[256,512]{1,0:T(8,128)(2,1)S(1)}, bf16[256,512]{1,0:T(8,128)(2,1)S(1)}, u32[]{:S(2)}, u32[]{:S(2)}) collective-permute-start(bf16[256,512]{1,0:T(8,128)(2,1)S(1)} %get-tuple-element.43), channel_id=1, source_target_pairs={{0,1},{1,0},{2,3},{3,2},{4,5},{5,4},{6,7},{7,6},{8,9},{9,8},{10,11... | collective-permute-start | bytes 786440 | tf_op jit(solution)/shard_map/ppermute | solution.py:321
  46.3 8.7 %collective-permute-start.6 = (bf16[256,512]{1,0:T(8,128)(2,1)S(1)}, bf16[256,512]{1,0:T(8,128)(2,1)S(1)}, u32[]{:S(2)}, u32[]{:S(2)}) collective-permute-start(bf16[256,512]{1,0:T(8,128)(2,1)S(1)} %get-tuple-element.40), channel_id=1, source_target_pairs={{0,1},{1,0},{2,3},{3,2},{4,5},{5,4},{6,7},{7,6},{8,9},{9,8},{10,11... | collective-permute-start | bytes 786440 | tf_op jit(solution)/shard_map/ppermute | solution.py:321
  49.7 15.7 %collective-permute-start.13 = (bf16[128,512]{1,0:T(8,128)(2,1)S(1)}, bf16[128,512]{1,0:T(8,128)(2,1)S(1)}, u32[]{:S(2)}, u32[]{:S(2)}) collective-permute-start(bf16[128,512]{1,0:T(8,128)(2,1)S(1)} %fusion.2), channel_id=1, source_target_pairs={{0,12},{1,13},{2,14},{3,15},{4,8},{5,9},{6,10},{7,11},{8,4},{9,5},... | collective-permute-start | bytes 393224 | tf_op jit(solution)/shard_map/ppermute | solution.py:321
  53.4 5.0 %collective-permute-start.10 = (bf16[128,512]{1,0:T(8,128)(2,1)S(1)}, bf16[128,512]{1,0:T(8,128)(2,1)S(1)}, u32[]{:S(2)}, u32[]{:S(2)}) collective-permute-start(bf16[128,512]{1,0:T(8,128)(2,1)S(1)} %slice.139), channel_id=1, source_target_pairs={{0,2},{1,3},{2,0},{3,1},{4,6},{5,7},{6,4},{7,5},{8,10},{9,11},{10,... | collective-permute-start | bytes 393224 | tf_op jit(solution)/shard_map/ppermute | solution.py:321
  58.4 5.3 %collective-permute-start.11 = (bf16[128,512]{1,0:T(8,128)(2,1)S(1)}, bf16[128,512]{1,0:T(8,128)(2,1)S(1)}, u32[]{:S(2)}, u32[]{:S(2)}) collective-permute-start(bf16[128,512]{1,0:T(8,128)(2,1)S(1)} %slice.140), channel_id=1, source_target_pairs={{0,2},{1,3},{2,0},{3,1},{4,6},{5,7},{6,4},{7,5},{8,10},{9,11},{10,... | collective-permute-start | bytes 393224 | tf_op jit(solution)/shard_map/ppermute | solution.py:321
  59.9 6.9 %collective-permute-start.14 = (bf16[128,512]{1,0:T(8,128)(2,1)S(1)}, bf16[128,512]{1,0:T(8,128)(2,1)S(1)}, u32[]{:S(2)}, u32[]{:S(2)}) collective-permute-start(bf16[128,512]{1,0:T(8,128)(2,1)S(1)} %fusion.1), channel_id=1, source_target_pairs={{0,8},{1,9},{2,10},{3,11},{4,12},{5,13},{6,14},{7,15},{8,0},{9,1},... | collective-permute-start | bytes 393224 | tf_op jit(solution)/shard_map/ppermute | solution.py:321
  65.2 5.2 %collective-permute-start.15 = (bf16[128,512]{1,0:T(8,128)(2,1)S(1)}, bf16[128,512]{1,0:T(8,128)(2,1)S(1)}, u32[]{:S(2)}, u32[]{:S(2)}) collective-permute-start(bf16[128,512]{1,0:T(8,128)(2,1)S(1)} %fusion), channel_id=1, source_target_pairs={{0,4},{1,5},{2,6},{3,7},{4,0},{5,1},{6,2},{7,3},{8,12},{9,13},{10,... | collective-permute-start | bytes 393224 | tf_op jit(solution)/shard_map/ppermute | solution.py:321
  65.3 6.0 %collective-permute-start = (bf16[2,4,8,512]{3,2,1,0:T(8,128)(2,1)S(1)}, bf16[2,4,8,512]{3,2,1,0:T(8,128)(2,1)S(1)}, u32[]{:S(2)}, u32[]{:S(2)}) collective-permute-start(bf16[2,4,8,512]{3,2,1,0:T(8,128)(2,1)S(1)} %bitcast.33), channel_id=1, source_target_pairs={{0,1},{1,0},{2,3},{3,2},{4,5},{5,4},{6,7},{7,6},{8,9},{9,8},{10,11... | collective-permute-start | bytes 196616 | tf_op jit(solution)/shard_map/ppermute | solution.py:321
  70.5 6.9 %collective-permute-start.16 = (bf16[128,512]{1,0:T(8,128)(2,1)S(1)}, bf16[128,512]{1,0:T(8,128)(2,1)S(1)}, u32[]{:S(2)}, u32[]{:S(2)}) collective-permute-start(bf16[128,512]{1,0:T(8,128)(2,1)S(1)} %fusion.6.refs_0_), channel_id=1, source_target_pairs={{0,12},{1,13},{2,14},{3,15},{4,8},{5,9},{6,10},{7,11},{8,4},{9,5},... | collective-permute-start | bytes 393224 | tf_op jit(solution)/shard_map/ppermute | solution.py:321
  71.3 6.1 %collective-permute-start.1 = (bf16[4,2,8,512]{3,2,1,0:T(8,128)(2,1)S(1)}, bf16[4,2,8,512]{3,2,1,0:T(8,128)(2,1)S(1)}, u32[]{:S(2)}, u32[]{:S(2)}) collective-permute-start(bf16[4,2,8,512]{3,2,1,0:T(8,128)(2,1)S(1)} %get-tuple-element.61), channel_id=1, source_target_pairs={{0,2},{1,3},{2,0},{3,1},{4,6},{5,7},{6,4},{7,5},{8,10},{9,11},{10,... | collective-permute-start | bytes 196616 | tf_op jit(solution)/shard_map/ppermute | solution.py:321
  71.5 17.2 %collective-permute-start.21 = (bf16[128,512]{1,0:T(8,128)(2,1)S(1)}, bf16[128,512]{1,0:T(8,128)(2,1)S(1)}, u32[]{:S(2)}, u32[]{:S(2)}) collective-permute-start(bf16[128,512]{1,0:T(8,128)(2,1)S(1)} %fusion.6.refs_0_), channel_id=1, source_target_pairs={{0,4},{1,5},{2,6},{3,7},{4,0},{5,1},{6,2},{7,3},{8,12},{9,13},{10,... | collective-permute-start | bytes 393224 | tf_op jit(solution)/shard_map/ppermute | solution.py:321
  71.5 21.2 %collective-permute-start.22 = (bf16[128,512]{1,0:T(8,128)(2,1)S(1)}, bf16[128,512]{1,0:T(8,128)(2,1)S(1)}, u32[]{:S(2)}, u32[]{:S(2)}) collective-permute-start(bf16[128,512]{1,0:T(8,128)(2,1)S(1)} %fusion.6.refs_0_), channel_id=1, source_target_pairs={{0,2},{1,3},{2,0},{3,1},{4,6},{5,7},{6,4},{7,5},{8,10},{9,11},{10,... | collective-permute-start | bytes 393224 | tf_op jit(solution)/shard_map/ppermute | solution.py:321
  73.4 19.2 %collective-permute-start.25 = (bf16[128,512]{1,0:T(8,128)(2,1)S(1)}, bf16[128,512]{1,0:T(8,128)(2,1)S(1)}, u32[]{:S(2)}, u32[]{:S(2)}) collective-permute-start(bf16[128,512]{1,0:T(8,128)(2,1)S(1)} %fusion.6.refs_0_), channel_id=1, source_target_pairs={{0,1},{1,0},{2,3},{3,2},{4,5},{5,4},{6,7},{7,6},{8,9},{9,8},{10,11... | collective-permute-start | bytes 393224 | tf_op jit(solution)/shard_map/ppermute | solution.py:321
  77.5 15.7 %collective-permute-start.17 = (bf16[128,512]{1,0:T(8,128)(2,1)S(1)}, bf16[128,512]{1,0:T(8,128)(2,1)S(1)}, u32[]{:S(2)}, u32[]{:S(2)}) collective-permute-start(bf16[128,512]{1,0:T(8,128)(2,1)S(1)} %fusion.6.refs_0_), channel_id=1, source_target_pairs={{0,8},{1,9},{2,10},{3,11},{4,12},{5,13},{6,14},{7,15},{8,0},{9,1},... | collective-permute-start | bytes 393224 | tf_op jit(solution)/shard_map/ppermute | solution.py:321
  86.6 5.7 %collective-permute-start.4 = (bf16[2,2,8,512]{3,2,1,0:T(8,128)(2,1)S(1)}, bf16[2,2,8,512]{3,2,1,0:T(8,128)(2,1)S(1)}, u32[]{:S(2)}, u32[]{:S(2)}) collective-permute-start(bf16[2,2,8,512]{3,2,1,0:T(8,128)(2,1)S(1)} %get-tuple-element.58), channel_id=1, source_target_pairs={{0,12},{1,13},{2,14},{3,15},{4,8},{5,9},{6,10},{7,11},{8,4},{9,5},... | collective-permute-start | bytes 98312 | tf_op jit(solution)/shard_map/ppermute | solution.py:321
  88.7 6.2 %collective-permute-start.23 = (bf16[128,512]{1,0:T(8,128)(2,1)S(1)}, bf16[128,512]{1,0:T(8,128)(2,1)S(1)}, u32[]{:S(2)}, u32[]{:S(2)}) collective-permute-start(bf16[128,512]{1,0:T(8,128)(2,1)S(1)} %collective-permute-done.21.refs_1_), channel_id=1, source_target_pairs={{0,2},{1,3},{2,0},{3,1},{4,6},{5,7},{6,4},{7,5},{8,10},{9,11},{10,... | collective-permute-start | bytes 393224 | tf_op jit(solution)/shard_map/ppermute | solution.py:321
  92.3 6.4 %collective-permute-start.24 = (bf16[128,512]{1,0:T(8,128)(2,1)S(1)}, bf16[128,512]{1,0:T(8,128)(2,1)S(1)}, u32[]{:S(2)}, u32[]{:S(2)}) collective-permute-start(bf16[128,512]{1,0:T(8,128)(2,1)S(1)} %collective-permute-done.16.refs_2_), channel_id=1, source_target_pairs={{0,2},{1,3},{2,0},{3,1},{4,6},{5,7},{6,4},{7,5},{8,10},{9,11},{10,... | collective-permute-start | bytes 393224 | tf_op jit(solution)/shard_map/ppermute | solution.py:321
  92.7 6.0 %collective-permute-start.26 = (bf16[128,512]{1,0:T(8,128)(2,1)S(1)}, bf16[128,512]{1,0:T(8,128)(2,1)S(1)}, u32[]{:S(2)}, u32[]{:S(2)}) collective-permute-start(bf16[128,512]{1,0:T(8,128)(2,1)S(1)} %collective-permute-done.21.refs_1_), channel_id=1, source_target_pairs={{0,1},{1,0},{2,3},{3,2},{4,5},{5,4},{6,7},{7,6},{8,9},{9,8},{10,11... | collective-permute-start | bytes 393224 | tf_op jit(solution)/shard_map/ppermute | solution.py:321
  92.7 6.5 %collective-permute-start.27 = (bf16[128,512]{1,0:T(8,128)(2,1)S(1)}, bf16[128,512]{1,0:T(8,128)(2,1)S(1)}, u32[]{:S(2)}, u32[]{:S(2)}) collective-permute-start(bf16[128,512]{1,0:T(8,128)(2,1)S(1)} %collective-permute-done.16.refs_2_), channel_id=1, source_target_pairs={{0,1},{1,0},{2,3},{3,2},{4,5},{5,4},{6,7},{7,6},{8,9},{9,8},{10,11... | collective-permute-start | bytes 393224 | tf_op jit(solution)/shard_map/ppermute | solution.py:321
  93.2 6.9 %collective-permute-start.18 = (bf16[128,512]{1,0:T(8,128)(2,1)S(1)}, bf16[128,512]{1,0:T(8,128)(2,1)S(1)}, u32[]{:S(2)}, u32[]{:S(2)}) collective-permute-start(bf16[128,512]{1,0:T(8,128)(2,1)S(1)} %collective-permute-done.17.refs_0_), channel_id=1, source_target_pairs={{0,2},{1,3},{2,0},{3,1},{4,6},{5,7},{6,4},{7,5},{8,10},{9,11},{10,... | collective-permute-start | bytes 393224 | tf_op jit(solution)/shard_map/ppermute | solution.py:321
  94.9 7.0 %collective-permute-start.28 = (bf16[128,512]{1,0:T(8,128)(2,1)S(1)}, bf16[128,512]{1,0:T(8,128)(2,1)S(1)}, u32[]{:S(2)}, u32[]{:S(2)}) collective-permute-start(bf16[128,512]{1,0:T(8,128)(2,1)S(1)} %collective-permute-done.22.refs_3_), channel_id=1, source_target_pairs={{0,1},{1,0},{2,3},{3,2},{4,5},{5,4},{6,7},{7,6},{8,9},{9,8},{10,11... | collective-permute-start | bytes 393224 | tf_op jit(solution)/shard_map/ppermute | solution.py:321
  (33 other events, 118.7 us)

commit v4 on v3

--- a/solution.py
+++ b/solution.py
@@ -71,6 +71,10 @@
     return pltpu.CompilerParams(vmem_limit_bytes=mib * MIB)
 
 
+def pinned(space, *values):
+    return [pltpu.with_memory_space_constraint(value, space) for value in values]
+
+
 def specs(space, count):
     return [pl.BlockSpec(memory_space=space)] * count
 
@@ -96,14 +100,16 @@
         out_ref[at * 128 : (at + 1) * 128, :] = dot_nn(some, grid_ref[...]).astype(BF16)
 
 
-def put_kernel(sizes, rows_ref, back_ref, out_ref, ordered_ref):
+def put_kernel(sizes, rows_hbm, back_ref, out_ref, ordered_ref, rows_ref, sems):
     outer, inner = sizes
+    (copy,) = load([(rows_hbm, rows_ref)], sems)
     cap = back_ref.shape[0] // (2 * outer * inner)
     back = back_ref[...].astype(F32)
     for at in range(2 * outer * inner):
         far_core, far_inner, far_outer = at % 2, at // 2 % inner, at // (2 * inner)
         owner = owner_at(sizes, far_outer, far_inner, far_core)
         ordered_ref[pl.ds(pl.multiple_of(owner * cap, cap), cap), :] = back[at * cap : (at + 1) * cap]
+    copy.wait()
     chosen = one_hot_rows(rows_ref[...], out_ref.shape[0])
     out_ref[...] = dot_nn(chosen, ordered_ref[...].astype(BF16))
 
@@ -184,9 +190,9 @@
 ):
     outer, inner = sizes
     mesh_out_ref, d_slots_ref = rest[:2]
-    send_refs, keep_refs = rest[2 : 2 + outer], rest[2 + outer : 2 + 2 * outer]
-    slope_ref, value_ref, both_ref, grads_ref, slot_grads_ref, ordered_ref = rest[2 + 2 * outer : 8 + 2 * outer]
-    slot_ref, dst_ref, mesh_ref, w1_ref, w2_ref, wn1_ref, wn2_ref, sems = rest[8 + 2 * outer :]
+    send_refs, keep_refs = rest[2:4], rest[4:6]
+    slope_ref, value_ref, both_ref, grads_ref, slot_grads_ref, ordered_ref = rest[6:12]
+    slot_ref, dst_ref, mesh_ref, w1_ref, w2_ref, wn1_ref, wn2_ref, sems = rest[12:]
     width = mesh_ref.shape[1]
     mesh_rows = mesh_ref.shape[0]
     slot_rows = slots_ref.shape[0]
@@ -253,11 +259,13 @@
                 from_rows = pl.ds(pl.multiple_of(owner * cap, cap), cap)
                 ordered_ref[at * cap : (at + 1) * cap, :] = slot_grads_ref[from_rows, :]
                 value = grads_ref[pl.ds(pl.multiple_of(owner * chunk, chunk), chunk), :]
-                rows = slice(far_inner * chunk, (far_inner + 1) * chunk)
+                group = 0 if far_outer >= outer // 2 else 1
+                line = far_inner * (outer // 2) + far_outer % (outer // 2)
+                rows = slice(line * chunk, (line + 1) * chunk)
                 if far_core:
-                    send_refs[far_outer][rows, :] = value.astype(BF16)
+                    send_refs[group][rows, :] = value.astype(BF16)
                 else:
-                    keep_refs[far_outer][rows, :] = value
+                    keep_refs[group][rows, :] = value
     d_slots_ref[...] = ordered_ref[...].astype(BF16)
 
 
@@ -341,7 +349,7 @@
         ],
         compiler_params=params(16),
         name="pick",
-    )(send_rows, grid_latent)
+    )(*pinned(pltpu.HBM, send_rows, grid_latent))
     slots = lax.all_to_all(
         outgoing.reshape(band_count, -1, width), "band", split_axis=0, concat_axis=0, tiled=True
     ).reshape(slot_rows, width)
@@ -349,11 +357,11 @@
     base, turned, hot, node, cot = pl.pallas_call(
         functools.partial(base_kernel, lines),
         out_shape=[
-            jax.ShapeDtypeStruct((edges, hidden_width), F32),
-            jax.ShapeDtypeStruct((width, edges), BF16),
-            jax.ShapeDtypeStruct((edges, mesh_rows), BF16),
-            jax.ShapeDtypeStruct((mesh_rows, hidden_width), F32),
-            jax.ShapeDtypeStruct((mesh_rows, hidden_width), F32),
+            pltpu.VMEM((edges, hidden_width), F32),
+            pltpu.VMEM((width, edges), BF16),
+            pltpu.VMEM((edges, mesh_rows), BF16),
+            pltpu.VMEM((mesh_rows, hidden_width), F32),
+            pltpu.VMEM((mesh_rows, hidden_width), F32),
         ],
         in_specs=specs(pltpu.HBM, 7),
         out_specs=specs(pltpu.VMEM, 5),
@@ -370,21 +378,21 @@
         compiler_params=params(20),
         cost_estimate=cost(2 * edges * width * hidden_width * 2, edges * width * 8),
         name="base",
-    )(dst_index, mesh_latent, edge_latent, mesh_cot, w_edge1, w_node1, w_node2)
+    )(*pinned(pltpu.HBM, dst_index, mesh_latent, edge_latent, mesh_cot, w_edge1, w_node1, w_node2))
 
     grad_rows = 3 * width + hidden_width
     chunk = grad_rows // band_count
-    group = (inner * chunk, hidden_width)
+    group = (band_count // 4 * chunk, hidden_width)
     mesh_out, d_slots, *sides = pl.pallas_call(
         functools.partial(main_kernel, lines, sizes),
         out_shape=[
             jax.ShapeDtypeStruct((mesh_rows, width), BF16),
             jax.ShapeDtypeStruct((slot_rows, width), BF16),
         ]
-        + [jax.ShapeDtypeStruct(group, BF16)] * outer
-        + [jax.ShapeDtypeStruct(group, F32)] * outer,
+        + [jax.ShapeDtypeStruct(group, BF16)] * 2
+        + [jax.ShapeDtypeStruct(group, F32)] * 2,
         in_specs=specs(pltpu.HBM, 7) + specs(pltpu.VMEM, 6),
-        out_specs=specs(pltpu.VMEM, 2 + 2 * outer),
+        out_specs=specs(pltpu.VMEM, 6),
         scratch_shapes=[
             pltpu.VMEM((edges, hidden_width), F32),
             pltpu.VMEM((edges, hidden_width), BF16),
@@ -404,76 +412,73 @@
         compiler_params=params(36),
         name="edges",
     )(
-        slot_index,
-        dst_index,
-        mesh_latent,
-        w_edge1,
-        w_edge2,
-        w_node1,
-        w_node2,
+        *pinned(pltpu.HBM, slot_index, dst_index, mesh_latent, w_edge1, w_edge2, w_node1, w_node2),
         slots,
-        base,
-        turned,
-        hot,
-        node,
-        cot,
+        *pinned(pltpu.VMEM, base, turned, hot, node, cot),
     )
-    sends, keeps = sides[:outer], sides[outer:]
-
     def after(value, *others):
         return lax.optimization_barrier((value, *others))[0]
 
-    order = list(range(outer - 1, -1, -1))
-    crossed = {order[0]: to_core(sends[order[0]])}
-    for far_outer in order[1:]:
-        crossed[far_outer] = to_core(after(sends[far_outer], crossed[order[0]]))
-    own_sums = None
-    arrived = []
-    before = None
-    for far_outer in order:
-        half = keeps[far_outer] + crossed[far_outer].astype(F32)
-        total = half[:chunk]
-        received = []
-        for far_inner in range(1, inner):
-            part = half[far_inner * chunk : (far_inner + 1) * chunk].astype(BF16)
-            if before is not None:
-                part = after(part, *before)
-            received.append(to_inner(part, far_inner))
-        before = received
+    far_send, near_send, far_keep, near_keep = sides
+    half = outer // 2
+    rows = half * chunk
+
+    def over_inner(total):
+        parts = [total[k * rows : (k + 1) * rows].astype(BF16) for k in range(1, inner)]
+        received = [to_inner(part, k + 1) for k, part in enumerate(parts)]
+        return total[:rows], received
+
+    def joined(total, received):
         for value in received:
             total = total + value.astype(F32)
-        if far_outer:
-            arrived.append(to_outer(total.astype(BF16), far_outer))
-        else:
-            own_sums = total
-    for value in arrived:
-        own_sums = own_sums + value.astype(F32)
-    own = own_sums.astype(BF16)
-
-    turns = []
-    for step in range(1, outer // 2 + 1):
-        turns += [outer - step] + [step] * (step != outer - step)
-    fetched = {0: own}
-    for at, far_outer in enumerate(turns):
-        value = own if at < 2 else after(own, fetched[turns[at - 2]])
-        fetched[far_outer] = to_outer(value, far_outer)
-    pieces = [fetched[far_outer] for far_outer in range(outer)]
-    for far_inner in range(1, inner):
-        pieces += [to_inner(value, far_inner) for value in pieces[:outer]]
-    pieces += [to_core(value) for value in pieces]
+        return total
+
+    def line(total, k):
+        return total[k * chunk : (k + 1) * chunk]
 
     cap = slot_rows // band_count
     back = d_slots.reshape(2, inner, outer, cap, width)
-    back = jnp.stack([back[0], to_core(back[1])], axis=2)
-    back = jnp.stack([back[0]] + [to_inner(back[k], k) for k in range(1, inner)], axis=1)
+    far_crossed = to_core(far_send)
+    near_crossed, slots_crossed = to_core(after(near_send, far_crossed)), to_core(back[1])
+    far_total, far_received = over_inner(far_keep + far_crossed.astype(F32))
+    back = jnp.stack([back[0], slots_crossed], axis=2)
+    back = jnp.stack([back[0]] + [to_inner(after(back[k], near_crossed), k) for k in range(1, inner)], axis=1)
+    near_total, near_received = over_inner(near_keep + near_crossed.astype(F32))
+    far_total = joined(far_total, [after(value, back) for value in far_received])
+    arrived = [to_outer(line(far_total, k).astype(BF16), half + k) for k in range(half - 1, -1, -1)]
     back = jnp.stack([back[0]] + [to_outer(back[k], k) for k in range(1, outer)], axis=0)
+    near_total = joined(near_total, [after(value, back) for value in near_received])
+    arrived += [to_outer(line(near_total, k).astype(BF16), k) for k in range(half - 1, 0, -1)]
+    own = joined(line(near_total, 0), arrived).astype(BF16)
+
+    turns = []
+    for step in range(1, half + 1):
+        turns += [outer - step] + [step] * (step != outer - step)
+    pieces = {0: own}
+    for far_inner in range(1, inner):
+        pieces[far_inner * outer] = to_inner(own, far_inner)
+    for at, far_outer in enumerate(turns):
+        value = own if at < 2 else after(own, pieces[outer])
+        pieces[far_outer] = to_outer(value, far_outer)
+    for far_inner in range(1, inner):
+        for far_outer in turns:
+            pieces[far_inner * outer + far_outer] = to_inner(pieces[far_outer], far_inner)
+    for at in range(band_count // 2):
+        pieces[band_count // 2 + at] = to_core(pieces[at])
+
     grid_grad = pl.pallas_call(
         functools.partial(put_kernel, sizes),
         out_shape=jax.ShapeDtypeStruct(grid_latent.shape, F32),
-        scratch_shapes=[pltpu.VMEM((slot_rows, width), F32)],
+        in_specs=specs(pltpu.HBM, 1) + specs(pltpu.VMEM, 1),
+        out_specs=pl.BlockSpec(memory_space=pltpu.VMEM),
+        scratch_shapes=[
+            pltpu.VMEM((slot_rows, width), F32),
+            pltpu.VMEM(send_rows.shape, jnp.int32),
+            pltpu.SemaphoreType.DMA((1,)),
+        ],
         compiler_params=params(16),
         name="put",
-    )(send_rows, back.reshape(slot_rows, width))
+    )(*pinned(pltpu.HBM, send_rows), back.reshape(slot_rows, width))
 
     late = [at for at in range(band_count) if at % outer == turns[-1]]
     early = [at for at in range(band_count) if at % outer != turns[-1]]

time: 106 us -> 91.3 us (0.86)
  local copies, waits for them, and re-layouts: 22.6 us -> 8.34 us
  waiting for transfers between devices: 33.8 us -> 27.7 us
  Pallas kernels: 16 us -> 19.5 us
  starting transfers between devices: 30.8 us -> 33.9 us
    unnamed x50 -> x16, local copies, waits for them, and re-layouts: 22.5 us -> 8.23 us
    ppermute x31 -> x27, waiting for transfers between devices: 33.8 us -> 27.7 us  [permute(): return lax.ppermute(value, 'band', pairs)]
    ppermute x31 -> x27, starting transfers between devices: 23.4 us -> 26.5 us  [permute(): return lax.ppermute(value, 'band', pairs)]
  transfers between devices with their start and end apart: 32 -> 28, of which waited for: 13 -> 11; matrix products, arithmetic and copies ran while one was open for 1% -> 1% of each run, Pallas kernels for 7% -> 9%
where the time goes in v4:
time: 91.3 us; the launch traced here: 90.9 us
  starting transfers between devices  33.9 us (37%)
  waiting for transfers between devices  27.7 us (30%)
  Pallas kernels  19.5 us (21%)
  local copies, waits for them, and re-layouts  8.34 us (9%)
    ppermute x27, waiting for transfers between devices, permute(): return lax.ppermute(value, 'band', pairs)  27.7 us
    ppermute x27, starting transfers between devices, permute(): return lax.ppermute(value, 'band', pairs)  26.5 us
    unnamed x16, local copies, waits for them, and re-layouts  8.23 us
    pallas_call x1, Pallas kernels, shards(): pl.pallas_call(functools.partial(main_kernel, lines, sizes), out_shape=[j...  7.85 us
    all_to_all x1, starting transfers between devices, shards(): lax.all_to_all(outgoing.reshape(band_count, -1, width), 'band', split_axi...  7.4 us
    pallas_call x1, Pallas kernels, shards(): pl.pallas_call(functools.partial(base_kernel, lines), out_shape=[pltpu.VM...  4.27 us
    pallas_call x2, Pallas kernels, shards(): pl.pallas_call(functools.partial(order_kernel, sizes, places, len(grads))...  2.8 us
    pallas_call x1, Pallas kernels, shards(): pl.pallas_call(functools.partial(put_kernel, sizes), out_shape=jax.ShapeD...  2.4 us
  transfers between devices with their start and end apart: 28, of which 11 were waited for; matrix products, arithmetic and copies ran while one was open for 1% of the time, Pallas kernels for 9%

profile of v4, /device:TPU:0, one launch (start us, length us, event | category | flops | bytes accessed | tf_op | source)
XLA Modules:
  0.0 90.9 jit_solution(17048516106606446942)
XLA Ops:
  0.6 2.2 %pick.1 = bf16[128,512]{1,0:T(8,128)(2,1)} custom-call(s32[1,128]{1,0:T(1,128)} %rows_hbm.3, bf16[1024,512]{1,0:T(8,128)(2,1)} %grid_hbm.1), custom_call_target="tpu_custom_call" | custom-call | tf_op jit(solution)/shard_map/pick/pallas_call | solution.py:340
  2.9 7.4 %all-to-all-start = ((bf16[16,8,512]{2,1,0:T(8,128)(2,1)}), bf16[16,8,512]{2,1,0:T(8,128)(2,1)S(1)}, u32[]{:S(2)}, u32[]{:S(2)}) async-start(bf16[16,8,512]{2,1,0:T(8,128)(2,1)} %bitcast.2), calls=%async_computation | async-start | bytes 262144 | tf_op jit(solution)/shard_map/all_to_all | solution.py:353
  10.3 4.3 %base.1 = (f32[1536,512]{1,0:T(8,128)S(1)}, bf16[512,1536]{1,0:T(8,128)(2,1)S(1)}, bf16[1536,256]{1,0:T(8,128)(2,1)S(1)}, f32[256,512]{1,0:T(8,128)S(1)}, f32[256,512]{1,0:T(8,128)S(1)}) custom-call(s32[12,128]{1,0:T(8,128)} %bitcast.36, bf16[256,512]{1,0:T(8,128)(2,1)} %mesh_hbm.3, bf16[1536,512]{1,0:T(8,128)(2,1)} %edge_hbm.1, bf16[256,512]{1,0:T(8,128)(2,1)} %cot_hbm.1, ...), custom_call_target="tpu_custom_call" | custom-call | flops 1610612736 | bytes 6291456 | tf_op jit(solution)/shard_map/base/pallas_call | solution.py:357
  22.8 7.8 %edges.1 = (bf16[256,512]{1,0:T(8,128)(2,1)}, bf16[128,512]{1,0:T(8,128)(2,1)S(1)}, bf16[512,512]{1,0:T(8,128)(2,1)S(1)}, bf16[512,512]{1,0:T(8,128)(2,1)S(1)}, ...) custom-call(s32[12,128]{1,0:T(8,128)} %bitcast.35, s32[12,128]{1,0:T(8,128)} %bitcast.37, bf16[256,512]{1,0:T(8,128)(2,1)} %mesh_hbm.3, ...), custom_call_target="tpu_custom_call" | custom-call | tf_op jit(solution)/shard_map/edges/pallas_call | solution.py:386
  31.1 1.5 %collective-permute-done.1 = bf16[512,512]{1,0:T(8,128)(2,1)S(1)} collective-permute-done((bf16[512,512]{1,0:T(8,128)(2,1)S(1)}, bf16[512,512]{1,0:T(8,128)(2,1)S(1)}, u32[]{:S(2)}, u32[]{:S(2)}) %collective-permute-start.1) | collective-permute-done | bytes 524320 | tf_op jit(solution)/shard_map/ppermute | solution.py:329
  33.2 1.7 %collective-permute-start.8 = (bf16[256,512]{1,0:T(8,128)(2,1)S(1)}, bf16[256,512]{1,0:T(8,128)(2,1)S(1)}, u32[]{:S(2)}, u32[]{:S(2)}) collective-permute-start(bf16[256,512]{1,0:T(8,128)(2,1)S(1)} %slice.141), channel_id=1, source_target_pairs={{0,2},{1,3},{2,0},{3,1},{4,6},{5,7},{6,4},{7,5},{8,10},{9,11},{10,... | collective-permute-start | bytes 786440 | tf_op jit(solution)/shard_map/ppermute | solution.py:329
  36.3 5.5 %collective-permute-done.8 = bf16[256,512]{1,0:T(8,128)(2,1)S(1)} collective-permute-done((bf16[256,512]{1,0:T(8,128)(2,1)S(1)}, bf16[256,512]{1,0:T(8,128)(2,1)S(1)}, u32[]{:S(2)}, u32[]{:S(2)}) %collective-permute-start.8) | collective-permute-done | bytes 262176 | tf_op jit(solution)/shard_map/ppermute | solution.py:329
  41.9 1.8 %collective-permute-start.3 = (bf16[4,2,8,512]{3,2,1,0:T(8,128)(2,1)S(1)}, bf16[4,2,8,512]{3,2,1,0:T(8,128)(2,1)S(1)}, u32[]{:S(2)}, u32[]{:S(2)}) collective-permute-start(bf16[4,2,8,512]{3,2,1,0:T(8,128)(2,1)S(1)} %get-tuple-element.34), channel_id=1, source_target_pairs={{0,2},{1,3},{2,0},{3,1},{4,6},{5,7},{6,4},{7,5},{8,10},{9,11},{10,... | collective-permute-start | bytes 196616 | tf_op jit(solution)/shard_map/ppermute | solution.py:329
  44.2 2.4 %collective-permute-done.3 = bf16[4,2,8,512]{3,2,1,0:T(8,128)(2,1)S(1)} collective-permute-done((bf16[4,2,8,512]{3,2,1,0:T(8,128)(2,1)S(1)}, bf16[4,2,8,512]{3,2,1,0:T(8,128)(2,1)S(1)}, u32[]{:S(2)}, u32[]{:S(2)}) %collective-permute-start.3) | collective-permute-done | bytes 65568 | tf_op jit(solution)/shard_map/ppermute | solution.py:329
  46.6 2.1 %collective-permute-start.4 = (bf16[2,2,8,512]{3,2,1,0:T(8,128)(2,1)S(1)}, bf16[2,2,8,512]{3,2,1,0:T(8,128)(2,1)S(1)}, u32[]{:S(2)}, u32[]{:S(2)}) collective-permute-start(bf16[2,2,8,512]{3,2,1,0:T(8,128)(2,1)S(1)} %get-tuple-element.47), channel_id=1, source_target_pairs={{0,4},{1,5},{2,6},{3,7},{4,0},{5,1},{6,2},{7,3},{8,12},{9,13},{10,... | collective-permute-start | bytes 98312 | tf_op jit(solution)/shard_map/ppermute | solution.py:329
  48.7 2.4 %collective-permute-start.5 = (bf16[2,2,8,512]{3,2,1,0:T(8,128)(2,1)S(1)}, bf16[2,2,8,512]{3,2,1,0:T(8,128)(2,1)S(1)}, u32[]{:S(2)}, u32[]{:S(2)}) collective-permute-start(bf16[2,2,8,512]{3,2,1,0:T(8,128)(2,1)S(1)} %get-tuple-element.48), channel_id=1, source_target_pairs={{0,8},{1,9},{2,10},{3,11},{4,12},{5,13},{6,14},{7,15},{8,0},{9,1},... | collective-permute-start | bytes 98312 | tf_op jit(solution)/shard_map/ppermute | solution.py:329
  51.2 2.0 %collective-permute-start.10 = (bf16[128,512]{1,0:T(8,128)(2,1)S(1)}, bf16[128,512]{1,0:T(8,128)(2,1)S(1)}, u32[]{:S(2)}, u32[]{:S(2)}) collective-permute-start(bf16[128,512]{1,0:T(8,128)(2,1)S(1)} %get-tuple-element.45), channel_id=1, source_target_pairs={{0,8},{1,9},{2,10},{3,11},{4,12},{5,13},{6,14},{7,15},{8,0},{9,1},... | collective-permute-start | bytes 393224 | tf_op jit(solution)/shard_map/ppermute | solution.py:329
  53.2 1.9 %collective-permute-start.9 = (bf16[128,512]{1,0:T(8,128)(2,1)S(1)}, bf16[128,512]{1,0:T(8,128)(2,1)S(1)}, u32[]{:S(2)}, u32[]{:S(2)}) collective-permute-start(bf16[128,512]{1,0:T(8,128)(2,1)S(1)} %get-tuple-element.44), channel_id=1, source_target_pairs={{0,12},{1,13},{2,14},{3,15},{4,8},{5,9},{6,10},{7,11},{8,4},{9,5},... | collective-permute-start | bytes 393224 | tf_op jit(solution)/shard_map/ppermute | solution.py:329
  55.1 2.7 %collective-permute-done.5 = bf16[2,2,8,512]{3,2,1,0:T(8,128)(2,1)S(1)} collective-permute-done((bf16[2,2,8,512]{3,2,1,0:T(8,128)(2,1)S(1)}, bf16[2,2,8,512]{3,2,1,0:T(8,128)(2,1)S(1)}, u32[]{:S(2)}, u32[]{:S(2)}) %collective-permute-start.5) | collective-permute-done | bytes 32800 | tf_op jit(solution)/shard_map/ppermute | solution.py:329
  57.9 2.0 %collective-permute-start.11 = (bf16[128,512]{1,0:T(8,128)(2,1)S(1)}, bf16[128,512]{1,0:T(8,128)(2,1)S(1)}, u32[]{:S(2)}, u32[]{:S(2)}) collective-permute-start(bf16[128,512]{1,0:T(8,128)(2,1)S(1)} %slice.143), channel_id=1, source_target_pairs={{0,4},{1,5},{2,6},{3,7},{4,0},{5,1},{6,2},{7,3},{8,12},{9,13},{10,... | collective-permute-start | bytes 393224 | tf_op jit(solution)/shard_map/ppermute | solution.py:329
  60.0 3.6 %collective-permute-done.10 = bf16[128,512]{1,0:T(8,128)(2,1)S(1)} collective-permute-done((bf16[128,512]{1,0:T(8,128)(2,1)S(1)}, bf16[128,512]{1,0:T(8,128)(2,1)S(1)}, u32[]{:S(2)}, u32[]{:S(2)}) %collective-permute-start.10) | collective-permute-done | bytes 131104 | tf_op jit(solution)/shard_map/ppermute | solution.py:329
  65.6 1.6 %collective-permute-start.17 = (bf16[128,512]{1,0:T(8,128)(2,1)S(1)}, bf16[128,512]{1,0:T(8,128)(2,1)S(1)}, u32[]{:S(2)}, u32[]{:S(2)}) collective-permute-start(bf16[128,512]{1,0:T(8,128)(2,1)S(1)} %fusion.3.refs_0_), channel_id=1, source_target_pairs={{0,4},{1,5},{2,6},{3,7},{4,0},{5,1},{6,2},{7,3},{8,12},{9,13},{10,... | collective-permute-start | bytes 393224 | tf_op jit(solution)/shard_map/ppermute | solution.py:329
  67.3 2.0 %collective-permute-start.18 = (bf16[128,512]{1,0:T(8,128)(2,1)S(1)}, bf16[128,512]{1,0:T(8,128)(2,1)S(1)}, u32[]{:S(2)}, u32[]{:S(2)}) collective-permute-start(bf16[128,512]{1,0:T(8,128)(2,1)S(1)} %fusion.3.refs_0_), channel_id=1, source_target_pairs={{0,12},{1,13},{2,14},{3,15},{4,8},{5,9},{6,10},{7,11},{8,4},{9,5},... | collective-permute-start | bytes 393224 | tf_op jit(solution)/shard_map/ppermute | solution.py:329
  69.3 2.0 %collective-permute-start.13 = (bf16[128,512]{1,0:T(8,128)(2,1)S(1)}, bf16[128,512]{1,0:T(8,128)(2,1)S(1)}, u32[]{:S(2)}, u32[]{:S(2)}) collective-permute-start(bf16[128,512]{1,0:T(8,128)(2,1)S(1)} %fusion.3.refs_0_), channel_id=1, source_target_pairs={{0,8},{1,9},{2,10},{3,11},{4,12},{5,13},{6,14},{7,15},{8,0},{9,1},... | collective-permute-start | bytes 393224 | tf_op jit(solution)/shard_map/ppermute | solution.py:329
  72.8 3.2 %collective-permute-done.18.refs_2_ = bf16[128,512]{1,0:T(8,128)(2,1)S(1)} collective-permute-done((bf16[128,512]{1,0:T(8,128)(2,1)S(1)}, bf16[128,512]{1,0:T(8,128)(2,1)S(1)}, u32[]{:S(2)}, u32[]{:S(2)}) %collective-permute-start.18) | collective-permute-done | bytes 131104 | tf_op jit(solution)/shard_map/ppermute | solution.py:329
  77.1 3.1 %collective-permute-done.13.refs_0_ = bf16[128,512]{1,0:T(8,128)(2,1)S(1)} collective-permute-done((bf16[128,512]{1,0:T(8,128)(2,1)S(1)}, bf16[128,512]{1,0:T(8,128)(2,1)S(1)}, u32[]{:S(2)}, u32[]{:S(2)}) %collective-permute-start.13) | collective-permute-done | bytes 131104 | tf_op jit(solution)/shard_map/ppermute | solution.py:329
  81.8 3.8 %collective-permute-done.14.refs_1_ = bf16[128,512]{1,0:T(8,128)(2,1)S(1)} collective-permute-done((bf16[128,512]{1,0:T(8,128)(2,1)S(1)}, bf16[128,512]{1,0:T(8,128)(2,1)S(1)}, u32[]{:S(2)}, u32[]{:S(2)}) %collective-permute-start.14) | collective-permute-done | bytes 131104 | tf_op jit(solution)/shard_map/ppermute | solution.py:329
  85.6 2.4 %put.1 = f32[1024,512]{1,0:T(8,128)} custom-call(s32[1,128]{1,0:T(1,128)} %rows_hbm.3, bf16[128,512]{1,0:T(8,128)(2,1)S(1)} %bitcast.26), custom_call_target="tpu_custom_call" | custom-call | tf_op jit(solution)/shard_map/put/pallas_call | solution.py:469
  88.0 1.8 %order.2 = (f32[1536,512]{1,0:T(8,128)}, f32[512,512]{1,0:T(8,128)}) custom-call(bf16[128,512]{1,0:T(8,128)(2,1)S(1)} %fusion.3.refs_0_, bf16[128,512]{1,0:T(8,128)(2,1)S(1)} %collective-permute-done.17.refs_1_, bf16[128,512]{1,0:T(8,128)(2,1)S(1)} %collective-permute-done.18.refs_2_, bf16[128,512]{1,0:T(8,128)(2,1)S(1)} %collective-permute-done.12.refs_3_, ...), custom_call_target="tpu_custom_call" | custom-call | tf_op jit(solution)/shard_map/order/pallas_call | solution.py:487
  (67 shorter events, 18.7 us)
Async XLA Ops:
  2.9 15.3 %all-to-all-start = ((bf16[16,8,512]{2,1,0:T(8,128)(2,1)}), bf16[16,8,512]{2,1,0:T(8,128)(2,1)S(1)}, u32[]{:S(2)}, u32[]{:S(2)}) async-start(bf16[16,8,512]{2,1,0:T(8,128)(2,1)} %bitcast.2), calls=%async_computation | async-start | bytes 262144 | tf_op jit(solution)/shard_map/all_to_all | solution.py:353
  32.7 9.2 %collective-permute-start.2 = (bf16[512,512]{1,0:T(8,128)(2,1)S(1)}, bf16[512,512]{1,0:T(8,128)(2,1)S(1)}, u32[]{:S(2)}, u32[]{:S(2)}) collective-permute-start(bf16[512,512]{1,0:T(8,128)(2,1)S(1)} %get-tuple-element.33), channel_id=1, source_target_pairs={{0,1},{1,0},{2,3},{3,2},{4,5},{5,4},{6,7},{7,6},{8,9},{9,8},{10,11... | collective-permute-start | bytes 1572872 | tf_op jit(solution)/shard_map/ppermute | solution.py:329
  33.2 8.6 %collective-permute-start.8 = (bf16[256,512]{1,0:T(8,128)(2,1)S(1)}, bf16[256,512]{1,0:T(8,128)(2,1)S(1)}, u32[]{:S(2)}, u32[]{:S(2)}) collective-permute-start(bf16[256,512]{1,0:T(8,128)(2,1)S(1)} %slice.141), channel_id=1, source_target_pairs={{0,2},{1,3},{2,0},{3,1},{4,6},{5,7},{6,4},{7,5},{8,10},{9,11},{10,... | collective-permute-start | bytes 786440 | tf_op jit(solution)/shard_map/ppermute | solution.py:329
  43.9 13.9 %collective-permute-start.7 = (bf16[256,512]{1,0:T(8,128)(2,1)S(1)}, bf16[256,512]{1,0:T(8,128)(2,1)S(1)}, u32[]{:S(2)}, u32[]{:S(2)}) collective-permute-start(bf16[256,512]{1,0:T(8,128)(2,1)S(1)} %slice.142), channel_id=1, source_target_pairs={{0,2},{1,3},{2,0},{3,1},{4,6},{5,7},{6,4},{7,5},{8,10},{9,11},{10,... | collective-permute-start | bytes 786440 | tf_op jit(solution)/shard_map/ppermute | solution.py:329
  46.6 6.6 %collective-permute-start.4 = (bf16[2,2,8,512]{3,2,1,0:T(8,128)(2,1)S(1)}, bf16[2,2,8,512]{3,2,1,0:T(8,128)(2,1)S(1)}, u32[]{:S(2)}, u32[]{:S(2)}) collective-permute-start(bf16[2,2,8,512]{3,2,1,0:T(8,128)(2,1)S(1)} %get-tuple-element.47), channel_id=1, source_target_pairs={{0,4},{1,5},{2,6},{3,7},{4,0},{5,1},{6,2},{7,3},{8,12},{9,13},{10,... | collective-permute-start | bytes 98312 | tf_op jit(solution)/shard_map/ppermute | solution.py:329
  48.7 9.1 %collective-permute-start.5 = (bf16[2,2,8,512]{3,2,1,0:T(8,128)(2,1)S(1)}, bf16[2,2,8,512]{3,2,1,0:T(8,128)(2,1)S(1)}, u32[]{:S(2)}, u32[]{:S(2)}) collective-permute-start(bf16[2,2,8,512]{3,2,1,0:T(8,128)(2,1)S(1)} %get-tuple-element.48), channel_id=1, source_target_pairs={{0,8},{1,9},{2,10},{3,11},{4,12},{5,13},{6,14},{7,15},{8,0},{9,1},... | collective-permute-start | bytes 98312 | tf_op jit(solution)/shard_map/ppermute | solution.py:329
  51.1 6.7 %collective-permute-start.6 = (bf16[2,2,8,512]{3,2,1,0:T(8,128)(2,1)S(1)}, bf16[2,2,8,512]{3,2,1,0:T(8,128)(2,1)S(1)}, u32[]{:S(2)}, u32[]{:S(2)}) collective-permute-start(bf16[2,2,8,512]{3,2,1,0:T(8,128)(2,1)S(1)} %get-tuple-element.49), channel_id=1, source_target_pairs={{0,12},{1,13},{2,14},{3,15},{4,8},{5,9},{6,10},{7,11},{8,4},{9,5},... | collective-permute-start | bytes 98312 | tf_op jit(solution)/shard_map/ppermute | solution.py:329
  51.2 12.4 %collective-permute-start.10 = (bf16[128,512]{1,0:T(8,128)(2,1)S(1)}, bf16[128,512]{1,0:T(8,128)(2,1)S(1)}, u32[]{:S(2)}, u32[]{:S(2)}) collective-permute-start(bf16[128,512]{1,0:T(8,128)(2,1)S(1)} %get-tuple-element.45), channel_id=1, source_target_pairs={{0,8},{1,9},{2,10},{3,11},{4,12},{5,13},{6,14},{7,15},{8,0},{9,1},... | collective-permute-start | bytes 393224 | tf_op jit(solution)/shard_map/ppermute | solution.py:329
  53.2 10.4 %collective-permute-start.9 = (bf16[128,512]{1,0:T(8,128)(2,1)S(1)}, bf16[128,512]{1,0:T(8,128)(2,1)S(1)}, u32[]{:S(2)}, u32[]{:S(2)}) collective-permute-start(bf16[128,512]{1,0:T(8,128)(2,1)S(1)} %get-tuple-element.44), channel_id=1, source_target_pairs={{0,12},{1,13},{2,14},{3,15},{4,8},{5,9},{6,10},{7,11},{8,4},{9,5},... | collective-permute-start | bytes 393224 | tf_op jit(solution)/shard_map/ppermute | solution.py:329
  57.9 6.2 %collective-permute-start.11 = (bf16[128,512]{1,0:T(8,128)(2,1)S(1)}, bf16[128,512]{1,0:T(8,128)(2,1)S(1)}, u32[]{:S(2)}, u32[]{:S(2)}) collective-permute-start(bf16[128,512]{1,0:T(8,128)(2,1)S(1)} %slice.143), channel_id=1, source_target_pairs={{0,4},{1,5},{2,6},{3,7},{4,0},{5,1},{6,2},{7,3},{8,12},{9,13},{10,... | collective-permute-start | bytes 393224 | tf_op jit(solution)/shard_map/ppermute | solution.py:329
  64.2 5.1 %collective-permute-start.12 = (bf16[128,512]{1,0:T(8,128)(2,1)S(1)}, bf16[128,512]{1,0:T(8,128)(2,1)S(1)}, u32[]{:S(2)}, u32[]{:S(2)}) collective-permute-start(bf16[128,512]{1,0:T(8,128)(2,1)S(1)} %fusion.3.refs_0_), channel_id=1, source_target_pairs={{0,2},{1,3},{2,0},{3,1},{4,6},{5,7},{6,4},{7,5},{8,10},{9,11},{10,... | collective-permute-start | bytes 393224 | tf_op jit(solution)/shard_map/ppermute | solution.py:329
  65.6 5.7 %collective-permute-start.17 = (bf16[128,512]{1,0:T(8,128)(2,1)S(1)}, bf16[128,512]{1,0:T(8,128)(2,1)S(1)}, u32[]{:S(2)}, u32[]{:S(2)}) collective-permute-start(bf16[128,512]{1,0:T(8,128)(2,1)S(1)} %fusion.3.refs_0_), channel_id=1, source_target_pairs={{0,4},{1,5},{2,6},{3,7},{4,0},{5,1},{6,2},{7,3},{8,12},{9,13},{10,... | collective-permute-start | bytes 393224 | tf_op jit(solution)/shard_map/ppermute | solution.py:329
  67.3 8.8 %collective-permute-start.18 = (bf16[128,512]{1,0:T(8,128)(2,1)S(1)}, bf16[128,512]{1,0:T(8,128)(2,1)S(1)}, u32[]{:S(2)}, u32[]{:S(2)}) collective-permute-start(bf16[128,512]{1,0:T(8,128)(2,1)S(1)} %fusion.3.refs_0_), channel_id=1, source_target_pairs={{0,12},{1,13},{2,14},{3,15},{4,8},{5,9},{6,10},{7,11},{8,4},{9,5},... | collective-permute-start | bytes 393224 | tf_op jit(solution)/shard_map/ppermute | solution.py:329
  69.3 7.3 %collective-permute-start.21 = (bf16[128,512]{1,0:T(8,128)(2,1)S(1)}, bf16[128,512]{1,0:T(8,128)(2,1)S(1)}, u32[]{:S(2)}, u32[]{:S(2)}) collective-permute-start(bf16[128,512]{1,0:T(8,128)(2,1)S(1)} %fusion.3.refs_0_), channel_id=1, source_target_pairs={{0,1},{1,0},{2,3},{3,2},{4,5},{5,4},{6,7},{7,6},{8,9},{9,8},{10,11... | collective-permute-start | bytes 393224 | tf_op jit(solution)/shard_map/ppermute | solution.py:329
  69.3 10.9 %collective-permute-start.13 = (bf16[128,512]{1,0:T(8,128)(2,1)S(1)}, bf16[128,512]{1,0:T(8,128)(2,1)S(1)}, u32[]{:S(2)}, u32[]{:S(2)}) collective-permute-start(bf16[128,512]{1,0:T(8,128)(2,1)S(1)} %fusion.3.refs_0_), channel_id=1, source_target_pairs={{0,8},{1,9},{2,10},{3,11},{4,12},{5,13},{6,14},{7,15},{8,0},{9,1},... | collective-permute-start | bytes 393224 | tf_op jit(solution)/shard_map/ppermute | solution.py:329
  71.4 9.4 %collective-permute-start.19 = (bf16[128,512]{1,0:T(8,128)(2,1)S(1)}, bf16[128,512]{1,0:T(8,128)(2,1)S(1)}, u32[]{:S(2)}, u32[]{:S(2)}) collective-permute-start(bf16[128,512]{1,0:T(8,128)(2,1)S(1)} %collective-permute-done.17.refs_1_), channel_id=1, source_target_pairs={{0,2},{1,3},{2,0},{3,1},{4,6},{5,7},{6,4},{7,5},{8,10},{9,11},{10,... | collective-permute-start | bytes 393224 | tf_op jit(solution)/shard_map/ppermute | solution.py:329
  76.0 5.0 %collective-permute-start.20 = (bf16[128,512]{1,0:T(8,128)(2,1)S(1)}, bf16[128,512]{1,0:T(8,128)(2,1)S(1)}, u32[]{:S(2)}, u32[]{:S(2)}) collective-permute-start(bf16[128,512]{1,0:T(8,128)(2,1)S(1)} %collective-permute-done.18.refs_2_), channel_id=1, source_target_pairs={{0,2},{1,3},{2,0},{3,1},{4,6},{5,7},{6,4},{7,5},{8,10},{9,11},{10,... | collective-permute-start | bytes 393224 | tf_op jit(solution)/shard_map/ppermute | solution.py:329
  76.6 4.7 %collective-permute-start.22 = (bf16[128,512]{1,0:T(8,128)(2,1)S(1)}, bf16[128,512]{1,0:T(8,128)(2,1)S(1)}, u32[]{:S(2)}, u32[]{:S(2)}) collective-permute-start(bf16[128,512]{1,0:T(8,128)(2,1)S(1)} %collective-permute-done.17.refs_1_), channel_id=1, source_target_pairs={{0,1},{1,0},{2,3},{3,2},{4,5},{5,4},{6,7},{7,6},{8,9},{9,8},{10,11... | collective-permute-start | bytes 393224 | tf_op jit(solution)/shard_map/ppermute | solution.py:329
  76.6 4.9 %collective-permute-start.23 = (bf16[128,512]{1,0:T(8,128)(2,1)S(1)}, bf16[128,512]{1,0:T(8,128)(2,1)S(1)}, u32[]{:S(2)}, u32[]{:S(2)}) collective-permute-start(bf16[128,512]{1,0:T(8,128)(2,1)S(1)} %collective-permute-done.18.refs_2_), channel_id=1, source_target_pairs={{0,1},{1,0},{2,3},{3,2},{4,5},{5,4},{6,7},{7,6},{8,9},{9,8},{10,11... | collective-permute-start | bytes 393224 | tf_op jit(solution)/shard_map/ppermute | solution.py:329
  80.2 5.4 %collective-permute-start.14 = (bf16[128,512]{1,0:T(8,128)(2,1)S(1)}, bf16[128,512]{1,0:T(8,128)(2,1)S(1)}, u32[]{:S(2)}, u32[]{:S(2)}) collective-permute-start(bf16[128,512]{1,0:T(8,128)(2,1)S(1)} %collective-permute-done.13.refs_0_), channel_id=1, source_target_pairs={{0,2},{1,3},{2,0},{3,1},{4,6},{5,7},{6,4},{7,5},{8,10},{9,11},{10,... | collective-permute-start | bytes 393224 | tf_op jit(solution)/shard_map/ppermute | solution.py:329
  80.8 7.2 %collective-permute-start.24 = (bf16[128,512]{1,0:T(8,128)(2,1)S(1)}, bf16[128,512]{1,0:T(8,128)(2,1)S(1)}, u32[]{:S(2)}, u32[]{:S(2)}) collective-permute-start(bf16[128,512]{1,0:T(8,128)(2,1)S(1)} %collective-permute-done.12.refs_3_), channel_id=1, source_target_pairs={{0,1},{1,0},{2,3},{3,2},{4,5},{5,4},{6,7},{7,6},{8,9},{9,8},{10,11... | collective-permute-start | bytes 393224 | tf_op jit(solution)/shard_map/ppermute | solution.py:329
  81.0 7.0 %collective-permute-start.25 = (bf16[128,512]{1,0:T(8,128)(2,1)S(1)}, bf16[128,512]{1,0:T(8,128)(2,1)S(1)}, u32[]{:S(2)}, u32[]{:S(2)}) collective-permute-start(bf16[128,512]{1,0:T(8,128)(2,1)S(1)} %collective-permute-done.19.refs_4_), channel_id=1, source_target_pairs={{0,1},{1,0},{2,3},{3,2},{4,5},{5,4},{6,7},{7,6},{8,9},{9,8},{10,11... | collective-permute-start | bytes 393224 | tf_op jit(solution)/shard_map/ppermute | solution.py:329
  81.3 6.7 %collective-permute-start.26 = (bf16[128,512]{1,0:T(8,128)(2,1)S(1)}, bf16[128,512]{1,0:T(8,128)(2,1)S(1)}, u32[]{:S(2)}, u32[]{:S(2)}) collective-permute-start(bf16[128,512]{1,0:T(8,128)(2,1)S(1)} %collective-permute-done.20.refs_5_), channel_id=1, source_target_pairs={{0,1},{1,0},{2,3},{3,2},{4,5},{5,4},{6,7},{7,6},{8,9},{9,8},{10,11... | collective-permute-start | bytes 393224 | tf_op jit(solution)/shard_map/ppermute | solution.py:329
  81.5 8.3 %collective-permute-start.15 = (bf16[128,512]{1,0:T(8,128)(2,1)S(1)}, bf16[128,512]{1,0:T(8,128)(2,1)S(1)}, u32[]{:S(2)}, u32[]{:S(2)}) collective-permute-start(bf16[128,512]{1,0:T(8,128)(2,1)S(1)} %collective-permute-done.13.refs_0_), channel_id=1, source_target_pairs={{0,1},{1,0},{2,3},{3,2},{4,5},{5,4},{6,7},{7,6},{8,9},{9,8},{10,11... | collective-permute-start | bytes 393224 | tf_op jit(solution)/shard_map/ppermute | solution.py:329
  (12 other events, 20.5 us)

commit v5 on v4

--- a/solution.py
+++ b/solution.py
@@ -54,6 +54,10 @@
 def tile_columns(index_ref, at, lines, columns):
     found = [one_hot_columns(index_ref[pl.ds(at * lines + k, 1), :], columns) for k in range(lines)]
     return jnp.concatenate(found, axis=0)
+
+
+def far_lines(outer):
+    return max(1, outer // 4)
 
 
 def place_of(sizes):
@@ -124,10 +128,10 @@
     wn1_hbm,
     wn2_hbm,
     base_ref,
-    turned_ref,
-    hot_ref,
-    node_ref,
-    cot_out_ref,
+    turned_hbm,
+    hot_hbm,
+    node_hbm,
+    cot_out_hbm,
     dst_ref,
     mesh_ref,
     edge_ref,
@@ -135,7 +139,12 @@
     w1_ref,
     wn1_ref,
     wn2_ref,
+    turned_ref,
+    hot_ref,
+    node_ref,
+    cot_out_ref,
     sems,
+    out_sems,
 ):
     width = mesh_ref.shape[1]
     mesh_rows = mesh_ref.shape[0]
@@ -145,29 +154,36 @@
         (dst_hbm, dst_ref),
         (mesh_hbm, mesh_ref),
         (w1_hbm.at[pl.ds(width, width), :], w1_ref.at[pl.ds(0, width), :]),
+        (wn1_hbm.at[pl.ds(0, width), :], wn1_ref),
+        (cot_hbm, cot_ref),
+        (wn2_hbm, wn2_ref),
         (w1_hbm.at[pl.ds(2 * width, width), :], w1_ref.at[pl.ds(width, width), :]),
     ]
     pairs += [(edge_hbm.at[pl.ds(at * tile, tile), :], edge_ref.at[pl.ds(at * tile, tile), :]) for at in range(tiles)]
-    pairs += [(wn1_hbm.at[pl.ds(0, width), :], wn1_ref), (cot_hbm, cot_ref), (wn2_hbm, wn2_ref)]
     copies = load(pairs, sems)
     same = lax.broadcasted_iota(jnp.int32, (256, 256), 0) == lax.broadcasted_iota(jnp.int32, (256, 256), 1)
     eye = jnp.where(same, 1.0, 0.0).astype(BF16)
-    for copy in copies[:4]:
+    copies[0].wait()
+    for at in range(tiles):
+        hot_ref[at * tile : (at + 1) * tile, :] = tile_columns(dst_ref, at, lines, mesh_rows)
+    for copy in copies[1:6]:
         copy.wait()
     moved = dot_nn(mesh_ref[...], w1_ref[:width, :]).astype(BF16)
+    node_ref[...] = dot_nn(mesh_ref[...], wn1_ref[...])
+    cot_out_ref[...] = dot_nt(cot_ref[...], wn2_ref[...])
+    done = load([(hot_ref, hot_hbm), (node_ref, node_hbm), (cot_out_ref, cot_out_hbm)], out_sems)
+    copies[6].wait()
     for at in range(tiles):
         rows = slice(at * tile, (at + 1) * tile)
-        to_mesh = tile_columns(dst_ref, at, lines, mesh_rows)
-        hot_ref[rows, :] = to_mesh
-        copies[4 + at].wait()
+        copies[7 + at].wait()
         edge = edge_ref[rows, :]
-        base_ref[rows, :] = dot_nn(edge, w1_ref[width:, :]) + dot_nn(to_mesh, moved)
         for start in range(0, width, 256):
             turned_ref[start : start + 256, rows] = dot_nt(eye, edge[:, start : start + 256]).astype(BF16)
-    for copy in copies[4 + tiles :]:
+        base_ref[rows, :] = dot_nn(edge, w1_ref[width:, :]) + dot_nn(hot_ref[rows, :], moved)
+    last = pltpu.make_async_copy(turned_ref, turned_hbm, out_sems.at[3])
+    last.start()
+    for copy in done + [last]:
         copy.wait()
-    node_ref[...] = dot_nn(mesh_ref[...], wn1_ref[...])
-    cot_out_ref[...] = dot_nt(cot_ref[...], wn2_ref[...])
 
 
 def main_kernel(
@@ -180,19 +196,19 @@
     w2_hbm,
     wn1_hbm,
     wn2_hbm,
+    turned_hbm,
+    hot_hbm,
+    node_hbm,
+    cot_hbm,
     slots_ref,
     base_ref,
-    turned_ref,
-    hot_ref,
-    node_ref,
-    cot_ref,
     *rest,
 ):
     outer, inner = sizes
-    mesh_out_ref, d_slots_ref = rest[:2]
-    send_refs, keep_refs = rest[2:4], rest[4:6]
+    mesh_out_ref, d_slots_ref, far_send_ref, near_send_ref, far_keep_ref, near_keep_ref = rest[:6]
     slope_ref, value_ref, both_ref, grads_ref, slot_grads_ref, ordered_ref = rest[6:12]
-    slot_ref, dst_ref, mesh_ref, w1_ref, w2_ref, wn1_ref, wn2_ref, sems = rest[12:]
+    slot_ref, dst_ref, mesh_ref, w1_ref, w2_ref, wn1_ref, wn2_ref = rest[12:19]
+    turned_ref, hot_ref, node_ref, cot_ref, sems = rest[19:]
     width = mesh_ref.shape[1]
     mesh_rows = mesh_ref.shape[0]
     slot_rows = slots_ref.shape[0]
@@ -205,7 +221,11 @@
         (w2_hbm, w2_ref),
         (wn1_hbm.at[pl.ds(width, wn1_ref.shape[0]), :], wn1_ref),
         (mesh_hbm, mesh_ref),
+        (node_hbm, node_ref),
+        (cot_hbm, cot_ref),
+        (hot_hbm, hot_ref),
         (wn2_hbm, wn2_ref),
+        (turned_hbm, turned_ref),
     ]
     copies = load(pairs, sems)
     for copy in copies[:3]:
@@ -224,7 +244,7 @@
         both_ref[:slot_rows, rows] = tile_rows(slot_ref, at, lines, slot_rows)
         both_ref[slot_rows:, rows] = tile_rows(dst_ref, at, lines, mesh_rows)
 
-    for copy in copies[3:]:
+    for copy in copies[3:-1]:
         copy.wait()
     hidden_sums = dot_nn(both_ref[slot_rows:, :], value_ref[...]).astype(BF16)
     received = dot_nn(hidden_sums, w2_ref[...]).astype(BF16)
@@ -247,10 +267,12 @@
     slot_grads_ref[...] = dot_nt(sums[:slot_rows], w1_ref[...])
     grads_ref[:width, :] = dot_tn(slots_ref[...], sums[:slot_rows])
     grads_ref[width : 2 * width, :] = dot_tn(mesh, sums[slot_rows:])
+    copies[-1].wait()
     grads_ref[2 * width : 3 * width, :] = dot_nn(turned_ref[...], value_ref[...])
 
     chunk = grads_ref.shape[0] // (2 * outer * inner)
     cap = slot_rows // (2 * outer * inner)
+    far_count = far_lines(outer)
     for far_core in range(2):
         for far_inner in range(inner):
             for far_outer in range(outer):
@@ -259,14 +281,42 @@
                 from_rows = pl.ds(pl.multiple_of(owner * cap, cap), cap)
                 ordered_ref[at * cap : (at + 1) * cap, :] = slot_grads_ref[from_rows, :]
                 value = grads_ref[pl.ds(pl.multiple_of(owner * chunk, chunk), chunk), :]
-                group = 0 if far_outer >= outer // 2 else 1
-                line = far_inner * (outer // 2) + far_outer % (outer // 2)
+                if far_outer >= outer - far_count:
+                    line = far_inner * far_count + far_outer - (outer - far_count)
+                    send_ref, keep_ref = far_send_ref, far_keep_ref
+                else:
+                    line = far_inner * (outer - far_count) + far_outer
+                    send_ref, keep_ref = near_send_ref, near_keep_ref
                 rows = slice(line * chunk, (line + 1) * chunk)
                 if far_core:
-                    send_refs[group][rows, :] = value.astype(BF16)
+                    send_ref[rows, :] = value.astype(BF16)
                 else:
-                    keep_refs[group][rows, :] = value
-    d_slots_ref[...] = ordered_ref[...].astype(BF16)
+                    keep_ref[rows, :] = value
+    halfway = slot_rows // 2
+    d_slots_ref[...] = ordered_ref[:halfway, :].astype(BF16)
+    near_send_ref[near_keep_ref.shape[0] :, :] = ordered_ref[halfway:, :].astype(BF16)
+
+
+def join_kernel(sizes, near_count, keep_ref, crossed_ref, d_slots_ref, total_ref, slots_ref, *part_refs):
+    outer, inner = sizes
+    rows = keep_ref.shape[0]
+    size = rows // inner
+    cap = d_slots_ref.shape[0] // (inner * outer)
+    own, far = d_slots_ref[...].astype(F32), crossed_ref[rows:, :].astype(F32)
+    for far_inner in range(inner):
+        here = slice(far_inner * size, (far_inner + 1) * size)
+        total = keep_ref[here, :] + crossed_ref[here, :].astype(F32)
+        mixed = []
+        for far_outer in range(outer):
+            at = (far_inner * outer + far_outer) * cap
+            mixed += [own[at : at + cap], far[at : at + cap]]
+        mixed = jnp.concatenate(mixed, axis=0).astype(BF16)
+        if far_inner:
+            part_refs[far_inner - 1][:size, :] = total.astype(BF16)
+            part_refs[far_inner - 1][size:, :] = mixed
+        else:
+            total_ref[...] = total
+            slots_ref[...] = mixed
 
 
 def order_kernel(sizes, places, aliased, *refs):
@@ -358,13 +408,13 @@
         functools.partial(base_kernel, lines),
         out_shape=[
             pltpu.VMEM((edges, hidden_width), F32),
-            pltpu.VMEM((width, edges), BF16),
-            pltpu.VMEM((edges, mesh_rows), BF16),
-            pltpu.VMEM((mesh_rows, hidden_width), F32),
-            pltpu.VMEM((mesh_rows, hidden_width), F32),
+            pltpu.HBM((width, edges), BF16),
+            pltpu.HBM((edges, mesh_rows), BF16),
+            pltpu.HBM((mesh_rows, hidden_width), F32),
+            pltpu.HBM((mesh_rows, hidden_width), F32),
         ],
         in_specs=specs(pltpu.HBM, 7),
-        out_specs=specs(pltpu.VMEM, 5),
+        out_specs=specs(pltpu.VMEM, 1) + specs(pltpu.HBM, 4),
         scratch_shapes=[
             pltpu.VMEM(dst_index.shape, jnp.int32),
             pltpu.VMEM(mesh_latent.shape, BF16),
@@ -373,7 +423,12 @@
             pltpu.VMEM((2 * width, hidden_width), BF16),
             pltpu.VMEM((width, hidden_width), BF16),
             pltpu.VMEM(w_node2.shape, BF16),
+            pltpu.VMEM((width, edges), BF16),
+            pltpu.VMEM((edges, mesh_rows), BF16),
+            pltpu.VMEM((mesh_rows, hidden_width), F32),
+            pltpu.VMEM((mesh_rows, hidden_width), F32),
             pltpu.SemaphoreType.DMA((7 + edges // (128 * lines),)),
+            pltpu.SemaphoreType.DMA((4,)),
         ],
         compiler_params=params(20),
         cost_estimate=cost(2 * edges * width * hidden_width * 2, edges * width * 8),
@@ -382,16 +437,22 @@
 
     grad_rows = 3 * width + hidden_width
     chunk = grad_rows // band_count
-    group = (band_count // 4 * chunk, hidden_width)
-    mesh_out, d_slots, *sides = pl.pallas_call(
+    far_count = far_lines(outer)
+    near_count = outer - far_count
+    far_group = (far_count * inner * chunk, hidden_width)
+    near_group = (near_count * inner * chunk, hidden_width)
+    near_rows, halfway = near_group[0], slot_rows // 2
+    mesh_out, d_slots, far_send, near_send, far_keep, near_keep = pl.pallas_call(
         functools.partial(main_kernel, lines, sizes),
         out_shape=[
             jax.ShapeDtypeStruct((mesh_rows, width), BF16),
-            jax.ShapeDtypeStruct((slot_rows, width), BF16),
-        ]
-        + [jax.ShapeDtypeStruct(group, BF16)] * 2
-        + [jax.ShapeDtypeStruct(group, F32)] * 2,
-        in_specs=specs(pltpu.HBM, 7) + specs(pltpu.VMEM, 6),
+            jax.ShapeDtypeStruct((halfway, width), BF16),
+            jax.ShapeDtypeStruct(far_group, BF16),
+            jax.ShapeDtypeStruct((near_rows + halfway, hidden_width), BF16),
+            jax.ShapeDtypeStruct(far_group, F32),
+            jax.ShapeDtypeStruct(near_group, F32),
+        ],
+        in_specs=specs(pltpu.HBM, 11) + specs(pltpu.VMEM, 2),
         out_specs=specs(pltpu.VMEM, 6),
         scratch_shapes=[
             pltpu.VMEM((edges, hidden_width), F32),
@@ -407,61 +468,74 @@
             pltpu.VMEM(w_edge2.shape, BF16),
             pltpu.VMEM((w_node1.shape[0] - width, w_node1.shape[1]), BF16),
             pltpu.VMEM(w_node2.shape, BF16),
-            pltpu.SemaphoreType.DMA((7,)),
+            pltpu.VMEM(turned.shape, BF16),
+            pltpu.VMEM(hot.shape, BF16),
+            pltpu.VMEM(node.shape, F32),
+            pltpu.VMEM(cot.shape, F32),
+            pltpu.SemaphoreType.DMA((11,)),
         ],
-        compiler_params=params(36),
+        compiler_params=params(40),
         name="edges",
     )(
         *pinned(pltpu.HBM, slot_index, dst_index, mesh_latent, w_edge1, w_edge2, w_node1, w_node2),
+        *pinned(pltpu.HBM, turned, hot, node, cot),
         slots,
-        *pinned(pltpu.VMEM, base, turned, hot, node, cot),
+        *pinned(pltpu.VMEM, base),
     )
-    def after(value, *others):
-        return lax.optimization_barrier((value, *others))[0]
-
-    far_send, near_send, far_keep, near_keep = sides
-    half = outer // 2
-    rows = half * chunk
-
-    def over_inner(total):
-        parts = [total[k * rows : (k + 1) * rows].astype(BF16) for k in range(1, inner)]
-        received = [to_inner(part, k + 1) for k, part in enumerate(parts)]
-        return total[:rows], received
-
-    def joined(total, received):
-        for value in received:
-            total = total + value.astype(F32)
-        return total
+    cap = slot_rows // band_count
 
     def line(total, k):
-        return total[k * chunk : (k + 1) * chunk]
-
-    cap = slot_rows // band_count
-    back = d_slots.reshape(2, inner, outer, cap, width)
-    far_crossed = to_core(far_send)
-    near_crossed, slots_crossed = to_core(after(near_send, far_crossed)), to_core(back[1])
-    far_total, far_received = over_inner(far_keep + far_crossed.astype(F32))
-    back = jnp.stack([back[0], slots_crossed], axis=2)
-    back = jnp.stack([back[0]] + [to_inner(after(back[k], near_crossed), k) for k in range(1, inner)], axis=1)
-    near_total, near_received = over_inner(near_keep + near_crossed.astype(F32))
-    far_total = joined(far_total, [after(value, back) for value in far_received])
-    arrived = [to_outer(line(far_total, k).astype(BF16), half + k) for k in range(half - 1, -1, -1)]
-    back = jnp.stack([back[0]] + [to_outer(back[k], k) for k in range(1, outer)], axis=0)
-    near_total = joined(near_total, [after(value, back) for value in near_received])
-    arrived += [to_outer(line(near_total, k).astype(BF16), k) for k in range(half - 1, 0, -1)]
-    own = joined(line(near_total, 0), arrived).astype(BF16)
-
-    turns = []
-    for step in range(1, half + 1):
-        turns += [outer - step] + [step] * (step != outer - step)
+        return total[k * chunk : (k + 1) * chunk].astype(BF16)
+
+    far_crossed, near_crossed = to_core(far_send), to_core(near_send)
+    far_rows, size = far_count * chunk, near_count * chunk
+    far_half = far_keep + far_crossed.astype(F32)
+    far_total = far_half[:far_rows]
+    far_parts = [far_half[k * far_rows : (k + 1) * far_rows].astype(BF16) for k in range(1, inner)]
+    near_crossed = lax.optimization_barrier((near_crossed, *far_parts))[0]
+    for k, part in enumerate(far_parts):
+        far_total = far_total + to_inner(part, k + 1).astype(F32)
+    mixed_rows = outer * 2 * cap
+    near_total, mixed, *parts = pl.pallas_call(
+        functools.partial(join_kernel, sizes, near_count),
+        out_shape=[
+            jax.ShapeDtypeStruct((size, hidden_width), F32),
+            jax.ShapeDtypeStruct((mixed_rows, width), BF16),
+        ]
+        + [jax.ShapeDtypeStruct((size + mixed_rows, width), BF16)] * (inner - 1),
+        compiler_params=params(16),
+        cost_estimate=cost(2 * 10**10, MIB),
+        name="join",
+    )(near_keep, near_crossed, d_slots)
+    parts = [to_inner(part, k + 1) for k, part in enumerate(parts)]
+    for part in parts:
+        near_total = near_total + part[:size].astype(F32)
+    back = [value.reshape(outer, 2, cap, width) for value in [mixed] + [part[size:] for part in parts]]
+    back = jnp.stack(back, axis=1)
+    arrived, returned = [], {0: back[0]}
+    for k in range(far_count):
+        arrived.append(to_outer(line(far_total, k), near_count + k))
+    near_total = lax.optimization_barrier((near_total, *arrived))[0]
+    for k in range(near_count - 1, 0, -1):
+        value = to_outer(jnp.concatenate([line(near_total, k), back[k].reshape(-1, width)], axis=0), k)
+        arrived.append(value[:chunk])
+        returned[k] = value[chunk:].reshape(back[0].shape)
+    for k in range(near_count, outer):
+        returned[k] = to_outer(back[k], k)
+    own = near_total[:chunk]
+    for value in arrived:
+        own = own + value.astype(F32)
+    own = own.astype(BF16)
+    back = jnp.stack([returned[k] for k in range(outer)], axis=0)
+
     pieces = {0: own}
+    stride = outer // 2
+    while stride:
+        for at in range(0, outer, 2 * stride):
+            pieces[at + stride] = to_outer(pieces[at], stride)
+        stride //= 2
     for far_inner in range(1, inner):
-        pieces[far_inner * outer] = to_inner(own, far_inner)
-    for at, far_outer in enumerate(turns):
-        value = own if at < 2 else after(own, pieces[outer])
-        pieces[far_outer] = to_outer(value, far_outer)
-    for far_inner in range(1, inner):
-        for far_outer in turns:
+        for far_outer in range(outer):
             pieces[far_inner * outer + far_outer] = to_inner(pieces[far_outer], far_inner)
     for at in range(band_count // 2):
         pieces[band_count // 2 + at] = to_core(pieces[at])
@@ -480,8 +554,8 @@
         name="put",
     )(*pinned(pltpu.HBM, send_rows), back.reshape(slot_rows, width))
 
-    late = [at for at in range(band_count) if at % outer == turns[-1]]
-    early = [at for at in range(band_count) if at % outer != turns[-1]]
+    late = [at for at in range(band_count) if at % outer == outer - 1]
+    early = [at for at in range(band_count) if at % outer != outer - 1]
     grads = []
     for places in (early, late):
         grads = pl.pallas_call(

time: 91.3 us -> 88.6 us (0.970)
  waiting for transfers between devices: 27.7 us -> 42.3 us
  starting transfers between devices: 33.9 us -> 23.8 us
  local copies, waits for them, and re-layouts: 8.34 us -> 0.05 us
  Pallas kernels: 19.5 us -> 20.8 us
    ppermute x27 -> x23, waiting for transfers between devices: 27.7 us -> 39.6 us  [permute(): return lax.ppermute(value, 'band', pairs)]
    ppermute x27 -> x23, starting transfers between devices: 26.5 us -> 16.4 us  [permute(): return lax.ppermute(value, 'band', pairs)]
    unnamed x16 -> x0, local copies, waits for them, and re-layouts: 8.23 us -> none
    all_to_all x1, waiting for transfers between devices: 0.04 us -> 2.73 us  [shards(): lax.all_to_all(outgoing.reshape(band_count, -1, width), 'band', split_axi...]
    pallas_call x1, Pallas kernels: 4.27 us -> 5.2 us  [shards(): pl.pallas_call(functools.partial(base_kernel, lines), out_shape=[pltpu.VM...]
  transfers between devices with their start and end apart: 28 -> 24, of which waited for: 11 -> 10; matrix products, arithmetic and copies ran while one was open for 1% -> 0% of each run, Pallas kernels for 9% -> 11%
where the time goes in v5:
time: 88.6 us; the launch traced here: 88.2 us
  waiting for transfers between devices  42.3 us (48%)
  starting transfers between devices  23.8 us (27%)
  Pallas kernels  20.8 us (23%)
    ppermute x23, waiting for transfers between devices, permute(): return lax.ppermute(value, 'band', pairs)  39.6 us
    ppermute x23, starting transfers between devices, permute(): return lax.ppermute(value, 'band', pairs)  16.4 us
    pallas_call x1, Pallas kernels, shards(): pl.pallas_call(functools.partial(main_kernel, lines, sizes), out_shape=[j...  8.05 us
    all_to_all x1, starting transfers between devices, shards(): lax.all_to_all(outgoing.reshape(band_count, -1, width), 'band', split_axi...  7.4 us
    pallas_call x1, Pallas kernels, shards(): pl.pallas_call(functools.partial(base_kernel, lines), out_shape=[pltpu.VM...  5.2 us
    pallas_call x2, Pallas kernels, shards(): pl.pallas_call(functools.partial(order_kernel, sizes, places, len(grads))...  2.81 us
    all_to_all x1, waiting for transfers between devices, shards(): lax.all_to_all(outgoing.reshape(band_count, -1, width), 'band', split_axi...  2.73 us
    pallas_call x1, Pallas kernels, shards(): pl.pallas_call(functools.partial(put_kernel, sizes), out_shape=jax.ShapeD...  2.4 us
  transfers between devices with their start and end apart: 24, of which 10 were waited for; matrix products, arithmetic and copies ran while one was open for 0% of the time, Pallas kernels for 11%

profile of v5, /device:TPU:0, one launch (start us, length us, event | category | flops | bytes accessed | tf_op | source)
XLA Modules:
  0.0 88.2 jit_solution(18156140014750305076)
XLA Ops:
  0.6 2.2 %pick.1 = bf16[128,512]{1,0:T(8,128)(2,1)} custom-call(s32[1,128]{1,0:T(1,128)} %rows_hbm.3, bf16[1024,512]{1,0:T(8,128)(2,1)} %grid_hbm.1), custom_call_target="tpu_custom_call" | custom-call | tf_op jit(solution)/shard_map/pick/pallas_call | solution.py:390
  2.9 7.4 %all-to-all-start = ((bf16[16,8,512]{2,1,0:T(8,128)(2,1)}), bf16[16,8,512]{2,1,0:T(8,128)(2,1)S(1)}, u32[]{:S(2)}, u32[]{:S(2)}) async-start(bf16[16,8,512]{2,1,0:T(8,128)(2,1)} %bitcast.2), calls=%async_computation | async-start | bytes 262144 | tf_op jit(solution)/shard_map/all_to_all | solution.py:403
  10.3 5.2 %base.1 = (f32[1536,512]{1,0:T(8,128)S(1)}, bf16[512,1536]{1,0:T(8,128)(2,1)}, bf16[1536,256]{1,0:T(8,128)(2,1)}, f32[256,512]{1,0:T(8,128)}, f32[256,512]{1,0:T(8,128)}) custom-call(s32[12,128]{1,0:T(8,128)} %bitcast.28, bf16[256,512]{1,0:T(8,128)(2,1)} %mesh_hbm.3, bf16[1536,512]{1,0:T(8,128)(2,1)} %edge_hbm.1, bf16[256,512]{1,0:T(8,128)(2,1)} %cot_hbm.1, ...), custom_call_target="tpu_custom_call" | custom-call | flops 1610612736 | bytes 6291456 | tf_op jit(solution)/shard_map/base/pallas_call | solution.py:407
  15.5 2.7 %all-to-all-done = bf16[16,8,512]{2,1,0:T(8,128)(2,1)S(1)} async-done(((bf16[16,8,512]{2,1,0:T(8,128)(2,1)}), bf16[16,8,512]{2,1,0:T(8,128)(2,1)S(1)}, u32[]{:S(2)}, u32[]{:S(2)}) %all-to-all-start) | async-done | bytes 131104 | tf_op jit(solution)/shard_map/all_to_all | solution.py:403
  18.2 8.1 %edges.1 = (bf16[256,512]{1,0:T(8,128)(2,1)}, bf16[64,512]{1,0:T(8,128)(2,1)S(1)}, bf16[256,512]{1,0:T(8,128)(2,1)S(1)}, bf16[832,512]{1,0:T(8,128)(2,1)S(1)}, f...) custom-call(s32[12,128]{1,0:T(8,128)} %bitcast.27, s32[12,128]{1,0:T(8,128)} %bitcast.29, bf16[256,512]{1,0:T(8,128)(2,1)} %mesh_hbm.3, ...), custom_call_target="tpu_custom_call" | custom-call | tf_op jit(solution)/shard_map/edges/pallas_call | solution.py:445
  26.8 2.2 %collective-permute-done.1 = bf16[256,512]{1,0:T(8,128)(2,1)S(1)} collective-permute-done((bf16[256,512]{1,0:T(8,128)(2,1)S(1)}, bf16[256,512]{1,0:T(8,128)(2,1)S(1)}, u32[]{:S(2)}, u32[]{:S(2)}) %collective-permute-start.1) | collective-permute-done | bytes 262176 | tf_op jit(solution)/shard_map/ppermute | solution.py:379
  29.4 2.0 %collective-permute-start.3 = (bf16[128,512]{1,0:T(8,128)(2,1)S(1)}, bf16[128,512]{1,0:T(8,128)(2,1)S(1)}, u32[]{:S(2)}, u32[]{:S(2)}) collective-permute-start(bf16[128,512]{1,0:T(8,128)(2,1)S(1)} %slice.105), channel_id=1, source_target_pairs={{0,2},{1,3},{2,0},{3,1},{4,6},{5,7},{6,4},{7,5},{8,10},{9,11},{10,... | collective-permute-start | bytes 393224 | tf_op jit(solution)/shard_map/ppermute | solution.py:379
  31.4 13.3 %collective-permute-done.3 = bf16[128,512]{1,0:T(8,128)(2,1)S(1)} collective-permute-done((bf16[128,512]{1,0:T(8,128)(2,1)S(1)}, bf16[128,512]{1,0:T(8,128)(2,1)S(1)}, u32[]{:S(2)}, u32[]{:S(2)}) %collective-permute-start.3) | collective-permute-done | bytes 131104 | tf_op jit(solution)/shard_map/ppermute | solution.py:379
  44.8 1.1 %collective-permute-start.4 = (bf16[128,512]{1,0:T(8,128)(2,1)S(1)}, bf16[128,512]{1,0:T(8,128)(2,1)S(1)}, u32[]{:S(2)}, u32[]{:S(2)}) collective-permute-start(bf16[128,512]{1,0:T(8,128)(2,1)S(1)} %fusion), channel_id=1, source_target_pairs={{0,12},{1,13},{2,14},{3,15},{4,8},{5,9},{6,10},{7,11},{8,4},{9,5},... | collective-permute-start | bytes 393224 | tf_op jit(solution)/shard_map/ppermute | solution.py:379
  46.0 5.7 %collective-permute-done.4 = bf16[128,512]{1,0:T(8,128)(2,1)S(1)} collective-permute-done((bf16[128,512]{1,0:T(8,128)(2,1)S(1)}, bf16[128,512]{1,0:T(8,128)(2,1)S(1)}, u32[]{:S(2)}, u32[]{:S(2)}) %collective-permute-start.4) | collective-permute-done | bytes 131104 | tf_op jit(solution)/shard_map/ppermute | solution.py:379
  53.6 5.6 %collective-permute-done.5 = bf16[160,512]{1,0:T(8,128)(2,1)S(1)} collective-permute-done((bf16[160,512]{1,0:T(8,128)(2,1)S(1)}, bf16[160,512]{1,0:T(8,128)(2,1)S(1)}, u32[]{:S(2)}, u32[]{:S(2)}) %collective-permute-start.5) | collective-permute-done | bytes 163872 | tf_op jit(solution)/shard_map/ppermute | solution.py:379
  59.2 3.2 %collective-permute-done.6 = bf16[160,512]{1,0:T(8,128)(2,1)S(1)} collective-permute-done((bf16[160,512]{1,0:T(8,128)(2,1)S(1)}, bf16[160,512]{1,0:T(8,128)(2,1)S(1)}, u32[]{:S(2)}, u32[]{:S(2)}) %collective-permute-start.6) | collective-permute-done | bytes 163872 | tf_op jit(solution)/shard_map/ppermute | solution.py:379
  62.5 3.0 %collective-permute-start.13 = (bf16[128,512]{1,0:T(8,128)(2,1)S(1)}, bf16[128,512]{1,0:T(8,128)(2,1)S(1)}, u32[]{:S(2)}, u32[]{:S(2)}) collective-permute-start(bf16[128,512]{1,0:T(8,128)(2,1)S(1)} %add_convert_fusion.refs_0_), channel_id=1, source_target_pairs={{0,4},{1,5},{2,6},{3,7},{4,0},{5,1},{6,2},{7,3},{8,12},{9,13},{10,... | collective-permute-start | bytes 393224 | tf_op jit(solution)/shard_map/ppermute | solution.py:379
  65.5 1.6 %collective-permute-start.14 = (bf16[128,512]{1,0:T(8,128)(2,1)S(1)}, bf16[128,512]{1,0:T(8,128)(2,1)S(1)}, u32[]{:S(2)}, u32[]{:S(2)}) collective-permute-start(bf16[128,512]{1,0:T(8,128)(2,1)S(1)} %add_convert_fusion.refs_0_), channel_id=1, source_target_pairs={{0,2},{1,3},{2,0},{3,1},{4,6},{5,7},{6,4},{7,5},{8,10},{9,11},{10,... | collective-permute-start | bytes 393224 | tf_op jit(solution)/shard_map/ppermute | solution.py:379
  67.1 2.3 %collective-permute-done.8.refs_2_ = bf16[128,512]{1,0:T(8,128)(2,1)S(1)} collective-permute-done((bf16[128,512]{1,0:T(8,128)(2,1)S(1)}, bf16[128,512]{1,0:T(8,128)(2,1)S(1)}, u32[]{:S(2)}, u32[]{:S(2)}) %collective-permute-start.8) | collective-permute-done | bytes 131104 | tf_op jit(solution)/shard_map/ppermute | solution.py:379
  69.4 1.5 %collective-permute-start.7 = (bf16[2,2,8,512]{3,2,1,0:T(8,128)(2,1)S(1)}, bf16[2,2,8,512]{3,2,1,0:T(8,128)(2,1)S(1)}, u32[]{:S(2)}, u32[]{:S(2)}) collective-permute-start(bf16[2,2,8,512]{3,2,1,0:T(8,128)(2,1)S(1)} %get-tuple-element.48), channel_id=1, source_target_pairs={{0,12},{1,13},{2,14},{3,15},{4,8},{5,9},{6,10},{7,11},{8,4},{9,5},... | collective-permute-start | bytes 98312 | tf_op jit(solution)/shard_map/ppermute | solution.py:379
  70.9 1.6 %collective-permute-start.15 = (bf16[128,512]{1,0:T(8,128)(2,1)S(1)}, bf16[128,512]{1,0:T(8,128)(2,1)S(1)}, u32[]{:S(2)}, u32[]{:S(2)}) collective-permute-start(bf16[128,512]{1,0:T(8,128)(2,1)S(1)} %collective-permute-done.13.refs_1_), channel_id=1, source_target_pairs={{0,2},{1,3},{2,0},{3,1},{4,6},{5,7},{6,4},{7,5},{8,10},{9,11},{10,... | collective-permute-start | bytes 393224 | tf_op jit(solution)/shard_map/ppermute | solution.py:379
  72.5 2.6 %collective-permute-done.7 = bf16[2,2,8,512]{3,2,1,0:T(8,128)(2,1)S(1)} collective-permute-done((bf16[2,2,8,512]{3,2,1,0:T(8,128)(2,1)S(1)}, bf16[2,2,8,512]{3,2,1,0:T(8,128)(2,1)S(1)}, u32[]{:S(2)}, u32[]{:S(2)}) %collective-permute-start.7) | collective-permute-done | bytes 32800 | tf_op jit(solution)/shard_map/ppermute | solution.py:379
  75.1 1.6 %collective-permute-start.16 = (bf16[128,512]{1,0:T(8,128)(2,1)S(1)}, bf16[128,512]{1,0:T(8,128)(2,1)S(1)}, u32[]{:S(2)}, u32[]{:S(2)}) collective-permute-start(bf16[128,512]{1,0:T(8,128)(2,1)S(1)} %collective-permute-done.8.refs_2_), channel_id=1, source_target_pairs={{0,2},{1,3},{2,0},{3,1},{4,6},{5,7},{6,4},{7,5},{8,10},{9,11},{10,... | collective-permute-start | bytes 393224 | tf_op jit(solution)/shard_map/ppermute | solution.py:379
  77.7 2.9 %collective-permute-done.16.refs_5_ = bf16[128,512]{1,0:T(8,128)(2,1)S(1)} collective-permute-done((bf16[128,512]{1,0:T(8,128)(2,1)S(1)}, bf16[128,512]{1,0:T(8,128)(2,1)S(1)}, u32[]{:S(2)}, u32[]{:S(2)}) %collective-permute-start.16) | collective-permute-done | bytes 131104 | tf_op jit(solution)/shard_map/ppermute | solution.py:379
  81.2 1.7 %collective-permute-done.10.refs_1_ = bf16[128,512]{1,0:T(8,128)(2,1)S(1)} collective-permute-done((bf16[128,512]{1,0:T(8,128)(2,1)S(1)}, bf16[128,512]{1,0:T(8,128)(2,1)S(1)}, u32[]{:S(2)}, u32[]{:S(2)}) %collective-permute-start.10) | collective-permute-done | bytes 131104 | tf_op jit(solution)/shard_map/ppermute | solution.py:379
  82.9 2.4 %put.1 = f32[1024,512]{1,0:T(8,128)} custom-call(s32[1,128]{1,0:T(1,128)} %rows_hbm.3, bf16[128,512]{1,0:T(8,128)(2,1)S(1)} %bitcast.18), custom_call_target="tpu_custom_call" | custom-call | tf_op jit(solution)/shard_map/put/pallas_call | solution.py:543
  85.4 1.8 %order.2 = (f32[1536,512]{1,0:T(8,128)}, f32[512,512]{1,0:T(8,128)}) custom-call(bf16[128,512]{1,0:T(8,128)(2,1)S(1)} %add_convert_fusion.refs_0_, bf16[128,512]{1,0:T(8,128)(2,1)S(1)} %collective-permute-done.13.refs_1_, bf16[128,512]{1,0:T(8,128)(2,1)S(1)} %collective-permute-done.8.refs_2_, bf16[128,512]{1,0:T(8,128)(2,1)S(1)} %collective-permute-done.14.refs_3_, ...), custom_call_target="tpu_custom_call" | custom-call | tf_op jit(solution)/shard_map/order/pallas_call | solution.py:561
  87.2 1.0 %order.3 = (f32[1536,512]{1,0:T(8,128)}, f32[512,512]{1,0:T(8,128)}) custom-call(bf16[128,512]{1,0:T(8,128)(2,1)S(1)} %collective-permute-done.9.refs_0_, bf16[128,512]{1,0:T(8,128)(2,1)S(1)} %collective-permute-done.10.refs_1_, bf16[128,512]{1,0:T(8,128)(2,1)S(1)} %collective-permute-done.11.refs_2_, ...), custom_call_target="tpu_custom_call", output_to_operand_aliasing={{0}: (4, {}), {1}: (5, {})} | custom-call | tf_op jit(solution)/shard_map/order/pallas_call | solution.py:561
  (45 shorter events, 4.6 us)
Async XLA Ops:
  2.9 15.3 %all-to-all-start = ((bf16[16,8,512]{2,1,0:T(8,128)(2,1)}), bf16[16,8,512]{2,1,0:T(8,128)(2,1)S(1)}, u32[]{:S(2)}, u32[]{:S(2)}) async-start(bf16[16,8,512]{2,1,0:T(8,128)(2,1)} %bitcast.2), calls=%async_computation | async-start | bytes 262144 | tf_op jit(solution)/shard_map/all_to_all | solution.py:403
  26.3 2.9 %collective-permute-start = (bf16[832,512]{1,0:T(8,128)(2,1)S(1)}, bf16[832,512]{1,0:T(8,128)(2,1)S(1)}, u32[]{:S(2)}, u32[]{:S(2)}) collective-permute-start(bf16[832,512]{1,0:T(8,128)(2,1)S(1)} %get-tuple-element.31), channel_id=1, source_target_pairs={{0,1},{1,0},{2,3},{3,2},{4,5},{5,4},{6,7},{7,6},{8,9},{9,8},{10,11... | collective-permute-start | bytes 2555912 | tf_op jit(solution)/shard_map/ppermute | solution.py:379
  26.3 2.7 %collective-permute-start.1 = (bf16[256,512]{1,0:T(8,128)(2,1)S(1)}, bf16[256,512]{1,0:T(8,128)(2,1)S(1)}, u32[]{:S(2)}, u32[]{:S(2)}) collective-permute-start(bf16[256,512]{1,0:T(8,128)(2,1)S(1)} %get-tuple-element.33), channel_id=1, source_target_pairs={{0,1},{1,0},{2,3},{3,2},{4,5},{5,4},{6,7},{7,6},{8,9},{9,8},{10,11... | collective-permute-start | bytes 786440 | tf_op jit(solution)/shard_map/ppermute | solution.py:379
  29.3 16.6 %collective-permute-start.2 = (bf16[448,512]{1,0:T(8,128)(2,1)S(1)}, bf16[448,512]{1,0:T(8,128)(2,1)S(1)}, u32[]{:S(2)}, u32[]{:S(2)}) collective-permute-start(bf16[448,512]{1,0:T(8,128)(2,1)S(1)} %get-tuple-element.37), channel_id=1, source_target_pairs={{0,2},{1,3},{2,0},{3,1},{4,6},{5,7},{6,4},{7,5},{8,10},{9,11},{10,... | collective-permute-start | bytes 1376264 | tf_op jit(solution)/shard_map/ppermute | solution.py:379
  29.4 15.4 %collective-permute-start.3 = (bf16[128,512]{1,0:T(8,128)(2,1)S(1)}, bf16[128,512]{1,0:T(8,128)(2,1)S(1)}, u32[]{:S(2)}, u32[]{:S(2)}) collective-permute-start(bf16[128,512]{1,0:T(8,128)(2,1)S(1)} %slice.105), channel_id=1, source_target_pairs={{0,2},{1,3},{2,0},{3,1},{4,6},{5,7},{6,4},{7,5},{8,10},{9,11},{10,... | collective-permute-start | bytes 393224 | tf_op jit(solution)/shard_map/ppermute | solution.py:379
  44.8 6.9 %collective-permute-start.4 = (bf16[128,512]{1,0:T(8,128)(2,1)S(1)}, bf16[128,512]{1,0:T(8,128)(2,1)S(1)}, u32[]{:S(2)}, u32[]{:S(2)}) collective-permute-start(bf16[128,512]{1,0:T(8,128)(2,1)S(1)} %fusion), channel_id=1, source_target_pairs={{0,12},{1,13},{2,14},{3,15},{4,8},{5,9},{6,10},{7,11},{8,4},{9,5},... | collective-permute-start | bytes 393224 | tf_op jit(solution)/shard_map/ppermute | solution.py:379
  51.8 7.4 %collective-permute-start.5 = (bf16[160,512]{1,0:T(8,128)(2,1)S(1)}, bf16[160,512]{1,0:T(8,128)(2,1)S(1)}, u32[]{:S(2)}, u32[]{:S(2)}) collective-permute-start(bf16[160,512]{1,0:T(8,128)(2,1)S(1)} %pad_maximum_fusion), channel_id=1, source_target_pairs={{0,4},{1,5},{2,6},{3,7},{4,0},{5,1},{6,2},{7,3},{8,12},{9,13},{10,... | collective-permute-start | bytes 491528 | tf_op jit(solution)/shard_map/ppermute | solution.py:379
  52.8 9.6 %collective-permute-start.6 = (bf16[160,512]{1,0:T(8,128)(2,1)S(1)}, bf16[160,512]{1,0:T(8,128)(2,1)S(1)}, u32[]{:S(2)}, u32[]{:S(2)}) collective-permute-start(bf16[160,512]{1,0:T(8,128)(2,1)S(1)} %pad_maximum_fusion.1), channel_id=1, source_target_pairs={{0,8},{1,9},{2,10},{3,11},{4,12},{5,13},{6,14},{7,15},{8,0},{9,1},... | collective-permute-start | bytes 491528 | tf_op jit(solution)/shard_map/ppermute | solution.py:379
  62.5 6.9 %collective-permute-start.8 = (bf16[128,512]{1,0:T(8,128)(2,1)S(1)}, bf16[128,512]{1,0:T(8,128)(2,1)S(1)}, u32[]{:S(2)}, u32[]{:S(2)}) collective-permute-start(bf16[128,512]{1,0:T(8,128)(2,1)S(1)} %add_convert_fusion.refs_0_), channel_id=1, source_target_pairs={{0,8},{1,9},{2,10},{3,11},{4,12},{5,13},{6,14},{7,15},{8,0},{9,1},... | collective-permute-start | bytes 393224 | tf_op jit(solution)/shard_map/ppermute | solution.py:379
  62.5 8.4 %collective-permute-start.13 = (bf16[128,512]{1,0:T(8,128)(2,1)S(1)}, bf16[128,512]{1,0:T(8,128)(2,1)S(1)}, u32[]{:S(2)}, u32[]{:S(2)}) collective-permute-start(bf16[128,512]{1,0:T(8,128)(2,1)S(1)} %add_convert_fusion.refs_0_), channel_id=1, source_target_pairs={{0,4},{1,5},{2,6},{3,7},{4,0},{5,1},{6,2},{7,3},{8,12},{9,13},{10,... | collective-permute-start | bytes 393224 | tf_op jit(solution)/shard_map/ppermute | solution.py:379
  65.5 11.2 %collective-permute-start.14 = (bf16[128,512]{1,0:T(8,128)(2,1)S(1)}, bf16[128,512]{1,0:T(8,128)(2,1)S(1)}, u32[]{:S(2)}, u32[]{:S(2)}) collective-permute-start(bf16[128,512]{1,0:T(8,128)(2,1)S(1)} %add_convert_fusion.refs_0_), channel_id=1, source_target_pairs={{0,2},{1,3},{2,0},{3,1},{4,6},{5,7},{6,4},{7,5},{8,10},{9,11},{10,... | collective-permute-start | bytes 393224 | tf_op jit(solution)/shard_map/ppermute | solution.py:379
  67.1 9.6 %collective-permute-start.17 = (bf16[128,512]{1,0:T(8,128)(2,1)S(1)}, bf16[128,512]{1,0:T(8,128)(2,1)S(1)}, u32[]{:S(2)}, u32[]{:S(2)}) collective-permute-start(bf16[128,512]{1,0:T(8,128)(2,1)S(1)} %add_convert_fusion.refs_0_), channel_id=1, source_target_pairs={{0,1},{1,0},{2,3},{3,2},{4,5},{5,4},{6,7},{7,6},{8,9},{9,8},{10,11... | collective-permute-start | bytes 393224 | tf_op jit(solution)/shard_map/ppermute | solution.py:379
  69.4 7.9 %collective-permute-start.9 = (bf16[128,512]{1,0:T(8,128)(2,1)S(1)}, bf16[128,512]{1,0:T(8,128)(2,1)S(1)}, u32[]{:S(2)}, u32[]{:S(2)}) collective-permute-start(bf16[128,512]{1,0:T(8,128)(2,1)S(1)} %collective-permute-done.8.refs_2_), channel_id=1, source_target_pairs={{0,4},{1,5},{2,6},{3,7},{4,0},{5,1},{6,2},{7,3},{8,12},{9,13},{10,... | collective-permute-start | bytes 393224 | tf_op jit(solution)/shard_map/ppermute | solution.py:379
  69.4 5.7 %collective-permute-start.7 = (bf16[2,2,8,512]{3,2,1,0:T(8,128)(2,1)S(1)}, bf16[2,2,8,512]{3,2,1,0:T(8,128)(2,1)S(1)}, u32[]{:S(2)}, u32[]{:S(2)}) collective-permute-start(bf16[2,2,8,512]{3,2,1,0:T(8,128)(2,1)S(1)} %get-tuple-element.48), channel_id=1, source_target_pairs={{0,12},{1,13},{2,14},{3,15},{4,8},{5,9},{6,10},{7,11},{8,4},{9,5},... | collective-permute-start | bytes 98312 | tf_op jit(solution)/shard_map/ppermute | solution.py:379
  70.9 6.8 %collective-permute-start.15 = (bf16[128,512]{1,0:T(8,128)(2,1)S(1)}, bf16[128,512]{1,0:T(8,128)(2,1)S(1)}, u32[]{:S(2)}, u32[]{:S(2)}) collective-permute-start(bf16[128,512]{1,0:T(8,128)(2,1)S(1)} %collective-permute-done.13.refs_1_), channel_id=1, source_target_pairs={{0,2},{1,3},{2,0},{3,1},{4,6},{5,7},{6,4},{7,5},{8,10},{9,11},{10,... | collective-permute-start | bytes 393224 | tf_op jit(solution)/shard_map/ppermute | solution.py:379
  75.1 5.4 %collective-permute-start.16 = (bf16[128,512]{1,0:T(8,128)(2,1)S(1)}, bf16[128,512]{1,0:T(8,128)(2,1)S(1)}, u32[]{:S(2)}, u32[]{:S(2)}) collective-permute-start(bf16[128,512]{1,0:T(8,128)(2,1)S(1)} %collective-permute-done.8.refs_2_), channel_id=1, source_target_pairs={{0,2},{1,3},{2,0},{3,1},{4,6},{5,7},{6,4},{7,5},{8,10},{9,11},{10,... | collective-permute-start | bytes 393224 | tf_op jit(solution)/shard_map/ppermute | solution.py:379
  76.7 3.8 %collective-permute-start.18 = (bf16[128,512]{1,0:T(8,128)(2,1)S(1)}, bf16[128,512]{1,0:T(8,128)(2,1)S(1)}, u32[]{:S(2)}, u32[]{:S(2)}) collective-permute-start(bf16[128,512]{1,0:T(8,128)(2,1)S(1)} %collective-permute-done.13.refs_1_), channel_id=1, source_target_pairs={{0,1},{1,0},{2,3},{3,2},{4,5},{5,4},{6,7},{7,6},{8,9},{9,8},{10,11... | collective-permute-start | bytes 393224 | tf_op jit(solution)/shard_map/ppermute | solution.py:379
  76.7 4.3 %collective-permute-start.19 = (bf16[128,512]{1,0:T(8,128)(2,1)S(1)}, bf16[128,512]{1,0:T(8,128)(2,1)S(1)}, u32[]{:S(2)}, u32[]{:S(2)}) collective-permute-start(bf16[128,512]{1,0:T(8,128)(2,1)S(1)} %collective-permute-done.8.refs_2_), channel_id=1, source_target_pairs={{0,1},{1,0},{2,3},{3,2},{4,5},{5,4},{6,7},{7,6},{8,9},{9,8},{10,11... | collective-permute-start | bytes 393224 | tf_op jit(solution)/shard_map/ppermute | solution.py:379
  77.2 5.7 %collective-permute-start.10 = (bf16[128,512]{1,0:T(8,128)(2,1)S(1)}, bf16[128,512]{1,0:T(8,128)(2,1)S(1)}, u32[]{:S(2)}, u32[]{:S(2)}) collective-permute-start(bf16[128,512]{1,0:T(8,128)(2,1)S(1)} %collective-permute-done.9.refs_0_), channel_id=1, source_target_pairs={{0,2},{1,3},{2,0},{3,1},{4,6},{5,7},{6,4},{7,5},{8,10},{9,11},{10,... | collective-permute-start | bytes 393224 | tf_op jit(solution)/shard_map/ppermute | solution.py:379
  77.7 7.7 %collective-permute-start.20 = (bf16[128,512]{1,0:T(8,128)(2,1)S(1)}, bf16[128,512]{1,0:T(8,128)(2,1)S(1)}, u32[]{:S(2)}, u32[]{:S(2)}) collective-permute-start(bf16[128,512]{1,0:T(8,128)(2,1)S(1)} %collective-permute-done.14.refs_3_), channel_id=1, source_target_pairs={{0,1},{1,0},{2,3},{3,2},{4,5},{5,4},{6,7},{7,6},{8,9},{9,8},{10,11... | collective-permute-start | bytes 393224 | tf_op jit(solution)/shard_map/ppermute | solution.py:379
  80.6 4.8 %collective-permute-start.21 = (bf16[128,512]{1,0:T(8,128)(2,1)S(1)}, bf16[128,512]{1,0:T(8,128)(2,1)S(1)}, u32[]{:S(2)}, u32[]{:S(2)}) collective-permute-start(bf16[128,512]{1,0:T(8,128)(2,1)S(1)} %collective-permute-done.15.refs_4_), channel_id=1, source_target_pairs={{0,1},{1,0},{2,3},{3,2},{4,5},{5,4},{6,7},{7,6},{8,9},{9,8},{10,11... | collective-permute-start | bytes 393224 | tf_op jit(solution)/shard_map/ppermute | solution.py:379
  80.6 4.8 %collective-permute-start.22 = (bf16[128,512]{1,0:T(8,128)(2,1)S(1)}, bf16[128,512]{1,0:T(8,128)(2,1)S(1)}, u32[]{:S(2)}, u32[]{:S(2)}) collective-permute-start(bf16[128,512]{1,0:T(8,128)(2,1)S(1)} %collective-permute-done.16.refs_5_), channel_id=1, source_target_pairs={{0,1},{1,0},{2,3},{3,2},{4,5},{5,4},{6,7},{7,6},{8,9},{9,8},{10,11... | collective-permute-start | bytes 393224 | tf_op jit(solution)/shard_map/ppermute | solution.py:379
  81.1 6.1 %collective-permute-start.11 = (bf16[128,512]{1,0:T(8,128)(2,1)S(1)}, bf16[128,512]{1,0:T(8,128)(2,1)S(1)}, u32[]{:S(2)}, u32[]{:S(2)}) collective-permute-start(bf16[128,512]{1,0:T(8,128)(2,1)S(1)} %collective-permute-done.9.refs_0_), channel_id=1, source_target_pairs={{0,1},{1,0},{2,3},{3,2},{4,5},{5,4},{6,7},{7,6},{8,9},{9,8},{10,11... | collective-permute-start | bytes 393224 | tf_op jit(solution)/shard_map/ppermute | solution.py:379
  82.9 4.3 %collective-permute-start.12 = (bf16[128,512]{1,0:T(8,128)(2,1)S(1)}, bf16[128,512]{1,0:T(8,128)(2,1)S(1)}, u32[]{:S(2)}, u32[]{:S(2)}) collective-permute-start(bf16[128,512]{1,0:T(8,128)(2,1)S(1)} %collective-permute-done.10.refs_1_), channel_id=1, source_target_pairs={{0,1},{1,0},{2,3},{3,2},{4,5},{5,4},{6,7},{7,6},{8,9},{9,8},{10,11... | collective-permute-start | bytes 393224 | tf_op jit(solution)/shard_map/ppermute | solution.py:379

commit v6 on v5

v6 whole, which is shorter than its diff:
```python
import functools

import jax
import jax.numpy as jnp
from jax import lax
from jax.experimental import pallas as pl
from jax.experimental.pallas import tpu as pltpu
from jax.sharding import PartitionSpec as P

BF16 = jnp.bfloat16
F32 = jnp.float32
MIB = 1024 * 1024


def dot_nn(a, b):
    return jnp.dot(a, b, preferred_element_type=F32)


def dot_tn(a, b):
    return lax.dot_general(a, b, (((0,), (0,)), ((), ())), preferred_element_type=F32)


def dot_nt(a, b):
    return lax.dot_general(a, b, (((1,), (1,)), ((), ())), preferred_element_type=F32)


def split(value):
    high = value.astype(BF16)
    low = (value - high.astype(F32)).astype(BF16)
    return high, low


def one_hot_rows(index_row, rows):
    shape = (rows, index_row.shape[1])
    hit = lax.broadcasted_iota(jnp.int32, shape, 0) == index_row
    return jnp.where(hit, 1.0, 0.0).astype(BF16)


def one_hot_columns(index_row, columns):
    lanes = index_row.shape[1]
    index = jnp.transpose(jnp.broadcast_to(index_row, (lanes, lanes)))
    pieces = []
    for start in range(0, columns, lanes):
        hit = lax.broadcasted_iota(jnp.int32, (lanes, lanes), 1) + start == index
        pieces.append(jnp.where(hit, 1.0, 0.0).astype(BF16))
    return pieces[0] if len(pieces) == 1 else jnp.concatenate(pieces, axis=1)


def tile_rows(index_ref, at, lines, rows):
    found = [one_hot_rows(index_ref[pl.ds(at * lines + k, 1), :], rows) for k in range(lines)]
    return jnp.concatenate(found, axis=1)


def tile_columns(index_ref, at, lines, columns):
    found = [one_hot_columns(index_ref[pl.ds(at * lines + k, 1), :], columns) for k in range(lines)]
    return jnp.concatenate(found, axis=0)


def place_of(sizes):
    outer, inner = sizes
    me = lax.axis_index("band")
    return me // (2 * inner), (me // 2) % inner, me % 2


def owner_at(sizes, far_outer, far_inner, far_core):
    my_outer, my_inner, my_core = place_of(sizes)
    return ((my_outer ^ far_outer) * sizes[1] + (my_inner ^ far_inner)) * 2 + (my_core ^ far_core)


def params(mib):
    return pltpu.CompilerParams(vmem_limit_bytes=mib * MIB)


def pinned(space, *values):
    return [pltpu.with_memory_space_constraint(value, space) for value in values]


def specs(space, count):
    return [pl.BlockSpec(memory_space=space)] * count


def cost(flops, nbytes):
    return pl.CostEstimate(flops=flops, bytes_accessed=nbytes, transcendentals=0)


def load(pairs, sems):
    copies = [pltpu.make_async_copy(source, target, sems.at[at]) for at, (source, target) in enumerate(pairs)]
    for copy in copies:
        copy.start()
    return copies


def pick_kernel(sizes, rows_hbm, grid_hbm, keep_ref, send_ref, rows_ref, grid_ref, picked_ref, sems):
    outer, inner = sizes
    rows_copy, grid_copy = load([(rows_hbm, rows_ref), (grid_hbm, grid_ref)], sems)
    rows_copy.wait()
    picked = picked_ref.shape[0]
    chosen = [one_hot_columns(rows_ref[:, at : at + 128], grid_ref.shape[0]) for at in range(0, picked, 128)]
    grid_copy.wait()
    for at, some in enumerate(chosen):
        picked_ref[at * 128 : (at + 1) * 128, :] = dot_nn(some, grid_ref[...])
    cap = picked // (2 * outer * inner)
    for far_core, target in enumerate((keep_ref, send_ref)):
        blocks = []
        for far_inner in range(inner):
            for far_outer in range(outer):
                owner = owner_at(sizes, far_outer, far_inner, far_core)
                blocks.append(picked_ref[pl.ds(pl.multiple_of(owner * cap, cap), cap), :])
        target[...] = jnp.concatenate(blocks, axis=0).astype(BF16)


def mix_kernel(count, minor, *refs):
    sources, targets = refs[:-count], refs[-count:]
    values = [ref[...].astype(F32) for ref in sources]
    unit = values[0].shape[0] // (count * minor)
    for at, target in enumerate(targets):
        starts = [(at * minor + k) * unit for k in range(minor)]
        blocks = [value[start : start + unit] for start in starts for value in values]
        target[...] = jnp.concatenate(blocks, axis=0).astype(BF16)


def put_kernel(sizes, rows_hbm, *refs):
    outer, inner = sizes
    blocks, (out_ref, ordered_ref, rows_ref, sems) = refs[:outer], refs[outer:]
    (copy,) = load([(rows_hbm, rows_ref)], sems)
    place_rows(sizes, blocks, ordered_ref)
    copy.wait()
    chosen = one_hot_rows(rows_ref[...], out_ref.shape[0])
    out_ref[...] = dot_nn(chosen, ordered_ref[...].astype(BF16))


def place_rows(sizes, blocks, ordered_ref):
    outer, inner = sizes
    cap = ordered_ref.shape[0] // (2 * outer * inner)
    for far_outer, block in enumerate(blocks):
        value = block[block.shape[0] - 2 * inner * cap :, :].astype(F32)
        for at in range(2 * inner):
            owner = owner_at(sizes, far_outer, at // 2, at % 2)
            ordered_ref[pl.ds(pl.multiple_of(owner * cap, cap), cap), :] = value[at * cap : (at + 1) * cap]


def ready_kernel(
    lines,
    dst_hbm,
    mesh_hbm,
    cot_hbm,
    w1_hbm,
    wn1_hbm,
    wn2_hbm,
    hot_hbm,
    node_hbm,
    cot_out_hbm,
    moved_ref,
    dst_ref,
    mesh_ref,
    cot_ref,
    w1_ref,
    wn1_ref,
    wn2_ref,
    hot_ref,
    node_ref,
    cot_out_ref,
    sems,
    out_sems,
):
    width = mesh_ref.shape[1]
    tile = lines * 128
    pairs = [
        (dst_hbm, dst_ref),
        (mesh_hbm, mesh_ref),
        (w1_hbm.at[pl.ds(width, width), :], w1_ref),
        (wn1_hbm.at[pl.ds(0, width), :], wn1_ref),
        (cot_hbm, cot_ref),
        (wn2_hbm, wn2_ref),
    ]
    copies = load(pairs, sems)
    copies[0].wait()
    for at in range(hot_ref.shape[0] // tile):
        hot_ref[at * tile : (at + 1) * tile, :] = tile_columns(dst_ref, at, lines, hot_ref.shape[1])
    for copy in copies[1:]:
        copy.wait()
    moved_ref[...] = dot_nn(mesh_ref[...], w1_ref[...]).astype(BF16)
    node_ref[...] = dot_nn(mesh_ref[...], wn1_ref[...])
    cot_out_ref[...] = dot_nt(cot_ref[...], wn2_ref[...])
    pairs = [(hot_ref, hot_hbm), (node_ref, node_hbm), (cot_out_ref, cot_out_hbm)]
    for copy in load(pairs, out_sems):
        copy.wait()


def base_kernel(
    lines,
    hot_hbm,
    edge_hbm,
    w1_hbm,
    moved_ref,
    base_ref,
    turned_hbm,
    hot_ref,
    edge_ref,
    w1_ref,
    turned_ref,
    sems,
    out_sems,
):
    width = edge_ref.shape[1]
    tile = lines * 128
    tiles = edge_ref.shape[0] // tile
    pairs = [(w1_hbm.at[pl.ds(2 * width, width), :], w1_ref), (hot_hbm, hot_ref)]
    pairs += [(edge_hbm.at[pl.ds(at * tile, tile), :], edge_ref.at[pl.ds(at * tile, tile), :]) for at in range(tiles)]
    copies = load(pairs, sems)
    same = lax.broadcasted_iota(jnp.int32, (256, 256), 0) == lax.broadcasted_iota(jnp.int32, (256, 256), 1)
    eye = jnp.where(same, 1.0, 0.0).astype(BF16)
    copies[0].wait()
    copies[1].wait()
    for at in range(tiles):
        rows = slice(at * tile, (at + 1) * tile)
        copies[2 + at].wait()
        edge = edge_ref[rows, :]
        for start in range(0, width, 256):
            turned_ref[start : start + 256, rows] = dot_nt(eye, edge[:, start : start + 256]).astype(BF16)
        base_ref[rows, :] = dot_nn(edge, w1_ref[...]) + dot_nn(hot_ref[rows, :], moved_ref[...])
    (last,) = load([(turned_ref, turned_hbm)], out_sems)
    last.wait()


def main_kernel(
    lines,
    sizes,
    slot_hbm,
    dst_hbm,
    mesh_hbm,
    w1_hbm,
    w2_hbm,
    wn1_hbm,
    wn2_hbm,
    turned_hbm,
    hot_hbm,
    node_hbm,
    cot_hbm,
    base_ref,
    *rest,
):
    outer, inner = sizes
    slot_blocks, rest = rest[:outer], rest[outer:]
    mesh_out_ref, d_slots_ref = rest[:2]
    send_refs, keep_refs, rest = rest[2 : 2 + outer], rest[2 + outer : 2 + 2 * outer], rest[2 + 2 * outer :]
    slope_ref, value_ref, both_ref, grads_ref, slot_grads_ref, ordered_ref = rest[:6]
    slot_ref, dst_ref, mesh_ref, w1_ref, w2_ref, wn1_ref, wn2_ref = rest[6:13]
    turned_ref, hot_ref, node_ref, cot_ref, sems = rest[13:]
    width = mesh_ref.shape[1]
    mesh_rows = mesh_ref.shape[0]
    slot_rows = ordered_ref.shape[0]
    tile = lines * 128
    tiles = base_ref.shape[0] // tile
    pairs = [
        (slot_hbm, slot_ref),
        (w1_hbm.at[pl.ds(0, width), :], w1_ref),
        (dst_hbm, dst_ref),
        (w2_hbm, w2_ref),
        (wn1_hbm.at[pl.ds(width, wn1_ref.shape[0]), :], wn1_ref),
        (mesh_hbm, mesh_ref),
        (node_hbm, node_ref),
        (cot_hbm, cot_ref),
        (hot_hbm, hot_ref),
        (wn2_hbm, wn2_ref),
        (turned_hbm, turned_ref),
    ]
    copies = load(pairs, sems)
    place_rows(sizes, slot_blocks, ordered_ref)
    slots_value = ordered_ref[...].astype(BF16)
    for copy in copies[:3]:
        copy.wait()

    slots = slots_value
    slot_pair = jnp.concatenate(split(dot_nn(slots, w1_ref[...])), axis=0)
    for at in range(tiles):
        rows = slice(at * tile, (at + 1) * tile)
        from_slot = tile_columns(slot_ref, at, lines, slot_rows)
        twice = jnp.concatenate([from_slot, from_slot], axis=1)
        pre = base_ref[rows, :] + dot_nn(twice, slot_pair)
        sigma = 0.5 + 0.5 * jnp.tanh(0.5 * pre)
        hidden = pre * sigma
        slope_ref[rows, :] = sigma + hidden * (1.0 - sigma)
        value_ref[rows, :] = hidden.astype(BF16)
        both_ref[:slot_rows, rows] = tile_rows(slot_ref, at, lines, slot_rows)
        both_ref[slot_rows:, rows] = tile_rows(dst_ref, at, lines, mesh_rows)

    for copy in copies[3:-1]:
        copy.wait()
    hidden_sums = dot_nn(both_ref[slot_rows:, :], value_ref[...]).astype(BF16)
    received = dot_nn(hidden_sums, w2_ref[...]).astype(BF16)
    mesh = mesh_ref[...]
    pre_node = node_ref[...] + dot_nn(received, wn1_ref[...])
    sigma = 0.5 + 0.5 * jnp.tanh(0.5 * pre_node)
    node = pre_node * sigma
    slope = sigma + node * (1.0 - sigma)
    d_pre_node = (cot_ref[...] * slope).astype(BF16)
    d_received = dot_nt(d_pre_node, wn1_ref[...]).astype(BF16)
    spread = dot_nt(d_received, w2_ref[...]).astype(BF16)

    for at in range(tiles):
        rows = slice(at * tile, (at + 1) * tile)
        value_ref[rows, :] = (dot_nn(hot_ref[rows, :], spread) * slope_ref[rows, :]).astype(BF16)

    grads_ref[3 * width :, :] = dot_tn(hidden_sums, d_received)
    mesh_out_ref[...] = (mesh.astype(F32) + dot_nn(node.astype(BF16), wn2_ref[...])).astype(BF16)
    sums = dot_nn(both_ref[...], value_ref[...]).astype(BF16)
    slot_grads_ref[...] = dot_nt(sums[:slot_rows], w1_ref[...])
    grads_ref[:width, :] = dot_tn(slots, sums[:slot_rows])
    grads_ref[width : 2 * width, :] = dot_tn(mesh, sums[slot_rows:])
    copies[-1].wait()
    grads_ref[2 * width : 3 * width, :] = dot_nn(turned_ref[...], value_ref[...])

    chunk = grads_ref.shape[0] // (2 * outer * inner)
    cap = slot_rows // (2 * outer * inner)
    for far_core in range(2):
        for far_outer in range(outer):
            for far_inner in range(inner):
                owner = owner_at(sizes, far_outer, far_inner, far_core)
                at = (far_core * outer + far_outer) * inner + far_inner
                from_rows = pl.ds(pl.multiple_of(owner * cap, cap), cap)
                ordered_ref[at * cap : (at + 1) * cap, :] = slot_grads_ref[from_rows, :]
                value = grads_ref[pl.ds(pl.multiple_of(owner * chunk, chunk), chunk), :]
                rows = slice(far_inner * chunk, (far_inner + 1) * chunk)
                if far_core:
                    send_refs[far_outer][rows, :] = value.astype(BF16)
                else:
                    keep_refs[far_outer][rows, :] = value
    halfway, share = slot_rows // 2, inner * cap
    d_slots_ref[...] = ordered_ref[:halfway, :].astype(BF16)
    for far_outer, send_ref in enumerate(send_refs):
        start = halfway + far_outer * share
        send_ref[inner * chunk :, :] = ordered_ref[start : start + share, :].astype(BF16)


def core_kernel(sizes, far_outer, keep_ref, crossed_ref, d_slots_ref, total_ref, mixed_ref, *part_refs):
    outer, inner = sizes
    chunk = total_ref.shape[0]
    cap = d_slots_ref.shape[0] // (outer * inner)
    start = far_outer * inner * cap
    own = d_slots_ref[start : start + inner * cap, :].astype(F32)
    far = crossed_ref[inner * chunk :, :].astype(F32)
    for far_inner in range(inner):
        rows, slots = slice(far_inner * chunk, (far_inner + 1) * chunk), slice(far_inner * cap, (far_inner + 1) * cap)
        total = keep_ref[rows, :] + crossed_ref[rows, :].astype(F32)
        mixed = jnp.concatenate([own[slots], far[slots]], axis=0).astype(BF16)
        if far_inner:
            part_refs[far_inner - 1][:chunk, :] = total.astype(BF16)
            part_refs[far_inner - 1][chunk:, :] = mixed
        else:
            total_ref[...] = total
            mixed_ref[...] = mixed


def inner_kernel(parts, arrivals, total_ref, mixed_ref, *refs):
    received, arrived, outs = refs[:parts], refs[parts : parts + arrivals], refs[parts + arrivals :]
    chunk = total_ref.shape[0]
    total = total_ref[...]
    mixed = [mixed_ref[...]]
    for part in received:
        total = total + part[:chunk, :].astype(F32)
        mixed.append(part[chunk:, :])
    for value in arrived:
        total = total + value[:chunk, :].astype(F32)
    mixed = jnp.concatenate(mixed, axis=0)
    if len(outs) == 1:
        outs[0][:chunk, :] = total.astype(BF16)
        outs[0][chunk:, :] = mixed
    else:
        outs[0][...] = total.astype(BF16)
        outs[1][...] = mixed


def order_kernel(sizes, places, aliased, *refs):
    outer, inner = sizes
    pieces = refs[: len(places)]
    first_hbm, second_hbm, stage_ref, sems = refs[len(places) + aliased :]
    chunk = pieces[0].shape[0]
    first_chunks = first_hbm.shape[0] // chunk

    def send(k, target, start):
        rows = pl.ds(pl.multiple_of(start, chunk), chunk)
        return pltpu.make_async_copy(stage_ref.at[k], target.at[rows, :], sems.at[k])

    for k, (at, piece) in enumerate(zip(places, pieces)):
        owner = owner_at(sizes, at % outer, at // outer % inner, at // (outer * inner))
        stage_ref[k] = piece[...].astype(F32)

        @pl.when(owner < first_chunks)
        def _():
            send(k, first_hbm, owner * chunk).start()

        @pl.when(owner >= first_chunks)
        def _():
            send(k, second_hbm, (owner - first_chunks) * chunk).start()

    for k in range(len(places)):
        send(k, first_hbm, 0).wait()


def shards(
    sizes,
    grid_latent,
    mesh_latent,
    edge_latent,
    mesh_cot,
    send_rows,
    edge_slot,
    edge_dst,
    w_edge1,
    w_edge2,
    w_node1,
    w_node2,
):
    outer, inner = sizes
    band_count = lax.axis_size("band")
    width = grid_latent.shape[1]
    hidden_width = w_edge1.shape[1]
    edges = edge_latent.shape[0]
    mesh_rows = mesh_latent.shape[0]
    slot_rows = send_rows.shape[1]
    lines = 4
    slot_index = edge_slot.reshape(edges // 128, 128)
    dst_index = edge_dst.reshape(edges // 128, 128)

    def permute(value, stride, size, shift):
        pairs = []
        for source in range(band_count):
            place = (source // stride) % size
            pairs.append((source, source + ((place ^ shift) - place) * stride))
        return lax.ppermute(value, "band", pairs)

    def to_core(value):
        return permute(value, 1, 2, 1)

    def to_inner(value, shift):
        return permute(value, 2, inner, shift)

    def to_outer(value, shift):
        return permute(value, 2 * inner, outer, shift)

    cap, halfway = slot_rows // band_count, slot_rows // 2
    kept, sent = pl.pallas_call(
        functools.partial(pick_kernel, sizes),
        out_shape=[jax.ShapeDtypeStruct((halfway, width), BF16)] * 2,
        in_specs=specs(pltpu.HBM, 2),
        out_specs=specs(pltpu.VMEM, 2),
        scratch_shapes=[
            pltpu.VMEM(send_rows.shape, jnp.int32),
            pltpu.VMEM(grid_latent.shape, BF16),
            pltpu.VMEM((slot_rows, width), F32),
            pltpu.SemaphoreType.DMA((2,)),
        ],
        compiler_params=params(16),
        name="pick",
    )(*pinned(pltpu.HBM, send_rows, grid_latent))

    def mix(values, count, minor):
        rows = len(values) * values[0].shape[0] // count
        return pl.pallas_call(
            functools.partial(mix_kernel, count, minor),
            out_shape=[jax.ShapeDtypeStruct((rows, width), BF16)] * count,
            compiler_params=params(16),
            name="mix",
        )(*values)

    hot, node, cot, moved = pl.pallas_call(
        functools.partial(ready_kernel, lines),
        out_shape=[
            pltpu.HBM((edges, mesh_rows), BF16),
            pltpu.HBM((mesh_rows, hidden_width), F32),
            pltpu.HBM((mesh_rows, hidden_width), F32),
            pltpu.VMEM((mesh_rows, hidden_width), BF16),
        ],
        in_specs=specs(pltpu.HBM, 6),
        out_specs=specs(pltpu.HBM, 3) + specs(pltpu.VMEM, 1),
        scratch_shapes=[
            pltpu.VMEM(dst_index.shape, jnp.int32),
            pltpu.VMEM(mesh_latent.shape, BF16),
            pltpu.VMEM(mesh_cot.shape, BF16),
            pltpu.VMEM((width, hidden_width), BF16),
            pltpu.VMEM((width, hidden_width), BF16),
            pltpu.VMEM(w_node2.shape, BF16),
            pltpu.VMEM((edges, mesh_rows), BF16),
            pltpu.VMEM((mesh_rows, hidden_width), F32),
            pltpu.VMEM((mesh_rows, hidden_width), F32),
            pltpu.SemaphoreType.DMA((6,)),
            pltpu.SemaphoreType.DMA((3,)),
        ],
        compiler_params=params(16),
        cost_estimate=cost(2 * 10**9, 4 * MIB),
        name="ready",
    )(*pinned(pltpu.HBM, dst_index, mesh_latent, mesh_cot, w_edge1, w_node1, w_node2))
    base, turned = pl.pallas_call(
        functools.partial(base_kernel, lines),
        out_shape=[
            pltpu.VMEM((edges, hidden_width), F32),
            pltpu.HBM((width, edges), BF16),
        ],
        in_specs=specs(pltpu.HBM, 3) + specs(pltpu.VMEM, 1),
        out_specs=specs(pltpu.VMEM, 1) + specs(pltpu.HBM, 1),
        scratch_shapes=[
            pltpu.VMEM((edges, mesh_rows), BF16),
            pltpu.VMEM(edge_latent.shape, BF16),
            pltpu.VMEM((width, hidden_width), BF16),
            pltpu.VMEM((width, edges), BF16),
            pltpu.SemaphoreType.DMA((2 + edges // (128 * lines),)),
            pltpu.SemaphoreType.DMA((1,)),
        ],
        compiler_params=params(16),
        cost_estimate=cost(4 * 10**9, 4 * MIB),
        name="base",
    )(*pinned(pltpu.HBM, hot, edge_latent, w_edge1), *pinned(pltpu.VMEM, moved))

    by_inner = mix([kept, to_core(sent)], inner, outer)
    by_inner = [by_inner[0]] + [to_inner(by_inner[k], k) for k in range(1, inner)]
    by_outer = mix(by_inner, outer, 1)
    slot_blocks = [by_outer[0]] + [to_outer(by_outer[k], k) for k in range(1, outer)]

    grad_rows = 3 * width + hidden_width
    chunk = grad_rows // band_count
    group = (inner * chunk, hidden_width)
    mesh_out, d_slots, *sides = pl.pallas_call(
        functools.partial(main_kernel, lines, sizes),
        out_shape=[
            jax.ShapeDtypeStruct((mesh_rows, width), BF16),
            jax.ShapeDtypeStruct((halfway, width), BF16),
        ]
        + [jax.ShapeDtypeStruct((group[0] + inner * cap, hidden_width), BF16)] * outer
        + [jax.ShapeDtypeStruct(group, F32)] * outer,
        in_specs=specs(pltpu.HBM, 11) + specs(pltpu.VMEM, 1 + outer),
        out_specs=specs(pltpu.VMEM, 2 + 2 * outer),
        scratch_shapes=[
            pltpu.VMEM((edges, hidden_width), F32),
            pltpu.VMEM((edges, hidden_width), BF16),
            pltpu.VMEM((slot_rows + mesh_rows, edges), BF16),
            pltpu.VMEM((grad_rows, hidden_width), F32),
            pltpu.VMEM((slot_rows, width), F32),
            pltpu.VMEM((slot_rows, width), F32),
            pltpu.VMEM(slot_index.shape, jnp.int32),
            pltpu.VMEM(dst_index.shape, jnp.int32),
            pltpu.VMEM(mesh_latent.shape, BF16),
            pltpu.VMEM((width, hidden_width), BF16),
            pltpu.VMEM(w_edge2.shape, BF16),
            pltpu.VMEM((w_node1.shape[0] - width, w_node1.shape[1]), BF16),
            pltpu.VMEM(w_node2.shape, BF16),
            pltpu.VMEM(turned.shape, BF16),
            pltpu.VMEM(hot.shape, BF16),
            pltpu.VMEM(node.shape, F32),
            pltpu.VMEM(cot.shape, F32),
            pltpu.SemaphoreType.DMA((11,)),
        ],
        compiler_params=params(40),
        name="edges",
    )(
        *pinned(pltpu.HBM, slot_index, dst_index, mesh_latent, w_edge1, w_edge2, w_node1, w_node2),
        *pinned(pltpu.HBM, turned, hot, node, cot),
        *pinned(pltpu.VMEM, base),
        *slot_blocks,
    )
    sends, keeps = sides[:outer], sides[outer:]
    small = (2 * cap, width)
    arrived = []
    first = None
    for k in range(outer - 1, -1, -1):
        send = sends[k] if first is None else lax.optimization_barrier((sends[k], first))[0]
        crossed = to_core(send)
        first = crossed if first is None else first
        total, mixed, *parts = pl.pallas_call(
            functools.partial(core_kernel, sizes, k),
            out_shape=[
                jax.ShapeDtypeStruct((chunk, hidden_width), F32),
                jax.ShapeDtypeStruct(small, BF16),
            ]
            + [jax.ShapeDtypeStruct((chunk + 2 * cap, width), BF16)] * (inner - 1),
            compiler_params=params(16),
            cost_estimate=cost(10**9, MIB),
            name="core",
        )(keeps[k], crossed, d_slots)
        parts = [to_inner(part, at + 1) for at, part in enumerate(parts)]
        block = 2 * inner * cap
        if k:
            (out,) = pl.pallas_call(
                functools.partial(inner_kernel, inner - 1, 0),
                out_shape=[jax.ShapeDtypeStruct((chunk + block, width), BF16)],
                compiler_params=params(16),
                name="inner",
            )(total, mixed, *parts)
            arrived.append(to_outer(out, k))
        else:
            own, home = pl.pallas_call(
                functools.partial(inner_kernel, inner - 1, outer - 1),
                out_shape=[
                    jax.ShapeDtypeStruct((chunk, hidden_width), BF16),
                    jax.ShapeDtypeStruct((block, width), BF16),
                ],
                compiler_params=params(16),
                name="own",
            )(total, mixed, *parts, *arrived)

    pieces = {0: own}
    stride = outer // 2
    while stride:
        for at in range(0, outer, 2 * stride):
            pieces[at + stride] = to_outer(pieces[at], stride)
        stride //= 2
    for far_inner in range(1, inner):
        for far_outer in range(outer):
            pieces[far_inner * outer + far_outer] = to_inner(pieces[far_outer], far_inner)
    for at in range(band_count // 2):
        pieces[band_count // 2 + at] = to_core(pieces[at])

    grid_grad = pl.pallas_call(
        functools.partial(put_kernel, sizes),
        out_shape=jax.ShapeDtypeStruct(grid_latent.shape, F32),
        in_specs=specs(pltpu.HBM, 1) + specs(pltpu.VMEM, outer),
        out_specs=pl.BlockSpec(memory_space=pltpu.VMEM),
        scratch_shapes=[
            pltpu.VMEM((slot_rows, width), F32),
            pltpu.VMEM(send_rows.shape, jnp.int32),
            pltpu.SemaphoreType.DMA((1,)),
        ],
        compiler_params=params(16),
        cost_estimate=cost(2 * 10**9, 2 * MIB),
        name="put",
    )(*pinned(pltpu.HBM, send_rows), home, *arrived[::-1])

    late = [at for at in range(band_count) if at % outer == outer - 1]
    early = [at for at in range(band_count) if at % outer != outer - 1]
    grads = []
    for places in (early, late):
        grads = pl.pallas_call(
            functools.partial(order_kernel, sizes, places, len(grads)),
            out_shape=[
                jax.ShapeDtypeStruct((3 * width, hidden_width), F32),
                jax.ShapeDtypeStruct((hidden_width, width), F32),
            ],
            in_specs=specs(pltpu.VMEM, len(places)) + specs(pltpu.HBM, len(grads)),
            out_specs=specs(pltpu.HBM, 2),
            scratch_shapes=[
                pltpu.VMEM((len(places), chunk, hidden_width), F32),
                pltpu.SemaphoreType.DMA((len(places),)),
            ],
            input_output_aliases={len(places) + k: k for k in range(len(grads))},
            compiler_params=params(16),
            cost_estimate=cost(15 * 10**7 * len(places), 2 * MIB),
            name="order",
        )(*[pieces[at] for at in places], *grads)
    grad_edge1, grad_edge2 = grads
    return (mesh_out, grid_grad, grad_edge1, grad_edge2)


def solution(mesh):
    chips = mesh.shape["band"] // 2
    inner = 1
    while inner * inner * 4 <= chips:
        inner *= 2
    sizes = (chips // inner, inner)
    in_specs = (
        P(("groups", "band"), None),
        P(("groups", "band"), None),
        P(("groups", "band"), None),
        P(("groups", "band"), None),
        P("band", None),
        P("band"),
        P("band"),
        P(),
        P(),
        P(),
        P(),
    )
    out_specs = (
        P(("groups", "band"), None),
        P(("groups", "band"), None),
        P("groups", None),
        P("groups", None),
    )
    return jax.shard_map(
        functools.partial(shards, sizes), mesh=mesh, in_specs=in_specs, out_specs=out_specs, check_vma=False
    )
```

time: 88.6 us -> 76.6 us (0.86)
  waiting for transfers between devices: 42.3 us -> 27.6 us
  Pallas kernels: 20.8 us -> 22.8 us
  starting transfers between devices: 23.8 us -> 25 us
    ppermute x23 -> x31, waiting for transfers between devices: 39.6 us -> 27.6 us  [permute(): return lax.ppermute(value, 'band', pairs)]
    ppermute x23 -> x31, starting transfers between devices: 16.4 us -> 25 us  [permute(): return lax.ppermute(value, 'band', pairs)]
    all_to_all x1 -> x0, starting transfers between devices: 7.4 us -> none  [shards(): lax.all_to_all(outgoing.reshape(band_count, -1, width), 'band', split_axi...]
    all_to_all x1 -> x0, waiting for transfers between devices: 2.73 us -> none  [shards(): lax.all_to_all(outgoing.reshape(band_count, -1, width), 'band', split_axi...]
    pallas_call x2 -> x12, Pallas kernels: 2.36 us -> 5.07 us  [the longest x1 3.12 us: shards(): pl.pallas_call(functools.partial(ready_kernel, lines), out_shape=[pltpu.H...]
  transfers between devices with their start and end apart: 24 -> 31, of which waited for: 10 -> 15; matrix products, arithmetic and copies ran while one was open for 0% -> 0% of each run, Pallas kernels for 11% -> 16%
where the time goes in v6:
time: 76.6 us; the launch traced here: 76.3 us
  waiting for transfers between devices  27.6 us (36%)
  starting transfers between devices  25 us (33%)
  Pallas kernels  22.8 us (30%)
  between operations  0.84 us (1%)
    ppermute x31, waiting for transfers between devices, permute(): return lax.ppermute(value, 'band', pairs)  27.6 us
    ppermute x31, starting transfers between devices, permute(): return lax.ppermute(value, 'band', pairs)  25 us
    pallas_call x1, Pallas kernels, shards(): pl.pallas_call(functools.partial(main_kernel, lines, sizes), out_shape=[j...  8.07 us
    pallas_call x1, Pallas kernels, shards(): pl.pallas_call(functools.partial(base_kernel, lines), out_shape=[pltpu.VM...  4.45 us
    pallas_call x1, Pallas kernels, shards(): pl.pallas_call(functools.partial(ready_kernel, lines), out_shape=[pltpu.H...  3.12 us
    pallas_call x2, Pallas kernels, shards(): pl.pallas_call(functools.partial(order_kernel, sizes, places, len(grads))...  2.81 us
    pallas_call x1, Pallas kernels, shards(): pl.pallas_call(functools.partial(put_kernel, sizes), out_shape=jax.ShapeD...  2.4 us
    pallas_call x1, Pallas kernels, shards(): pl.pallas_call(functools.partial(pick_kernel, sizes), out_shape=[jax.Shap...  1.59 us
  transfers between devices with their start and end apart: 31, of which 15 were waited for; matrix products, arithmetic and copies ran while one was open for 0% of the time, Pallas kernels for 16%

profile of v6, /device:TPU:0, one launch (start us, length us, event | category | flops | bytes accessed | tf_op | source)
XLA Modules:
  0.0 76.3 jit_solution(16329138597466954914)
XLA Ops:
  0.6 1.6 %pick.1 = (bf16[64,512]{1,0:T(8,128)(2,1)S(1)}, bf16[64,512]{1,0:T(8,128)(2,1)S(1)}) custom-call(s32[1,128]{1,0:T(1,128)} %rows_hbm.3, bf16[1024,512]{1,0:T(8,128)(2,1)} %grid_hbm.1), custom_call_target="tpu_custom_call" | custom-call | tf_op jit(solution)/shard_map/pick/pallas_call | solution.py:443
  3.7 2.9 %collective-permute-start.1 = (bf16[64,512]{1,0:T(8,128)(2,1)S(1)}, bf16[64,512]{1,0:T(8,128)(2,1)S(1)}, u32[]{:S(2)}, u32[]{:S(2)}) collective-permute-start(bf16[64,512]{1,0:T(8,128)(2,1)S(1)} %get-tuple-element.58), channel_id=1, source_target_pairs={{0,2},{1,3},{2,0},{3,1},{4,6},{5,7},{6,4},{7,5},{8,10},{9,11},{10,... | collective-permute-start | bytes 196616 | tf_op jit(solution)/shard_map/ppermute | solution.py:431
  6.6 3.1 %ready.1 = (bf16[1536,256]{1,0:T(8,128)(2,1)}, f32[256,512]{1,0:T(8,128)}, f32[256,512]{1,0:T(8,128)}, bf16[256,512]{1,0:T(8,128)(2,1)S(1)}) custom-call(s32[12,128]{1,0:T(8,128)} %bitcast.3, bf16[256,512]{1,0:T(8,128)(2,1)} %mesh_hbm.3, bf16[256,512]{1,0:T(8,128)(2,1)} %cot_hbm.1, bf16[1536,512]{1,0:T(8,128)(2,1)} %w1_hbm.5, bf16[1024,512]{1,0:T(8,128)(2,1)} %wn1_hbm.3, ...), custom_call_target="tpu_custom_call" | custom-call | flops 2000000000 | bytes 4194304 | tf_op jit(solution)/shard_map/ready/pallas_call | solution.py:467
  9.8 1.6 %collective-permute-start.2 = (bf16[32,512]{1,0:T(8,128)(2,1)S(1)}, bf16[32,512]{1,0:T(8,128)(2,1)S(1)}, u32[]{:S(2)}, u32[]{:S(2)}) collective-permute-start(bf16[32,512]{1,0:T(8,128)(2,1)S(1)} %get-tuple-element.60), channel_id=1, source_target_pairs={{0,4},{1,5},{2,6},{3,7},{4,0},{5,1},{6,2},{7,3},{8,12},{9,13},{10,... | collective-permute-start | bytes 98312 | tf_op jit(solution)/shard_map/ppermute | solution.py:431
  11.4 2.6 %collective-permute-start.3 = (bf16[32,512]{1,0:T(8,128)(2,1)S(1)}, bf16[32,512]{1,0:T(8,128)(2,1)S(1)}, u32[]{:S(2)}, u32[]{:S(2)}) collective-permute-start(bf16[32,512]{1,0:T(8,128)(2,1)S(1)} %get-tuple-element.61), channel_id=1, source_target_pairs={{0,8},{1,9},{2,10},{3,11},{4,12},{5,13},{6,14},{7,15},{8,0},{9,1},... | collective-permute-start | bytes 98312 | tf_op jit(solution)/shard_map/ppermute | solution.py:431
  14.2 4.5 %base.1 = (f32[1536,512]{1,0:T(8,128)S(1)}, bf16[512,1536]{1,0:T(8,128)(2,1)}) custom-call(bf16[1536,256]{1,0:T(8,128)(2,1)} %get-tuple-element.49.hot_hbm, bf16[1536,512]{1,0:T(8,128)(2,1)} %edge_hbm.1, bf16[1536,512]{1,0:T(8,128)(2,1)} %w1_hbm.5, bf16[256,512]{1,0:T(8,128)(2,1)S(1)} %get-tuple-element.50.moved_ref), custom_call_target="tpu_custom_call" | custom-call | flops 4000000000 | bytes 4194304 | tf_op jit(solution)/shard_map/base/pallas_call | solution.py:494
  19.7 8.1 %edges.1 = (bf16[256,512]{1,0:T(8,128)(2,1)}, bf16[64,512]{1,0:T(8,128)(2,1)S(1)}, bf16[272,512]{1,0:T(8,128)(2,1)S(1)}, bf16[272,512]{1,0:T(8,128)(2,1)S(1)}, b...) custom-call(s32[12,128]{1,0:T(8,128)} %bitcast.2, ...), custom_call_target="tpu_custom_call" | custom-call | tf_op jit(solution)/shard_map/edges/pallas_call | solution.py:523
  27.9 1.5 %collective-permute-done.5.crossed_ref = bf16[272,512]{1,0:T(8,128)(2,1)S(1)} collective-permute-done((bf16[272,512]{1,0:T(8,128)(2,1)S(1)}, bf16[272,512]{1,0:T(8,128)(2,1)S(1)}, u32[]{:S(2)}, u32[]{:S(2)}) %collective-permute-start.5) | collective-permute-done | bytes 278560 | tf_op jit(solution)/shard_map/ppermute | solution.py:431
  30.0 1.2 %collective-permute-start.8 = (bf16[144,512]{1,0:T(8,128)(2,1)S(1)}, bf16[144,512]{1,0:T(8,128)(2,1)S(1)}, u32[]{:S(2)}, u32[]{:S(2)}) collective-permute-start(bf16[144,512]{1,0:T(8,128)(2,1)S(1)} %get-tuple-element.75), channel_id=1, source_target_pairs={{0,2},{1,3},{2,0},{3,1},{4,6},{5,7},{6,4},{7,5},{8,10},{9,11},{10,... | collective-permute-start | bytes 442376 | tf_op jit(solution)/shard_map/ppermute | solution.py:431
  33.4 3.3 %collective-permute-done.8.refs_0_ = bf16[144,512]{1,0:T(8,128)(2,1)S(1)} collective-permute-done((bf16[144,512]{1,0:T(8,128)(2,1)S(1)}, bf16[144,512]{1,0:T(8,128)(2,1)S(1)}, u32[]{:S(2)}, u32[]{:S(2)}) %collective-permute-start.8) | collective-permute-done | bytes 147488 | tf_op jit(solution)/shard_map/ppermute | solution.py:431
  36.8 2.7 %collective-permute-start.9 = (bf16[160,512]{1,0:T(8,128)(2,1)S(1)}, bf16[160,512]{1,0:T(8,128)(2,1)S(1)}, u32[]{:S(2)}, u32[]{:S(2)}) collective-permute-start(bf16[160,512]{1,0:T(8,128)(2,1)S(1)} %inner.3), channel_id=1, source_target_pairs={{0,12},{1,13},{2,14},{3,15},{4,8},{5,9},{6,10},{7,11},{8,4},{9,5},... | collective-permute-start | bytes 491528 | tf_op jit(solution)/shard_map/ppermute | solution.py:431
  40.0 2.3 %collective-permute-done.11.refs_0_ = bf16[144,512]{1,0:T(8,128)(2,1)S(1)} collective-permute-done((bf16[144,512]{1,0:T(8,128)(2,1)S(1)}, bf16[144,512]{1,0:T(8,128)(2,1)S(1)}, u32[]{:S(2)}, u32[]{:S(2)}) %collective-permute-start.11) | collective-permute-done | bytes 147488 | tf_op jit(solution)/shard_map/ppermute | solution.py:431
  43.3 1.2 %collective-permute-start.7 = (bf16[144,512]{1,0:T(8,128)(2,1)S(1)}, bf16[144,512]{1,0:T(8,128)(2,1)S(1)}, u32[]{:S(2)}, u32[]{:S(2)}) collective-permute-start(bf16[144,512]{1,0:T(8,128)(2,1)S(1)} %get-tuple-element.71), channel_id=1, source_target_pairs={{0,2},{1,3},{2,0},{3,1},{4,6},{5,7},{6,4},{7,5},{8,10},{9,11},{10,... | collective-permute-start | bytes 442376 | tf_op jit(solution)/shard_map/ppermute | solution.py:431
  44.5 1.3 %collective-permute-done.9.refs_1_.refs_3_ = bf16[160,512]{1,0:T(8,128)(2,1)S(1)} collective-permute-done((bf16[160,512]{1,0:T(8,128)(2,1)S(1)}, bf16[160,512]{1,0:T(8,128)(2,1)S(1)}, u32[]{:S(2)}, u32[]{:S(2)}) %collective-permute-start.9) | collective-permute-done | bytes 163872 | tf_op jit(solution)/shard_map/ppermute | solution.py:431
  45.8 2.7 %collective-permute-done.7.refs_0_ = bf16[144,512]{1,0:T(8,128)(2,1)S(1)} collective-permute-done((bf16[144,512]{1,0:T(8,128)(2,1)S(1)}, bf16[144,512]{1,0:T(8,128)(2,1)S(1)}, u32[]{:S(2)}, u32[]{:S(2)}) %collective-permute-start.7) | collective-permute-done | bytes 147488 | tf_op jit(solution)/shard_map/ppermute | solution.py:431
  48.5 3.9 %collective-permute-done.12.refs_2_ = bf16[160,512]{1,0:T(8,128)(2,1)S(1)} collective-permute-done((bf16[160,512]{1,0:T(8,128)(2,1)S(1)}, bf16[160,512]{1,0:T(8,128)(2,1)S(1)}, u32[]{:S(2)}, u32[]{:S(2)}) %collective-permute-start.12) | collective-permute-done | bytes 163872 | tf_op jit(solution)/shard_map/ppermute | solution.py:431
  52.6 2.8 %collective-permute-start.16 = (bf16[128,512]{1,0:T(8,128)(2,1)S(1)}, bf16[128,512]{1,0:T(8,128)(2,1)S(1)}, u32[]{:S(2)}, u32[]{:S(2)}) collective-permute-start(bf16[128,512]{1,0:T(8,128)(2,1)S(1)} %get-tuple-element.89.refs_0_), channel_id=1, source_target_pairs={{0,8},{1,9},{2,10},{3,11},{4,12},{5,13},{6,14},{7,15},{8,0},{9,1},... | collective-permute-start | bytes 393224 | tf_op jit(solution)/shard_map/ppermute | solution.py:431
  56.5 3.4 %collective-permute-done.21.refs_1_ = bf16[128,512]{1,0:T(8,128)(2,1)S(1)} collective-permute-done((bf16[128,512]{1,0:T(8,128)(2,1)S(1)}, bf16[128,512]{1,0:T(8,128)(2,1)S(1)}, u32[]{:S(2)}, u32[]{:S(2)}) %collective-permute-start.21) | collective-permute-done | bytes 131104 | tf_op jit(solution)/shard_map/ppermute | solution.py:431
  63.0 2.1 %collective-permute-done.23.refs_4_ = bf16[128,512]{1,0:T(8,128)(2,1)S(1)} collective-permute-done((bf16[128,512]{1,0:T(8,128)(2,1)S(1)}, bf16[128,512]{1,0:T(8,128)(2,1)S(1)}, u32[]{:S(2)}, u32[]{:S(2)}) %collective-permute-start.23) | collective-permute-done | bytes 131104 | tf_op jit(solution)/shard_map/ppermute | solution.py:431
  65.0 1.4 %collective-permute-done.24.refs_5_ = bf16[128,512]{1,0:T(8,128)(2,1)S(1)} collective-permute-done((bf16[128,512]{1,0:T(8,128)(2,1)S(1)}, bf16[128,512]{1,0:T(8,128)(2,1)S(1)}, u32[]{:S(2)}, u32[]{:S(2)}) %collective-permute-start.24) | collective-permute-done | bytes 131104 | tf_op jit(solution)/shard_map/ppermute | solution.py:431
  66.9 1.4 %collective-permute-done.17.refs_0_ = bf16[128,512]{1,0:T(8,128)(2,1)S(1)} collective-permute-done((bf16[128,512]{1,0:T(8,128)(2,1)S(1)}, bf16[128,512]{1,0:T(8,128)(2,1)S(1)}, u32[]{:S(2)}, u32[]{:S(2)}) %collective-permute-start.17) | collective-permute-done | bytes 131104 | tf_op jit(solution)/shard_map/ppermute | solution.py:431
  69.2 2.4 %put.1 = f32[1024,512]{1,0:T(8,128)} custom-call(s32[1,128]{1,0:T(1,128)} %rows_hbm.3, bf16[32,512]{1,0:T(8,128)(2,1)S(1)} %get-tuple-element.88.refs_0_, bf16[160,512]{1,0:T(8,128)(2,1)S(1)} %collective-permute-done.15.refs_3_.refs_1_, bf16[160,512]{1,0:T(8,128)(2,1)S(1)} %collective-permute-done.12.refs_2_, ...), custom_call_target="tpu_custom_call" | custom-call | flops 2000000000 | bytes 2097152 | tf_op jit(solution)/shard_map/put/pallas_call | solution.py:613
  71.7 1.7 %collective-permute-done.18.refs_1_ = bf16[128,512]{1,0:T(8,128)(2,1)S(1)} collective-permute-done((bf16[128,512]{1,0:T(8,128)(2,1)S(1)}, bf16[128,512]{1,0:T(8,128)(2,1)S(1)}, u32[]{:S(2)}, u32[]{:S(2)}) %collective-permute-start.18) | collective-permute-done | bytes 131104 | tf_op jit(solution)/shard_map/ppermute | solution.py:431
  73.4 1.8 %order.2 = (f32[1536,512]{1,0:T(8,128)}, f32[512,512]{1,0:T(8,128)}) custom-call(bf16[128,512]{1,0:T(8,128)(2,1)S(1)} %get-tuple-element.89.refs_0_, bf16[128,512]{1,0:T(8,128)(2,1)S(1)} %collective-permute-done.21.refs_1_, bf16[128,512]{1,0:T(8,128)(2,1)S(1)} %collective-permute-done.16.refs_2_, bf16[128,512]{1,0:T(8,128)(2,1)S(1)} %collective-permute-done.22.refs_3_, ...), custom_call_target="tpu_custom_call" | custom-call | flops 1800000000 | bytes 2097152 | tf_op jit(solution)/shard_map/order/pallas_call | solution.py:632
  (55 shorter events, 14.1 us)
Async XLA Ops:
  3.7 6.1 %collective-permute-start.1 = (bf16[64,512]{1,0:T(8,128)(2,1)S(1)}, bf16[64,512]{1,0:T(8,128)(2,1)S(1)}, u32[]{:S(2)}, u32[]{:S(2)}) collective-permute-start(bf16[64,512]{1,0:T(8,128)(2,1)S(1)} %get-tuple-element.58), channel_id=1, source_target_pairs={{0,2},{1,3},{2,0},{3,1},{4,6},{5,7},{6,4},{7,5},{8,10},{9,11},{10,... | collective-permute-start | bytes 196616 | tf_op jit(solution)/shard_map/ppermute | solution.py:431
  9.8 8.9 %collective-permute-start.2 = (bf16[32,512]{1,0:T(8,128)(2,1)S(1)}, bf16[32,512]{1,0:T(8,128)(2,1)S(1)}, u32[]{:S(2)}, u32[]{:S(2)}) collective-permute-start(bf16[32,512]{1,0:T(8,128)(2,1)S(1)} %get-tuple-element.60), channel_id=1, source_target_pairs={{0,4},{1,5},{2,6},{3,7},{4,0},{5,1},{6,2},{7,3},{8,12},{9,13},{10,... | collective-permute-start | bytes 98312 | tf_op jit(solution)/shard_map/ppermute | solution.py:431
  11.4 7.3 %collective-permute-start.3 = (bf16[32,512]{1,0:T(8,128)(2,1)S(1)}, bf16[32,512]{1,0:T(8,128)(2,1)S(1)}, u32[]{:S(2)}, u32[]{:S(2)}) collective-permute-start(bf16[32,512]{1,0:T(8,128)(2,1)S(1)} %get-tuple-element.61), channel_id=1, source_target_pairs={{0,8},{1,9},{2,10},{3,11},{4,12},{5,13},{6,14},{7,15},{8,0},{9,1},... | collective-permute-start | bytes 98312 | tf_op jit(solution)/shard_map/ppermute | solution.py:431
  14.0 5.7 %collective-permute-start.4 = (bf16[32,512]{1,0:T(8,128)(2,1)S(1)}, bf16[32,512]{1,0:T(8,128)(2,1)S(1)}, u32[]{:S(2)}, u32[]{:S(2)}) collective-permute-start(bf16[32,512]{1,0:T(8,128)(2,1)S(1)} %get-tuple-element.62), channel_id=1, source_target_pairs={{0,12},{1,13},{2,14},{3,15},{4,8},{5,9},{6,10},{7,11},{8,4},{9,5},... | collective-permute-start | bytes 98312 | tf_op jit(solution)/shard_map/ppermute | solution.py:431
  30.0 6.8 %collective-permute-start.8 = (bf16[144,512]{1,0:T(8,128)(2,1)S(1)}, bf16[144,512]{1,0:T(8,128)(2,1)S(1)}, u32[]{:S(2)}, u32[]{:S(2)}) collective-permute-start(bf16[144,512]{1,0:T(8,128)(2,1)S(1)} %get-tuple-element.75), channel_id=1, source_target_pairs={{0,2},{1,3},{2,0},{3,1},{4,6},{5,7},{6,4},{7,5},{8,10},{9,11},{10,... | collective-permute-start | bytes 442376 | tf_op jit(solution)/shard_map/ppermute | solution.py:431
  31.1 12.1 %collective-permute-start.6 = (bf16[272,512]{1,0:T(8,128)(2,1)S(1)}, bf16[272,512]{1,0:T(8,128)(2,1)S(1)}, u32[]{:S(2)}, u32[]{:S(2)}) collective-permute-start(bf16[272,512]{1,0:T(8,128)(2,1)S(1)} %get-tuple-element.67), channel_id=1, source_target_pairs={{0,1},{1,0},{2,3},{3,2},{4,5},{5,4},{6,7},{7,6},{8,9},{9,8},{10,11... | collective-permute-start | bytes 835592 | tf_op jit(solution)/shard_map/ppermute | solution.py:431
  31.2 8.7 %collective-permute-start.14 = (bf16[144,512]{1,0:T(8,128)(2,1)S(1)}, bf16[144,512]{1,0:T(8,128)(2,1)S(1)}, u32[]{:S(2)}, u32[]{:S(2)}) collective-permute-start(bf16[144,512]{1,0:T(8,128)(2,1)S(1)} %get-tuple-element.87), channel_id=1, source_target_pairs={{0,2},{1,3},{2,0},{3,1},{4,6},{5,7},{6,4},{7,5},{8,10},{9,11},{10,... | collective-permute-start | bytes 442376 | tf_op jit(solution)/shard_map/ppermute | solution.py:431
  32.2 10.0 %collective-permute-start.11 = (bf16[144,512]{1,0:T(8,128)(2,1)S(1)}, bf16[144,512]{1,0:T(8,128)(2,1)S(1)}, u32[]{:S(2)}, u32[]{:S(2)}) collective-permute-start(bf16[144,512]{1,0:T(8,128)(2,1)S(1)} %get-tuple-element.81), channel_id=1, source_target_pairs={{0,2},{1,3},{2,0},{3,1},{4,6},{5,7},{6,4},{7,5},{8,10},{9,11},{10,... | collective-permute-start | bytes 442376 | tf_op jit(solution)/shard_map/ppermute | solution.py:431
  36.8 9.0 %collective-permute-start.9 = (bf16[160,512]{1,0:T(8,128)(2,1)S(1)}, bf16[160,512]{1,0:T(8,128)(2,1)S(1)}, u32[]{:S(2)}, u32[]{:S(2)}) collective-permute-start(bf16[160,512]{1,0:T(8,128)(2,1)S(1)} %inner.3), channel_id=1, source_target_pairs={{0,12},{1,13},{2,14},{3,15},{4,8},{5,9},{6,10},{7,11},{8,4},{9,5},... | collective-permute-start | bytes 491528 | tf_op jit(solution)/shard_map/ppermute | solution.py:431
  39.9 8.6 %collective-permute-start.15 = (bf16[160,512]{1,0:T(8,128)(2,1)S(1)}, bf16[160,512]{1,0:T(8,128)(2,1)S(1)}, u32[]{:S(2)}, u32[]{:S(2)}) collective-permute-start(bf16[160,512]{1,0:T(8,128)(2,1)S(1)} %inner.5), channel_id=1, source_target_pairs={{0,4},{1,5},{2,6},{3,7},{4,0},{5,1},{6,2},{7,3},{8,12},{9,13},{10,... | collective-permute-start | bytes 491528 | tf_op jit(solution)/shard_map/ppermute | solution.py:431
  42.3 10.2 %collective-permute-start.12 = (bf16[160,512]{1,0:T(8,128)(2,1)S(1)}, bf16[160,512]{1,0:T(8,128)(2,1)S(1)}, u32[]{:S(2)}, u32[]{:S(2)}) collective-permute-start(bf16[160,512]{1,0:T(8,128)(2,1)S(1)} %inner.4), channel_id=1, source_target_pairs={{0,8},{1,9},{2,10},{3,11},{4,12},{5,13},{6,14},{7,15},{8,0},{9,1},... | collective-permute-start | bytes 491528 | tf_op jit(solution)/shard_map/ppermute | solution.py:431
  43.3 5.2 %collective-permute-start.7 = (bf16[144,512]{1,0:T(8,128)(2,1)S(1)}, bf16[144,512]{1,0:T(8,128)(2,1)S(1)}, u32[]{:S(2)}, u32[]{:S(2)}) collective-permute-start(bf16[144,512]{1,0:T(8,128)(2,1)S(1)} %get-tuple-element.71), channel_id=1, source_target_pairs={{0,2},{1,3},{2,0},{3,1},{4,6},{5,7},{6,4},{7,5},{8,10},{9,11},{10,... | collective-permute-start | bytes 442376 | tf_op jit(solution)/shard_map/ppermute | solution.py:431
  52.5 7.4 %collective-permute-start.21 = (bf16[128,512]{1,0:T(8,128)(2,1)S(1)}, bf16[128,512]{1,0:T(8,128)(2,1)S(1)}, u32[]{:S(2)}, u32[]{:S(2)}) collective-permute-start(bf16[128,512]{1,0:T(8,128)(2,1)S(1)} %get-tuple-element.89.refs_0_), channel_id=1, source_target_pairs={{0,4},{1,5},{2,6},{3,7},{4,0},{5,1},{6,2},{7,3},{8,12},{9,13},{10,... | collective-permute-start | bytes 393224 | tf_op jit(solution)/shard_map/ppermute | solution.py:431
  52.6 8.7 %collective-permute-start.16 = (bf16[128,512]{1,0:T(8,128)(2,1)S(1)}, bf16[128,512]{1,0:T(8,128)(2,1)S(1)}, u32[]{:S(2)}, u32[]{:S(2)}) collective-permute-start(bf16[128,512]{1,0:T(8,128)(2,1)S(1)} %get-tuple-element.89.refs_0_), channel_id=1, source_target_pairs={{0,8},{1,9},{2,10},{3,11},{4,12},{5,13},{6,14},{7,15},{8,0},{9,1},... | collective-permute-start | bytes 393224 | tf_op jit(solution)/shard_map/ppermute | solution.py:431
  55.4 7.0 %collective-permute-start.22 = (bf16[128,512]{1,0:T(8,128)(2,1)S(1)}, bf16[128,512]{1,0:T(8,128)(2,1)S(1)}, u32[]{:S(2)}, u32[]{:S(2)}) collective-permute-start(bf16[128,512]{1,0:T(8,128)(2,1)S(1)} %get-tuple-element.89.refs_0_), channel_id=1, source_target_pairs={{0,2},{1,3},{2,0},{3,1},{4,6},{5,7},{6,4},{7,5},{8,10},{9,11},{10,... | collective-permute-start | bytes 393224 | tf_op jit(solution)/shard_map/ppermute | solution.py:431
  56.5 6.1 %collective-permute-start.25 = (bf16[128,512]{1,0:T(8,128)(2,1)S(1)}, bf16[128,512]{1,0:T(8,128)(2,1)S(1)}, u32[]{:S(2)}, u32[]{:S(2)}) collective-permute-start(bf16[128,512]{1,0:T(8,128)(2,1)S(1)} %get-tuple-element.89.refs_0_), channel_id=1, source_target_pairs={{0,1},{1,0},{2,3},{3,2},{4,5},{5,4},{6,7},{7,6},{8,9},{9,8},{10,11... | collective-permute-start | bytes 393224 | tf_op jit(solution)/shard_map/ppermute | solution.py:431
  59.9 5.1 %collective-permute-start.23 = (bf16[128,512]{1,0:T(8,128)(2,1)S(1)}, bf16[128,512]{1,0:T(8,128)(2,1)S(1)}, u32[]{:S(2)}, u32[]{:S(2)}) collective-permute-start(bf16[128,512]{1,0:T(8,128)(2,1)S(1)} %collective-permute-done.21.refs_1_), channel_id=1, source_target_pairs={{0,2},{1,3},{2,0},{3,1},{4,6},{5,7},{6,4},{7,5},{8,10},{9,11},{10,... | collective-permute-start | bytes 393224 | tf_op jit(solution)/shard_map/ppermute | solution.py:431
  61.3 5.2 %collective-permute-start.24 = (bf16[128,512]{1,0:T(8,128)(2,1)S(1)}, bf16[128,512]{1,0:T(8,128)(2,1)S(1)}, u32[]{:S(2)}, u32[]{:S(2)}) collective-permute-start(bf16[128,512]{1,0:T(8,128)(2,1)S(1)} %collective-permute-done.16.refs_2_), channel_id=1, source_target_pairs={{0,2},{1,3},{2,0},{3,1},{4,6},{5,7},{6,4},{7,5},{8,10},{9,11},{10,... | collective-permute-start | bytes 393224 | tf_op jit(solution)/shard_map/ppermute | solution.py:431
  62.4 5.9 %collective-permute-start.17 = (bf16[128,512]{1,0:T(8,128)(2,1)S(1)}, bf16[128,512]{1,0:T(8,128)(2,1)S(1)}, u32[]{:S(2)}, u32[]{:S(2)}) collective-permute-start(bf16[128,512]{1,0:T(8,128)(2,1)S(1)} %collective-permute-done.16.refs_2_), channel_id=1, source_target_pairs={{0,4},{1,5},{2,6},{3,7},{4,0},{5,1},{6,2},{7,3},{8,12},{9,13},{10,... | collective-permute-start | bytes 393224 | tf_op jit(solution)/shard_map/ppermute | solution.py:431
  62.6 9.0 %collective-permute-start.27 = (bf16[128,512]{1,0:T(8,128)(2,1)S(1)}, bf16[128,512]{1,0:T(8,128)(2,1)S(1)}, u32[]{:S(2)}, u32[]{:S(2)}) collective-permute-start(bf16[128,512]{1,0:T(8,128)(2,1)S(1)} %collective-permute-done.16.refs_2_), channel_id=1, source_target_pairs={{0,1},{1,0},{2,3},{3,2},{4,5},{5,4},{6,7},{7,6},{8,9},{9,8},{10,11... | collective-permute-start | bytes 393224 | tf_op jit(solution)/shard_map/ppermute | solution.py:431
  65.0 8.4 %collective-permute-start.28 = (bf16[128,512]{1,0:T(8,128)(2,1)S(1)}, bf16[128,512]{1,0:T(8,128)(2,1)S(1)}, u32[]{:S(2)}, u32[]{:S(2)}) collective-permute-start(bf16[128,512]{1,0:T(8,128)(2,1)S(1)} %collective-permute-done.22.refs_3_), channel_id=1, source_target_pairs={{0,1},{1,0},{2,3},{3,2},{4,5},{5,4},{6,7},{7,6},{8,9},{9,8},{10,11... | collective-permute-start | bytes 393224 | tf_op jit(solution)/shard_map/ppermute | solution.py:431
  66.4 7.0 %collective-permute-start.29 = (bf16[128,512]{1,0:T(8,128)(2,1)S(1)}, bf16[128,512]{1,0:T(8,128)(2,1)S(1)}, u32[]{:S(2)}, u32[]{:S(2)}) collective-permute-start(bf16[128,512]{1,0:T(8,128)(2,1)S(1)} %collective-permute-done.23.refs_4_), channel_id=1, source_target_pairs={{0,1},{1,0},{2,3},{3,2},{4,5},{5,4},{6,7},{7,6},{8,9},{9,8},{10,11... | collective-permute-start | bytes 393224 | tf_op jit(solution)/shard_map/ppermute | solution.py:431
  66.4 7.0 %collective-permute-start.30 = (bf16[128,512]{1,0:T(8,128)(2,1)S(1)}, bf16[128,512]{1,0:T(8,128)(2,1)S(1)}, u32[]{:S(2)}, u32[]{:S(2)}) collective-permute-start(bf16[128,512]{1,0:T(8,128)(2,1)S(1)} %collective-permute-done.24.refs_5_), channel_id=1, source_target_pairs={{0,1},{1,0},{2,3},{3,2},{4,5},{5,4},{6,7},{7,6},{8,9},{9,8},{10,11... | collective-permute-start | bytes 393224 | tf_op jit(solution)/shard_map/ppermute | solution.py:431
  68.3 5.1 %collective-permute-start.18 = (bf16[128,512]{1,0:T(8,128)(2,1)S(1)}, bf16[128,512]{1,0:T(8,128)(2,1)S(1)}, u32[]{:S(2)}, u32[]{:S(2)}) collective-permute-start(bf16[128,512]{1,0:T(8,128)(2,1)S(1)} %collective-permute-done.17.refs_0_), channel_id=1, source_target_pairs={{0,2},{1,3},{2,0},{3,1},{4,6},{5,7},{6,4},{7,5},{8,10},{9,11},{10,... | collective-permute-start | bytes 393224 | tf_op jit(solution)/shard_map/ppermute | solution.py:431
  (7 other events, 16.9 us)

commit v7 on v6

--- a/solution.py
+++ b/solution.py
@@ -174,16 +174,25 @@
         (wn2_hbm, wn2_ref),
     ]
     copies = load(pairs, sems)
+    outs = [
+        pltpu.make_async_copy(source, target, out_sems.at[at])
+        for at, (source, target) in enumerate([(hot_ref, hot_hbm), (node_ref, node_hbm), (cot_out_ref, cot_out_hbm)])
+    ]
     copies[0].wait()
     for at in range(hot_ref.shape[0] // tile):
         hot_ref[at * tile : (at + 1) * tile, :] = tile_columns(dst_ref, at, lines, hot_ref.shape[1])
-    for copy in copies[1:]:
-        copy.wait()
+    outs[0].start()
+    copies[1].wait()
+    copies[3].wait()
+    node_ref[...] = dot_nn(mesh_ref[...], wn1_ref[...])
+    outs[1].start()
+    copies[4].wait()
+    copies[5].wait()
+    cot_out_ref[...] = dot_nt(cot_ref[...], wn2_ref[...])
+    outs[2].start()
+    copies[2].wait()
     moved_ref[...] = dot_nn(mesh_ref[...], w1_ref[...]).astype(BF16)
-    node_ref[...] = dot_nn(mesh_ref[...], wn1_ref[...])
-    cot_out_ref[...] = dot_nt(cot_ref[...], wn2_ref[...])
-    pairs = [(hot_ref, hot_hbm), (node_ref, node_hbm), (cot_out_ref, cot_out_hbm)]
-    for copy in load(pairs, out_sems):
+    for copy in outs:
         copy.wait()
 
 
@@ -242,11 +251,11 @@
 ):
     outer, inner = sizes
     slot_blocks, rest = rest[:outer], rest[outer:]
-    mesh_out_ref, d_slots_ref = rest[:2]
+    mesh_out_hbm, d_slots_ref = rest[:2]
     send_refs, keep_refs, rest = rest[2 : 2 + outer], rest[2 + outer : 2 + 2 * outer], rest[2 + 2 * outer :]
     slope_ref, value_ref, both_ref, grads_ref, slot_grads_ref, ordered_ref = rest[:6]
     slot_ref, dst_ref, mesh_ref, w1_ref, w2_ref, wn1_ref, wn2_ref = rest[6:13]
-    turned_ref, hot_ref, node_ref, cot_ref, sems = rest[13:]
+    turned_ref, hot_ref, node_ref, cot_ref, mesh_out_ref, sems, out_sems = rest[13:]
     width = mesh_ref.shape[1]
     mesh_rows = mesh_ref.shape[0]
     slot_rows = ordered_ref.shape[0]
@@ -304,6 +313,7 @@
 
     grads_ref[3 * width :, :] = dot_tn(hidden_sums, d_received)
     mesh_out_ref[...] = (mesh.astype(F32) + dot_nn(node.astype(BF16), wn2_ref[...])).astype(BF16)
+    (mesh_copy,) = load([(mesh_out_ref, mesh_out_hbm)], out_sems)
     sums = dot_nn(both_ref[...], value_ref[...]).astype(BF16)
     slot_grads_ref[...] = dot_nt(sums[:slot_rows], w1_ref[...])
     grads_ref[:width, :] = dot_tn(slots, sums[:slot_rows])
@@ -331,6 +341,7 @@
     for far_outer, send_ref in enumerate(send_refs):
         start = halfway + far_outer * share
         send_ref[inner * chunk :, :] = ordered_ref[start : start + share, :].astype(BF16)
+    mesh_copy.wait()
 
 
 def core_kernel(sizes, far_outer, keep_ref, crossed_ref, d_slots_ref, total_ref, mixed_ref, *part_refs):
@@ -529,7 +540,7 @@
         + [jax.ShapeDtypeStruct((group[0] + inner * cap, hidden_width), BF16)] * outer
         + [jax.ShapeDtypeStruct(group, F32)] * outer,
         in_specs=specs(pltpu.HBM, 11) + specs(pltpu.VMEM, 1 + outer),
-        out_specs=specs(pltpu.VMEM, 2 + 2 * outer),
+        out_specs=specs(pltpu.HBM, 1) + specs(pltpu.VMEM, 1 + 2 * outer),
         scratch_shapes=[
             pltpu.VMEM((edges, hidden_width), F32),
             pltpu.VMEM((edges, hidden_width), BF16),
@@ -548,7 +559,9 @@
             pltpu.VMEM(hot.shape, BF16),
             pltpu.VMEM(node.shape, F32),
             pltpu.VMEM(cot.shape, F32),
+            pltpu.VMEM((mesh_rows, width), BF16),
             pltpu.SemaphoreType.DMA((11,)),
+            pltpu.SemaphoreType.DMA((1,)),
         ],
         compiler_params=params(40),
         name="edges",
@@ -560,7 +573,7 @@
     )
     sends, keeps = sides[:outer], sides[outer:]
     small = (2 * cap, width)
-    arrived = []
+    arrived, before = [], []
     first = None
     for k in range(outer - 1, -1, -1):
         send = sends[k] if first is None else lax.optimization_barrier((sends[k], first))[0]
@@ -577,7 +590,9 @@
             cost_estimate=cost(10**9, MIB),
             name="core",
         )(keeps[k], crossed, d_slots)
+        parts = [lax.optimization_barrier((part, *before))[0] for part in parts]
         parts = [to_inner(part, at + 1) for at, part in enumerate(parts)]
+        before = parts if k >= outer - 2 else before
         block = 2 * inner * cap
         if k:
             (out,) = pl.pallas_call(
@@ -604,11 +619,16 @@
         for at in range(0, outer, 2 * stride):
             pieces[at + stride] = to_outer(pieces[at], stride)
         stride //= 2
+    halfway_at = band_count // 2
+    pieces[halfway_at] = to_core(own)
     for far_inner in range(1, inner):
         for far_outer in range(outer):
-            pieces[far_inner * outer + far_outer] = to_inner(pieces[far_outer], far_inner)
-    for at in range(band_count // 2):
-        pieces[band_count // 2 + at] = to_core(pieces[at])
+            value = pieces[far_outer]
+            if far_outer == outer // 2:
+                value = lax.optimization_barrier((value, pieces[halfway_at]))[0]
+            pieces[far_inner * outer + far_outer] = to_inner(value, far_inner)
+    for at in range(1, halfway_at):
+        pieces[halfway_at + at] = to_core(pieces[at])
 
     grid_grad = pl.pallas_call(
         functools.partial(put_kernel, sizes),
@@ -625,10 +645,16 @@
         name="put",
     )(*pinned(pltpu.HBM, send_rows), home, *arrived[::-1])
 
-    late = [at for at in range(band_count) if at % outer == outer - 1]
-    early = [at for at in range(band_count) if at % outer != outer - 1]
+    last = outer - 1
+    stages = [[], [], []]
+    for at in range(band_count):
+        far_outer, far_inner, far_core = at % outer, at // outer % inner, at // halfway_at
+        if far_outer == last:
+            stages[2 if far_inner else 1].append(at)
+        else:
+            stages[1 if far_inner and (far_core or far_outer == outer // 2) else 0].append(at)
     grads = []
-    for places in (early, late):
+    for places in stages:
         grads = pl.pallas_call(
             functools.partial(order_kernel, sizes, places, len(grads)),
             out_shape=[

time: 76.6 us -> 78.7 us (1.027)
  waiting for transfers between devices: 27.6 us -> 31 us
  starting transfers between devices: 25 us -> 24.2 us
    ppermute x31, waiting for transfers between devices: 27.6 us -> 31 us  [permute(): return lax.ppermute(value, 'band', pairs)]
    ppermute x31, starting transfers between devices: 25 us -> 24.2 us  [permute(): return lax.ppermute(value, 'band', pairs)]
    pallas_call x2 -> x3, Pallas kernels: 2.81 us -> 3.46 us  [shards(): pl.pallas_call(functools.partial(order_kernel, sizes, places, len(grads))...]
  transfers between devices with their start and end apart: 31 -> 31, of which waited for: 15 -> 16; matrix products, arithmetic and copies ran while one was open for 0% -> 0% of each run, Pallas kernels for 16% -> 16%
where the time goes in v7:
time: 78.7 us; the launch traced here: 78.4 us
  waiting for transfers between devices  31 us (39%)
  starting transfers between devices  24.2 us (31%)
  Pallas kernels  22.4 us (28%)
  between operations  0.84 us (1%)
    ppermute x31, waiting for transfers between devices, permute(): return lax.ppermute(value, 'band', pairs)  31 us
    ppermute x31, starting transfers between devices, permute(): return lax.ppermute(value, 'band', pairs)  24.2 us
    pallas_call x1, Pallas kernels, shards(): pl.pallas_call(functools.partial(main_kernel, lines, sizes), out_shape=[j...  7.38 us
    pallas_call x1, Pallas kernels, shards(): pl.pallas_call(functools.partial(base_kernel, lines), out_shape=[pltpu.VM...  4.45 us
    pallas_call x3, Pallas kernels, shards(): pl.pallas_call(functools.partial(order_kernel, sizes, places, len(grads))...  3.46 us
    pallas_call x1, Pallas kernels, shards(): pl.pallas_call(functools.partial(ready_kernel, lines), out_shape=[pltpu.H...  2.8 us
    pallas_call x1, Pallas kernels, shards(): pl.pallas_call(functools.partial(put_kernel, sizes), out_shape=jax.ShapeD...  2.4 us
    pallas_call x1, Pallas kernels, shards(): pl.pallas_call(functools.partial(pick_kernel, sizes), out_shape=[jax.Shap...  1.59 us
  transfers between devices with their start and end apart: 31, of which 16 were waited for; matrix products, arithmetic and copies ran while one was open for 0% of the time, Pallas kernels for 16%

profile of v7, /device:TPU:0, one launch (start us, length us, event | category | flops | bytes accessed | tf_op | source)
XLA Modules:
  0.0 78.4 jit_solution(5526420479174054917)
XLA Ops:
  0.6 1.6 %pick.1 = (bf16[64,512]{1,0:T(8,128)(2,1)S(1)}, bf16[64,512]{1,0:T(8,128)(2,1)S(1)}) custom-call(s32[1,128]{1,0:T(1,128)} %rows_hbm.3, bf16[1024,512]{1,0:T(8,128)(2,1)} %grid_hbm.1), custom_call_target="tpu_custom_call" | custom-call | tf_op jit(solution)/shard_map/pick/pallas_call | solution.py:454
  3.7 2.9 %collective-permute-start.1 = (bf16[64,512]{1,0:T(8,128)(2,1)S(1)}, bf16[64,512]{1,0:T(8,128)(2,1)S(1)}, u32[]{:S(2)}, u32[]{:S(2)}) collective-permute-start(bf16[64,512]{1,0:T(8,128)(2,1)S(1)} %get-tuple-element.64), channel_id=1, source_target_pairs={{0,2},{1,3},{2,0},{3,1},{4,6},{5,7},{6,4},{7,5},{8,10},{9,11},{10,... | collective-permute-start | bytes 196616 | tf_op jit(solution)/shard_map/ppermute | solution.py:442
  6.6 2.8 %ready.1 = (bf16[1536,256]{1,0:T(8,128)(2,1)}, f32[256,512]{1,0:T(8,128)}, f32[256,512]{1,0:T(8,128)}, bf16[256,512]{1,0:T(8,128)(2,1)S(1)}) custom-call(s32[12,128]{1,0:T(8,128)} %bitcast.3, bf16[256,512]{1,0:T(8,128)(2,1)} %mesh_hbm.3, bf16[256,512]{1,0:T(8,128)(2,1)} %cot_hbm.1, bf16[1536,512]{1,0:T(8,128)(2,1)} %w1_hbm.5, bf16[1024,512]{1,0:T(8,128)(2,1)} %wn1_hbm.3, ...), custom_call_target="tpu_custom_call" | custom-call | flops 2000000000 | bytes 4194304 | tf_op jit(solution)/shard_map/ready/pallas_call | solution.py:478
  9.4 1.6 %collective-permute-start.2 = (bf16[32,512]{1,0:T(8,128)(2,1)S(1)}, bf16[32,512]{1,0:T(8,128)(2,1)S(1)}, u32[]{:S(2)}, u32[]{:S(2)}) collective-permute-start(bf16[32,512]{1,0:T(8,128)(2,1)S(1)} %get-tuple-element.66), channel_id=1, source_target_pairs={{0,4},{1,5},{2,6},{3,7},{4,0},{5,1},{6,2},{7,3},{8,12},{9,13},{10,... | collective-permute-start | bytes 98312 | tf_op jit(solution)/shard_map/ppermute | solution.py:442
  11.1 2.6 %collective-permute-start.3 = (bf16[32,512]{1,0:T(8,128)(2,1)S(1)}, bf16[32,512]{1,0:T(8,128)(2,1)S(1)}, u32[]{:S(2)}, u32[]{:S(2)}) collective-permute-start(bf16[32,512]{1,0:T(8,128)(2,1)S(1)} %get-tuple-element.67), channel_id=1, source_target_pairs={{0,8},{1,9},{2,10},{3,11},{4,12},{5,13},{6,14},{7,15},{8,0},{9,1},... | collective-permute-start | bytes 98312 | tf_op jit(solution)/shard_map/ppermute | solution.py:442
  13.9 4.4 %base.1 = (f32[1536,512]{1,0:T(8,128)S(1)}, bf16[512,1536]{1,0:T(8,128)(2,1)}) custom-call(bf16[1536,256]{1,0:T(8,128)(2,1)} %get-tuple-element.55.hot_hbm, bf16[1536,512]{1,0:T(8,128)(2,1)} %edge_hbm.1, bf16[1536,512]{1,0:T(8,128)(2,1)} %w1_hbm.5, bf16[256,512]{1,0:T(8,128)(2,1)S(1)} %get-tuple-element.56.moved_ref), custom_call_target="tpu_custom_call" | custom-call | flops 4000000000 | bytes 4194304 | tf_op jit(solution)/shard_map/base/pallas_call | solution.py:505
  18.4 1.0 %collective-permute-done.4.rest_3_ = bf16[32,512]{1,0:T(8,128)(2,1)S(1)} collective-permute-done((bf16[32,512]{1,0:T(8,128)(2,1)S(1)}, bf16[32,512]{1,0:T(8,128)(2,1)S(1)}, u32[]{:S(2)}, u32[]{:S(2)}) %collective-permute-start.4) | collective-permute-done | bytes 32800 | tf_op jit(solution)/shard_map/ppermute | solution.py:442
  19.4 7.4 %edges.1 = (bf16[256,512]{1,0:T(8,128)(2,1)}, bf16[64,512]{1,0:T(8,128)(2,1)S(1)}, bf16[272,512]{1,0:T(8,128)(2,1)S(1)}, bf16[272,512]{1,0:T(8,128)(2,1)S(1)}, b...) custom-call(s32[12,128]{1,0:T(8,128)} %bitcast.2, ...), custom_call_target="tpu_custom_call" | custom-call | tf_op jit(solution)/shard_map/edges/pallas_call | solution.py:534
  26.8 1.5 %collective-permute-done.5.crossed_ref = bf16[272,512]{1,0:T(8,128)(2,1)S(1)} collective-permute-done((bf16[272,512]{1,0:T(8,128)(2,1)S(1)}, bf16[272,512]{1,0:T(8,128)(2,1)S(1)}, u32[]{:S(2)}, u32[]{:S(2)}) %collective-permute-start.5) | collective-permute-done | bytes 278560 | tf_op jit(solution)/shard_map/ppermute | solution.py:442
  29.0 1.5 %collective-permute-start.8 = (bf16[144,512]{1,0:T(8,128)(2,1)S(1)}, bf16[144,512]{1,0:T(8,128)(2,1)S(1)}, u32[]{:S(2)}, u32[]{:S(2)}) collective-permute-start(bf16[144,512]{1,0:T(8,128)(2,1)S(1)} %get-tuple-element.83), channel_id=1, source_target_pairs={{0,2},{1,3},{2,0},{3,1},{4,6},{5,7},{6,4},{7,5},{8,10},{9,11},{10,... | collective-permute-start | bytes 442376 | tf_op jit(solution)/shard_map/ppermute | solution.py:442
  30.5 4.4 %collective-permute-done.8.refs_0_ = bf16[144,512]{1,0:T(8,128)(2,1)S(1)} collective-permute-done((bf16[144,512]{1,0:T(8,128)(2,1)S(1)}, bf16[144,512]{1,0:T(8,128)(2,1)S(1)}, u32[]{:S(2)}, u32[]{:S(2)}) %collective-permute-start.8) | collective-permute-done | bytes 147488 | tf_op jit(solution)/shard_map/ppermute | solution.py:442
  34.9 1.4 %collective-permute-start.9 = (bf16[144,512]{1,0:T(8,128)(2,1)S(1)}, bf16[144,512]{1,0:T(8,128)(2,1)S(1)}, u32[]{:S(2)}, u32[]{:S(2)}) collective-permute-start(bf16[144,512]{1,0:T(8,128)(2,1)S(1)} %get-tuple-element.84), channel_id=1, source_target_pairs={{0,2},{1,3},{2,0},{3,1},{4,6},{5,7},{6,4},{7,5},{8,10},{9,11},{10,... | collective-permute-start | bytes 442376 | tf_op jit(solution)/shard_map/ppermute | solution.py:442
  36.4 3.6 %collective-permute-done.9.refs_0_ = bf16[144,512]{1,0:T(8,128)(2,1)S(1)} collective-permute-done((bf16[144,512]{1,0:T(8,128)(2,1)S(1)}, bf16[144,512]{1,0:T(8,128)(2,1)S(1)}, u32[]{:S(2)}, u32[]{:S(2)}) %collective-permute-start.9) | collective-permute-done | bytes 147488 | tf_op jit(solution)/shard_map/ppermute | solution.py:442
  40.1 1.4 %collective-permute-start.14 = (bf16[144,512]{1,0:T(8,128)(2,1)S(1)}, bf16[144,512]{1,0:T(8,128)(2,1)S(1)}, u32[]{:S(2)}, u32[]{:S(2)}) collective-permute-start(bf16[144,512]{1,0:T(8,128)(2,1)S(1)} %get-tuple-element.96), channel_id=1, source_target_pairs={{0,2},{1,3},{2,0},{3,1},{4,6},{5,7},{6,4},{7,5},{8,10},{9,11},{10,... | collective-permute-start | bytes 442376 | tf_op jit(solution)/shard_map/ppermute | solution.py:442
  41.5 2.7 %collective-permute-start.11 = (bf16[160,512]{1,0:T(8,128)(2,1)S(1)}, bf16[160,512]{1,0:T(8,128)(2,1)S(1)}, u32[]{:S(2)}, u32[]{:S(2)}) collective-permute-start(bf16[160,512]{1,0:T(8,128)(2,1)S(1)} %inner.3), channel_id=1, source_target_pairs={{0,12},{1,13},{2,14},{3,15},{4,8},{5,9},{6,10},{7,11},{8,4},{9,5},... | collective-permute-start | bytes 491528 | tf_op jit(solution)/shard_map/ppermute | solution.py:442
  46.9 3.6 %collective-permute-done.11.refs_1_.refs_3_ = bf16[160,512]{1,0:T(8,128)(2,1)S(1)} collective-permute-done((bf16[160,512]{1,0:T(8,128)(2,1)S(1)}, bf16[160,512]{1,0:T(8,128)(2,1)S(1)}, u32[]{:S(2)}, u32[]{:S(2)}) %collective-permute-start.11) | collective-permute-done | bytes 163872 | tf_op jit(solution)/shard_map/ppermute | solution.py:442
  51.4 4.7 %collective-permute-done.12.refs_2_ = bf16[160,512]{1,0:T(8,128)(2,1)S(1)} collective-permute-done((bf16[160,512]{1,0:T(8,128)(2,1)S(1)}, bf16[160,512]{1,0:T(8,128)(2,1)S(1)}, u32[]{:S(2)}, u32[]{:S(2)}) %collective-permute-start.12) | collective-permute-done | bytes 163872 | tf_op jit(solution)/shard_map/ppermute | solution.py:442
  56.3 3.2 %collective-permute-start.16 = (bf16[128,512]{1,0:T(8,128)(2,1)S(1)}, bf16[128,512]{1,0:T(8,128)(2,1)S(1)}, u32[]{:S(2)}, u32[]{:S(2)}) collective-permute-start(bf16[128,512]{1,0:T(8,128)(2,1)S(1)} %get-tuple-element.98.refs_0_), channel_id=1, source_target_pairs={{0,8},{1,9},{2,10},{3,11},{4,12},{5,13},{6,14},{7,15},{8,0},{9,1},... | collective-permute-start | bytes 393224 | tf_op jit(solution)/shard_map/ppermute | solution.py:442
  60.1 2.7 %collective-permute-done.25.refs_1_ = bf16[128,512]{1,0:T(8,128)(2,1)S(1)} collective-permute-done((bf16[128,512]{1,0:T(8,128)(2,1)S(1)}, bf16[128,512]{1,0:T(8,128)(2,1)S(1)}, u32[]{:S(2)}, u32[]{:S(2)}) %collective-permute-start.25) | collective-permute-done | bytes 131104 | tf_op jit(solution)/shard_map/ppermute | solution.py:442
  65.8 3.1 %collective-permute-done.26.refs_4_ = bf16[128,512]{1,0:T(8,128)(2,1)S(1)} collective-permute-done((bf16[128,512]{1,0:T(8,128)(2,1)S(1)}, bf16[128,512]{1,0:T(8,128)(2,1)S(1)}, u32[]{:S(2)}, u32[]{:S(2)}) %collective-permute-start.26) | collective-permute-done | bytes 131104 | tf_op jit(solution)/shard_map/ppermute | solution.py:442
  70.0 1.0 %collective-permute-done.21.refs_1_ = bf16[128,512]{1,0:T(8,128)(2,1)S(1)} collective-permute-done((bf16[128,512]{1,0:T(8,128)(2,1)S(1)}, bf16[128,512]{1,0:T(8,128)(2,1)S(1)}, u32[]{:S(2)}, u32[]{:S(2)}) %collective-permute-start.21) | collective-permute-done | bytes 131104 | tf_op jit(solution)/shard_map/ppermute | solution.py:442
  71.5 2.4 %put.1 = f32[1024,512]{1,0:T(8,128)} custom-call(s32[1,128]{1,0:T(1,128)} %rows_hbm.3, bf16[32,512]{1,0:T(8,128)(2,1)S(1)} %get-tuple-element.97.refs_0_, bf16[160,512]{1,0:T(8,128)(2,1)S(1)} %collective-permute-done.15.refs_3_.refs_1_, bf16[160,512]{1,0:T(8,128)(2,1)S(1)} %collective-permute-done.12.refs_2_, ...), custom_call_target="tpu_custom_call" | custom-call | flops 2000000000 | bytes 2097152 | tf_op jit(solution)/shard_map/put/pallas_call | solution.py:633
  74.9 1.4 %order.3 = (f32[1536,512]{1,0:T(8,128)}, f32[512,512]{1,0:T(8,128)}) custom-call(bf16[128,512]{1,0:T(8,128)(2,1)S(1)} %get-tuple-element.98.refs_0_, bf16[128,512]{1,0:T(8,128)(2,1)S(1)} %collective-permute-done.25.refs_1_, bf16[128,512]{1,0:T(8,128)(2,1)S(1)} %collective-permute-done.16.refs_2_, bf16[128,512]{1,0:T(8,128)(2,1)S(1)} %collective-permute-done.23.refs_3_, ...), custom_call_target="tpu_custom_call" | custom-call | flops 1200000000 | bytes 2097152 | tf_op jit(solution)/shard_map/order/pallas_call | solution.py:658
  76.3 1.2 %order.4 = (f32[1536,512]{1,0:T(8,128)}, f32[512,512]{1,0:T(8,128)}) custom-call(bf16[128,512]{1,0:T(8,128)(2,1)S(1)} %collective-permute-done.17.refs_0_, bf16[128,512]{1,0:T(8,128)(2,1)S(1)} %collective-permute-done.21.refs_1_, bf16[128,512]{1,0:T(8,128)(2,1)S(1)} %collective-permute-done.22.refs_2_, ...), custom_call_target="tpu_custom_call", output_to_operand_aliasing={{0}: (6, {}), {1}: (7, {})} | custom-call | flops 900000000 | bytes 2097152 | tf_op jit(solution)/shard_map/order/pallas_call | solution.py:658
  (56 shorter events, 13.3 us)
Async XLA Ops:
  3.7 5.7 %collective-permute-start.1 = (bf16[64,512]{1,0:T(8,128)(2,1)S(1)}, bf16[64,512]{1,0:T(8,128)(2,1)S(1)}, u32[]{:S(2)}, u32[]{:S(2)}) collective-permute-start(bf16[64,512]{1,0:T(8,128)(2,1)S(1)} %get-tuple-element.64), channel_id=1, source_target_pairs={{0,2},{1,3},{2,0},{3,1},{4,6},{5,7},{6,4},{7,5},{8,10},{9,11},{10,... | collective-permute-start | bytes 196616 | tf_op jit(solution)/shard_map/ppermute | solution.py:442
  9.4 8.9 %collective-permute-start.2 = (bf16[32,512]{1,0:T(8,128)(2,1)S(1)}, bf16[32,512]{1,0:T(8,128)(2,1)S(1)}, u32[]{:S(2)}, u32[]{:S(2)}) collective-permute-start(bf16[32,512]{1,0:T(8,128)(2,1)S(1)} %get-tuple-element.66), channel_id=1, source_target_pairs={{0,4},{1,5},{2,6},{3,7},{4,0},{5,1},{6,2},{7,3},{8,12},{9,13},{10,... | collective-permute-start | bytes 98312 | tf_op jit(solution)/shard_map/ppermute | solution.py:442
  11.1 7.3 %collective-permute-start.3 = (bf16[32,512]{1,0:T(8,128)(2,1)S(1)}, bf16[32,512]{1,0:T(8,128)(2,1)S(1)}, u32[]{:S(2)}, u32[]{:S(2)}) collective-permute-start(bf16[32,512]{1,0:T(8,128)(2,1)S(1)} %get-tuple-element.67), channel_id=1, source_target_pairs={{0,8},{1,9},{2,10},{3,11},{4,12},{5,13},{6,14},{7,15},{8,0},{9,1},... | collective-permute-start | bytes 98312 | tf_op jit(solution)/shard_map/ppermute | solution.py:442
  13.7 5.7 %collective-permute-start.4 = (bf16[32,512]{1,0:T(8,128)(2,1)S(1)}, bf16[32,512]{1,0:T(8,128)(2,1)S(1)}, u32[]{:S(2)}, u32[]{:S(2)}) collective-permute-start(bf16[32,512]{1,0:T(8,128)(2,1)S(1)} %get-tuple-element.68), channel_id=1, source_target_pairs={{0,12},{1,13},{2,14},{3,15},{4,8},{5,9},{6,10},{7,11},{8,4},{9,5},... | collective-permute-start | bytes 98312 | tf_op jit(solution)/shard_map/ppermute | solution.py:442
  28.5 7.8 %collective-permute-start.13 = (bf16[272,512]{1,0:T(8,128)(2,1)S(1)}, bf16[272,512]{1,0:T(8,128)(2,1)S(1)}, u32[]{:S(2)}, u32[]{:S(2)}) collective-permute-start(bf16[272,512]{1,0:T(8,128)(2,1)S(1)} %get-tuple-element.92), channel_id=1, source_target_pairs={{0,1},{1,0},{2,3},{3,2},{4,5},{5,4},{6,7},{7,6},{8,9},{9,8},{10,11... | collective-permute-start | bytes 835592 | tf_op jit(solution)/shard_map/ppermute | solution.py:442
  29.0 6.0 %collective-permute-start.8 = (bf16[144,512]{1,0:T(8,128)(2,1)S(1)}, bf16[144,512]{1,0:T(8,128)(2,1)S(1)}, u32[]{:S(2)}, u32[]{:S(2)}) collective-permute-start(bf16[144,512]{1,0:T(8,128)(2,1)S(1)} %get-tuple-element.83), channel_id=1, source_target_pairs={{0,2},{1,3},{2,0},{3,1},{4,6},{5,7},{6,4},{7,5},{8,10},{9,11},{10,... | collective-permute-start | bytes 442376 | tf_op jit(solution)/shard_map/ppermute | solution.py:442
  34.9 5.1 %collective-permute-start.9 = (bf16[144,512]{1,0:T(8,128)(2,1)S(1)}, bf16[144,512]{1,0:T(8,128)(2,1)S(1)}, u32[]{:S(2)}, u32[]{:S(2)}) collective-permute-start(bf16[144,512]{1,0:T(8,128)(2,1)S(1)} %get-tuple-element.84), channel_id=1, source_target_pairs={{0,2},{1,3},{2,0},{3,1},{4,6},{5,7},{6,4},{7,5},{8,10},{9,11},{10,... | collective-permute-start | bytes 442376 | tf_op jit(solution)/shard_map/ppermute | solution.py:442
  36.3 9.8 %collective-permute-start.6 = (bf16[272,512]{1,0:T(8,128)(2,1)S(1)}, bf16[272,512]{1,0:T(8,128)(2,1)S(1)}, u32[]{:S(2)}, u32[]{:S(2)}) collective-permute-start(bf16[272,512]{1,0:T(8,128)(2,1)S(1)} %get-tuple-element.73), channel_id=1, source_target_pairs={{0,1},{1,0},{2,3},{3,2},{4,5},{5,4},{6,7},{7,6},{8,9},{9,8},{10,11... | collective-permute-start | bytes 835592 | tf_op jit(solution)/shard_map/ppermute | solution.py:442
  40.1 5.1 %collective-permute-start.14 = (bf16[144,512]{1,0:T(8,128)(2,1)S(1)}, bf16[144,512]{1,0:T(8,128)(2,1)S(1)}, u32[]{:S(2)}, u32[]{:S(2)}) collective-permute-start(bf16[144,512]{1,0:T(8,128)(2,1)S(1)} %get-tuple-element.96), channel_id=1, source_target_pairs={{0,2},{1,3},{2,0},{3,1},{4,6},{5,7},{6,4},{7,5},{8,10},{9,11},{10,... | collective-permute-start | bytes 442376 | tf_op jit(solution)/shard_map/ppermute | solution.py:442
  41.5 9.0 %collective-permute-start.11 = (bf16[160,512]{1,0:T(8,128)(2,1)S(1)}, bf16[160,512]{1,0:T(8,128)(2,1)S(1)}, u32[]{:S(2)}, u32[]{:S(2)}) collective-permute-start(bf16[160,512]{1,0:T(8,128)(2,1)S(1)} %inner.3), channel_id=1, source_target_pairs={{0,12},{1,13},{2,14},{3,15},{4,8},{5,9},{6,10},{7,11},{8,4},{9,5},... | collective-permute-start | bytes 491528 | tf_op jit(solution)/shard_map/ppermute | solution.py:442
  44.2 11.9 %collective-permute-start.12 = (bf16[160,512]{1,0:T(8,128)(2,1)S(1)}, bf16[160,512]{1,0:T(8,128)(2,1)S(1)}, u32[]{:S(2)}, u32[]{:S(2)}) collective-permute-start(bf16[160,512]{1,0:T(8,128)(2,1)S(1)} %inner.4), channel_id=1, source_target_pairs={{0,8},{1,9},{2,10},{3,11},{4,12},{5,13},{6,14},{7,15},{8,0},{9,1},... | collective-permute-start | bytes 491528 | tf_op jit(solution)/shard_map/ppermute | solution.py:442
  45.2 10.9 %collective-permute-start.15 = (bf16[160,512]{1,0:T(8,128)(2,1)S(1)}, bf16[160,512]{1,0:T(8,128)(2,1)S(1)}, u32[]{:S(2)}, u32[]{:S(2)}) collective-permute-start(bf16[160,512]{1,0:T(8,128)(2,1)S(1)} %inner.5), channel_id=1, source_target_pairs={{0,4},{1,5},{2,6},{3,7},{4,0},{5,1},{6,2},{7,3},{8,12},{9,13},{10,... | collective-permute-start | bytes 491528 | tf_op jit(solution)/shard_map/ppermute | solution.py:442
  46.2 5.2 %collective-permute-start.10 = (bf16[144,512]{1,0:T(8,128)(2,1)S(1)}, bf16[144,512]{1,0:T(8,128)(2,1)S(1)}, u32[]{:S(2)}, u32[]{:S(2)}) collective-permute-start(bf16[144,512]{1,0:T(8,128)(2,1)S(1)} %get-tuple-element.85), channel_id=1, source_target_pairs={{0,2},{1,3},{2,0},{3,1},{4,6},{5,7},{6,4},{7,5},{8,10},{9,11},{10,... | collective-permute-start | bytes 442376 | tf_op jit(solution)/shard_map/ppermute | solution.py:442
  56.2 6.5 %collective-permute-start.25 = (bf16[128,512]{1,0:T(8,128)(2,1)S(1)}, bf16[128,512]{1,0:T(8,128)(2,1)S(1)}, u32[]{:S(2)}, u32[]{:S(2)}) collective-permute-start(bf16[128,512]{1,0:T(8,128)(2,1)S(1)} %get-tuple-element.98.refs_0_), channel_id=1, source_target_pairs={{0,4},{1,5},{2,6},{3,7},{4,0},{5,1},{6,2},{7,3},{8,12},{9,13},{10,... | collective-permute-start | bytes 393224 | tf_op jit(solution)/shard_map/ppermute | solution.py:442
  56.3 7.7 %collective-permute-start.16 = (bf16[128,512]{1,0:T(8,128)(2,1)S(1)}, bf16[128,512]{1,0:T(8,128)(2,1)S(1)}, u32[]{:S(2)}, u32[]{:S(2)}) collective-permute-start(bf16[128,512]{1,0:T(8,128)(2,1)S(1)} %get-tuple-element.98.refs_0_), channel_id=1, source_target_pairs={{0,8},{1,9},{2,10},{3,11},{4,12},{5,13},{6,14},{7,15},{8,0},{9,1},... | collective-permute-start | bytes 393224 | tf_op jit(solution)/shard_map/ppermute | solution.py:442
  59.5 6.3 %collective-permute-start.23 = (bf16[128,512]{1,0:T(8,128)(2,1)S(1)}, bf16[128,512]{1,0:T(8,128)(2,1)S(1)}, u32[]{:S(2)}, u32[]{:S(2)}) collective-permute-start(bf16[128,512]{1,0:T(8,128)(2,1)S(1)} %get-tuple-element.98.refs_0_), channel_id=1, source_target_pairs={{0,2},{1,3},{2,0},{3,1},{4,6},{5,7},{6,4},{7,5},{8,10},{9,11},{10,... | collective-permute-start | bytes 393224 | tf_op jit(solution)/shard_map/ppermute | solution.py:442
  62.7 6.2 %collective-permute-start.26 = (bf16[128,512]{1,0:T(8,128)(2,1)S(1)}, bf16[128,512]{1,0:T(8,128)(2,1)S(1)}, u32[]{:S(2)}, u32[]{:S(2)}) collective-permute-start(bf16[128,512]{1,0:T(8,128)(2,1)S(1)} %collective-permute-done.25.refs_1_), channel_id=1, source_target_pairs={{0,2},{1,3},{2,0},{3,1},{4,6},{5,7},{6,4},{7,5},{8,10},{9,11},{10,... | collective-permute-start | bytes 393224 | tf_op jit(solution)/shard_map/ppermute | solution.py:442
  64.3 6.6 %collective-permute-start.21 = (bf16[128,512]{1,0:T(8,128)(2,1)S(1)}, bf16[128,512]{1,0:T(8,128)(2,1)S(1)}, u32[]{:S(2)}, u32[]{:S(2)}) collective-permute-start(bf16[128,512]{1,0:T(8,128)(2,1)S(1)} %collective-permute-done.16.refs_2_), channel_id=1, source_target_pairs={{0,2},{1,3},{2,0},{3,1},{4,6},{5,7},{6,4},{7,5},{8,10},{9,11},{10,... | collective-permute-start | bytes 393224 | tf_op jit(solution)/shard_map/ppermute | solution.py:442
  65.8 5.2 %collective-permute-start.30 = (bf16[128,512]{1,0:T(8,128)(2,1)S(1)}, bf16[128,512]{1,0:T(8,128)(2,1)S(1)}, u32[]{:S(2)}, u32[]{:S(2)}) collective-permute-start(bf16[128,512]{1,0:T(8,128)(2,1)S(1)} %collective-permute-done.16.refs_2_), channel_id=1, source_target_pairs={{0,1},{1,0},{2,3},{3,2},{4,5},{5,4},{6,7},{7,6},{8,9},{9,8},{10,11... | collective-permute-start | bytes 393224 | tf_op jit(solution)/shard_map/ppermute | solution.py:442
  68.9 7.4 %collective-permute-start.24 = (bf16[128,512]{1,0:T(8,128)(2,1)S(1)}, bf16[128,512]{1,0:T(8,128)(2,1)S(1)}, u32[]{:S(2)}, u32[]{:S(2)}) collective-permute-start(bf16[128,512]{1,0:T(8,128)(2,1)S(1)} %collective-permute-done.23.refs_3_), channel_id=1, source_target_pairs={{0,1},{1,0},{2,3},{3,2},{4,5},{5,4},{6,7},{7,6},{8,9},{9,8},{10,11... | collective-permute-start | bytes 393224 | tf_op jit(solution)/shard_map/ppermute | solution.py:442
  69.0 7.4 %collective-permute-start.22 = (bf16[128,512]{1,0:T(8,128)(2,1)S(1)}, bf16[128,512]{1,0:T(8,128)(2,1)S(1)}, u32[]{:S(2)}, u32[]{:S(2)}) collective-permute-start(bf16[128,512]{1,0:T(8,128)(2,1)S(1)} %collective-permute-done.17.refs_0_), channel_id=1, source_target_pairs={{0,1},{1,0},{2,3},{3,2},{4,5},{5,4},{6,7},{7,6},{8,9},{9,8},{10,11... | collective-permute-start | bytes 393224 | tf_op jit(solution)/shard_map/ppermute | solution.py:442
  69.4 5.5 %collective-permute-start.18 = (bf16[128,512]{1,0:T(8,128)(2,1)S(1)}, bf16[128,512]{1,0:T(8,128)(2,1)S(1)}, u32[]{:S(2)}, u32[]{:S(2)}) collective-permute-start(bf16[128,512]{1,0:T(8,128)(2,1)S(1)} %collective-permute-done.17.refs_0_), channel_id=1, source_target_pairs={{0,2},{1,3},{2,0},{3,1},{4,6},{5,7},{6,4},{7,5},{8,10},{9,11},{10,... | collective-permute-start | bytes 393224 | tf_op jit(solution)/shard_map/ppermute | solution.py:442
  71.0 5.3 %collective-permute-start.28 = (bf16[128,512]{1,0:T(8,128)(2,1)S(1)}, bf16[128,512]{1,0:T(8,128)(2,1)S(1)}, u32[]{:S(2)}, u32[]{:S(2)}) collective-permute-start(bf16[128,512]{1,0:T(8,128)(2,1)S(1)} %collective-permute-done.21.refs_1_), channel_id=1, source_target_pairs={{0,1},{1,0},{2,3},{3,2},{4,5},{5,4},{6,7},{7,6},{8,9},{9,8},{10,11... | collective-permute-start | bytes 393224 | tf_op jit(solution)/shard_map/ppermute | solution.py:442
  71.0 5.3 %collective-permute-start.27 = (bf16[128,512]{1,0:T(8,128)(2,1)S(1)}, bf16[128,512]{1,0:T(8,128)(2,1)S(1)}, u32[]{:S(2)}, u32[]{:S(2)}) collective-permute-start(bf16[128,512]{1,0:T(8,128)(2,1)S(1)} %collective-permute-done.26.refs_4_), channel_id=1, source_target_pairs={{0,1},{1,0},{2,3},{3,2},{4,5},{5,4},{6,7},{7,6},{8,9},{9,8},{10,11... | collective-permute-start | bytes 393224 | tf_op jit(solution)/shard_map/ppermute | solution.py:442
  (7 other events, 22.7 us)

commit v8 on v7

--- a/solution.py
+++ b/solution.py
@@ -214,22 +214,27 @@
     width = edge_ref.shape[1]
     tile = lines * 128
     tiles = edge_ref.shape[0] // tile
-    pairs = [(w1_hbm.at[pl.ds(2 * width, width), :], w1_ref), (hot_hbm, hot_ref)]
-    pairs += [(edge_hbm.at[pl.ds(at * tile, tile), :], edge_ref.at[pl.ds(at * tile, tile), :]) for at in range(tiles)]
+    pairs = [(edge_hbm.at[pl.ds(at * tile, tile), :], edge_ref.at[pl.ds(at * tile, tile), :]) for at in range(tiles)]
+    pairs[1:1] = [(w1_hbm.at[pl.ds(2 * width, width), :], w1_ref), (hot_hbm, hot_ref)]
     copies = load(pairs, sems)
     same = lax.broadcasted_iota(jnp.int32, (256, 256), 0) == lax.broadcasted_iota(jnp.int32, (256, 256), 1)
     eye = jnp.where(same, 1.0, 0.0).astype(BF16)
-    copies[0].wait()
-    copies[1].wait()
+    outs = []
     for at in range(tiles):
         rows = slice(at * tile, (at + 1) * tile)
-        copies[2 + at].wait()
+        copies[2 + at if at else 0].wait()
         edge = edge_ref[rows, :]
         for start in range(0, width, 256):
             turned_ref[start : start + 256, rows] = dot_nt(eye, edge[:, start : start + 256]).astype(BF16)
+        out = pltpu.make_async_copy(turned_ref.at[:, pl.ds(at * tile, tile)], turned_hbm.at[:, pl.ds(at * tile, tile)], out_sems.at[at])
+        out.start()
+        outs.append(out)
+        if at == 0:
+            copies[1].wait()
+            copies[2].wait()
         base_ref[rows, :] = dot_nn(edge, w1_ref[...]) + dot_nn(hot_ref[rows, :], moved_ref[...])
-    (last,) = load([(turned_ref, turned_hbm)], out_sems)
-    last.wait()
+    for out in outs:
+        out.wait()
 
 
 def main_kernel(
@@ -255,7 +260,7 @@
     send_refs, keep_refs, rest = rest[2 : 2 + outer], rest[2 + outer : 2 + 2 * outer], rest[2 + 2 * outer :]
     slope_ref, value_ref, both_ref, grads_ref, slot_grads_ref, ordered_ref = rest[:6]
     slot_ref, dst_ref, mesh_ref, w1_ref, w2_ref, wn1_ref, wn2_ref = rest[6:13]
-    turned_ref, hot_ref, node_ref, cot_ref, mesh_out_ref, sems, out_sems = rest[13:]
+    turned_ref, hot_ref, node_ref, cot_ref, mesh_out_ref, picks_ref, sems, out_sems = rest[13:]
     width = mesh_ref.shape[1]
     mesh_rows = mesh_ref.shape[0]
     slot_rows = ordered_ref.shape[0]
@@ -263,8 +268,8 @@
     tiles = base_ref.shape[0] // tile
     pairs = [
         (slot_hbm, slot_ref),
+        (dst_hbm, dst_ref),
         (w1_hbm.at[pl.ds(0, width), :], w1_ref),
-        (dst_hbm, dst_ref),
         (w2_hbm, w2_ref),
         (wn1_hbm.at[pl.ds(width, wn1_ref.shape[0]), :], wn1_ref),
         (mesh_hbm, mesh_ref),
@@ -277,22 +282,26 @@
     copies = load(pairs, sems)
     place_rows(sizes, slot_blocks, ordered_ref)
     slots_value = ordered_ref[...].astype(BF16)
-    for copy in copies[:3]:
+    for copy in copies[:2]:
         copy.wait()
+    for at in range(tiles):
+        rows = slice(at * tile, (at + 1) * tile)
+        picks_ref[rows, :] = tile_columns(slot_ref, at, lines, slot_rows)
+        both_ref[:slot_rows, rows] = tile_rows(slot_ref, at, lines, slot_rows)
+        both_ref[slot_rows:, rows] = tile_rows(dst_ref, at, lines, mesh_rows)
+    copies[2].wait()
 
     slots = slots_value
     slot_pair = jnp.concatenate(split(dot_nn(slots, w1_ref[...])), axis=0)
     for at in range(tiles):
         rows = slice(at * tile, (at + 1) * tile)
-        from_slot = tile_columns(slot_ref, at, lines, slot_rows)
+        from_slot = picks_ref[rows, :]
         twice = jnp.concatenate([from_slot, from_slot], axis=1)
         pre = base_ref[rows, :] + dot_nn(twice, slot_pair)
         sigma = 0.5 + 0.5 * jnp.tanh(0.5 * pre)
         hidden = pre * sigma
         slope_ref[rows, :] = sigma + hidden * (1.0 - sigma)
         value_ref[rows, :] = hidden.astype(BF16)
-        both_ref[:slot_rows, rows] = tile_rows(slot_ref, at, lines, slot_rows)
-        both_ref[slot_rows:, rows] = tile_rows(dst_ref, at, lines, mesh_rows)
 
     for copy in copies[3:-1]:
         copy.wait()
@@ -516,7 +525,7 @@
             pltpu.VMEM((width, hidden_width), BF16),
             pltpu.VMEM((width, edges), BF16),
             pltpu.SemaphoreType.DMA((2 + edges // (128 * lines),)),
-            pltpu.SemaphoreType.DMA((1,)),
+            pltpu.SemaphoreType.DMA((edges // (128 * lines),)),
         ],
         compiler_params=params(16),
         cost_estimate=cost(4 * 10**9, 4 * MIB),
@@ -560,6 +569,7 @@
             pltpu.VMEM(node.shape, F32),
             pltpu.VMEM(cot.shape, F32),
             pltpu.VMEM((mesh_rows, width), BF16),
+            pltpu.VMEM((edges, slot_rows), BF16),
             pltpu.SemaphoreType.DMA((11,)),
             pltpu.SemaphoreType.DMA((1,)),
         ],
@@ -573,9 +583,9 @@
     )
     sends, keeps = sides[:outer], sides[outer:]
     small = (2 * cap, width)
-    arrived, before = [], []
+    arrived = {}
     first = None
-    for k in range(outer - 1, -1, -1):
+    for k in [outer - 1, *range(1, outer - 1), 0]:
         send = sends[k] if first is None else lax.optimization_barrier((sends[k], first))[0]
         crossed = to_core(send)
         first = crossed if first is None else first
@@ -590,9 +600,7 @@
             cost_estimate=cost(10**9, MIB),
             name="core",
         )(keeps[k], crossed, d_slots)
-        parts = [lax.optimization_barrier((part, *before))[0] for part in parts]
         parts = [to_inner(part, at + 1) for at, part in enumerate(parts)]
-        before = parts if k >= outer - 2 else before
         block = 2 * inner * cap
         if k:
             (out,) = pl.pallas_call(
@@ -601,7 +609,7 @@
                 compiler_params=params(16),
                 name="inner",
             )(total, mixed, *parts)
-            arrived.append(to_outer(out, k))
+            arrived[k] = to_outer(out, k)
         else:
             own, home = pl.pallas_call(
                 functools.partial(inner_kernel, inner - 1, outer - 1),
@@ -611,7 +619,7 @@
                 ],
                 compiler_params=params(16),
                 name="own",
-            )(total, mixed, *parts, *arrived)
+            )(total, mixed, *parts, *[arrived[at] for at in range(1, outer)])
 
     pieces = {0: own}
     stride = outer // 2
@@ -627,7 +635,7 @@
             if far_outer == outer // 2:
                 value = lax.optimization_barrier((value, pieces[halfway_at]))[0]
             pieces[far_inner * outer + far_outer] = to_inner(value, far_inner)
-    for at in range(1, halfway_at):
+    for at in range(1, halfway_at - 1):
         pieces[halfway_at + at] = to_core(pieces[at])
 
     grid_grad = pl.pallas_call(
@@ -643,7 +651,7 @@
         compiler_params=params(16),
         cost_estimate=cost(2 * 10**9, 2 * MIB),
         name="put",
-    )(*pinned(pltpu.HBM, send_rows), home, *arrived[::-1])
+    )(*pinned(pltpu.HBM, send_rows), home, *[arrived[at] for at in range(1, outer)])
 
     last = outer - 1
     stages = [[], [], []]
@@ -655,6 +663,9 @@
             stages[1 if far_inner and (far_core or far_outer == outer // 2) else 0].append(at)
     grads = []
     for places in stages:
+        if places is stages[1]:
+            value = lax.optimization_barrier((pieces[halfway_at - 1], grid_grad, *grads))[0]
+            pieces[band_count - 1] = to_core(value)
         grads = pl.pallas_call(
             functools.partial(order_kernel, sizes, places, len(grads)),
             out_shape=[

time: 78.7 us -> 72.1 us (0.916)
  waiting for transfers between devices: 31 us -> 22.5 us
  starting transfers between devices: 24.2 us -> 26.8 us
    ppermute x31, waiting for transfers between devices: 31 us -> 22.5 us  [permute(): return lax.ppermute(value, 'band', pairs)]
    ppermute x31, starting transfers between devices: 24.2 us -> 26.8 us  [permute(): return lax.ppermute(value, 'band', pairs)]
  transfers between devices with their start and end apart: 31 -> 31, of which waited for: 16 -> 13; matrix products, arithmetic and copies ran while one was open for 0% -> 0% of each run, Pallas kernels for 16% -> 17%
where the time goes in v8:
time: 72.1 us; the launch traced here: 71.9 us
  starting transfers between devices  26.8 us (37%)
  waiting for transfers between devices  22.5 us (31%)
  Pallas kernels  21.9 us (30%)
  between operations  0.84 us (1%)
    ppermute x31, starting transfers between devices, permute(): return lax.ppermute(value, 'band', pairs)  26.8 us
    ppermute x31, waiting for transfers between devices, permute(): return lax.ppermute(value, 'band', pairs)  22.5 us
    pallas_call x1, Pallas kernels, shards(): pl.pallas_call(functools.partial(main_kernel, lines, sizes), out_shape=[j...  7.3 us
    pallas_call x1, Pallas kernels, shards(): pl.pallas_call(functools.partial(base_kernel, lines), out_shape=[pltpu.VM...  3.95 us
    pallas_call x3, Pallas kernels, shards(): pl.pallas_call(functools.partial(order_kernel, sizes, places, len(grads))...  3.46 us
    pallas_call x1, Pallas kernels, shards(): pl.pallas_call(functools.partial(ready_kernel, lines), out_shape=[pltpu.H...  2.8 us
    pallas_call x1, Pallas kernels, shards(): pl.pallas_call(functools.partial(put_kernel, sizes), out_shape=jax.ShapeD...  2.39 us
    pallas_call x1, Pallas kernels, shards(): pl.pallas_call(functools.partial(pick_kernel, sizes), out_shape=[jax.Shap...  1.59 us
  transfers between devices with their start and end apart: 31, of which 13 were waited for; matrix products, arithmetic and copies ran while one was open for 0% of the time, Pallas kernels for 17%

profile of v8, /device:TPU:0, one launch (start us, length us, event | category | flops | bytes accessed | tf_op | source)
XLA Modules:
  0.0 71.9 jit_solution(15033739146696624465)
XLA Ops:
  0.6 1.6 %pick.1 = (bf16[64,512]{1,0:T(8,128)(2,1)S(1)}, bf16[64,512]{1,0:T(8,128)(2,1)S(1)}) custom-call(s32[1,128]{1,0:T(1,128)} %rows_hbm.3, bf16[1024,512]{1,0:T(8,128)(2,1)} %grid_hbm.1), custom_call_target="tpu_custom_call" | custom-call | tf_op jit(solution)/shard_map/pick/pallas_call | solution.py:463
  3.7 2.9 %collective-permute-start.1 = (bf16[64,512]{1,0:T(8,128)(2,1)S(1)}, bf16[64,512]{1,0:T(8,128)(2,1)S(1)}, u32[]{:S(2)}, u32[]{:S(2)}) collective-permute-start(bf16[64,512]{1,0:T(8,128)(2,1)S(1)} %get-tuple-element.62), channel_id=1, source_target_pairs={{0,2},{1,3},{2,0},{3,1},{4,6},{5,7},{6,4},{7,5},{8,10},{9,11},{10,... | collective-permute-start | bytes 196616 | tf_op jit(solution)/shard_map/ppermute | solution.py:451
  6.6 2.8 %ready.1 = (bf16[1536,256]{1,0:T(8,128)(2,1)}, f32[256,512]{1,0:T(8,128)}, f32[256,512]{1,0:T(8,128)}, bf16[256,512]{1,0:T(8,128)(2,1)S(1)}) custom-call(s32[12,128]{1,0:T(8,128)} %bitcast.3, bf16[256,512]{1,0:T(8,128)(2,1)} %mesh_hbm.3, bf16[256,512]{1,0:T(8,128)(2,1)} %cot_hbm.1, bf16[1536,512]{1,0:T(8,128)(2,1)} %w1_hbm.5, bf16[1024,512]{1,0:T(8,128)(2,1)} %wn1_hbm.3, ...), custom_call_target="tpu_custom_call" | custom-call | flops 2000000000 | bytes 4194304 | tf_op jit(solution)/shard_map/ready/pallas_call | solution.py:487
  9.4 1.6 %collective-permute-start.2 = (bf16[32,512]{1,0:T(8,128)(2,1)S(1)}, bf16[32,512]{1,0:T(8,128)(2,1)S(1)}, u32[]{:S(2)}, u32[]{:S(2)}) collective-permute-start(bf16[32,512]{1,0:T(8,128)(2,1)S(1)} %get-tuple-element.64), channel_id=1, source_target_pairs={{0,4},{1,5},{2,6},{3,7},{4,0},{5,1},{6,2},{7,3},{8,12},{9,13},{10,... | collective-permute-start | bytes 98312 | tf_op jit(solution)/shard_map/ppermute | solution.py:451
  11.1 2.6 %collective-permute-start.3 = (bf16[32,512]{1,0:T(8,128)(2,1)S(1)}, bf16[32,512]{1,0:T(8,128)(2,1)S(1)}, u32[]{:S(2)}, u32[]{:S(2)}) collective-permute-start(bf16[32,512]{1,0:T(8,128)(2,1)S(1)} %get-tuple-element.65), channel_id=1, source_target_pairs={{0,8},{1,9},{2,10},{3,11},{4,12},{5,13},{6,14},{7,15},{8,0},{9,1},... | collective-permute-start | bytes 98312 | tf_op jit(solution)/shard_map/ppermute | solution.py:451
  13.9 4.0 %base.1 = (f32[1536,512]{1,0:T(8,128)S(1)}, bf16[512,1536]{1,0:T(8,128)(2,1)}) custom-call(bf16[1536,256]{1,0:T(8,128)(2,1)} %get-tuple-element.53.hot_hbm, bf16[1536,512]{1,0:T(8,128)(2,1)} %edge_hbm.1, bf16[1536,512]{1,0:T(8,128)(2,1)} %w1_hbm.5, bf16[256,512]{1,0:T(8,128)(2,1)S(1)} %get-tuple-element.54.moved_ref), custom_call_target="tpu_custom_call" | custom-call | flops 4000000000 | bytes 4194304 | tf_op jit(solution)/shard_map/base/pallas_call | solution.py:514
  17.9 1.5 %collective-permute-done.4.rest_3_ = bf16[32,512]{1,0:T(8,128)(2,1)S(1)} collective-permute-done((bf16[32,512]{1,0:T(8,128)(2,1)S(1)}, bf16[32,512]{1,0:T(8,128)(2,1)S(1)}, u32[]{:S(2)}, u32[]{:S(2)}) %collective-permute-start.4) | collective-permute-done | bytes 32800 | tf_op jit(solution)/shard_map/ppermute | solution.py:451
  19.4 7.3 %edges.1 = (bf16[256,512]{1,0:T(8,128)(2,1)}, bf16[64,512]{1,0:T(8,128)(2,1)S(1)}, bf16[272,512]{1,0:T(8,128)(2,1)S(1)}, bf16[272,512]{1,0:T(8,128)(2,1)S(1)}, b...) custom-call(s32[12,128]{1,0:T(8,128)} %bitcast.2, ...), custom_call_target="tpu_custom_call" | custom-call | tf_op jit(solution)/shard_map/edges/pallas_call | solution.py:543
  26.8 1.5 %collective-permute-done.5.crossed_ref = bf16[272,512]{1,0:T(8,128)(2,1)S(1)} collective-permute-done((bf16[272,512]{1,0:T(8,128)(2,1)S(1)}, bf16[272,512]{1,0:T(8,128)(2,1)S(1)}, u32[]{:S(2)}, u32[]{:S(2)}) %collective-permute-start.5) | collective-permute-done | bytes 278560 | tf_op jit(solution)/shard_map/ppermute | solution.py:451
  28.9 1.5 %collective-permute-start.14 = (bf16[144,512]{1,0:T(8,128)(2,1)S(1)}, bf16[144,512]{1,0:T(8,128)(2,1)S(1)}, u32[]{:S(2)}, u32[]{:S(2)}) collective-permute-start(bf16[144,512]{1,0:T(8,128)(2,1)S(1)} %get-tuple-element.91), channel_id=1, source_target_pairs={{0,2},{1,3},{2,0},{3,1},{4,6},{5,7},{6,4},{7,5},{8,10},{9,11},{10,... | collective-permute-start | bytes 442376 | tf_op jit(solution)/shard_map/ppermute | solution.py:451
  32.6 3.0 %collective-permute-done.14.refs_0_ = bf16[144,512]{1,0:T(8,128)(2,1)S(1)} collective-permute-done((bf16[144,512]{1,0:T(8,128)(2,1)S(1)}, bf16[144,512]{1,0:T(8,128)(2,1)S(1)}, u32[]{:S(2)}, u32[]{:S(2)}) %collective-permute-start.14) | collective-permute-done | bytes 147488 | tf_op jit(solution)/shard_map/ppermute | solution.py:451
  35.7 2.2 %collective-permute-start.15 = (bf16[160,512]{1,0:T(8,128)(2,1)S(1)}, bf16[160,512]{1,0:T(8,128)(2,1)S(1)}, u32[]{:S(2)}, u32[]{:S(2)}) collective-permute-start(bf16[160,512]{1,0:T(8,128)(2,1)S(1)} %inner.5), channel_id=1, source_target_pairs={{0,12},{1,13},{2,14},{3,15},{4,8},{5,9},{6,10},{7,11},{8,4},{9,5},... | collective-permute-start | bytes 491528 | tf_op jit(solution)/shard_map/ppermute | solution.py:451
  39.1 2.1 %collective-permute-done.9.refs_0_ = bf16[144,512]{1,0:T(8,128)(2,1)S(1)} collective-permute-done((bf16[144,512]{1,0:T(8,128)(2,1)S(1)}, bf16[144,512]{1,0:T(8,128)(2,1)S(1)}, u32[]{:S(2)}, u32[]{:S(2)}) %collective-permute-start.9) | collective-permute-done | bytes 147488 | tf_op jit(solution)/shard_map/ppermute | solution.py:451
  41.7 1.5 %collective-permute-start.7 = (bf16[144,512]{1,0:T(8,128)(2,1)S(1)}, bf16[144,512]{1,0:T(8,128)(2,1)S(1)}, u32[]{:S(2)}, u32[]{:S(2)}) collective-permute-start(bf16[144,512]{1,0:T(8,128)(2,1)S(1)} %get-tuple-element.75), channel_id=1, source_target_pairs={{0,2},{1,3},{2,0},{3,1},{4,6},{5,7},{6,4},{7,5},{8,10},{9,11},{10,... | collective-permute-start | bytes 442376 | tf_op jit(solution)/shard_map/ppermute | solution.py:451
  44.3 2.6 %collective-permute-done.7.refs_0_ = bf16[144,512]{1,0:T(8,128)(2,1)S(1)} collective-permute-done((bf16[144,512]{1,0:T(8,128)(2,1)S(1)}, bf16[144,512]{1,0:T(8,128)(2,1)S(1)}, u32[]{:S(2)}, u32[]{:S(2)}) %collective-permute-start.7) | collective-permute-done | bytes 147488 | tf_op jit(solution)/shard_map/ppermute | solution.py:451
  46.9 3.3 %collective-permute-done.13.refs_2_ = bf16[160,512]{1,0:T(8,128)(2,1)S(1)} collective-permute-done((bf16[160,512]{1,0:T(8,128)(2,1)S(1)}, bf16[160,512]{1,0:T(8,128)(2,1)S(1)}, u32[]{:S(2)}, u32[]{:S(2)}) %collective-permute-start.13) | collective-permute-done | bytes 163872 | tf_op jit(solution)/shard_map/ppermute | solution.py:451
  51.3 2.4 %collective-permute-start.19 = (bf16[128,512]{1,0:T(8,128)(2,1)S(1)}, bf16[128,512]{1,0:T(8,128)(2,1)S(1)}, u32[]{:S(2)}, u32[]{:S(2)}) collective-permute-start(bf16[128,512]{1,0:T(8,128)(2,1)S(1)} %get-tuple-element.93.refs_0_), channel_id=1, source_target_pairs={{0,4},{1,5},{2,6},{3,7},{4,0},{5,1},{6,2},{7,3},{8,12},{9,13},{10,... | collective-permute-start | bytes 393224 | tf_op jit(solution)/shard_map/ppermute | solution.py:451
  53.8 1.4 %collective-permute-start.20 = (bf16[128,512]{1,0:T(8,128)(2,1)S(1)}, bf16[128,512]{1,0:T(8,128)(2,1)S(1)}, u32[]{:S(2)}, u32[]{:S(2)}) collective-permute-start(bf16[128,512]{1,0:T(8,128)(2,1)S(1)} %get-tuple-element.93.refs_0_), channel_id=1, source_target_pairs={{0,2},{1,3},{2,0},{3,1},{4,6},{5,7},{6,4},{7,5},{8,10},{9,11},{10,... | collective-permute-start | bytes 393224 | tf_op jit(solution)/shard_map/ppermute | solution.py:451
  55.2 3.1 %collective-permute-done.16.refs_2_ = bf16[128,512]{1,0:T(8,128)(2,1)S(1)} collective-permute-done((bf16[128,512]{1,0:T(8,128)(2,1)S(1)}, bf16[128,512]{1,0:T(8,128)(2,1)S(1)}, u32[]{:S(2)}, u32[]{:S(2)}) %collective-permute-start.16) | collective-permute-done | bytes 131104 | tf_op jit(solution)/shard_map/ppermute | solution.py:451
  58.3 1.4 %collective-permute-start.26 = (bf16[128,512]{1,0:T(8,128)(2,1)S(1)}, bf16[128,512]{1,0:T(8,128)(2,1)S(1)}, u32[]{:S(2)}, u32[]{:S(2)}) collective-permute-start(bf16[128,512]{1,0:T(8,128)(2,1)S(1)} %collective-permute-done.16.refs_2_), channel_id=1, source_target_pairs={{0,2},{1,3},{2,0},{3,1},{4,6},{5,7},{6,4},{7,5},{8,10},{9,11},{10,... | collective-permute-start | bytes 393224 | tf_op jit(solution)/shard_map/ppermute | solution.py:451
  59.9 1.4 %collective-permute-start.21 = (bf16[128,512]{1,0:T(8,128)(2,1)S(1)}, bf16[128,512]{1,0:T(8,128)(2,1)S(1)}, u32[]{:S(2)}, u32[]{:S(2)}) collective-permute-start(bf16[128,512]{1,0:T(8,128)(2,1)S(1)} %collective-permute-done.19.refs_1_), channel_id=1, source_target_pairs={{0,2},{1,3},{2,0},{3,1},{4,6},{5,7},{6,4},{7,5},{8,10},{9,11},{10,... | collective-permute-start | bytes 393224 | tf_op jit(solution)/shard_map/ppermute | solution.py:451
  61.9 1.4 %collective-permute-done.17.refs_0_ = bf16[128,512]{1,0:T(8,128)(2,1)S(1)} collective-permute-done((bf16[128,512]{1,0:T(8,128)(2,1)S(1)}, bf16[128,512]{1,0:T(8,128)(2,1)S(1)}, u32[]{:S(2)}, u32[]{:S(2)}) %collective-permute-start.17) | collective-permute-done | bytes 131104 | tf_op jit(solution)/shard_map/ppermute | solution.py:451
  63.3 1.4 %collective-permute-start.18 = (bf16[128,512]{1,0:T(8,128)(2,1)S(1)}, bf16[128,512]{1,0:T(8,128)(2,1)S(1)}, u32[]{:S(2)}, u32[]{:S(2)}) collective-permute-start(bf16[128,512]{1,0:T(8,128)(2,1)S(1)} %collective-permute-done.17.refs_0_), channel_id=1, source_target_pairs={{0,2},{1,3},{2,0},{3,1},{4,6},{5,7},{6,4},{7,5},{8,10},{9,11},{10,... | collective-permute-start | bytes 393224 | tf_op jit(solution)/shard_map/ppermute | solution.py:451
  64.7 2.4 %put.1 = f32[1024,512]{1,0:T(8,128)} custom-call(s32[1,128]{1,0:T(1,128)} %rows_hbm.3, bf16[32,512]{1,0:T(8,128)(2,1)S(1)} %get-tuple-element.92.refs_0_, bf16[160,512]{1,0:T(8,128)(2,1)S(1)} %collective-permute-done.10.refs_1_, bf16[160,512]{1,0:T(8,128)(2,1)S(1)} %collective-permute-done.13.refs_2_, bf16[160,512]{1,0:T(8,128)(2,1)S(1)} %collective-permute-done.15.refs_3_), custom_call_target="tpu_custom_call" | custom-call | flops 2000000000 | bytes 2097152 | tf_op jit(solution)/shard_map/put/pallas_call | solution.py:641
  (56 shorter events, 13.9 us)
Async XLA Ops:
  3.7 5.7 %collective-permute-start.1 = (bf16[64,512]{1,0:T(8,128)(2,1)S(1)}, bf16[64,512]{1,0:T(8,128)(2,1)S(1)}, u32[]{:S(2)}, u32[]{:S(2)}) collective-permute-start(bf16[64,512]{1,0:T(8,128)(2,1)S(1)} %get-tuple-element.62), channel_id=1, source_target_pairs={{0,2},{1,3},{2,0},{3,1},{4,6},{5,7},{6,4},{7,5},{8,10},{9,11},{10,... | collective-permute-start | bytes 196616 | tf_op jit(solution)/shard_map/ppermute | solution.py:451
  9.4 8.4 %collective-permute-start.2 = (bf16[32,512]{1,0:T(8,128)(2,1)S(1)}, bf16[32,512]{1,0:T(8,128)(2,1)S(1)}, u32[]{:S(2)}, u32[]{:S(2)}) collective-permute-start(bf16[32,512]{1,0:T(8,128)(2,1)S(1)} %get-tuple-element.64), channel_id=1, source_target_pairs={{0,4},{1,5},{2,6},{3,7},{4,0},{5,1},{6,2},{7,3},{8,12},{9,13},{10,... | collective-permute-start | bytes 98312 | tf_op jit(solution)/shard_map/ppermute | solution.py:451
  11.1 6.8 %collective-permute-start.3 = (bf16[32,512]{1,0:T(8,128)(2,1)S(1)}, bf16[32,512]{1,0:T(8,128)(2,1)S(1)}, u32[]{:S(2)}, u32[]{:S(2)}) collective-permute-start(bf16[32,512]{1,0:T(8,128)(2,1)S(1)} %get-tuple-element.65), channel_id=1, source_target_pairs={{0,8},{1,9},{2,10},{3,11},{4,12},{5,13},{6,14},{7,15},{8,0},{9,1},... | collective-permute-start | bytes 98312 | tf_op jit(solution)/shard_map/ppermute | solution.py:451
  13.7 5.7 %collective-permute-start.4 = (bf16[32,512]{1,0:T(8,128)(2,1)S(1)}, bf16[32,512]{1,0:T(8,128)(2,1)S(1)}, u32[]{:S(2)}, u32[]{:S(2)}) collective-permute-start(bf16[32,512]{1,0:T(8,128)(2,1)S(1)} %get-tuple-element.66), channel_id=1, source_target_pairs={{0,12},{1,13},{2,14},{3,15},{4,8},{5,9},{6,10},{7,11},{8,4},{9,5},... | collective-permute-start | bytes 98312 | tf_op jit(solution)/shard_map/ppermute | solution.py:451
  28.5 3.0 %collective-permute-start.8 = (bf16[272,512]{1,0:T(8,128)(2,1)S(1)}, bf16[272,512]{1,0:T(8,128)(2,1)S(1)}, u32[]{:S(2)}, u32[]{:S(2)}) collective-permute-start(bf16[272,512]{1,0:T(8,128)(2,1)S(1)} %get-tuple-element.78), channel_id=1, source_target_pairs={{0,1},{1,0},{2,3},{3,2},{4,5},{5,4},{6,7},{7,6},{8,9},{9,8},{10,11... | collective-permute-start | bytes 835592 | tf_op jit(solution)/shard_map/ppermute | solution.py:451
  28.9 6.8 %collective-permute-start.14 = (bf16[144,512]{1,0:T(8,128)(2,1)S(1)}, bf16[144,512]{1,0:T(8,128)(2,1)S(1)}, u32[]{:S(2)}, u32[]{:S(2)}) collective-permute-start(bf16[144,512]{1,0:T(8,128)(2,1)S(1)} %get-tuple-element.91), channel_id=1, source_target_pairs={{0,2},{1,3},{2,0},{3,1},{4,6},{5,7},{6,4},{7,5},{8,10},{9,11},{10,... | collective-permute-start | bytes 442376 | tf_op jit(solution)/shard_map/ppermute | solution.py:451
  30.4 11.3 %collective-permute-start.6 = (bf16[272,512]{1,0:T(8,128)(2,1)S(1)}, bf16[272,512]{1,0:T(8,128)(2,1)S(1)}, u32[]{:S(2)}, u32[]{:S(2)}) collective-permute-start(bf16[272,512]{1,0:T(8,128)(2,1)S(1)} %get-tuple-element.71), channel_id=1, source_target_pairs={{0,1},{1,0},{2,3},{3,2},{4,5},{5,4},{6,7},{7,6},{8,9},{9,8},{10,11... | collective-permute-start | bytes 835592 | tf_op jit(solution)/shard_map/ppermute | solution.py:451
  30.4 8.4 %collective-permute-start.12 = (bf16[144,512]{1,0:T(8,128)(2,1)S(1)}, bf16[144,512]{1,0:T(8,128)(2,1)S(1)}, u32[]{:S(2)}, u32[]{:S(2)}) collective-permute-start(bf16[144,512]{1,0:T(8,128)(2,1)S(1)} %get-tuple-element.87), channel_id=1, source_target_pairs={{0,2},{1,3},{2,0},{3,1},{4,6},{5,7},{6,4},{7,5},{8,10},{9,11},{10,... | collective-permute-start | bytes 442376 | tf_op jit(solution)/shard_map/ppermute | solution.py:451
  31.5 9.7 %collective-permute-start.9 = (bf16[144,512]{1,0:T(8,128)(2,1)S(1)}, bf16[144,512]{1,0:T(8,128)(2,1)S(1)}, u32[]{:S(2)}, u32[]{:S(2)}) collective-permute-start(bf16[144,512]{1,0:T(8,128)(2,1)S(1)} %get-tuple-element.81), channel_id=1, source_target_pairs={{0,2},{1,3},{2,0},{3,1},{4,6},{5,7},{6,4},{7,5},{8,10},{9,11},{10,... | collective-permute-start | bytes 442376 | tf_op jit(solution)/shard_map/ppermute | solution.py:451
  35.7 8.6 %collective-permute-start.15 = (bf16[160,512]{1,0:T(8,128)(2,1)S(1)}, bf16[160,512]{1,0:T(8,128)(2,1)S(1)}, u32[]{:S(2)}, u32[]{:S(2)}) collective-permute-start(bf16[160,512]{1,0:T(8,128)(2,1)S(1)} %inner.5), channel_id=1, source_target_pairs={{0,12},{1,13},{2,14},{3,15},{4,8},{5,9},{6,10},{7,11},{8,4},{9,5},... | collective-permute-start | bytes 491528 | tf_op jit(solution)/shard_map/ppermute | solution.py:451
  38.8 11.4 %collective-permute-start.13 = (bf16[160,512]{1,0:T(8,128)(2,1)S(1)}, bf16[160,512]{1,0:T(8,128)(2,1)S(1)}, u32[]{:S(2)}, u32[]{:S(2)}) collective-permute-start(bf16[160,512]{1,0:T(8,128)(2,1)S(1)} %inner.4), channel_id=1, source_target_pairs={{0,8},{1,9},{2,10},{3,11},{4,12},{5,13},{6,14},{7,15},{8,0},{9,1},... | collective-permute-start | bytes 491528 | tf_op jit(solution)/shard_map/ppermute | solution.py:451
  41.2 9.8 %collective-permute-start.10 = (bf16[160,512]{1,0:T(8,128)(2,1)S(1)}, bf16[160,512]{1,0:T(8,128)(2,1)S(1)}, u32[]{:S(2)}, u32[]{:S(2)}) collective-permute-start(bf16[160,512]{1,0:T(8,128)(2,1)S(1)} %inner.3), channel_id=1, source_target_pairs={{0,4},{1,5},{2,6},{3,7},{4,0},{5,1},{6,2},{7,3},{8,12},{9,13},{10,... | collective-permute-start | bytes 491528 | tf_op jit(solution)/shard_map/ppermute | solution.py:451
  41.7 5.2 %collective-permute-start.7 = (bf16[144,512]{1,0:T(8,128)(2,1)S(1)}, bf16[144,512]{1,0:T(8,128)(2,1)S(1)}, u32[]{:S(2)}, u32[]{:S(2)}) collective-permute-start(bf16[144,512]{1,0:T(8,128)(2,1)S(1)} %get-tuple-element.75), channel_id=1, source_target_pairs={{0,2},{1,3},{2,0},{3,1},{4,6},{5,7},{6,4},{7,5},{8,10},{9,11},{10,... | collective-permute-start | bytes 442376 | tf_op jit(solution)/shard_map/ppermute | solution.py:451
  51.0 7.3 %collective-permute-start.16 = (bf16[128,512]{1,0:T(8,128)(2,1)S(1)}, bf16[128,512]{1,0:T(8,128)(2,1)S(1)}, u32[]{:S(2)}, u32[]{:S(2)}) collective-permute-start(bf16[128,512]{1,0:T(8,128)(2,1)S(1)} %get-tuple-element.93.refs_0_), channel_id=1, source_target_pairs={{0,8},{1,9},{2,10},{3,11},{4,12},{5,13},{6,14},{7,15},{8,0},{9,1},... | collective-permute-start | bytes 393224 | tf_op jit(solution)/shard_map/ppermute | solution.py:451
  51.3 7.0 %collective-permute-start.22 = (bf16[128,512]{1,0:T(8,128)(2,1)S(1)}, bf16[128,512]{1,0:T(8,128)(2,1)S(1)}, u32[]{:S(2)}, u32[]{:S(2)}) collective-permute-start(bf16[128,512]{1,0:T(8,128)(2,1)S(1)} %get-tuple-element.93.refs_0_), channel_id=1, source_target_pairs={{0,1},{1,0},{2,3},{3,2},{4,5},{5,4},{6,7},{7,6},{8,9},{9,8},{10,11... | collective-permute-start | bytes 393224 | tf_op jit(solution)/shard_map/ppermute | solution.py:451
  51.3 8.6 %collective-permute-start.19 = (bf16[128,512]{1,0:T(8,128)(2,1)S(1)}, bf16[128,512]{1,0:T(8,128)(2,1)S(1)}, u32[]{:S(2)}, u32[]{:S(2)}) collective-permute-start(bf16[128,512]{1,0:T(8,128)(2,1)S(1)} %get-tuple-element.93.refs_0_), channel_id=1, source_target_pairs={{0,4},{1,5},{2,6},{3,7},{4,0},{5,1},{6,2},{7,3},{8,12},{9,13},{10,... | collective-permute-start | bytes 393224 | tf_op jit(solution)/shard_map/ppermute | solution.py:451
  53.8 7.6 %collective-permute-start.20 = (bf16[128,512]{1,0:T(8,128)(2,1)S(1)}, bf16[128,512]{1,0:T(8,128)(2,1)S(1)}, u32[]{:S(2)}, u32[]{:S(2)}) collective-permute-start(bf16[128,512]{1,0:T(8,128)(2,1)S(1)} %get-tuple-element.93.refs_0_), channel_id=1, source_target_pairs={{0,2},{1,3},{2,0},{3,1},{4,6},{5,7},{6,4},{7,5},{8,10},{9,11},{10,... | collective-permute-start | bytes 393224 | tf_op jit(solution)/shard_map/ppermute | solution.py:451
  58.3 5.0 %collective-permute-start.17 = (bf16[128,512]{1,0:T(8,128)(2,1)S(1)}, bf16[128,512]{1,0:T(8,128)(2,1)S(1)}, u32[]{:S(2)}, u32[]{:S(2)}) collective-permute-start(bf16[128,512]{1,0:T(8,128)(2,1)S(1)} %collective-permute-done.16.refs_2_), channel_id=1, source_target_pairs={{0,4},{1,5},{2,6},{3,7},{4,0},{5,1},{6,2},{7,3},{8,12},{9,13},{10,... | collective-permute-start | bytes 393224 | tf_op jit(solution)/shard_map/ppermute | solution.py:451
  58.3 8.8 %collective-permute-start.26 = (bf16[128,512]{1,0:T(8,128)(2,1)S(1)}, bf16[128,512]{1,0:T(8,128)(2,1)S(1)}, u32[]{:S(2)}, u32[]{:S(2)}) collective-permute-start(bf16[128,512]{1,0:T(8,128)(2,1)S(1)} %collective-permute-done.16.refs_2_), channel_id=1, source_target_pairs={{0,2},{1,3},{2,0},{3,1},{4,6},{5,7},{6,4},{7,5},{8,10},{9,11},{10,... | collective-permute-start | bytes 393224 | tf_op jit(solution)/shard_map/ppermute | solution.py:451
  59.9 7.3 %collective-permute-start.21 = (bf16[128,512]{1,0:T(8,128)(2,1)S(1)}, bf16[128,512]{1,0:T(8,128)(2,1)S(1)}, u32[]{:S(2)}, u32[]{:S(2)}) collective-permute-start(bf16[128,512]{1,0:T(8,128)(2,1)S(1)} %collective-permute-done.19.refs_1_), channel_id=1, source_target_pairs={{0,2},{1,3},{2,0},{3,1},{4,6},{5,7},{6,4},{7,5},{8,10},{9,11},{10,... | collective-permute-start | bytes 393224 | tf_op jit(solution)/shard_map/ppermute | solution.py:451
  61.3 6.4 %collective-permute-start.23 = (bf16[128,512]{1,0:T(8,128)(2,1)S(1)}, bf16[128,512]{1,0:T(8,128)(2,1)S(1)}, u32[]{:S(2)}, u32[]{:S(2)}) collective-permute-start(bf16[128,512]{1,0:T(8,128)(2,1)S(1)} %collective-permute-done.19.refs_1_), channel_id=1, source_target_pairs={{0,1},{1,0},{2,3},{3,2},{4,5},{5,4},{6,7},{7,6},{8,9},{9,8},{10,11... | collective-permute-start | bytes 393224 | tf_op jit(solution)/shard_map/ppermute | solution.py:451
  61.3 6.5 %collective-permute-start.24 = (bf16[128,512]{1,0:T(8,128)(2,1)S(1)}, bf16[128,512]{1,0:T(8,128)(2,1)S(1)}, u32[]{:S(2)}, u32[]{:S(2)}) collective-permute-start(bf16[128,512]{1,0:T(8,128)(2,1)S(1)} %collective-permute-done.16.refs_2_), channel_id=1, source_target_pairs={{0,1},{1,0},{2,3},{3,2},{4,5},{5,4},{6,7},{7,6},{8,9},{9,8},{10,11... | collective-permute-start | bytes 393224 | tf_op jit(solution)/shard_map/ppermute | solution.py:451
  63.3 6.3 %collective-permute-start.18 = (bf16[128,512]{1,0:T(8,128)(2,1)S(1)}, bf16[128,512]{1,0:T(8,128)(2,1)S(1)}, u32[]{:S(2)}, u32[]{:S(2)}) collective-permute-start(bf16[128,512]{1,0:T(8,128)(2,1)S(1)} %collective-permute-done.17.refs_0_), channel_id=1, source_target_pairs={{0,2},{1,3},{2,0},{3,1},{4,6},{5,7},{6,4},{7,5},{8,10},{9,11},{10,... | collective-permute-start | bytes 393224 | tf_op jit(solution)/shard_map/ppermute | solution.py:451
  67.1 2.7 %collective-permute-start.28 = (bf16[128,512]{1,0:T(8,128)(2,1)S(1)}, bf16[128,512]{1,0:T(8,128)(2,1)S(1)}, u32[]{:S(2)}, u32[]{:S(2)}) collective-permute-start(bf16[128,512]{1,0:T(8,128)(2,1)S(1)} %collective-permute-done.20.refs_3_), channel_id=1, source_target_pairs={{0,1},{1,0},{2,3},{3,2},{4,5},{5,4},{6,7},{7,6},{8,9},{9,8},{10,11... | collective-permute-start | bytes 393224 | tf_op jit(solution)/shard_map/ppermute | solution.py:451
  (7 other events, 13.2 us)

commit v9 on v8

--- a/solution.py
+++ b/solution.py
@@ -215,24 +215,26 @@
     tile = lines * 128
     tiles = edge_ref.shape[0] // tile
     pairs = [(edge_hbm.at[pl.ds(at * tile, tile), :], edge_ref.at[pl.ds(at * tile, tile), :]) for at in range(tiles)]
-    pairs[1:1] = [(w1_hbm.at[pl.ds(2 * width, width), :], w1_ref), (hot_hbm, hot_ref)]
+    pairs += [(w1_hbm.at[pl.ds(2 * width, width), :], w1_ref), (hot_hbm, hot_ref)]
     copies = load(pairs, sems)
     same = lax.broadcasted_iota(jnp.int32, (256, 256), 0) == lax.broadcasted_iota(jnp.int32, (256, 256), 1)
     eye = jnp.where(same, 1.0, 0.0).astype(BF16)
     outs = []
     for at in range(tiles):
         rows = slice(at * tile, (at + 1) * tile)
-        copies[2 + at if at else 0].wait()
-        edge = edge_ref[rows, :]
+        copies[at].wait()
         for start in range(0, width, 256):
-            turned_ref[start : start + 256, rows] = dot_nt(eye, edge[:, start : start + 256]).astype(BF16)
-        out = pltpu.make_async_copy(turned_ref.at[:, pl.ds(at * tile, tile)], turned_hbm.at[:, pl.ds(at * tile, tile)], out_sems.at[at])
+            block = dot_nt(eye, edge_ref[rows, start : start + 256])
+            turned_ref[start : start + 256, rows] = block.astype(BF16)
+        columns = pl.ds(at * tile, tile)
+        out = pltpu.make_async_copy(turned_ref.at[:, columns], turned_hbm.at[:, columns], out_sems.at[at])
         out.start()
         outs.append(out)
-        if at == 0:
-            copies[1].wait()
-            copies[2].wait()
-        base_ref[rows, :] = dot_nn(edge, w1_ref[...]) + dot_nn(hot_ref[rows, :], moved_ref[...])
+    copies[tiles].wait()
+    copies[tiles + 1].wait()
+    for at in range(tiles):
+        rows = slice(at * tile, (at + 1) * tile)
+        base_ref[rows, :] = dot_nn(edge_ref[rows, :], w1_ref[...]) + dot_nn(hot_ref[rows, :], moved_ref[...])
     for out in outs:
         out.wait()
 
@@ -260,7 +262,7 @@
     send_refs, keep_refs, rest = rest[2 : 2 + outer], rest[2 + outer : 2 + 2 * outer], rest[2 + 2 * outer :]
     slope_ref, value_ref, both_ref, grads_ref, slot_grads_ref, ordered_ref = rest[:6]
     slot_ref, dst_ref, mesh_ref, w1_ref, w2_ref, wn1_ref, wn2_ref = rest[6:13]
-    turned_ref, hot_ref, node_ref, cot_ref, mesh_out_ref, picks_ref, sems, out_sems = rest[13:]
+    hot_ref, node_ref, cot_ref, mesh_out_ref, picks_ref, sems, out_sems = rest[13:]
     width = mesh_ref.shape[1]
     mesh_rows = mesh_ref.shape[0]
     slot_rows = ordered_ref.shape[0]
@@ -277,7 +279,7 @@
         (cot_hbm, cot_ref),
         (hot_hbm, hot_ref),
         (wn2_hbm, wn2_ref),
-        (turned_hbm, turned_ref),
+        (turned_hbm, both_ref.at[pl.ds(slot_rows + mesh_rows, width), :]),
     ]
     copies = load(pairs, sems)
     place_rows(sizes, slot_blocks, ordered_ref)
@@ -288,7 +290,7 @@
         rows = slice(at * tile, (at + 1) * tile)
         picks_ref[rows, :] = tile_columns(slot_ref, at, lines, slot_rows)
         both_ref[:slot_rows, rows] = tile_rows(slot_ref, at, lines, slot_rows)
-        both_ref[slot_rows:, rows] = tile_rows(dst_ref, at, lines, mesh_rows)
+        both_ref[slot_rows : slot_rows + mesh_rows, rows] = tile_rows(dst_ref, at, lines, mesh_rows)
     copies[2].wait()
 
     slots = slots_value
@@ -305,7 +307,7 @@
 
     for copy in copies[3:-1]:
         copy.wait()
-    hidden_sums = dot_nn(both_ref[slot_rows:, :], value_ref[...]).astype(BF16)
+    hidden_sums = dot_nn(both_ref[slot_rows : slot_rows + mesh_rows, :], value_ref[...]).astype(BF16)
     received = dot_nn(hidden_sums, w2_ref[...]).astype(BF16)
     mesh = mesh_ref[...]
     pre_node = node_ref[...] + dot_nn(received, wn1_ref[...])
@@ -323,12 +325,13 @@
     grads_ref[3 * width :, :] = dot_tn(hidden_sums, d_received)
     mesh_out_ref[...] = (mesh.astype(F32) + dot_nn(node.astype(BF16), wn2_ref[...])).astype(BF16)
     (mesh_copy,) = load([(mesh_out_ref, mesh_out_hbm)], out_sems)
-    sums = dot_nn(both_ref[...], value_ref[...]).astype(BF16)
+    copies[-1].wait()
+    product = dot_nn(both_ref[...], value_ref[...])
+    sums = product[: slot_rows + mesh_rows].astype(BF16)
+    grads_ref[2 * width : 3 * width, :] = product[slot_rows + mesh_rows :]
     slot_grads_ref[...] = dot_nt(sums[:slot_rows], w1_ref[...])
     grads_ref[:width, :] = dot_tn(slots, sums[:slot_rows])
     grads_ref[width : 2 * width, :] = dot_tn(mesh, sums[slot_rows:])
-    copies[-1].wait()
-    grads_ref[2 * width : 3 * width, :] = dot_nn(turned_ref[...], value_ref[...])
 
     chunk = grads_ref.shape[0] // (2 * outer * inner)
     cap = slot_rows // (2 * outer * inner)
@@ -553,7 +556,7 @@
         scratch_shapes=[
             pltpu.VMEM((edges, hidden_width), F32),
             pltpu.VMEM((edges, hidden_width), BF16),
-            pltpu.VMEM((slot_rows + mesh_rows, edges), BF16),
+            pltpu.VMEM((slot_rows + mesh_rows + width, edges), BF16),
             pltpu.VMEM((grad_rows, hidden_width), F32),
             pltpu.VMEM((slot_rows, width), F32),
             pltpu.VMEM((slot_rows, width), F32),
@@ -564,7 +567,6 @@
             pltpu.VMEM(w_edge2.shape, BF16),
             pltpu.VMEM((w_node1.shape[0] - width, w_node1.shape[1]), BF16),
             pltpu.VMEM(w_node2.shape, BF16),
-            pltpu.VMEM(turned.shape, BF16),
             pltpu.VMEM(hot.shape, BF16),
             pltpu.VMEM(node.shape, F32),
             pltpu.VMEM(cot.shape, F32),
@@ -588,7 +590,6 @@
     for k in [outer - 1, *range(1, outer - 1), 0]:
         send = sends[k] if first is None else lax.optimization_barrier((sends[k], first))[0]
         crossed = to_core(send)
-        first = crossed if first is None else first
         total, mixed, *parts = pl.pallas_call(
             functools.partial(core_kernel, sizes, k),
             out_shape=[
@@ -600,6 +601,7 @@
             cost_estimate=cost(10**9, MIB),
             name="core",
         )(keeps[k], crossed, d_slots)
+        first = parts[0] if first is None else first
         parts = [to_inner(part, at + 1) for at, part in enumerate(parts)]
         block = 2 * inner * cap
         if k:
@@ -621,23 +623,6 @@
                 name="own",
             )(total, mixed, *parts, *[arrived[at] for at in range(1, outer)])
 
-    pieces = {0: own}
-    stride = outer // 2
-    while stride:
-        for at in range(0, outer, 2 * stride):
-            pieces[at + stride] = to_outer(pieces[at], stride)
-        stride //= 2
-    halfway_at = band_count // 2
-    pieces[halfway_at] = to_core(own)
-    for far_inner in range(1, inner):
-        for far_outer in range(outer):
-            value = pieces[far_outer]
-            if far_outer == outer // 2:
-                value = lax.optimization_barrier((value, pieces[halfway_at]))[0]
-            pieces[far_inner * outer + far_outer] = to_inner(value, far_inner)
-    for at in range(1, halfway_at - 1):
-        pieces[halfway_at + at] = to_core(pieces[at])
-
     grid_grad = pl.pallas_call(
         functools.partial(put_kernel, sizes),
         out_shape=jax.ShapeDtypeStruct(grid_latent.shape, F32),
@@ -653,6 +638,26 @@
         name="put",
     )(*pinned(pltpu.HBM, send_rows), home, *[arrived[at] for at in range(1, outer)])
 
+    pieces = {0: own}
+    stride = outer // 2
+    while stride:
+        for at in range(0, outer, 2 * stride):
+            value = pieces[at]
+            if at + stride == 1:
+                value = lax.optimization_barrier((value, grid_grad))[0]
+            pieces[at + stride] = to_outer(value, stride)
+        stride //= 2
+    halfway_at = band_count // 2
+    pieces[halfway_at] = to_core(own)
+    for far_inner in range(1, inner):
+        for far_outer in range(outer):
+            value = pieces[far_outer]
+            if far_outer == outer // 2:
+                value = lax.optimization_barrier((value, pieces[halfway_at]))[0]
+            pieces[far_inner * outer + far_outer] = to_inner(value, far_inner)
+    for at in range(1, halfway_at - 1):
+        pieces[halfway_at + at] = to_core(pieces[at])
+
     last = outer - 1
     stages = [[], [], []]
     for at in range(band_count):
@@ -664,7 +669,7 @@
     grads = []
     for places in stages:
         if places is stages[1]:
-            value = lax.optimization_barrier((pieces[halfway_at - 1], grid_grad, *grads))[0]
+            value = lax.optimization_barrier((pieces[halfway_at - 1], *grads))[0]
             pieces[band_count - 1] = to_core(value)
         grads = pl.pallas_call(
             functools.partial(order_kernel, sizes, places, len(grads)),

time: 72.1 us -> 72.6 us (level)
  waiting for transfers between devices: 22.5 us -> 25 us
  starting transfers between devices: 26.8 us -> 25.1 us
    ppermute x31, waiting for transfers between devices: 22.5 us -> 25 us  [permute(): return lax.ppermute(value, 'band', pairs)]
    ppermute x31, starting transfers between devices: 26.8 us -> 25.1 us  [permute(): return lax.ppermute(value, 'band', pairs)]
  transfers between devices with their start and end apart: 31 -> 31, of which waited for: 13 -> 15; matrix products, arithmetic and copies ran while one was open for 0% -> 0% of each run, Pallas kernels for 17% -> 16%
where the time goes in v9:
time: 72.6 us; the launch traced here: 72.4 us
  starting transfers between devices  25.1 us (35%)
  waiting for transfers between devices  25 us (34%)
  Pallas kernels  21.5 us (30%)
  between operations  0.85 us (1%)
    ppermute x31, starting transfers between devices, permute(): return lax.ppermute(value, 'band', pairs)  25.1 us
    ppermute x31, waiting for transfers between devices, permute(): return lax.ppermute(value, 'band', pairs)  25 us
    pallas_call x1, Pallas kernels, shards(): pl.pallas_call(functools.partial(main_kernel, lines, sizes), out_shape=[j...  7.35 us
    pallas_call x1, Pallas kernels, shards(): pl.pallas_call(functools.partial(base_kernel, lines), out_shape=[pltpu.VM...  3.52 us
    pallas_call x3, Pallas kernels, shards(): pl.pallas_call(functools.partial(order_kernel, sizes, places, len(grads))...  3.46 us
    pallas_call x1, Pallas kernels, shards(): pl.pallas_call(functools.partial(ready_kernel, lines), out_shape=[pltpu.H...  2.8 us
    pallas_call x1, Pallas kernels, shards(): pl.pallas_call(functools.partial(put_kernel, sizes), out_shape=jax.ShapeD...  2.41 us
    pallas_call x1, Pallas kernels, shards(): pl.pallas_call(functools.partial(pick_kernel, sizes), out_shape=[jax.Shap...  1.59 us
  transfers between devices with their start and end apart: 31, of which 15 were waited for; matrix products, arithmetic and copies ran while one was open for 0% of the time, Pallas kernels for 16%

profile of v9, /device:TPU:0, one launch (start us, length us, event | category | flops | bytes accessed | tf_op | source)
XLA Modules:
  0.0 72.4 jit_solution(4005333496107229650)
XLA Ops:
  0.6 1.6 %pick.1 = (bf16[64,512]{1,0:T(8,128)(2,1)S(1)}, bf16[64,512]{1,0:T(8,128)(2,1)S(1)}) custom-call(s32[1,128]{1,0:T(1,128)} %rows_hbm.3, bf16[1024,512]{1,0:T(8,128)(2,1)} %grid_hbm.1), custom_call_target="tpu_custom_call" | custom-call | tf_op jit(solution)/shard_map/pick/pallas_call | solution.py:466
  3.7 2.9 %collective-permute-start.1 = (bf16[64,512]{1,0:T(8,128)(2,1)S(1)}, bf16[64,512]{1,0:T(8,128)(2,1)S(1)}, u32[]{:S(2)}, u32[]{:S(2)}) collective-permute-start(bf16[64,512]{1,0:T(8,128)(2,1)S(1)} %get-tuple-element.63), channel_id=1, source_target_pairs={{0,2},{1,3},{2,0},{3,1},{4,6},{5,7},{6,4},{7,5},{8,10},{9,11},{10,... | collective-permute-start | bytes 196616 | tf_op jit(solution)/shard_map/ppermute | solution.py:454
  6.6 2.8 %ready.1 = (bf16[1536,256]{1,0:T(8,128)(2,1)}, f32[256,512]{1,0:T(8,128)}, f32[256,512]{1,0:T(8,128)}, bf16[256,512]{1,0:T(8,128)(2,1)S(1)}) custom-call(s32[12,128]{1,0:T(8,128)} %bitcast.3, bf16[256,512]{1,0:T(8,128)(2,1)} %mesh_hbm.3, bf16[256,512]{1,0:T(8,128)(2,1)} %cot_hbm.1, bf16[1536,512]{1,0:T(8,128)(2,1)} %w1_hbm.5, bf16[1024,512]{1,0:T(8,128)(2,1)} %wn1_hbm.3, ...), custom_call_target="tpu_custom_call" | custom-call | flops 2000000000 | bytes 4194304 | tf_op jit(solution)/shard_map/ready/pallas_call | solution.py:490
  9.4 1.6 %collective-permute-start.2 = (bf16[32,512]{1,0:T(8,128)(2,1)S(1)}, bf16[32,512]{1,0:T(8,128)(2,1)S(1)}, u32[]{:S(2)}, u32[]{:S(2)}) collective-permute-start(bf16[32,512]{1,0:T(8,128)(2,1)S(1)} %get-tuple-element.65), channel_id=1, source_target_pairs={{0,4},{1,5},{2,6},{3,7},{4,0},{5,1},{6,2},{7,3},{8,12},{9,13},{10,... | collective-permute-start | bytes 98312 | tf_op jit(solution)/shard_map/ppermute | solution.py:454
  11.1 2.6 %collective-permute-start.3 = (bf16[32,512]{1,0:T(8,128)(2,1)S(1)}, bf16[32,512]{1,0:T(8,128)(2,1)S(1)}, u32[]{:S(2)}, u32[]{:S(2)}) collective-permute-start(bf16[32,512]{1,0:T(8,128)(2,1)S(1)} %get-tuple-element.66), channel_id=1, source_target_pairs={{0,8},{1,9},{2,10},{3,11},{4,12},{5,13},{6,14},{7,15},{8,0},{9,1},... | collective-permute-start | bytes 98312 | tf_op jit(solution)/shard_map/ppermute | solution.py:454
  13.9 3.5 %base.1 = (f32[1536,512]{1,0:T(8,128)S(1)}, bf16[512,1536]{1,0:T(8,128)(2,1)}) custom-call(bf16[1536,256]{1,0:T(8,128)(2,1)} %get-tuple-element.54.hot_hbm, bf16[1536,512]{1,0:T(8,128)(2,1)} %edge_hbm.1, bf16[1536,512]{1,0:T(8,128)(2,1)} %w1_hbm.5, bf16[256,512]{1,0:T(8,128)(2,1)S(1)} %get-tuple-element.55.moved_ref), custom_call_target="tpu_custom_call" | custom-call | flops 4000000000 | bytes 4194304 | tf_op jit(solution)/shard_map/base/pallas_call | solution.py:517
  17.4 1.9 %collective-permute-done.4.rest_3_ = bf16[32,512]{1,0:T(8,128)(2,1)S(1)} collective-permute-done((bf16[32,512]{1,0:T(8,128)(2,1)S(1)}, bf16[32,512]{1,0:T(8,128)(2,1)S(1)}, u32[]{:S(2)}, u32[]{:S(2)}) %collective-permute-start.4) | collective-permute-done | bytes 32800 | tf_op jit(solution)/shard_map/ppermute | solution.py:454
  19.4 7.3 %edges.1 = (bf16[256,512]{1,0:T(8,128)(2,1)}, bf16[64,512]{1,0:T(8,128)(2,1)S(1)}, bf16[272,512]{1,0:T(8,128)(2,1)S(1)}, bf16[272,512]{1,0:T(8,128)(2,1)S(1)}, b...) custom-call(s32[12,128]{1,0:T(8,128)} %bitcast.2, ...), custom_call_target="tpu_custom_call" | custom-call | tf_op jit(solution)/shard_map/edges/pallas_call | solution.py:546
  26.8 1.5 %collective-permute-done.5.crossed_ref = bf16[272,512]{1,0:T(8,128)(2,1)S(1)} collective-permute-done((bf16[272,512]{1,0:T(8,128)(2,1)S(1)}, bf16[272,512]{1,0:T(8,128)(2,1)S(1)}, u32[]{:S(2)}, u32[]{:S(2)}) %collective-permute-start.5) | collective-permute-done | bytes 278560 | tf_op jit(solution)/shard_map/ppermute | solution.py:454
  29.0 1.4 %collective-permute-start.14 = (bf16[144,512]{1,0:T(8,128)(2,1)S(1)}, bf16[144,512]{1,0:T(8,128)(2,1)S(1)}, u32[]{:S(2)}, u32[]{:S(2)}) collective-permute-start(bf16[144,512]{1,0:T(8,128)(2,1)S(1)} %get-tuple-element.74), channel_id=1, source_target_pairs={{0,2},{1,3},{2,0},{3,1},{4,6},{5,7},{6,4},{7,5},{8,10},{9,11},{10,... | collective-permute-start | bytes 442376 | tf_op jit(solution)/shard_map/ppermute | solution.py:454
  32.7 3.0 %collective-permute-done.14.refs_0_ = bf16[144,512]{1,0:T(8,128)(2,1)S(1)} collective-permute-done((bf16[144,512]{1,0:T(8,128)(2,1)S(1)}, bf16[144,512]{1,0:T(8,128)(2,1)S(1)}, u32[]{:S(2)}, u32[]{:S(2)}) %collective-permute-start.14) | collective-permute-done | bytes 147488 | tf_op jit(solution)/shard_map/ppermute | solution.py:454
  35.7 1.7 %collective-permute-start.15 = (bf16[160,512]{1,0:T(8,128)(2,1)S(1)}, bf16[160,512]{1,0:T(8,128)(2,1)S(1)}, u32[]{:S(2)}, u32[]{:S(2)}) collective-permute-start(bf16[160,512]{1,0:T(8,128)(2,1)S(1)} %inner.5), channel_id=1, source_target_pairs={{0,12},{1,13},{2,14},{3,15},{4,8},{5,9},{6,10},{7,11},{8,4},{9,5},... | collective-permute-start | bytes 491528 | tf_op jit(solution)/shard_map/ppermute | solution.py:454
  38.9 2.3 %collective-permute-done.9.refs_0_ = bf16[144,512]{1,0:T(8,128)(2,1)S(1)} collective-permute-done((bf16[144,512]{1,0:T(8,128)(2,1)S(1)}, bf16[144,512]{1,0:T(8,128)(2,1)S(1)}, u32[]{:S(2)}, u32[]{:S(2)}) %collective-permute-start.9) | collective-permute-done | bytes 147488 | tf_op jit(solution)/shard_map/ppermute | solution.py:454
  41.4 1.5 %collective-permute-start.7 = (bf16[144,512]{1,0:T(8,128)(2,1)S(1)}, bf16[144,512]{1,0:T(8,128)(2,1)S(1)}, u32[]{:S(2)}, u32[]{:S(2)}) collective-permute-start(bf16[144,512]{1,0:T(8,128)(2,1)S(1)} %get-tuple-element.78), channel_id=1, source_target_pairs={{0,2},{1,3},{2,0},{3,1},{4,6},{5,7},{6,4},{7,5},{8,10},{9,11},{10,... | collective-permute-start | bytes 442376 | tf_op jit(solution)/shard_map/ppermute | solution.py:454
  42.9 1.8 %collective-permute-done.15.refs_3_ = bf16[160,512]{1,0:T(8,128)(2,1)S(1)} collective-permute-done((bf16[160,512]{1,0:T(8,128)(2,1)S(1)}, bf16[160,512]{1,0:T(8,128)(2,1)S(1)}, u32[]{:S(2)}, u32[]{:S(2)}) %collective-permute-start.15) | collective-permute-done | bytes 163872 | tf_op jit(solution)/shard_map/ppermute | solution.py:454
  44.7 1.9 %collective-permute-done.7.refs_0_ = bf16[144,512]{1,0:T(8,128)(2,1)S(1)} collective-permute-done((bf16[144,512]{1,0:T(8,128)(2,1)S(1)}, bf16[144,512]{1,0:T(8,128)(2,1)S(1)}, u32[]{:S(2)}, u32[]{:S(2)}) %collective-permute-start.7) | collective-permute-done | bytes 147488 | tf_op jit(solution)/shard_map/ppermute | solution.py:454
  46.6 3.3 %collective-permute-done.13.refs_2_ = bf16[160,512]{1,0:T(8,128)(2,1)S(1)} collective-permute-done((bf16[160,512]{1,0:T(8,128)(2,1)S(1)}, bf16[160,512]{1,0:T(8,128)(2,1)S(1)}, u32[]{:S(2)}, u32[]{:S(2)}) %collective-permute-start.13) | collective-permute-done | bytes 163872 | tf_op jit(solution)/shard_map/ppermute | solution.py:454
  51.2 2.4 %put.1 = f32[1024,512]{1,0:T(8,128)} custom-call(s32[1,128]{1,0:T(1,128)} %rows_hbm.3, bf16[32,512]{1,0:T(8,128)(2,1)S(1)} %get-tuple-element.93.refs_0_, bf16[160,512]{1,0:T(8,128)(2,1)S(1)} %collective-permute-done.10.refs_1_, bf16[160,512]{1,0:T(8,128)(2,1)S(1)} %collective-permute-done.13.refs_2_, bf16[160,512]{1,0:T(8,128)(2,1)S(1)} %collective-permute-done.15.refs_3_), custom_call_target="tpu_custom_call" | custom-call | flops 2000000000 | bytes 2097152 | tf_op jit(solution)/shard_map/put/pallas_call | solution.py:626
  53.7 2.2 %collective-permute-start.19 = (bf16[128,512]{1,0:T(8,128)(2,1)S(1)}, bf16[128,512]{1,0:T(8,128)(2,1)S(1)}, u32[]{:S(2)}, u32[]{:S(2)}) collective-permute-start(bf16[128,512]{1,0:T(8,128)(2,1)S(1)} %get-tuple-element.95.refs_0_), channel_id=1, source_target_pairs={{0,4},{1,5},{2,6},{3,7},{4,0},{5,1},{6,2},{7,3},{8,12},{9,13},{10,... | collective-permute-start | bytes 393224 | tf_op jit(solution)/shard_map/ppermute | solution.py:454
  57.3 1.4 %collective-permute-done.16.refs_2_ = bf16[128,512]{1,0:T(8,128)(2,1)S(1)} collective-permute-done((bf16[128,512]{1,0:T(8,128)(2,1)S(1)}, bf16[128,512]{1,0:T(8,128)(2,1)S(1)}, u32[]{:S(2)}, u32[]{:S(2)}) %collective-permute-start.16) | collective-permute-done | bytes 131104 | tf_op jit(solution)/shard_map/ppermute | solution.py:454
  58.7 1.4 %collective-permute-start.26 = (bf16[128,512]{1,0:T(8,128)(2,1)S(1)}, bf16[128,512]{1,0:T(8,128)(2,1)S(1)}, u32[]{:S(2)}, u32[]{:S(2)}) collective-permute-start(bf16[128,512]{1,0:T(8,128)(2,1)S(1)} %collective-permute-done.16.refs_2_), channel_id=1, source_target_pairs={{0,2},{1,3},{2,0},{3,1},{4,6},{5,7},{6,4},{7,5},{8,10},{9,11},{10,... | collective-permute-start | bytes 393224 | tf_op jit(solution)/shard_map/ppermute | solution.py:454
  61.4 1.4 %collective-permute-start.21 = (bf16[128,512]{1,0:T(8,128)(2,1)S(1)}, bf16[128,512]{1,0:T(8,128)(2,1)S(1)}, u32[]{:S(2)}, u32[]{:S(2)}) collective-permute-start(bf16[128,512]{1,0:T(8,128)(2,1)S(1)} %collective-permute-done.19.refs_1_), channel_id=1, source_target_pairs={{0,2},{1,3},{2,0},{3,1},{4,6},{5,7},{6,4},{7,5},{8,10},{9,11},{10,... | collective-permute-start | bytes 393224 | tf_op jit(solution)/shard_map/ppermute | solution.py:454
  64.2 1.4 %collective-permute-start.18 = (bf16[128,512]{1,0:T(8,128)(2,1)S(1)}, bf16[128,512]{1,0:T(8,128)(2,1)S(1)}, u32[]{:S(2)}, u32[]{:S(2)}) collective-permute-start(bf16[128,512]{1,0:T(8,128)(2,1)S(1)} %collective-permute-done.17.refs_0_), channel_id=1, source_target_pairs={{0,2},{1,3},{2,0},{3,1},{4,6},{5,7},{6,4},{7,5},{8,10},{9,11},{10,... | collective-permute-start | bytes 393224 | tf_op jit(solution)/shard_map/ppermute | solution.py:454
  65.7 2.1 %collective-permute-done.21.refs_4_ = bf16[128,512]{1,0:T(8,128)(2,1)S(1)} collective-permute-done((bf16[128,512]{1,0:T(8,128)(2,1)S(1)}, bf16[128,512]{1,0:T(8,128)(2,1)S(1)}, u32[]{:S(2)}, u32[]{:S(2)}) %collective-permute-start.21) | collective-permute-done | bytes 131104 | tf_op jit(solution)/shard_map/ppermute | solution.py:454
  (56 shorter events, 16.2 us)
Async XLA Ops:
  3.7 5.7 %collective-permute-start.1 = (bf16[64,512]{1,0:T(8,128)(2,1)S(1)}, bf16[64,512]{1,0:T(8,128)(2,1)S(1)}, u32[]{:S(2)}, u32[]{:S(2)}) collective-permute-start(bf16[64,512]{1,0:T(8,128)(2,1)S(1)} %get-tuple-element.63), channel_id=1, source_target_pairs={{0,2},{1,3},{2,0},{3,1},{4,6},{5,7},{6,4},{7,5},{8,10},{9,11},{10,... | collective-permute-start | bytes 196616 | tf_op jit(solution)/shard_map/ppermute | solution.py:454
  9.4 8.0 %collective-permute-start.2 = (bf16[32,512]{1,0:T(8,128)(2,1)S(1)}, bf16[32,512]{1,0:T(8,128)(2,1)S(1)}, u32[]{:S(2)}, u32[]{:S(2)}) collective-permute-start(bf16[32,512]{1,0:T(8,128)(2,1)S(1)} %get-tuple-element.65), channel_id=1, source_target_pairs={{0,4},{1,5},{2,6},{3,7},{4,0},{5,1},{6,2},{7,3},{8,12},{9,13},{10,... | collective-permute-start | bytes 98312 | tf_op jit(solution)/shard_map/ppermute | solution.py:454
  11.1 6.3 %collective-permute-start.3 = (bf16[32,512]{1,0:T(8,128)(2,1)S(1)}, bf16[32,512]{1,0:T(8,128)(2,1)S(1)}, u32[]{:S(2)}, u32[]{:S(2)}) collective-permute-start(bf16[32,512]{1,0:T(8,128)(2,1)S(1)} %get-tuple-element.66), channel_id=1, source_target_pairs={{0,8},{1,9},{2,10},{3,11},{4,12},{5,13},{6,14},{7,15},{8,0},{9,1},... | collective-permute-start | bytes 98312 | tf_op jit(solution)/shard_map/ppermute | solution.py:454
  13.7 5.7 %collective-permute-start.4 = (bf16[32,512]{1,0:T(8,128)(2,1)S(1)}, bf16[32,512]{1,0:T(8,128)(2,1)S(1)}, u32[]{:S(2)}, u32[]{:S(2)}) collective-permute-start(bf16[32,512]{1,0:T(8,128)(2,1)S(1)} %get-tuple-element.67), channel_id=1, source_target_pairs={{0,12},{1,13},{2,14},{3,15},{4,8},{5,9},{6,10},{7,11},{8,4},{9,5},... | collective-permute-start | bytes 98312 | tf_op jit(solution)/shard_map/ppermute | solution.py:454
  28.6 3.0 %collective-permute-start.8 = (bf16[272,512]{1,0:T(8,128)(2,1)S(1)}, bf16[272,512]{1,0:T(8,128)(2,1)S(1)}, u32[]{:S(2)}, u32[]{:S(2)}) collective-permute-start(bf16[272,512]{1,0:T(8,128)(2,1)S(1)} %get-tuple-element.81), channel_id=1, source_target_pairs={{0,1},{1,0},{2,3},{3,2},{4,5},{5,4},{6,7},{7,6},{8,9},{9,8},{10,11... | collective-permute-start | bytes 835592 | tf_op jit(solution)/shard_map/ppermute | solution.py:454
  29.0 6.7 %collective-permute-start.14 = (bf16[144,512]{1,0:T(8,128)(2,1)S(1)}, bf16[144,512]{1,0:T(8,128)(2,1)S(1)}, u32[]{:S(2)}, u32[]{:S(2)}) collective-permute-start(bf16[144,512]{1,0:T(8,128)(2,1)S(1)} %get-tuple-element.74), channel_id=1, source_target_pairs={{0,2},{1,3},{2,0},{3,1},{4,6},{5,7},{6,4},{7,5},{8,10},{9,11},{10,... | collective-permute-start | bytes 442376 | tf_op jit(solution)/shard_map/ppermute | solution.py:454
  30.4 10.9 %collective-permute-start.6 = (bf16[272,512]{1,0:T(8,128)(2,1)S(1)}, bf16[272,512]{1,0:T(8,128)(2,1)S(1)}, u32[]{:S(2)}, u32[]{:S(2)}) collective-permute-start(bf16[272,512]{1,0:T(8,128)(2,1)S(1)} %get-tuple-element.75), channel_id=1, source_target_pairs={{0,1},{1,0},{2,3},{3,2},{4,5},{5,4},{6,7},{7,6},{8,9},{9,8},{10,11... | collective-permute-start | bytes 835592 | tf_op jit(solution)/shard_map/ppermute | solution.py:454
  30.5 8.4 %collective-permute-start.12 = (bf16[144,512]{1,0:T(8,128)(2,1)S(1)}, bf16[144,512]{1,0:T(8,128)(2,1)S(1)}, u32[]{:S(2)}, u32[]{:S(2)}) collective-permute-start(bf16[144,512]{1,0:T(8,128)(2,1)S(1)} %get-tuple-element.90), channel_id=1, source_target_pairs={{0,2},{1,3},{2,0},{3,1},{4,6},{5,7},{6,4},{7,5},{8,10},{9,11},{10,... | collective-permute-start | bytes 442376 | tf_op jit(solution)/shard_map/ppermute | solution.py:454
  31.6 9.6 %collective-permute-start.9 = (bf16[144,512]{1,0:T(8,128)(2,1)S(1)}, bf16[144,512]{1,0:T(8,128)(2,1)S(1)}, u32[]{:S(2)}, u32[]{:S(2)}) collective-permute-start(bf16[144,512]{1,0:T(8,128)(2,1)S(1)} %get-tuple-element.84), channel_id=1, source_target_pairs={{0,2},{1,3},{2,0},{3,1},{4,6},{5,7},{6,4},{7,5},{8,10},{9,11},{10,... | collective-permute-start | bytes 442376 | tf_op jit(solution)/shard_map/ppermute | solution.py:454
  35.7 9.0 %collective-permute-start.15 = (bf16[160,512]{1,0:T(8,128)(2,1)S(1)}, bf16[160,512]{1,0:T(8,128)(2,1)S(1)}, u32[]{:S(2)}, u32[]{:S(2)}) collective-permute-start(bf16[160,512]{1,0:T(8,128)(2,1)S(1)} %inner.5), channel_id=1, source_target_pairs={{0,12},{1,13},{2,14},{3,15},{4,8},{5,9},{6,10},{7,11},{8,4},{9,5},... | collective-permute-start | bytes 491528 | tf_op jit(solution)/shard_map/ppermute | solution.py:454
  38.9 11.1 %collective-permute-start.13 = (bf16[160,512]{1,0:T(8,128)(2,1)S(1)}, bf16[160,512]{1,0:T(8,128)(2,1)S(1)}, u32[]{:S(2)}, u32[]{:S(2)}) collective-permute-start(bf16[160,512]{1,0:T(8,128)(2,1)S(1)} %inner.4), channel_id=1, source_target_pairs={{0,8},{1,9},{2,10},{3,11},{4,12},{5,13},{6,14},{7,15},{8,0},{9,1},... | collective-permute-start | bytes 491528 | tf_op jit(solution)/shard_map/ppermute | solution.py:454
  41.2 9.8 %collective-permute-start.10 = (bf16[160,512]{1,0:T(8,128)(2,1)S(1)}, bf16[160,512]{1,0:T(8,128)(2,1)S(1)}, u32[]{:S(2)}, u32[]{:S(2)}) collective-permute-start(bf16[160,512]{1,0:T(8,128)(2,1)S(1)} %inner.3), channel_id=1, source_target_pairs={{0,4},{1,5},{2,6},{3,7},{4,0},{5,1},{6,2},{7,3},{8,12},{9,13},{10,... | collective-permute-start | bytes 491528 | tf_op jit(solution)/shard_map/ppermute | solution.py:454
  41.4 5.2 %collective-permute-start.7 = (bf16[144,512]{1,0:T(8,128)(2,1)S(1)}, bf16[144,512]{1,0:T(8,128)(2,1)S(1)}, u32[]{:S(2)}, u32[]{:S(2)}) collective-permute-start(bf16[144,512]{1,0:T(8,128)(2,1)S(1)} %get-tuple-element.78), channel_id=1, source_target_pairs={{0,2},{1,3},{2,0},{3,1},{4,6},{5,7},{6,4},{7,5},{8,10},{9,11},{10,... | collective-permute-start | bytes 442376 | tf_op jit(solution)/shard_map/ppermute | solution.py:454
  51.1 7.6 %collective-permute-start.16 = (bf16[128,512]{1,0:T(8,128)(2,1)S(1)}, bf16[128,512]{1,0:T(8,128)(2,1)S(1)}, u32[]{:S(2)}, u32[]{:S(2)}) collective-permute-start(bf16[128,512]{1,0:T(8,128)(2,1)S(1)} %get-tuple-element.95.refs_0_), channel_id=1, source_target_pairs={{0,8},{1,9},{2,10},{3,11},{4,12},{5,13},{6,14},{7,15},{8,0},{9,1},... | collective-permute-start | bytes 393224 | tf_op jit(solution)/shard_map/ppermute | solution.py:454
  51.2 7.6 %collective-permute-start.22 = (bf16[128,512]{1,0:T(8,128)(2,1)S(1)}, bf16[128,512]{1,0:T(8,128)(2,1)S(1)}, u32[]{:S(2)}, u32[]{:S(2)}) collective-permute-start(bf16[128,512]{1,0:T(8,128)(2,1)S(1)} %get-tuple-element.95.refs_0_), channel_id=1, source_target_pairs={{0,1},{1,0},{2,3},{3,2},{4,5},{5,4},{6,7},{7,6},{8,9},{9,8},{10,11... | collective-permute-start | bytes 393224 | tf_op jit(solution)/shard_map/ppermute | solution.py:454
  53.7 7.8 %collective-permute-start.19 = (bf16[128,512]{1,0:T(8,128)(2,1)S(1)}, bf16[128,512]{1,0:T(8,128)(2,1)S(1)}, u32[]{:S(2)}, u32[]{:S(2)}) collective-permute-start(bf16[128,512]{1,0:T(8,128)(2,1)S(1)} %get-tuple-element.95.refs_0_), channel_id=1, source_target_pairs={{0,4},{1,5},{2,6},{3,7},{4,0},{5,1},{6,2},{7,3},{8,12},{9,13},{10,... | collective-permute-start | bytes 393224 | tf_op jit(solution)/shard_map/ppermute | solution.py:454
  55.9 7.0 %collective-permute-start.20 = (bf16[128,512]{1,0:T(8,128)(2,1)S(1)}, bf16[128,512]{1,0:T(8,128)(2,1)S(1)}, u32[]{:S(2)}, u32[]{:S(2)}) collective-permute-start(bf16[128,512]{1,0:T(8,128)(2,1)S(1)} %get-tuple-element.95.refs_0_), channel_id=1, source_target_pairs={{0,2},{1,3},{2,0},{3,1},{4,6},{5,7},{6,4},{7,5},{8,10},{9,11},{10,... | collective-permute-start | bytes 393224 | tf_op jit(solution)/shard_map/ppermute | solution.py:454
  58.7 5.5 %collective-permute-start.17 = (bf16[128,512]{1,0:T(8,128)(2,1)S(1)}, bf16[128,512]{1,0:T(8,128)(2,1)S(1)}, u32[]{:S(2)}, u32[]{:S(2)}) collective-permute-start(bf16[128,512]{1,0:T(8,128)(2,1)S(1)} %collective-permute-done.16.refs_2_), channel_id=1, source_target_pairs={{0,4},{1,5},{2,6},{3,7},{4,0},{5,1},{6,2},{7,3},{8,12},{9,13},{10,... | collective-permute-start | bytes 393224 | tf_op jit(solution)/shard_map/ppermute | solution.py:454
  58.7 6.9 %collective-permute-start.26 = (bf16[128,512]{1,0:T(8,128)(2,1)S(1)}, bf16[128,512]{1,0:T(8,128)(2,1)S(1)}, u32[]{:S(2)}, u32[]{:S(2)}) collective-permute-start(bf16[128,512]{1,0:T(8,128)(2,1)S(1)} %collective-permute-done.16.refs_2_), channel_id=1, source_target_pairs={{0,2},{1,3},{2,0},{3,1},{4,6},{5,7},{6,4},{7,5},{8,10},{9,11},{10,... | collective-permute-start | bytes 393224 | tf_op jit(solution)/shard_map/ppermute | solution.py:454
  61.4 6.4 %collective-permute-start.21 = (bf16[128,512]{1,0:T(8,128)(2,1)S(1)}, bf16[128,512]{1,0:T(8,128)(2,1)S(1)}, u32[]{:S(2)}, u32[]{:S(2)}) collective-permute-start(bf16[128,512]{1,0:T(8,128)(2,1)S(1)} %collective-permute-done.19.refs_1_), channel_id=1, source_target_pairs={{0,2},{1,3},{2,0},{3,1},{4,6},{5,7},{6,4},{7,5},{8,10},{9,11},{10,... | collective-permute-start | bytes 393224 | tf_op jit(solution)/shard_map/ppermute | solution.py:454
  62.9 4.9 %collective-permute-start.23 = (bf16[128,512]{1,0:T(8,128)(2,1)S(1)}, bf16[128,512]{1,0:T(8,128)(2,1)S(1)}, u32[]{:S(2)}, u32[]{:S(2)}) collective-permute-start(bf16[128,512]{1,0:T(8,128)(2,1)S(1)} %collective-permute-done.19.refs_1_), channel_id=1, source_target_pairs={{0,1},{1,0},{2,3},{3,2},{4,5},{5,4},{6,7},{7,6},{8,9},{9,8},{10,11... | collective-permute-start | bytes 393224 | tf_op jit(solution)/shard_map/ppermute | solution.py:454
  62.9 5.4 %collective-permute-start.24 = (bf16[128,512]{1,0:T(8,128)(2,1)S(1)}, bf16[128,512]{1,0:T(8,128)(2,1)S(1)}, u32[]{:S(2)}, u32[]{:S(2)}) collective-permute-start(bf16[128,512]{1,0:T(8,128)(2,1)S(1)} %collective-permute-done.16.refs_2_), channel_id=1, source_target_pairs={{0,1},{1,0},{2,3},{3,2},{4,5},{5,4},{6,7},{7,6},{8,9},{9,8},{10,11... | collective-permute-start | bytes 393224 | tf_op jit(solution)/shard_map/ppermute | solution.py:454
  64.2 5.7 %collective-permute-start.18 = (bf16[128,512]{1,0:T(8,128)(2,1)S(1)}, bf16[128,512]{1,0:T(8,128)(2,1)S(1)}, u32[]{:S(2)}, u32[]{:S(2)}) collective-permute-start(bf16[128,512]{1,0:T(8,128)(2,1)S(1)} %collective-permute-done.17.refs_0_), channel_id=1, source_target_pairs={{0,2},{1,3},{2,0},{3,1},{4,6},{5,7},{6,4},{7,5},{8,10},{9,11},{10,... | collective-permute-start | bytes 393224 | tf_op jit(solution)/shard_map/ppermute | solution.py:454
  65.7 4.6 %collective-permute-start.28 = (bf16[128,512]{1,0:T(8,128)(2,1)S(1)}, bf16[128,512]{1,0:T(8,128)(2,1)S(1)}, u32[]{:S(2)}, u32[]{:S(2)}) collective-permute-start(bf16[128,512]{1,0:T(8,128)(2,1)S(1)} %collective-permute-done.20.refs_3_), channel_id=1, source_target_pairs={{0,1},{1,0},{2,3},{3,2},{4,5},{5,4},{6,7},{7,6},{8,9},{9,8},{10,11... | collective-permute-start | bytes 393224 | tf_op jit(solution)/shard_map/ppermute | solution.py:454
  (7 other events, 13.7 us)

commit v10 on v9

--- a/solution.py
+++ b/solution.py
@@ -92,11 +92,14 @@
 
 def pick_kernel(sizes, rows_hbm, grid_hbm, keep_ref, send_ref, rows_ref, grid_ref, picked_ref, sems):
     outer, inner = sizes
-    rows_copy, grid_copy = load([(rows_hbm, rows_ref), (grid_hbm, grid_ref)], sems)
-    rows_copy.wait()
+    block = grid_ref.shape[0] // 4
+    parts = [pl.ds(at * block, block) for at in range(4)]
+    copies = load([(rows_hbm, rows_ref)] + [(grid_hbm.at[part, :], grid_ref.at[part, :]) for part in parts], sems)
+    copies[0].wait()
     picked = picked_ref.shape[0]
     chosen = [one_hot_columns(rows_ref[:, at : at + 128], grid_ref.shape[0]) for at in range(0, picked, 128)]
-    grid_copy.wait()
+    for copy in copies[1:]:
+        copy.wait()
     for at, some in enumerate(chosen):
         picked_ref[at * 128 : (at + 1) * 128, :] = dot_nn(some, grid_ref[...])
     cap = picked // (2 * outer * inner)
@@ -201,8 +204,13 @@
     hot_hbm,
     edge_hbm,
     w1_hbm,
+    slot_hbm,
+    dst_hbm,
     moved_ref,
     base_ref,
+    slot_ref,
+    dst_ref,
+    top_ref,
     turned_hbm,
     hot_ref,
     edge_ref,
@@ -216,6 +224,7 @@
     tiles = edge_ref.shape[0] // tile
     pairs = [(edge_hbm.at[pl.ds(at * tile, tile), :], edge_ref.at[pl.ds(at * tile, tile), :]) for at in range(tiles)]
     pairs += [(w1_hbm.at[pl.ds(2 * width, width), :], w1_ref), (hot_hbm, hot_ref)]
+    pairs += [(w1_hbm.at[pl.ds(0, width), :], top_ref), (slot_hbm, slot_ref), (dst_hbm, dst_ref)]
     copies = load(pairs, sems)
     same = lax.broadcasted_iota(jnp.int32, (256, 256), 0) == lax.broadcasted_iota(jnp.int32, (256, 256), 1)
     eye = jnp.where(same, 1.0, 0.0).astype(BF16)
@@ -235,63 +244,54 @@
     for at in range(tiles):
         rows = slice(at * tile, (at + 1) * tile)
         base_ref[rows, :] = dot_nn(edge_ref[rows, :], w1_ref[...]) + dot_nn(hot_ref[rows, :], moved_ref[...])
-    for out in outs:
+    for out in outs + copies[tiles + 2 :]:
         out.wait()
 
 
 def main_kernel(
     lines,
     sizes,
-    slot_hbm,
-    dst_hbm,
     mesh_hbm,
-    w1_hbm,
     w2_hbm,
     wn1_hbm,
-    wn2_hbm,
     turned_hbm,
     hot_hbm,
     node_hbm,
     cot_hbm,
     base_ref,
+    slot_ref,
+    dst_ref,
+    w1_ref,
     *rest,
 ):
     outer, inner = sizes
     slot_blocks, rest = rest[:outer], rest[outer:]
-    mesh_out_hbm, d_slots_ref = rest[:2]
+    node_out_ref, d_slots_ref = rest[:2]
     send_refs, keep_refs, rest = rest[2 : 2 + outer], rest[2 + outer : 2 + 2 * outer], rest[2 + 2 * outer :]
     slope_ref, value_ref, both_ref, grads_ref, slot_grads_ref, ordered_ref = rest[:6]
-    slot_ref, dst_ref, mesh_ref, w1_ref, w2_ref, wn1_ref, wn2_ref = rest[6:13]
-    hot_ref, node_ref, cot_ref, mesh_out_ref, picks_ref, sems, out_sems = rest[13:]
+    mesh_ref, w2_ref, wn1_ref, hot_ref, node_ref, cot_ref, picks_ref, sems = rest[6:]
     width = mesh_ref.shape[1]
     mesh_rows = mesh_ref.shape[0]
     slot_rows = ordered_ref.shape[0]
     tile = lines * 128
     tiles = base_ref.shape[0] // tile
     pairs = [
-        (slot_hbm, slot_ref),
-        (dst_hbm, dst_ref),
-        (w1_hbm.at[pl.ds(0, width), :], w1_ref),
         (w2_hbm, w2_ref),
         (wn1_hbm.at[pl.ds(width, wn1_ref.shape[0]), :], wn1_ref),
         (mesh_hbm, mesh_ref),
         (node_hbm, node_ref),
         (cot_hbm, cot_ref),
         (hot_hbm, hot_ref),
-        (wn2_hbm, wn2_ref),
         (turned_hbm, both_ref.at[pl.ds(slot_rows + mesh_rows, width), :]),
     ]
     copies = load(pairs, sems)
     place_rows(sizes, slot_blocks, ordered_ref)
     slots_value = ordered_ref[...].astype(BF16)
-    for copy in copies[:2]:
-        copy.wait()
     for at in range(tiles):
         rows = slice(at * tile, (at + 1) * tile)
         picks_ref[rows, :] = tile_columns(slot_ref, at, lines, slot_rows)
         both_ref[:slot_rows, rows] = tile_rows(slot_ref, at, lines, slot_rows)
         both_ref[slot_rows : slot_rows + mesh_rows, rows] = tile_rows(dst_ref, at, lines, mesh_rows)
-    copies[2].wait()
 
     slots = slots_value
     slot_pair = jnp.concatenate(split(dot_nn(slots, w1_ref[...])), axis=0)
@@ -305,7 +305,7 @@
         slope_ref[rows, :] = sigma + hidden * (1.0 - sigma)
         value_ref[rows, :] = hidden.astype(BF16)
 
-    for copy in copies[3:-1]:
+    for copy in copies[:-1]:
         copy.wait()
     hidden_sums = dot_nn(both_ref[slot_rows : slot_rows + mesh_rows, :], value_ref[...]).astype(BF16)
     received = dot_nn(hidden_sums, w2_ref[...]).astype(BF16)
@@ -323,8 +323,7 @@
         value_ref[rows, :] = (dot_nn(hot_ref[rows, :], spread) * slope_ref[rows, :]).astype(BF16)
 
     grads_ref[3 * width :, :] = dot_tn(hidden_sums, d_received)
-    mesh_out_ref[...] = (mesh.astype(F32) + dot_nn(node.astype(BF16), wn2_ref[...])).astype(BF16)
-    (mesh_copy,) = load([(mesh_out_ref, mesh_out_hbm)], out_sems)
+    node_out_ref[...] = node.astype(BF16)
     copies[-1].wait()
     product = dot_nn(both_ref[...], value_ref[...])
     sums = product[: slot_rows + mesh_rows].astype(BF16)
@@ -353,7 +352,12 @@
     for far_outer, send_ref in enumerate(send_refs):
         start = halfway + far_outer * share
         send_ref[inner * chunk :, :] = ordered_ref[start : start + share, :].astype(BF16)
-    mesh_copy.wait()
+
+
+def mesh_kernel(mesh_hbm, wn2_hbm, node_ref, out_ref, mesh_ref, wn2_ref, sems):
+    for copy in load([(mesh_hbm, mesh_ref), (wn2_hbm, wn2_ref)], sems):
+        copy.wait()
+    out_ref[...] = (mesh_ref[...].astype(F32) + dot_nn(node_ref[...], wn2_ref[...])).astype(BF16)
 
 
 def core_kernel(sizes, far_outer, keep_ref, crossed_ref, d_slots_ref, total_ref, mixed_ref, *part_refs):
@@ -472,7 +476,7 @@
             pltpu.VMEM(send_rows.shape, jnp.int32),
             pltpu.VMEM(grid_latent.shape, BF16),
             pltpu.VMEM((slot_rows, width), F32),
-            pltpu.SemaphoreType.DMA((2,)),
+            pltpu.SemaphoreType.DMA((5,)),
         ],
         compiler_params=params(16),
         name="pick",
@@ -514,26 +518,29 @@
         cost_estimate=cost(2 * 10**9, 4 * MIB),
         name="ready",
     )(*pinned(pltpu.HBM, dst_index, mesh_latent, mesh_cot, w_edge1, w_node1, w_node2))
-    base, turned = pl.pallas_call(
+    base, *ahead, turned = pl.pallas_call(
         functools.partial(base_kernel, lines),
         out_shape=[
             pltpu.VMEM((edges, hidden_width), F32),
+            pltpu.VMEM(slot_index.shape, jnp.int32),
+            pltpu.VMEM(dst_index.shape, jnp.int32),
+            pltpu.VMEM((width, hidden_width), BF16),
             pltpu.HBM((width, edges), BF16),
         ],
-        in_specs=specs(pltpu.HBM, 3) + specs(pltpu.VMEM, 1),
-        out_specs=specs(pltpu.VMEM, 1) + specs(pltpu.HBM, 1),
+        in_specs=specs(pltpu.HBM, 5) + specs(pltpu.VMEM, 1),
+        out_specs=specs(pltpu.VMEM, 4) + specs(pltpu.HBM, 1),
         scratch_shapes=[
             pltpu.VMEM((edges, mesh_rows), BF16),
             pltpu.VMEM(edge_latent.shape, BF16),
             pltpu.VMEM((width, hidden_width), BF16),
             pltpu.VMEM((width, edges), BF16),
-            pltpu.SemaphoreType.DMA((2 + edges // (128 * lines),)),
+            pltpu.SemaphoreType.DMA((5 + edges // (128 * lines),)),
             pltpu.SemaphoreType.DMA((edges // (128 * lines),)),
         ],
         compiler_params=params(16),
         cost_estimate=cost(4 * 10**9, 4 * MIB),
         name="base",
-    )(*pinned(pltpu.HBM, hot, edge_latent, w_edge1), *pinned(pltpu.VMEM, moved))
+    )(*pinned(pltpu.HBM, hot, edge_latent, w_edge1, slot_index, dst_index), *pinned(pltpu.VMEM, moved))
 
     by_inner = mix([kept, to_core(sent)], inner, outer)
     by_inner = [by_inner[0]] + [to_inner(by_inner[k], k) for k in range(1, inner)]
@@ -543,7 +550,7 @@
     grad_rows = 3 * width + hidden_width
     chunk = grad_rows // band_count
     group = (inner * chunk, hidden_width)
-    mesh_out, d_slots, *sides = pl.pallas_call(
+    node_out, d_slots, *sides = pl.pallas_call(
         functools.partial(main_kernel, lines, sizes),
         out_shape=[
             jax.ShapeDtypeStruct((mesh_rows, width), BF16),
@@ -551,8 +558,8 @@
         ]
         + [jax.ShapeDtypeStruct((group[0] + inner * cap, hidden_width), BF16)] * outer
         + [jax.ShapeDtypeStruct(group, F32)] * outer,
-        in_specs=specs(pltpu.HBM, 11) + specs(pltpu.VMEM, 1 + outer),
-        out_specs=specs(pltpu.HBM, 1) + specs(pltpu.VMEM, 1 + 2 * outer),
+        in_specs=specs(pltpu.HBM, 7) + specs(pltpu.VMEM, 4 + outer),
+        out_specs=specs(pltpu.VMEM, 2 + 2 * outer),
         scratch_shapes=[
             pltpu.VMEM((edges, hidden_width), F32),
             pltpu.VMEM((edges, hidden_width), BF16),
@@ -560,29 +567,36 @@
             pltpu.VMEM((grad_rows, hidden_width), F32),
             pltpu.VMEM((slot_rows, width), F32),
             pltpu.VMEM((slot_rows, width), F32),
-            pltpu.VMEM(slot_index.shape, jnp.int32),
-            pltpu.VMEM(dst_index.shape, jnp.int32),
             pltpu.VMEM(mesh_latent.shape, BF16),
-            pltpu.VMEM((width, hidden_width), BF16),
             pltpu.VMEM(w_edge2.shape, BF16),
             pltpu.VMEM((w_node1.shape[0] - width, w_node1.shape[1]), BF16),
-            pltpu.VMEM(w_node2.shape, BF16),
             pltpu.VMEM(hot.shape, BF16),
             pltpu.VMEM(node.shape, F32),
             pltpu.VMEM(cot.shape, F32),
-            pltpu.VMEM((mesh_rows, width), BF16),
             pltpu.VMEM((edges, slot_rows), BF16),
-            pltpu.SemaphoreType.DMA((11,)),
-            pltpu.SemaphoreType.DMA((1,)),
+            pltpu.SemaphoreType.DMA((7,)),
         ],
         compiler_params=params(40),
         name="edges",
     )(
-        *pinned(pltpu.HBM, slot_index, dst_index, mesh_latent, w_edge1, w_edge2, w_node1, w_node2),
-        *pinned(pltpu.HBM, turned, hot, node, cot),
-        *pinned(pltpu.VMEM, base),
+        *pinned(pltpu.HBM, mesh_latent, w_edge2, w_node1, turned, hot, node, cot),
+        *pinned(pltpu.VMEM, base, *ahead),
         *slot_blocks,
     )
+    mesh_out = pl.pallas_call(
+        mesh_kernel,
+        out_shape=jax.ShapeDtypeStruct((mesh_rows, width), BF16),
+        in_specs=specs(pltpu.HBM, 2) + specs(pltpu.VMEM, 1),
+        out_specs=pl.BlockSpec(memory_space=pltpu.VMEM),
+        scratch_shapes=[
+            pltpu.VMEM(mesh_latent.shape, BF16),
+            pltpu.VMEM(w_node2.shape, BF16),
+            pltpu.SemaphoreType.DMA((2,)),
+        ],
+        compiler_params=params(16),
+        cost_estimate=cost(10**9, MIB),
+        name="mesh",
+    )(*pinned(pltpu.HBM, mesh_latent, w_node2), node_out)
     sends, keeps = sides[:outer], sides[outer:]
     small = (2 * cap, width)
     arrived = {}
@@ -590,6 +604,8 @@
     for k in [outer - 1, *range(1, outer - 1), 0]:
         send = sends[k] if first is None else lax.optimization_barrier((sends[k], first))[0]
         crossed = to_core(send)
+        if first is None:
+            crossed = lax.optimization_barrier((crossed, mesh_out))[0]
         total, mixed, *parts = pl.pallas_call(
             functools.partial(core_kernel, sizes, k),
             out_shape=[

time: 72.6 us -> 72.9 us (level)
  Pallas kernels: 21.5 us -> 23 us
  waiting for transfers between devices: 25 us -> 23.5 us
    pallas_call x0 -> x1, Pallas kernels: none -> 2.15 us  [shards(): pl.pallas_call(mesh_kernel, out_shape=jax.ShapeDtypeStruct((mesh_rows, wi...]
    ppermute x31, waiting for transfers between devices: 25 us -> 23.5 us  [permute(): return lax.ppermute(value, 'band', pairs)]
  transfers between devices with their start and end apart: 31 -> 31, of which waited for: 15 -> 14; matrix products, arithmetic and copies ran while one was open for 0% -> 0% of each run, Pallas kernels for 16% -> 19%
where the time goes in v10:
time: 72.9 us; the launch traced here: 72.7 us
  starting transfers between devices  25.3 us (35%)
  waiting for transfers between devices  23.5 us (32%)
  Pallas kernels  23 us (32%)
  between operations  0.87 us (1%)
    ppermute x31, starting transfers between devices, permute(): return lax.ppermute(value, 'band', pairs)  25.3 us
    ppermute x31, waiting for transfers between devices, permute(): return lax.ppermute(value, 'band', pairs)  23.5 us
    pallas_call x1, Pallas kernels, shards(): pl.pallas_call(functools.partial(main_kernel, lines, sizes), out_shape=[j...  6.74 us
    pallas_call x1, Pallas kernels, shards(): pl.pallas_call(functools.partial(base_kernel, lines), out_shape=[pltpu.VM...  3.54 us
    pallas_call x3, Pallas kernels, shards(): pl.pallas_call(functools.partial(order_kernel, sizes, places, len(grads))...  3.46 us
    pallas_call x1, Pallas kernels, shards(): pl.pallas_call(functools.partial(ready_kernel, lines), out_shape=[pltpu.H...  2.8 us
    pallas_call x1, Pallas kernels, shards(): pl.pallas_call(functools.partial(put_kernel, sizes), out_shape=jax.ShapeD...  2.41 us
    pallas_call x1, Pallas kernels, shards(): pl.pallas_call(mesh_kernel, out_shape=jax.ShapeDtypeStruct((mesh_rows, wi...  2.15 us
  transfers between devices with their start and end apart: 31, of which 14 were waited for; matrix products, arithmetic and copies ran while one was open for 0% of the time, Pallas kernels for 19%

profile of v10, /device:TPU:0, one launch (start us, length us, event | category | flops | bytes accessed | tf_op | source)
XLA Modules:
  0.0 72.7 jit_solution(15798209201027498318)
XLA Ops:
  0.6 1.6 %pick.1 = (bf16[64,512]{1,0:T(8,128)(2,1)S(1)}, bf16[64,512]{1,0:T(8,128)(2,1)S(1)}) custom-call(s32[1,128]{1,0:T(1,128)} %rows_hbm.3, bf16[1024,512]{1,0:T(8,128)(2,1)} %grid_hbm.1), custom_call_target="tpu_custom_call" | custom-call | tf_op jit(solution)/shard_map/pick/pallas_call | solution.py:470
  3.6 2.9 %collective-permute-start.1 = (bf16[64,512]{1,0:T(8,128)(2,1)S(1)}, bf16[64,512]{1,0:T(8,128)(2,1)S(1)}, u32[]{:S(2)}, u32[]{:S(2)}) collective-permute-start(bf16[64,512]{1,0:T(8,128)(2,1)S(1)} %get-tuple-element.70), channel_id=1, source_target_pairs={{0,2},{1,3},{2,0},{3,1},{4,6},{5,7},{6,4},{7,5},{8,10},{9,11},{10,... | collective-permute-start | bytes 196616 | tf_op jit(solution)/shard_map/ppermute | solution.py:458
  6.6 2.8 %ready.1 = (bf16[1536,256]{1,0:T(8,128)(2,1)}, f32[256,512]{1,0:T(8,128)}, f32[256,512]{1,0:T(8,128)}, bf16[256,512]{1,0:T(8,128)(2,1)S(1)}) custom-call(s32[12,128]{1,0:T(8,128)} %bitcast.2, bf16[256,512]{1,0:T(8,128)(2,1)} %mesh_hbm.5, bf16[256,512]{1,0:T(8,128)(2,1)} %cot_hbm.1, bf16[1536,512]{1,0:T(8,128)(2,1)} %w1_hbm.3, bf16[1024,512]{1,0:T(8,128)(2,1)} %wn1_hbm.3, ...), custom_call_target="tpu_custom_call" | custom-call | flops 2000000000 | bytes 4194304 | tf_op jit(solution)/shard_map/ready/pallas_call | solution.py:494
  9.4 1.6 %collective-permute-start.2 = (bf16[32,512]{1,0:T(8,128)(2,1)S(1)}, bf16[32,512]{1,0:T(8,128)(2,1)S(1)}, u32[]{:S(2)}, u32[]{:S(2)}) collective-permute-start(bf16[32,512]{1,0:T(8,128)(2,1)S(1)} %get-tuple-element.72), channel_id=1, source_target_pairs={{0,4},{1,5},{2,6},{3,7},{4,0},{5,1},{6,2},{7,3},{8,12},{9,13},{10,... | collective-permute-start | bytes 98312 | tf_op jit(solution)/shard_map/ppermute | solution.py:458
  11.1 2.6 %collective-permute-start.3 = (bf16[32,512]{1,0:T(8,128)(2,1)S(1)}, bf16[32,512]{1,0:T(8,128)(2,1)S(1)}, u32[]{:S(2)}, u32[]{:S(2)}) collective-permute-start(bf16[32,512]{1,0:T(8,128)(2,1)S(1)} %get-tuple-element.73), channel_id=1, source_target_pairs={{0,8},{1,9},{2,10},{3,11},{4,12},{5,13},{6,14},{7,15},{8,0},{9,1},... | collective-permute-start | bytes 98312 | tf_op jit(solution)/shard_map/ppermute | solution.py:458
  13.9 3.5 %base.1 = (f32[1536,512]{1,0:T(8,128)S(1)}, s32[12,128]{1,0:T(8,128)S(1)}, s32[12,128]{1,0:T(8,128)S(1)}, bf16[512,512]{1,0:T(8,128)(2,1)S(1)}, bf16[512,1536]{1,0:T(8,128)(2,1)}) custom-call(bf16[1536,256]{1,0:T(8,128)(2,1)} %get-tuple-element.58.hot_hbm, bf16[1536,512]{1,0:T(8,128)(2,1)} %edge_hbm.1, bf16[1536,512]{1,0:T(8,128)(2,1)} %w1_hbm.3, ...), custom_call_target="tpu_custom_call" | custom-call | flops 4000000000 | bytes 4194304 | tf_op jit(solution)/shard_map/base/pallas_call | solution.py:521
  17.4 1.9 %collective-permute-done.4.rest_3_ = bf16[32,512]{1,0:T(8,128)(2,1)S(1)} collective-permute-done((bf16[32,512]{1,0:T(8,128)(2,1)S(1)}, bf16[32,512]{1,0:T(8,128)(2,1)S(1)}, u32[]{:S(2)}, u32[]{:S(2)}) %collective-permute-start.4) | collective-permute-done | bytes 32800 | tf_op jit(solution)/shard_map/ppermute | solution.py:458
  19.4 6.7 %edges.1 = (bf16[256,512]{1,0:T(8,128)(2,1)S(1)}, bf16[64,512]{1,0:T(8,128)(2,1)S(1)}, bf16[272,512]{1,0:T(8,128)(2,1)S(1)}, bf16[272,512]{1,0:T(8,128)(2,1)S(1)...) custom-call(bf16[256,512]{1,0:T(8,128)(2,1)} %mesh_hbm.5, ...), custom_call_target="tpu_custom_call" | custom-call | tf_op jit(solution)/shard_map/edges/pallas_call | solution.py:553
  26.2 2.1 %mesh.1 = bf16[256,512]{1,0:T(8,128)(2,1)} custom-call(bf16[256,512]{1,0:T(8,128)(2,1)} %mesh_hbm.5, bf16[512,512]{1,0:T(8,128)(2,1)} %wn2_hbm.3, bf16[256,512]{1,0:T(8,128)(2,1)S(1)} %get-tuple-element.75.node_ref), custom_call_target="tpu_custom_call" | custom-call | flops 1000000000 | bytes 1048576 | tf_op jit(solution)/shard_map/mesh/pallas_call | solution.py:586
  29.1 1.4 %collective-permute-start.14 = (bf16[144,512]{1,0:T(8,128)(2,1)S(1)}, bf16[144,512]{1,0:T(8,128)(2,1)S(1)}, u32[]{:S(2)}, u32[]{:S(2)}) collective-permute-start(bf16[144,512]{1,0:T(8,128)(2,1)S(1)} %get-tuple-element.82), channel_id=1, source_target_pairs={{0,2},{1,3},{2,0},{3,1},{4,6},{5,7},{6,4},{7,5},{8,10},{9,11},{10,... | collective-permute-start | bytes 442376 | tf_op jit(solution)/shard_map/ppermute | solution.py:458
  32.9 2.8 %collective-permute-done.14.refs_0_ = bf16[144,512]{1,0:T(8,128)(2,1)S(1)} collective-permute-done((bf16[144,512]{1,0:T(8,128)(2,1)S(1)}, bf16[144,512]{1,0:T(8,128)(2,1)S(1)}, u32[]{:S(2)}, u32[]{:S(2)}) %collective-permute-start.14) | collective-permute-done | bytes 147488 | tf_op jit(solution)/shard_map/ppermute | solution.py:458
  35.7 1.8 %collective-permute-start.15 = (bf16[160,512]{1,0:T(8,128)(2,1)S(1)}, bf16[160,512]{1,0:T(8,128)(2,1)S(1)}, u32[]{:S(2)}, u32[]{:S(2)}) collective-permute-start(bf16[160,512]{1,0:T(8,128)(2,1)S(1)} %inner.5), channel_id=1, source_target_pairs={{0,12},{1,13},{2,14},{3,15},{4,8},{5,9},{6,10},{7,11},{8,4},{9,5},... | collective-permute-start | bytes 491528 | tf_op jit(solution)/shard_map/ppermute | solution.py:458
  39.0 2.6 %collective-permute-done.9.refs_0_ = bf16[144,512]{1,0:T(8,128)(2,1)S(1)} collective-permute-done((bf16[144,512]{1,0:T(8,128)(2,1)S(1)}, bf16[144,512]{1,0:T(8,128)(2,1)S(1)}, u32[]{:S(2)}, u32[]{:S(2)}) %collective-permute-start.9) | collective-permute-done | bytes 147488 | tf_op jit(solution)/shard_map/ppermute | solution.py:458
  41.8 1.5 %collective-permute-start.7 = (bf16[144,512]{1,0:T(8,128)(2,1)S(1)}, bf16[144,512]{1,0:T(8,128)(2,1)S(1)}, u32[]{:S(2)}, u32[]{:S(2)}) collective-permute-start(bf16[144,512]{1,0:T(8,128)(2,1)S(1)} %get-tuple-element.86), channel_id=1, source_target_pairs={{0,2},{1,3},{2,0},{3,1},{4,6},{5,7},{6,4},{7,5},{8,10},{9,11},{10,... | collective-permute-start | bytes 442376 | tf_op jit(solution)/shard_map/ppermute | solution.py:458
  43.3 1.6 %collective-permute-done.15.refs_3_ = bf16[160,512]{1,0:T(8,128)(2,1)S(1)} collective-permute-done((bf16[160,512]{1,0:T(8,128)(2,1)S(1)}, bf16[160,512]{1,0:T(8,128)(2,1)S(1)}, u32[]{:S(2)}, u32[]{:S(2)}) %collective-permute-start.15) | collective-permute-done | bytes 163872 | tf_op jit(solution)/shard_map/ppermute | solution.py:458
  44.9 2.4 %collective-permute-done.7.refs_0_ = bf16[144,512]{1,0:T(8,128)(2,1)S(1)} collective-permute-done((bf16[144,512]{1,0:T(8,128)(2,1)S(1)}, bf16[144,512]{1,0:T(8,128)(2,1)S(1)}, u32[]{:S(2)}, u32[]{:S(2)}) %collective-permute-start.7) | collective-permute-done | bytes 147488 | tf_op jit(solution)/shard_map/ppermute | solution.py:458
  47.2 2.8 %collective-permute-done.13.refs_2_ = bf16[160,512]{1,0:T(8,128)(2,1)S(1)} collective-permute-done((bf16[160,512]{1,0:T(8,128)(2,1)S(1)}, bf16[160,512]{1,0:T(8,128)(2,1)S(1)}, u32[]{:S(2)}, u32[]{:S(2)}) %collective-permute-start.13) | collective-permute-done | bytes 163872 | tf_op jit(solution)/shard_map/ppermute | solution.py:458
  51.5 2.4 %put.1 = f32[1024,512]{1,0:T(8,128)} custom-call(s32[1,128]{1,0:T(1,128)} %rows_hbm.3, bf16[32,512]{1,0:T(8,128)(2,1)S(1)} %get-tuple-element.101.refs_0_, bf16[160,512]{1,0:T(8,128)(2,1)S(1)} %collective-permute-done.10.refs_1_, bf16[160,512]{1,0:T(8,128)(2,1)S(1)} %collective-permute-done.13.refs_2_, bf16[160,512]{1,0:T(8,128)(2,1)S(1)} %collective-permute-done.15.refs_3_), custom_call_target="tpu_custom_call" | custom-call | flops 2000000000 | bytes 2097152 | tf_op jit(solution)/shard_map/put/pallas_call | solution.py:642
  54.0 2.3 %collective-permute-start.19 = (bf16[128,512]{1,0:T(8,128)(2,1)S(1)}, bf16[128,512]{1,0:T(8,128)(2,1)S(1)}, u32[]{:S(2)}, u32[]{:S(2)}) collective-permute-start(bf16[128,512]{1,0:T(8,128)(2,1)S(1)} %get-tuple-element.103.refs_0_), channel_id=1, source_target_pairs={{0,4},{1,5},{2,6},{3,7},{4,0},{5,1},{6,2},{7,3},{8,12},{9,13},{10,... | collective-permute-start | bytes 393224 | tf_op jit(solution)/shard_map/ppermute | solution.py:458
  56.3 1.4 %collective-permute-start.20 = (bf16[128,512]{1,0:T(8,128)(2,1)S(1)}, bf16[128,512]{1,0:T(8,128)(2,1)S(1)}, u32[]{:S(2)}, u32[]{:S(2)}) collective-permute-start(bf16[128,512]{1,0:T(8,128)(2,1)S(1)} %get-tuple-element.103.refs_0_), channel_id=1, source_target_pairs={{0,2},{1,3},{2,0},{3,1},{4,6},{5,7},{6,4},{7,5},{8,10},{9,11},{10,... | collective-permute-start | bytes 393224 | tf_op jit(solution)/shard_map/ppermute | solution.py:458
  59.0 1.4 %collective-permute-start.26 = (bf16[128,512]{1,0:T(8,128)(2,1)S(1)}, bf16[128,512]{1,0:T(8,128)(2,1)S(1)}, u32[]{:S(2)}, u32[]{:S(2)}) collective-permute-start(bf16[128,512]{1,0:T(8,128)(2,1)S(1)} %collective-permute-done.16.refs_2_), channel_id=1, source_target_pairs={{0,2},{1,3},{2,0},{3,1},{4,6},{5,7},{6,4},{7,5},{8,10},{9,11},{10,... | collective-permute-start | bytes 393224 | tf_op jit(solution)/shard_map/ppermute | solution.py:458
  61.7 1.4 %collective-permute-start.21 = (bf16[128,512]{1,0:T(8,128)(2,1)S(1)}, bf16[128,512]{1,0:T(8,128)(2,1)S(1)}, u32[]{:S(2)}, u32[]{:S(2)}) collective-permute-start(bf16[128,512]{1,0:T(8,128)(2,1)S(1)} %collective-permute-done.19.refs_1_), channel_id=1, source_target_pairs={{0,2},{1,3},{2,0},{3,1},{4,6},{5,7},{6,4},{7,5},{8,10},{9,11},{10,... | collective-permute-start | bytes 393224 | tf_op jit(solution)/shard_map/ppermute | solution.py:458
  64.5 1.4 %collective-permute-start.18 = (bf16[128,512]{1,0:T(8,128)(2,1)S(1)}, bf16[128,512]{1,0:T(8,128)(2,1)S(1)}, u32[]{:S(2)}, u32[]{:S(2)}) collective-permute-start(bf16[128,512]{1,0:T(8,128)(2,1)S(1)} %collective-permute-done.17.refs_0_), channel_id=1, source_target_pairs={{0,2},{1,3},{2,0},{3,1},{4,6},{5,7},{6,4},{7,5},{8,10},{9,11},{10,... | collective-permute-start | bytes 393224 | tf_op jit(solution)/shard_map/ppermute | solution.py:458
  65.9 2.1 %collective-permute-done.21.refs_4_ = bf16[128,512]{1,0:T(8,128)(2,1)S(1)} collective-permute-done((bf16[128,512]{1,0:T(8,128)(2,1)S(1)}, bf16[128,512]{1,0:T(8,128)(2,1)S(1)}, u32[]{:S(2)}, u32[]{:S(2)}) %collective-permute-start.21) | collective-permute-done | bytes 131104 | tf_op jit(solution)/shard_map/ppermute | solution.py:458
  (57 shorter events, 16.5 us)
Async XLA Ops:
  3.6 5.7 %collective-permute-start.1 = (bf16[64,512]{1,0:T(8,128)(2,1)S(1)}, bf16[64,512]{1,0:T(8,128)(2,1)S(1)}, u32[]{:S(2)}, u32[]{:S(2)}) collective-permute-start(bf16[64,512]{1,0:T(8,128)(2,1)S(1)} %get-tuple-element.70), channel_id=1, source_target_pairs={{0,2},{1,3},{2,0},{3,1},{4,6},{5,7},{6,4},{7,5},{8,10},{9,11},{10,... | collective-permute-start | bytes 196616 | tf_op jit(solution)/shard_map/ppermute | solution.py:458
  9.4 8.0 %collective-permute-start.2 = (bf16[32,512]{1,0:T(8,128)(2,1)S(1)}, bf16[32,512]{1,0:T(8,128)(2,1)S(1)}, u32[]{:S(2)}, u32[]{:S(2)}) collective-permute-start(bf16[32,512]{1,0:T(8,128)(2,1)S(1)} %get-tuple-element.72), channel_id=1, source_target_pairs={{0,4},{1,5},{2,6},{3,7},{4,0},{5,1},{6,2},{7,3},{8,12},{9,13},{10,... | collective-permute-start | bytes 98312 | tf_op jit(solution)/shard_map/ppermute | solution.py:458
  11.1 6.4 %collective-permute-start.3 = (bf16[32,512]{1,0:T(8,128)(2,1)S(1)}, bf16[32,512]{1,0:T(8,128)(2,1)S(1)}, u32[]{:S(2)}, u32[]{:S(2)}) collective-permute-start(bf16[32,512]{1,0:T(8,128)(2,1)S(1)} %get-tuple-element.73), channel_id=1, source_target_pairs={{0,8},{1,9},{2,10},{3,11},{4,12},{5,13},{6,14},{7,15},{8,0},{9,1},... | collective-permute-start | bytes 98312 | tf_op jit(solution)/shard_map/ppermute | solution.py:458
  13.7 5.7 %collective-permute-start.4 = (bf16[32,512]{1,0:T(8,128)(2,1)S(1)}, bf16[32,512]{1,0:T(8,128)(2,1)S(1)}, u32[]{:S(2)}, u32[]{:S(2)}) collective-permute-start(bf16[32,512]{1,0:T(8,128)(2,1)S(1)} %get-tuple-element.74), channel_id=1, source_target_pairs={{0,12},{1,13},{2,14},{3,15},{4,8},{5,9},{6,10},{7,11},{8,4},{9,5},... | collective-permute-start | bytes 98312 | tf_op jit(solution)/shard_map/ppermute | solution.py:458
  29.0 2.8 %collective-permute-start.8 = (bf16[272,512]{1,0:T(8,128)(2,1)S(1)}, bf16[272,512]{1,0:T(8,128)(2,1)S(1)}, u32[]{:S(2)}, u32[]{:S(2)}) collective-permute-start(bf16[272,512]{1,0:T(8,128)(2,1)S(1)} %get-tuple-element.89), channel_id=1, source_target_pairs={{0,1},{1,0},{2,3},{3,2},{4,5},{5,4},{6,7},{7,6},{8,9},{9,8},{10,11... | collective-permute-start | bytes 835592 | tf_op jit(solution)/shard_map/ppermute | solution.py:458
  29.1 6.6 %collective-permute-start.14 = (bf16[144,512]{1,0:T(8,128)(2,1)S(1)}, bf16[144,512]{1,0:T(8,128)(2,1)S(1)}, u32[]{:S(2)}, u32[]{:S(2)}) collective-permute-start(bf16[144,512]{1,0:T(8,128)(2,1)S(1)} %get-tuple-element.82), channel_id=1, source_target_pairs={{0,2},{1,3},{2,0},{3,1},{4,6},{5,7},{6,4},{7,5},{8,10},{9,11},{10,... | collective-permute-start | bytes 442376 | tf_op jit(solution)/shard_map/ppermute | solution.py:458
  30.5 11.2 %collective-permute-start.6 = (bf16[272,512]{1,0:T(8,128)(2,1)S(1)}, bf16[272,512]{1,0:T(8,128)(2,1)S(1)}, u32[]{:S(2)}, u32[]{:S(2)}) collective-permute-start(bf16[272,512]{1,0:T(8,128)(2,1)S(1)} %get-tuple-element.83), channel_id=1, source_target_pairs={{0,1},{1,0},{2,3},{3,2},{4,5},{5,4},{6,7},{7,6},{8,9},{9,8},{10,11... | collective-permute-start | bytes 835592 | tf_op jit(solution)/shard_map/ppermute | solution.py:458
  30.7 8.2 %collective-permute-start.12 = (bf16[144,512]{1,0:T(8,128)(2,1)S(1)}, bf16[144,512]{1,0:T(8,128)(2,1)S(1)}, u32[]{:S(2)}, u32[]{:S(2)}) collective-permute-start(bf16[144,512]{1,0:T(8,128)(2,1)S(1)} %get-tuple-element.98), channel_id=1, source_target_pairs={{0,2},{1,3},{2,0},{3,1},{4,6},{5,7},{6,4},{7,5},{8,10},{9,11},{10,... | collective-permute-start | bytes 442376 | tf_op jit(solution)/shard_map/ppermute | solution.py:458
  31.8 9.8 %collective-permute-start.9 = (bf16[144,512]{1,0:T(8,128)(2,1)S(1)}, bf16[144,512]{1,0:T(8,128)(2,1)S(1)}, u32[]{:S(2)}, u32[]{:S(2)}) collective-permute-start(bf16[144,512]{1,0:T(8,128)(2,1)S(1)} %get-tuple-element.92), channel_id=1, source_target_pairs={{0,2},{1,3},{2,0},{3,1},{4,6},{5,7},{6,4},{7,5},{8,10},{9,11},{10,... | collective-permute-start | bytes 442376 | tf_op jit(solution)/shard_map/ppermute | solution.py:458
  35.7 9.1 %collective-permute-start.15 = (bf16[160,512]{1,0:T(8,128)(2,1)S(1)}, bf16[160,512]{1,0:T(8,128)(2,1)S(1)}, u32[]{:S(2)}, u32[]{:S(2)}) collective-permute-start(bf16[160,512]{1,0:T(8,128)(2,1)S(1)} %inner.5), channel_id=1, source_target_pairs={{0,12},{1,13},{2,14},{3,15},{4,8},{5,9},{6,10},{7,11},{8,4},{9,5},... | collective-permute-start | bytes 491528 | tf_op jit(solution)/shard_map/ppermute | solution.py:458
  38.9 11.1 %collective-permute-start.13 = (bf16[160,512]{1,0:T(8,128)(2,1)S(1)}, bf16[160,512]{1,0:T(8,128)(2,1)S(1)}, u32[]{:S(2)}, u32[]{:S(2)}) collective-permute-start(bf16[160,512]{1,0:T(8,128)(2,1)S(1)} %inner.4), channel_id=1, source_target_pairs={{0,8},{1,9},{2,10},{3,11},{4,12},{5,13},{6,14},{7,15},{8,0},{9,1},... | collective-permute-start | bytes 491528 | tf_op jit(solution)/shard_map/ppermute | solution.py:458
  41.6 9.7 %collective-permute-start.10 = (bf16[160,512]{1,0:T(8,128)(2,1)S(1)}, bf16[160,512]{1,0:T(8,128)(2,1)S(1)}, u32[]{:S(2)}, u32[]{:S(2)}) collective-permute-start(bf16[160,512]{1,0:T(8,128)(2,1)S(1)} %inner.3), channel_id=1, source_target_pairs={{0,4},{1,5},{2,6},{3,7},{4,0},{5,1},{6,2},{7,3},{8,12},{9,13},{10,... | collective-permute-start | bytes 491528 | tf_op jit(solution)/shard_map/ppermute | solution.py:458
  41.8 5.5 %collective-permute-start.7 = (bf16[144,512]{1,0:T(8,128)(2,1)S(1)}, bf16[144,512]{1,0:T(8,128)(2,1)S(1)}, u32[]{:S(2)}, u32[]{:S(2)}) collective-permute-start(bf16[144,512]{1,0:T(8,128)(2,1)S(1)} %get-tuple-element.86), channel_id=1, source_target_pairs={{0,2},{1,3},{2,0},{3,1},{4,6},{5,7},{6,4},{7,5},{8,10},{9,11},{10,... | collective-permute-start | bytes 442376 | tf_op jit(solution)/shard_map/ppermute | solution.py:458
  51.4 7.6 %collective-permute-start.16 = (bf16[128,512]{1,0:T(8,128)(2,1)S(1)}, bf16[128,512]{1,0:T(8,128)(2,1)S(1)}, u32[]{:S(2)}, u32[]{:S(2)}) collective-permute-start(bf16[128,512]{1,0:T(8,128)(2,1)S(1)} %get-tuple-element.103.refs_0_), channel_id=1, source_target_pairs={{0,8},{1,9},{2,10},{3,11},{4,12},{5,13},{6,14},{7,15},{8,0},{9,1},... | collective-permute-start | bytes 393224 | tf_op jit(solution)/shard_map/ppermute | solution.py:458
  51.5 7.5 %collective-permute-start.22 = (bf16[128,512]{1,0:T(8,128)(2,1)S(1)}, bf16[128,512]{1,0:T(8,128)(2,1)S(1)}, u32[]{:S(2)}, u32[]{:S(2)}) collective-permute-start(bf16[128,512]{1,0:T(8,128)(2,1)S(1)} %get-tuple-element.103.refs_0_), channel_id=1, source_target_pairs={{0,1},{1,0},{2,3},{3,2},{4,5},{5,4},{6,7},{7,6},{8,9},{9,8},{10,11... | collective-permute-start | bytes 393224 | tf_op jit(solution)/shard_map/ppermute | solution.py:458
  54.0 7.7 %collective-permute-start.19 = (bf16[128,512]{1,0:T(8,128)(2,1)S(1)}, bf16[128,512]{1,0:T(8,128)(2,1)S(1)}, u32[]{:S(2)}, u32[]{:S(2)}) collective-permute-start(bf16[128,512]{1,0:T(8,128)(2,1)S(1)} %get-tuple-element.103.refs_0_), channel_id=1, source_target_pairs={{0,4},{1,5},{2,6},{3,7},{4,0},{5,1},{6,2},{7,3},{8,12},{9,13},{10,... | collective-permute-start | bytes 393224 | tf_op jit(solution)/shard_map/ppermute | solution.py:458
  56.3 6.8 %collective-permute-start.20 = (bf16[128,512]{1,0:T(8,128)(2,1)S(1)}, bf16[128,512]{1,0:T(8,128)(2,1)S(1)}, u32[]{:S(2)}, u32[]{:S(2)}) collective-permute-start(bf16[128,512]{1,0:T(8,128)(2,1)S(1)} %get-tuple-element.103.refs_0_), channel_id=1, source_target_pairs={{0,2},{1,3},{2,0},{3,1},{4,6},{5,7},{6,4},{7,5},{8,10},{9,11},{10,... | collective-permute-start | bytes 393224 | tf_op jit(solution)/shard_map/ppermute | solution.py:458
  59.0 5.5 %collective-permute-start.17 = (bf16[128,512]{1,0:T(8,128)(2,1)S(1)}, bf16[128,512]{1,0:T(8,128)(2,1)S(1)}, u32[]{:S(2)}, u32[]{:S(2)}) collective-permute-start(bf16[128,512]{1,0:T(8,128)(2,1)S(1)} %collective-permute-done.16.refs_2_), channel_id=1, source_target_pairs={{0,4},{1,5},{2,6},{3,7},{4,0},{5,1},{6,2},{7,3},{8,12},{9,13},{10,... | collective-permute-start | bytes 393224 | tf_op jit(solution)/shard_map/ppermute | solution.py:458
  59.0 6.9 %collective-permute-start.26 = (bf16[128,512]{1,0:T(8,128)(2,1)S(1)}, bf16[128,512]{1,0:T(8,128)(2,1)S(1)}, u32[]{:S(2)}, u32[]{:S(2)}) collective-permute-start(bf16[128,512]{1,0:T(8,128)(2,1)S(1)} %collective-permute-done.16.refs_2_), channel_id=1, source_target_pairs={{0,2},{1,3},{2,0},{3,1},{4,6},{5,7},{6,4},{7,5},{8,10},{9,11},{10,... | collective-permute-start | bytes 393224 | tf_op jit(solution)/shard_map/ppermute | solution.py:458
  61.7 6.4 %collective-permute-start.21 = (bf16[128,512]{1,0:T(8,128)(2,1)S(1)}, bf16[128,512]{1,0:T(8,128)(2,1)S(1)}, u32[]{:S(2)}, u32[]{:S(2)}) collective-permute-start(bf16[128,512]{1,0:T(8,128)(2,1)S(1)} %collective-permute-done.19.refs_1_), channel_id=1, source_target_pairs={{0,2},{1,3},{2,0},{3,1},{4,6},{5,7},{6,4},{7,5},{8,10},{9,11},{10,... | collective-permute-start | bytes 393224 | tf_op jit(solution)/shard_map/ppermute | solution.py:458
  63.1 4.9 %collective-permute-start.23 = (bf16[128,512]{1,0:T(8,128)(2,1)S(1)}, bf16[128,512]{1,0:T(8,128)(2,1)S(1)}, u32[]{:S(2)}, u32[]{:S(2)}) collective-permute-start(bf16[128,512]{1,0:T(8,128)(2,1)S(1)} %collective-permute-done.19.refs_1_), channel_id=1, source_target_pairs={{0,1},{1,0},{2,3},{3,2},{4,5},{5,4},{6,7},{7,6},{8,9},{9,8},{10,11... | collective-permute-start | bytes 393224 | tf_op jit(solution)/shard_map/ppermute | solution.py:458
  63.1 5.4 %collective-permute-start.24 = (bf16[128,512]{1,0:T(8,128)(2,1)S(1)}, bf16[128,512]{1,0:T(8,128)(2,1)S(1)}, u32[]{:S(2)}, u32[]{:S(2)}) collective-permute-start(bf16[128,512]{1,0:T(8,128)(2,1)S(1)} %collective-permute-done.16.refs_2_), channel_id=1, source_target_pairs={{0,1},{1,0},{2,3},{3,2},{4,5},{5,4},{6,7},{7,6},{8,9},{9,8},{10,11... | collective-permute-start | bytes 393224 | tf_op jit(solution)/shard_map/ppermute | solution.py:458
  64.5 5.9 %collective-permute-start.18 = (bf16[128,512]{1,0:T(8,128)(2,1)S(1)}, bf16[128,512]{1,0:T(8,128)(2,1)S(1)}, u32[]{:S(2)}, u32[]{:S(2)}) collective-permute-start(bf16[128,512]{1,0:T(8,128)(2,1)S(1)} %collective-permute-done.17.refs_0_), channel_id=1, source_target_pairs={{0,2},{1,3},{2,0},{3,1},{4,6},{5,7},{6,4},{7,5},{8,10},{9,11},{10,... | collective-permute-start | bytes 393224 | tf_op jit(solution)/shard_map/ppermute | solution.py:458
  65.9 4.6 %collective-permute-start.28 = (bf16[128,512]{1,0:T(8,128)(2,1)S(1)}, bf16[128,512]{1,0:T(8,128)(2,1)S(1)}, u32[]{:S(2)}, u32[]{:S(2)}) collective-permute-start(bf16[128,512]{1,0:T(8,128)(2,1)S(1)} %collective-permute-done.20.refs_3_), channel_id=1, source_target_pairs={{0,1},{1,0},{2,3},{3,2},{4,5},{5,4},{6,7},{7,6},{8,9},{9,8},{10,11... | collective-permute-start | bytes 393224 | tf_op jit(solution)/shard_map/ppermute | solution.py:458
  (7 other events, 14.4 us)

commit v11 on v10

--- a/solution.py
+++ b/solution.py
@@ -604,8 +604,6 @@
     for k in [outer - 1, *range(1, outer - 1), 0]:
         send = sends[k] if first is None else lax.optimization_barrier((sends[k], first))[0]
         crossed = to_core(send)
-        if first is None:
-            crossed = lax.optimization_barrier((crossed, mesh_out))[0]
         total, mixed, *parts = pl.pallas_call(
             functools.partial(core_kernel, sizes, k),
             out_shape=[
@@ -629,6 +627,7 @@
             )(total, mixed, *parts)
             arrived[k] = to_outer(out, k)
         else:
+            total = lax.optimization_barrier((total, mesh_out))[0]
             own, home = pl.pallas_call(
                 functools.partial(inner_kernel, inner - 1, outer - 1),
                 out_shape=[
@@ -659,7 +658,7 @@
     while stride:
         for at in range(0, outer, 2 * stride):
             value = pieces[at]
-            if at + stride == 1:
+            if at == outer // 2 and stride == outer // 4:
                 value = lax.optimization_barrier((value, grid_grad))[0]
             pieces[at + stride] = to_outer(value, stride)
         stride //= 2

time: 72.9 us -> 72.1 us (0.989)
  transfers between devices with their start and end apart: 31 -> 31, of which waited for: 14 -> 12; matrix products, arithmetic and copies ran while one was open for 0% -> 0% of each run, Pallas kernels for 19% -> 19%
where the time goes in v11:
time: 72.1 us; the launch traced here: 71.9 us
  starting transfers between devices  25.2 us (35%)
  Pallas kernels  23 us (32%)
  waiting for transfers between devices  22.8 us (32%)
  between operations  0.87 us (1%)
    ppermute x31, starting transfers between devices, permute(): return lax.ppermute(value, 'band', pairs)  25.2 us
    ppermute x31, waiting for transfers between devices, permute(): return lax.ppermute(value, 'band', pairs)  22.8 us
    pallas_call x1, Pallas kernels, shards(): pl.pallas_call(functools.partial(main_kernel, lines, sizes), out_shape=[j...  6.74 us
    pallas_call x1, Pallas kernels, shards(): pl.pallas_call(functools.partial(base_kernel, lines), out_shape=[pltpu.VM...  3.54 us
    pallas_call x3, Pallas kernels, shards(): pl.pallas_call(functools.partial(order_kernel, sizes, places, len(grads))...  3.46 us
    pallas_call x1, Pallas kernels, shards(): pl.pallas_call(functools.partial(ready_kernel, lines), out_shape=[pltpu.H...  2.8 us
    pallas_call x1, Pallas kernels, shards(): pl.pallas_call(functools.partial(put_kernel, sizes), out_shape=jax.ShapeD...  2.4 us
    pallas_call x1, Pallas kernels, shards(): pl.pallas_call(mesh_kernel, out_shape=jax.ShapeDtypeStruct((mesh_rows, wi...  2.14 us
  transfers between devices with their start and end apart: 31, of which 12 were waited for; matrix products, arithmetic and copies ran while one was open for 0% of the time, Pallas kernels for 19%

profile of v11, /device:TPU:0, one launch (start us, length us, event | category | flops | bytes accessed | tf_op | source)
XLA Modules:
  0.0 71.9 jit_solution(13167812213437334678)
XLA Ops:
  0.6 1.6 %pick.1 = (bf16[64,512]{1,0:T(8,128)(2,1)S(1)}, bf16[64,512]{1,0:T(8,128)(2,1)S(1)}) custom-call(s32[1,128]{1,0:T(1,128)} %rows_hbm.3, bf16[1024,512]{1,0:T(8,128)(2,1)} %grid_hbm.1), custom_call_target="tpu_custom_call" | custom-call | tf_op jit(solution)/shard_map/pick/pallas_call | solution.py:470
  3.6 2.9 %collective-permute-start.1 = (bf16[64,512]{1,0:T(8,128)(2,1)S(1)}, bf16[64,512]{1,0:T(8,128)(2,1)S(1)}, u32[]{:S(2)}, u32[]{:S(2)}) collective-permute-start(bf16[64,512]{1,0:T(8,128)(2,1)S(1)} %get-tuple-element.70), channel_id=1, source_target_pairs={{0,2},{1,3},{2,0},{3,1},{4,6},{5,7},{6,4},{7,5},{8,10},{9,11},{10,... | collective-permute-start | bytes 196616 | tf_op jit(solution)/shard_map/ppermute | solution.py:458
  6.6 2.8 %ready.1 = (bf16[1536,256]{1,0:T(8,128)(2,1)}, f32[256,512]{1,0:T(8,128)}, f32[256,512]{1,0:T(8,128)}, bf16[256,512]{1,0:T(8,128)(2,1)S(1)}) custom-call(s32[12,128]{1,0:T(8,128)} %bitcast.2, bf16[256,512]{1,0:T(8,128)(2,1)} %mesh_hbm.5, bf16[256,512]{1,0:T(8,128)(2,1)} %cot_hbm.1, bf16[1536,512]{1,0:T(8,128)(2,1)} %w1_hbm.3, bf16[1024,512]{1,0:T(8,128)(2,1)} %wn1_hbm.3, ...), custom_call_target="tpu_custom_call" | custom-call | flops 2000000000 | bytes 4194304 | tf_op jit(solution)/shard_map/ready/pallas_call | solution.py:494
  9.4 1.6 %collective-permute-start.2 = (bf16[32,512]{1,0:T(8,128)(2,1)S(1)}, bf16[32,512]{1,0:T(8,128)(2,1)S(1)}, u32[]{:S(2)}, u32[]{:S(2)}) collective-permute-start(bf16[32,512]{1,0:T(8,128)(2,1)S(1)} %get-tuple-element.72), channel_id=1, source_target_pairs={{0,4},{1,5},{2,6},{3,7},{4,0},{5,1},{6,2},{7,3},{8,12},{9,13},{10,... | collective-permute-start | bytes 98312 | tf_op jit(solution)/shard_map/ppermute | solution.py:458
  11.1 2.6 %collective-permute-start.3 = (bf16[32,512]{1,0:T(8,128)(2,1)S(1)}, bf16[32,512]{1,0:T(8,128)(2,1)S(1)}, u32[]{:S(2)}, u32[]{:S(2)}) collective-permute-start(bf16[32,512]{1,0:T(8,128)(2,1)S(1)} %get-tuple-element.73), channel_id=1, source_target_pairs={{0,8},{1,9},{2,10},{3,11},{4,12},{5,13},{6,14},{7,15},{8,0},{9,1},... | collective-permute-start | bytes 98312 | tf_op jit(solution)/shard_map/ppermute | solution.py:458
  13.9 3.5 %base.1 = (f32[1536,512]{1,0:T(8,128)S(1)}, s32[12,128]{1,0:T(8,128)S(1)}, s32[12,128]{1,0:T(8,128)S(1)}, bf16[512,512]{1,0:T(8,128)(2,1)S(1)}, bf16[512,1536]{1,0:T(8,128)(2,1)}) custom-call(bf16[1536,256]{1,0:T(8,128)(2,1)} %get-tuple-element.58.hot_hbm, bf16[1536,512]{1,0:T(8,128)(2,1)} %edge_hbm.1, bf16[1536,512]{1,0:T(8,128)(2,1)} %w1_hbm.3, ...), custom_call_target="tpu_custom_call" | custom-call | flops 4000000000 | bytes 4194304 | tf_op jit(solution)/shard_map/base/pallas_call | solution.py:521
  17.4 1.9 %collective-permute-done.4.rest_3_ = bf16[32,512]{1,0:T(8,128)(2,1)S(1)} collective-permute-done((bf16[32,512]{1,0:T(8,128)(2,1)S(1)}, bf16[32,512]{1,0:T(8,128)(2,1)S(1)}, u32[]{:S(2)}, u32[]{:S(2)}) %collective-permute-start.4) | collective-permute-done | bytes 32800 | tf_op jit(solution)/shard_map/ppermute | solution.py:458
  19.4 6.7 %edges.1 = (bf16[256,512]{1,0:T(8,128)(2,1)S(1)}, bf16[64,512]{1,0:T(8,128)(2,1)S(1)}, bf16[272,512]{1,0:T(8,128)(2,1)S(1)}, bf16[272,512]{1,0:T(8,128)(2,1)S(1)...) custom-call(bf16[256,512]{1,0:T(8,128)(2,1)} %mesh_hbm.5, ...), custom_call_target="tpu_custom_call" | custom-call | tf_op jit(solution)/shard_map/edges/pallas_call | solution.py:553
  26.2 1.5 %collective-permute-done.5.crossed_ref = bf16[272,512]{1,0:T(8,128)(2,1)S(1)} collective-permute-done((bf16[272,512]{1,0:T(8,128)(2,1)S(1)}, bf16[272,512]{1,0:T(8,128)(2,1)S(1)}, u32[]{:S(2)}, u32[]{:S(2)}) %collective-permute-start.5) | collective-permute-done | bytes 278560 | tf_op jit(solution)/shard_map/ppermute | solution.py:458
  32.1 3.0 %collective-permute-done.14.refs_0_ = bf16[144,512]{1,0:T(8,128)(2,1)S(1)} collective-permute-done((bf16[144,512]{1,0:T(8,128)(2,1)S(1)}, bf16[144,512]{1,0:T(8,128)(2,1)S(1)}, u32[]{:S(2)}, u32[]{:S(2)}) %collective-permute-start.14) | collective-permute-done | bytes 147488 | tf_op jit(solution)/shard_map/ppermute | solution.py:458
  35.1 1.8 %collective-permute-start.15 = (bf16[160,512]{1,0:T(8,128)(2,1)S(1)}, bf16[160,512]{1,0:T(8,128)(2,1)S(1)}, u32[]{:S(2)}, u32[]{:S(2)}) collective-permute-start(bf16[160,512]{1,0:T(8,128)(2,1)S(1)} %inner.5), channel_id=1, source_target_pairs={{0,12},{1,13},{2,14},{3,15},{4,8},{5,9},{6,10},{7,11},{8,4},{9,5},... | collective-permute-start | bytes 491528 | tf_op jit(solution)/shard_map/ppermute | solution.py:458
  38.3 2.3 %collective-permute-done.9.refs_0_ = bf16[144,512]{1,0:T(8,128)(2,1)S(1)} collective-permute-done((bf16[144,512]{1,0:T(8,128)(2,1)S(1)}, bf16[144,512]{1,0:T(8,128)(2,1)S(1)}, u32[]{:S(2)}, u32[]{:S(2)}) %collective-permute-start.9) | collective-permute-done | bytes 147488 | tf_op jit(solution)/shard_map/ppermute | solution.py:458
  40.8 1.5 %collective-permute-start.7 = (bf16[144,512]{1,0:T(8,128)(2,1)S(1)}, bf16[144,512]{1,0:T(8,128)(2,1)S(1)}, u32[]{:S(2)}, u32[]{:S(2)}) collective-permute-start(bf16[144,512]{1,0:T(8,128)(2,1)S(1)} %get-tuple-element.86), channel_id=1, source_target_pairs={{0,2},{1,3},{2,0},{3,1},{4,6},{5,7},{6,4},{7,5},{8,10},{9,11},{10,... | collective-permute-start | bytes 442376 | tf_op jit(solution)/shard_map/ppermute | solution.py:458
  42.3 2.1 %mesh.1 = bf16[256,512]{1,0:T(8,128)(2,1)} custom-call(bf16[256,512]{1,0:T(8,128)(2,1)} %mesh_hbm.5, bf16[512,512]{1,0:T(8,128)(2,1)} %wn2_hbm.3, bf16[256,512]{1,0:T(8,128)(2,1)S(1)} %get-tuple-element.75.node_ref), custom_call_target="tpu_custom_call" | custom-call | flops 1000000000 | bytes 1048576 | tf_op jit(solution)/shard_map/mesh/pallas_call | solution.py:586
  44.4 1.5 %collective-permute-done.7.refs_0_ = bf16[144,512]{1,0:T(8,128)(2,1)S(1)} collective-permute-done((bf16[144,512]{1,0:T(8,128)(2,1)S(1)}, bf16[144,512]{1,0:T(8,128)(2,1)S(1)}, u32[]{:S(2)}, u32[]{:S(2)}) %collective-permute-start.7) | collective-permute-done | bytes 147488 | tf_op jit(solution)/shard_map/ppermute | solution.py:458
  46.0 3.4 %collective-permute-done.13.refs_2_ = bf16[160,512]{1,0:T(8,128)(2,1)S(1)} collective-permute-done((bf16[160,512]{1,0:T(8,128)(2,1)S(1)}, bf16[160,512]{1,0:T(8,128)(2,1)S(1)}, u32[]{:S(2)}, u32[]{:S(2)}) %collective-permute-start.13) | collective-permute-done | bytes 163872 | tf_op jit(solution)/shard_map/ppermute | solution.py:458
  50.6 2.2 %collective-permute-start.19 = (bf16[128,512]{1,0:T(8,128)(2,1)S(1)}, bf16[128,512]{1,0:T(8,128)(2,1)S(1)}, u32[]{:S(2)}, u32[]{:S(2)}) collective-permute-start(bf16[128,512]{1,0:T(8,128)(2,1)S(1)} %get-tuple-element.102.refs_0_), channel_id=1, source_target_pairs={{0,4},{1,5},{2,6},{3,7},{4,0},{5,1},{6,2},{7,3},{8,12},{9,13},{10,... | collective-permute-start | bytes 393224 | tf_op jit(solution)/shard_map/ppermute | solution.py:458
  52.8 1.4 %collective-permute-start.20 = (bf16[128,512]{1,0:T(8,128)(2,1)S(1)}, bf16[128,512]{1,0:T(8,128)(2,1)S(1)}, u32[]{:S(2)}, u32[]{:S(2)}) collective-permute-start(bf16[128,512]{1,0:T(8,128)(2,1)S(1)} %get-tuple-element.102.refs_0_), channel_id=1, source_target_pairs={{0,2},{1,3},{2,0},{3,1},{4,6},{5,7},{6,4},{7,5},{8,10},{9,11},{10,... | collective-permute-start | bytes 393224 | tf_op jit(solution)/shard_map/ppermute | solution.py:458
  54.2 2.4 %put.1 = f32[1024,512]{1,0:T(8,128)} custom-call(s32[1,128]{1,0:T(1,128)} %rows_hbm.3, bf16[32,512]{1,0:T(8,128)(2,1)S(1)} %get-tuple-element.101.refs_0_, bf16[160,512]{1,0:T(8,128)(2,1)S(1)} %collective-permute-done.10.refs_1_, bf16[160,512]{1,0:T(8,128)(2,1)S(1)} %collective-permute-done.13.refs_2_, bf16[160,512]{1,0:T(8,128)(2,1)S(1)} %collective-permute-done.15.refs_3_), custom_call_target="tpu_custom_call" | custom-call | flops 2000000000 | bytes 2097152 | tf_op jit(solution)/shard_map/put/pallas_call | solution.py:641
  56.7 1.4 %collective-permute-done.16.refs_2_ = bf16[128,512]{1,0:T(8,128)(2,1)S(1)} collective-permute-done((bf16[128,512]{1,0:T(8,128)(2,1)S(1)}, bf16[128,512]{1,0:T(8,128)(2,1)S(1)}, u32[]{:S(2)}, u32[]{:S(2)}) %collective-permute-start.16) | collective-permute-done | bytes 131104 | tf_op jit(solution)/shard_map/ppermute | solution.py:458
  58.1 1.4 %collective-permute-start.26 = (bf16[128,512]{1,0:T(8,128)(2,1)S(1)}, bf16[128,512]{1,0:T(8,128)(2,1)S(1)}, u32[]{:S(2)}, u32[]{:S(2)}) collective-permute-start(bf16[128,512]{1,0:T(8,128)(2,1)S(1)} %collective-permute-done.16.refs_2_), channel_id=1, source_target_pairs={{0,2},{1,3},{2,0},{3,1},{4,6},{5,7},{6,4},{7,5},{8,10},{9,11},{10,... | collective-permute-start | bytes 393224 | tf_op jit(solution)/shard_map/ppermute | solution.py:458
  59.6 1.4 %collective-permute-start.21 = (bf16[128,512]{1,0:T(8,128)(2,1)S(1)}, bf16[128,512]{1,0:T(8,128)(2,1)S(1)}, u32[]{:S(2)}, u32[]{:S(2)}) collective-permute-start(bf16[128,512]{1,0:T(8,128)(2,1)S(1)} %collective-permute-done.19.refs_1_), channel_id=1, source_target_pairs={{0,2},{1,3},{2,0},{3,1},{4,6},{5,7},{6,4},{7,5},{8,10},{9,11},{10,... | collective-permute-start | bytes 393224 | tf_op jit(solution)/shard_map/ppermute | solution.py:458
  61.5 1.8 %collective-permute-done.17.refs_0_ = bf16[128,512]{1,0:T(8,128)(2,1)S(1)} collective-permute-done((bf16[128,512]{1,0:T(8,128)(2,1)S(1)}, bf16[128,512]{1,0:T(8,128)(2,1)S(1)}, u32[]{:S(2)}, u32[]{:S(2)}) %collective-permute-start.17) | collective-permute-done | bytes 131104 | tf_op jit(solution)/shard_map/ppermute | solution.py:458
  64.8 2.5 %collective-permute-done.21.refs_4_ = bf16[128,512]{1,0:T(8,128)(2,1)S(1)} collective-permute-done((bf16[128,512]{1,0:T(8,128)(2,1)S(1)}, bf16[128,512]{1,0:T(8,128)(2,1)S(1)}, u32[]{:S(2)}, u32[]{:S(2)}) %collective-permute-start.21) | collective-permute-done | bytes 131104 | tf_op jit(solution)/shard_map/ppermute | solution.py:458
  (57 shorter events, 15.5 us)
Async XLA Ops:
  3.6 5.7 %collective-permute-start.1 = (bf16[64,512]{1,0:T(8,128)(2,1)S(1)}, bf16[64,512]{1,0:T(8,128)(2,1)S(1)}, u32[]{:S(2)}, u32[]{:S(2)}) collective-permute-start(bf16[64,512]{1,0:T(8,128)(2,1)S(1)} %get-tuple-element.70), channel_id=1, source_target_pairs={{0,2},{1,3},{2,0},{3,1},{4,6},{5,7},{6,4},{7,5},{8,10},{9,11},{10,... | collective-permute-start | bytes 196616 | tf_op jit(solution)/shard_map/ppermute | solution.py:458
  9.4 8.0 %collective-permute-start.2 = (bf16[32,512]{1,0:T(8,128)(2,1)S(1)}, bf16[32,512]{1,0:T(8,128)(2,1)S(1)}, u32[]{:S(2)}, u32[]{:S(2)}) collective-permute-start(bf16[32,512]{1,0:T(8,128)(2,1)S(1)} %get-tuple-element.72), channel_id=1, source_target_pairs={{0,4},{1,5},{2,6},{3,7},{4,0},{5,1},{6,2},{7,3},{8,12},{9,13},{10,... | collective-permute-start | bytes 98312 | tf_op jit(solution)/shard_map/ppermute | solution.py:458
  11.1 6.4 %collective-permute-start.3 = (bf16[32,512]{1,0:T(8,128)(2,1)S(1)}, bf16[32,512]{1,0:T(8,128)(2,1)S(1)}, u32[]{:S(2)}, u32[]{:S(2)}) collective-permute-start(bf16[32,512]{1,0:T(8,128)(2,1)S(1)} %get-tuple-element.73), channel_id=1, source_target_pairs={{0,8},{1,9},{2,10},{3,11},{4,12},{5,13},{6,14},{7,15},{8,0},{9,1},... | collective-permute-start | bytes 98312 | tf_op jit(solution)/shard_map/ppermute | solution.py:458
  13.7 5.7 %collective-permute-start.4 = (bf16[32,512]{1,0:T(8,128)(2,1)S(1)}, bf16[32,512]{1,0:T(8,128)(2,1)S(1)}, u32[]{:S(2)}, u32[]{:S(2)}) collective-permute-start(bf16[32,512]{1,0:T(8,128)(2,1)S(1)} %get-tuple-element.74), channel_id=1, source_target_pairs={{0,12},{1,13},{2,14},{3,15},{4,8},{5,9},{6,10},{7,11},{8,4},{9,5},... | collective-permute-start | bytes 98312 | tf_op jit(solution)/shard_map/ppermute | solution.py:458
  28.0 3.0 %collective-permute-start.8 = (bf16[272,512]{1,0:T(8,128)(2,1)S(1)}, bf16[272,512]{1,0:T(8,128)(2,1)S(1)}, u32[]{:S(2)}, u32[]{:S(2)}) collective-permute-start(bf16[272,512]{1,0:T(8,128)(2,1)S(1)} %get-tuple-element.89), channel_id=1, source_target_pairs={{0,1},{1,0},{2,3},{3,2},{4,5},{5,4},{6,7},{7,6},{8,9},{9,8},{10,11... | collective-permute-start | bytes 835592 | tf_op jit(solution)/shard_map/ppermute | solution.py:458
  28.4 6.7 %collective-permute-start.14 = (bf16[144,512]{1,0:T(8,128)(2,1)S(1)}, bf16[144,512]{1,0:T(8,128)(2,1)S(1)}, u32[]{:S(2)}, u32[]{:S(2)}) collective-permute-start(bf16[144,512]{1,0:T(8,128)(2,1)S(1)} %get-tuple-element.81), channel_id=1, source_target_pairs={{0,2},{1,3},{2,0},{3,1},{4,6},{5,7},{6,4},{7,5},{8,10},{9,11},{10,... | collective-permute-start | bytes 442376 | tf_op jit(solution)/shard_map/ppermute | solution.py:458
  29.8 10.9 %collective-permute-start.6 = (bf16[272,512]{1,0:T(8,128)(2,1)S(1)}, bf16[272,512]{1,0:T(8,128)(2,1)S(1)}, u32[]{:S(2)}, u32[]{:S(2)}) collective-permute-start(bf16[272,512]{1,0:T(8,128)(2,1)S(1)} %get-tuple-element.82), channel_id=1, source_target_pairs={{0,1},{1,0},{2,3},{3,2},{4,5},{5,4},{6,7},{7,6},{8,9},{9,8},{10,11... | collective-permute-start | bytes 835592 | tf_op jit(solution)/shard_map/ppermute | solution.py:458
  29.9 8.4 %collective-permute-start.12 = (bf16[144,512]{1,0:T(8,128)(2,1)S(1)}, bf16[144,512]{1,0:T(8,128)(2,1)S(1)}, u32[]{:S(2)}, u32[]{:S(2)}) collective-permute-start(bf16[144,512]{1,0:T(8,128)(2,1)S(1)} %get-tuple-element.98), channel_id=1, source_target_pairs={{0,2},{1,3},{2,0},{3,1},{4,6},{5,7},{6,4},{7,5},{8,10},{9,11},{10,... | collective-permute-start | bytes 442376 | tf_op jit(solution)/shard_map/ppermute | solution.py:458
  31.0 9.6 %collective-permute-start.9 = (bf16[144,512]{1,0:T(8,128)(2,1)S(1)}, bf16[144,512]{1,0:T(8,128)(2,1)S(1)}, u32[]{:S(2)}, u32[]{:S(2)}) collective-permute-start(bf16[144,512]{1,0:T(8,128)(2,1)S(1)} %get-tuple-element.92), channel_id=1, source_target_pairs={{0,2},{1,3},{2,0},{3,1},{4,6},{5,7},{6,4},{7,5},{8,10},{9,11},{10,... | collective-permute-start | bytes 442376 | tf_op jit(solution)/shard_map/ppermute | solution.py:458
  35.1 9.3 %collective-permute-start.15 = (bf16[160,512]{1,0:T(8,128)(2,1)S(1)}, bf16[160,512]{1,0:T(8,128)(2,1)S(1)}, u32[]{:S(2)}, u32[]{:S(2)}) collective-permute-start(bf16[160,512]{1,0:T(8,128)(2,1)S(1)} %inner.5), channel_id=1, source_target_pairs={{0,12},{1,13},{2,14},{3,15},{4,8},{5,9},{6,10},{7,11},{8,4},{9,5},... | collective-permute-start | bytes 491528 | tf_op jit(solution)/shard_map/ppermute | solution.py:458
  38.2 11.1 %collective-permute-start.13 = (bf16[160,512]{1,0:T(8,128)(2,1)S(1)}, bf16[160,512]{1,0:T(8,128)(2,1)S(1)}, u32[]{:S(2)}, u32[]{:S(2)}) collective-permute-start(bf16[160,512]{1,0:T(8,128)(2,1)S(1)} %inner.4), channel_id=1, source_target_pairs={{0,8},{1,9},{2,10},{3,11},{4,12},{5,13},{6,14},{7,15},{8,0},{9,1},... | collective-permute-start | bytes 491528 | tf_op jit(solution)/shard_map/ppermute | solution.py:458
  40.6 9.8 %collective-permute-start.10 = (bf16[160,512]{1,0:T(8,128)(2,1)S(1)}, bf16[160,512]{1,0:T(8,128)(2,1)S(1)}, u32[]{:S(2)}, u32[]{:S(2)}) collective-permute-start(bf16[160,512]{1,0:T(8,128)(2,1)S(1)} %inner.3), channel_id=1, source_target_pairs={{0,4},{1,5},{2,6},{3,7},{4,0},{5,1},{6,2},{7,3},{8,12},{9,13},{10,... | collective-permute-start | bytes 491528 | tf_op jit(solution)/shard_map/ppermute | solution.py:458
  40.8 5.2 %collective-permute-start.7 = (bf16[144,512]{1,0:T(8,128)(2,1)S(1)}, bf16[144,512]{1,0:T(8,128)(2,1)S(1)}, u32[]{:S(2)}, u32[]{:S(2)}) collective-permute-start(bf16[144,512]{1,0:T(8,128)(2,1)S(1)} %get-tuple-element.86), channel_id=1, source_target_pairs={{0,2},{1,3},{2,0},{3,1},{4,6},{5,7},{6,4},{7,5},{8,10},{9,11},{10,... | collective-permute-start | bytes 442376 | tf_op jit(solution)/shard_map/ppermute | solution.py:458
  50.5 7.6 %collective-permute-start.16 = (bf16[128,512]{1,0:T(8,128)(2,1)S(1)}, bf16[128,512]{1,0:T(8,128)(2,1)S(1)}, u32[]{:S(2)}, u32[]{:S(2)}) collective-permute-start(bf16[128,512]{1,0:T(8,128)(2,1)S(1)} %get-tuple-element.102.refs_0_), channel_id=1, source_target_pairs={{0,8},{1,9},{2,10},{3,11},{4,12},{5,13},{6,14},{7,15},{8,0},{9,1},... | collective-permute-start | bytes 393224 | tf_op jit(solution)/shard_map/ppermute | solution.py:458
  50.5 7.6 %collective-permute-start.22 = (bf16[128,512]{1,0:T(8,128)(2,1)S(1)}, bf16[128,512]{1,0:T(8,128)(2,1)S(1)}, u32[]{:S(2)}, u32[]{:S(2)}) collective-permute-start(bf16[128,512]{1,0:T(8,128)(2,1)S(1)} %get-tuple-element.102.refs_0_), channel_id=1, source_target_pairs={{0,1},{1,0},{2,3},{3,2},{4,5},{5,4},{6,7},{7,6},{8,9},{9,8},{10,11... | collective-permute-start | bytes 393224 | tf_op jit(solution)/shard_map/ppermute | solution.py:458
  50.6 9.0 %collective-permute-start.19 = (bf16[128,512]{1,0:T(8,128)(2,1)S(1)}, bf16[128,512]{1,0:T(8,128)(2,1)S(1)}, u32[]{:S(2)}, u32[]{:S(2)}) collective-permute-start(bf16[128,512]{1,0:T(8,128)(2,1)S(1)} %get-tuple-element.102.refs_0_), channel_id=1, source_target_pairs={{0,4},{1,5},{2,6},{3,7},{4,0},{5,1},{6,2},{7,3},{8,12},{9,13},{10,... | collective-permute-start | bytes 393224 | tf_op jit(solution)/shard_map/ppermute | solution.py:458
  52.8 8.2 %collective-permute-start.20 = (bf16[128,512]{1,0:T(8,128)(2,1)S(1)}, bf16[128,512]{1,0:T(8,128)(2,1)S(1)}, u32[]{:S(2)}, u32[]{:S(2)}) collective-permute-start(bf16[128,512]{1,0:T(8,128)(2,1)S(1)} %get-tuple-element.102.refs_0_), channel_id=1, source_target_pairs={{0,2},{1,3},{2,0},{3,1},{4,6},{5,7},{6,4},{7,5},{8,10},{9,11},{10,... | collective-permute-start | bytes 393224 | tf_op jit(solution)/shard_map/ppermute | solution.py:458
  58.1 5.3 %collective-permute-start.17 = (bf16[128,512]{1,0:T(8,128)(2,1)S(1)}, bf16[128,512]{1,0:T(8,128)(2,1)S(1)}, u32[]{:S(2)}, u32[]{:S(2)}) collective-permute-start(bf16[128,512]{1,0:T(8,128)(2,1)S(1)} %collective-permute-done.16.refs_2_), channel_id=1, source_target_pairs={{0,4},{1,5},{2,6},{3,7},{4,0},{5,1},{6,2},{7,3},{8,12},{9,13},{10,... | collective-permute-start | bytes 393224 | tf_op jit(solution)/shard_map/ppermute | solution.py:458
  58.1 6.7 %collective-permute-start.26 = (bf16[128,512]{1,0:T(8,128)(2,1)S(1)}, bf16[128,512]{1,0:T(8,128)(2,1)S(1)}, u32[]{:S(2)}, u32[]{:S(2)}) collective-permute-start(bf16[128,512]{1,0:T(8,128)(2,1)S(1)} %collective-permute-done.16.refs_2_), channel_id=1, source_target_pairs={{0,2},{1,3},{2,0},{3,1},{4,6},{5,7},{6,4},{7,5},{8,10},{9,11},{10,... | collective-permute-start | bytes 393224 | tf_op jit(solution)/shard_map/ppermute | solution.py:458
  59.6 7.7 %collective-permute-start.21 = (bf16[128,512]{1,0:T(8,128)(2,1)S(1)}, bf16[128,512]{1,0:T(8,128)(2,1)S(1)}, u32[]{:S(2)}, u32[]{:S(2)}) collective-permute-start(bf16[128,512]{1,0:T(8,128)(2,1)S(1)} %collective-permute-done.19.refs_1_), channel_id=1, source_target_pairs={{0,2},{1,3},{2,0},{3,1},{4,6},{5,7},{6,4},{7,5},{8,10},{9,11},{10,... | collective-permute-start | bytes 393224 | tf_op jit(solution)/shard_map/ppermute | solution.py:458
  61.0 6.3 %collective-permute-start.23 = (bf16[128,512]{1,0:T(8,128)(2,1)S(1)}, bf16[128,512]{1,0:T(8,128)(2,1)S(1)}, u32[]{:S(2)}, u32[]{:S(2)}) collective-permute-start(bf16[128,512]{1,0:T(8,128)(2,1)S(1)} %collective-permute-done.19.refs_1_), channel_id=1, source_target_pairs={{0,1},{1,0},{2,3},{3,2},{4,5},{5,4},{6,7},{7,6},{8,9},{9,8},{10,11... | collective-permute-start | bytes 393224 | tf_op jit(solution)/shard_map/ppermute | solution.py:458
  61.0 6.8 %collective-permute-start.24 = (bf16[128,512]{1,0:T(8,128)(2,1)S(1)}, bf16[128,512]{1,0:T(8,128)(2,1)S(1)}, u32[]{:S(2)}, u32[]{:S(2)}) collective-permute-start(bf16[128,512]{1,0:T(8,128)(2,1)S(1)} %collective-permute-done.16.refs_2_), channel_id=1, source_target_pairs={{0,1},{1,0},{2,3},{3,2},{4,5},{5,4},{6,7},{7,6},{8,9},{9,8},{10,11... | collective-permute-start | bytes 393224 | tf_op jit(solution)/shard_map/ppermute | solution.py:458
  63.4 5.9 %collective-permute-start.18 = (bf16[128,512]{1,0:T(8,128)(2,1)S(1)}, bf16[128,512]{1,0:T(8,128)(2,1)S(1)}, u32[]{:S(2)}, u32[]{:S(2)}) collective-permute-start(bf16[128,512]{1,0:T(8,128)(2,1)S(1)} %collective-permute-done.17.refs_0_), channel_id=1, source_target_pairs={{0,2},{1,3},{2,0},{3,1},{4,6},{5,7},{6,4},{7,5},{8,10},{9,11},{10,... | collective-permute-start | bytes 393224 | tf_op jit(solution)/shard_map/ppermute | solution.py:458
  64.8 5.0 %collective-permute-start.28 = (bf16[128,512]{1,0:T(8,128)(2,1)S(1)}, bf16[128,512]{1,0:T(8,128)(2,1)S(1)}, u32[]{:S(2)}, u32[]{:S(2)}) collective-permute-start(bf16[128,512]{1,0:T(8,128)(2,1)S(1)} %collective-permute-done.20.refs_3_), channel_id=1, source_target_pairs={{0,1},{1,0},{2,3},{3,2},{4,5},{5,4},{6,7},{7,6},{8,9},{9,8},{10,11... | collective-permute-start | bytes 393224 | tf_op jit(solution)/shard_map/ppermute | solution.py:458
  (7 other events, 13.9 us)

commit v12 on v11

--- a/solution.py
+++ b/solution.py
@@ -670,22 +670,25 @@
             if far_outer == outer // 2:
                 value = lax.optimization_barrier((value, pieces[halfway_at]))[0]
             pieces[far_inner * outer + far_outer] = to_inner(value, far_inner)
-    for at in range(1, halfway_at - 1):
-        pieces[halfway_at + at] = to_core(pieces[at])
+    late = [at for at in range(halfway_at) if at > outer or at == 1]
+    for at in range(1, halfway_at):
+        if at not in late:
+            pieces[halfway_at + at] = to_core(pieces[at])
 
     last = outer - 1
     stages = [[], [], []]
     for at in range(band_count):
-        far_outer, far_inner, far_core = at % outer, at // outer % inner, at // halfway_at
+        far_outer, far_inner = at % outer, at // outer % inner
         if far_outer == last:
             stages[2 if far_inner else 1].append(at)
         else:
-            stages[1 if far_inner and (far_core or far_outer == outer // 2) else 0].append(at)
+            stages[1 if at - halfway_at in late or at in late and at > 1 else 0].append(at)
     grads = []
     for places in stages:
         if places is stages[1]:
-            value = lax.optimization_barrier((pieces[halfway_at - 1], *grads))[0]
-            pieces[band_count - 1] = to_core(value)
+            for at in late:
+                value = lax.optimization_barrier((pieces[at], *grads))[0]
+                pieces[halfway_at + at] = to_core(value)
         grads = pl.pallas_call(
             functools.partial(order_kernel, sizes, places, len(grads)),
             out_shape=[

time: 72.1 us -> 72.2 us (level)
  starting transfers between devices: 25.2 us -> 23.5 us
  waiting for transfers between devices: 22.8 us -> 24.5 us
    ppermute x31, starting transfers between devices: 25.2 us -> 23.5 us  [permute(): return lax.ppermute(value, 'band', pairs)]
    ppermute x31, waiting for transfers between devices: 22.8 us -> 24.5 us  [permute(): return lax.ppermute(value, 'band', pairs)]
  transfers between devices with their start and end apart: 31 -> 31, of which waited for: 12 -> 14; matrix products, arithmetic and copies ran while one was open for 0% -> 0% of each run, Pallas kernels for 19% -> 19%
where the time goes in v12:
time: 72.2 us; the launch traced here: 71.9 us
  waiting for transfers between devices  24.5 us (34%)
  starting transfers between devices  23.5 us (33%)
  Pallas kernels  23 us (32%)
  between operations  0.89 us (1%)
    ppermute x31, waiting for transfers between devices, permute(): return lax.ppermute(value, 'band', pairs)  24.5 us
    ppermute x31, starting transfers between devices, permute(): return lax.ppermute(value, 'band', pairs)  23.5 us
    pallas_call x1, Pallas kernels, shards(): pl.pallas_call(functools.partial(main_kernel, lines, sizes), out_shape=[j...  6.74 us
    pallas_call x1, Pallas kernels, shards(): pl.pallas_call(functools.partial(base_kernel, lines), out_shape=[pltpu.VM...  3.54 us
    pallas_call x3, Pallas kernels, shards(): pl.pallas_call(functools.partial(order_kernel, sizes, places, len(grads))...  3.47 us
    pallas_call x1, Pallas kernels, shards(): pl.pallas_call(functools.partial(ready_kernel, lines), out_shape=[pltpu.H...  2.8 us
    pallas_call x1, Pallas kernels, shards(): pl.pallas_call(functools.partial(put_kernel, sizes), out_shape=jax.ShapeD...  2.4 us
    pallas_call x1, Pallas kernels, shards(): pl.pallas_call(mesh_kernel, out_shape=jax.ShapeDtypeStruct((mesh_rows, wi...  2.14 us
  transfers between devices with their start and end apart: 31, of which 14 were waited for; matrix products, arithmetic and copies ran while one was open for 0% of the time, Pallas kernels for 19%

profile of v12, /device:TPU:0, one launch (start us, length us, event | category | flops | bytes accessed | tf_op | source)
XLA Modules:
  0.0 71.9 jit_solution(17026540477708853317)
XLA Ops:
  0.6 1.6 %pick.1 = (bf16[64,512]{1,0:T(8,128)(2,1)S(1)}, bf16[64,512]{1,0:T(8,128)(2,1)S(1)}) custom-call(s32[1,128]{1,0:T(1,128)} %rows_hbm.3, bf16[1024,512]{1,0:T(8,128)(2,1)} %grid_hbm.1), custom_call_target="tpu_custom_call" | custom-call | tf_op jit(solution)/shard_map/pick/pallas_call | solution.py:470
  3.6 2.9 %collective-permute-start.1 = (bf16[64,512]{1,0:T(8,128)(2,1)S(1)}, bf16[64,512]{1,0:T(8,128)(2,1)S(1)}, u32[]{:S(2)}, u32[]{:S(2)}) collective-permute-start(bf16[64,512]{1,0:T(8,128)(2,1)S(1)} %get-tuple-element.73), channel_id=1, source_target_pairs={{0,2},{1,3},{2,0},{3,1},{4,6},{5,7},{6,4},{7,5},{8,10},{9,11},{10,... | collective-permute-start | bytes 196616 | tf_op jit(solution)/shard_map/ppermute | solution.py:458
  6.6 2.8 %ready.1 = (bf16[1536,256]{1,0:T(8,128)(2,1)}, f32[256,512]{1,0:T(8,128)}, f32[256,512]{1,0:T(8,128)}, bf16[256,512]{1,0:T(8,128)(2,1)S(1)}) custom-call(s32[12,128]{1,0:T(8,128)} %bitcast.2, bf16[256,512]{1,0:T(8,128)(2,1)} %mesh_hbm.5, bf16[256,512]{1,0:T(8,128)(2,1)} %cot_hbm.1, bf16[1536,512]{1,0:T(8,128)(2,1)} %w1_hbm.3, bf16[1024,512]{1,0:T(8,128)(2,1)} %wn1_hbm.3, ...), custom_call_target="tpu_custom_call" | custom-call | flops 2000000000 | bytes 4194304 | tf_op jit(solution)/shard_map/ready/pallas_call | solution.py:494
  9.4 1.6 %collective-permute-start.2 = (bf16[32,512]{1,0:T(8,128)(2,1)S(1)}, bf16[32,512]{1,0:T(8,128)(2,1)S(1)}, u32[]{:S(2)}, u32[]{:S(2)}) collective-permute-start(bf16[32,512]{1,0:T(8,128)(2,1)S(1)} %get-tuple-element.75), channel_id=1, source_target_pairs={{0,4},{1,5},{2,6},{3,7},{4,0},{5,1},{6,2},{7,3},{8,12},{9,13},{10,... | collective-permute-start | bytes 98312 | tf_op jit(solution)/shard_map/ppermute | solution.py:458
  11.1 2.6 %collective-permute-start.3 = (bf16[32,512]{1,0:T(8,128)(2,1)S(1)}, bf16[32,512]{1,0:T(8,128)(2,1)S(1)}, u32[]{:S(2)}, u32[]{:S(2)}) collective-permute-start(bf16[32,512]{1,0:T(8,128)(2,1)S(1)} %get-tuple-element.76), channel_id=1, source_target_pairs={{0,8},{1,9},{2,10},{3,11},{4,12},{5,13},{6,14},{7,15},{8,0},{9,1},... | collective-permute-start | bytes 98312 | tf_op jit(solution)/shard_map/ppermute | solution.py:458
  13.9 3.5 %base.1 = (f32[1536,512]{1,0:T(8,128)S(1)}, s32[12,128]{1,0:T(8,128)S(1)}, s32[12,128]{1,0:T(8,128)S(1)}, bf16[512,512]{1,0:T(8,128)(2,1)S(1)}, bf16[512,1536]{1,0:T(8,128)(2,1)}) custom-call(bf16[1536,256]{1,0:T(8,128)(2,1)} %get-tuple-element.61.hot_hbm, bf16[1536,512]{1,0:T(8,128)(2,1)} %edge_hbm.1, bf16[1536,512]{1,0:T(8,128)(2,1)} %w1_hbm.3, ...), custom_call_target="tpu_custom_call" | custom-call | flops 4000000000 | bytes 4194304 | tf_op jit(solution)/shard_map/base/pallas_call | solution.py:521
  17.4 1.9 %collective-permute-done.4.rest_3_ = bf16[32,512]{1,0:T(8,128)(2,1)S(1)} collective-permute-done((bf16[32,512]{1,0:T(8,128)(2,1)S(1)}, bf16[32,512]{1,0:T(8,128)(2,1)S(1)}, u32[]{:S(2)}, u32[]{:S(2)}) %collective-permute-start.4) | collective-permute-done | bytes 32800 | tf_op jit(solution)/shard_map/ppermute | solution.py:458
  19.4 6.7 %edges.1 = (bf16[256,512]{1,0:T(8,128)(2,1)S(1)}, bf16[64,512]{1,0:T(8,128)(2,1)S(1)}, bf16[272,512]{1,0:T(8,128)(2,1)S(1)}, bf16[272,512]{1,0:T(8,128)(2,1)S(1)...) custom-call(bf16[256,512]{1,0:T(8,128)(2,1)} %mesh_hbm.5, ...), custom_call_target="tpu_custom_call" | custom-call | tf_op jit(solution)/shard_map/edges/pallas_call | solution.py:553
  26.2 1.5 %collective-permute-done.5.crossed_ref = bf16[272,512]{1,0:T(8,128)(2,1)S(1)} collective-permute-done((bf16[272,512]{1,0:T(8,128)(2,1)S(1)}, bf16[272,512]{1,0:T(8,128)(2,1)S(1)}, u32[]{:S(2)}, u32[]{:S(2)}) %collective-permute-start.5) | collective-permute-done | bytes 278560 | tf_op jit(solution)/shard_map/ppermute | solution.py:458
  28.4 1.4 %collective-permute-start.14 = (bf16[144,512]{1,0:T(8,128)(2,1)S(1)}, bf16[144,512]{1,0:T(8,128)(2,1)S(1)}, u32[]{:S(2)}, u32[]{:S(2)}) collective-permute-start(bf16[144,512]{1,0:T(8,128)(2,1)S(1)} %get-tuple-element.84), channel_id=1, source_target_pairs={{0,2},{1,3},{2,0},{3,1},{4,6},{5,7},{6,4},{7,5},{8,10},{9,11},{10,... | collective-permute-start | bytes 442376 | tf_op jit(solution)/shard_map/ppermute | solution.py:458
  32.1 3.0 %collective-permute-done.14.refs_0_ = bf16[144,512]{1,0:T(8,128)(2,1)S(1)} collective-permute-done((bf16[144,512]{1,0:T(8,128)(2,1)S(1)}, bf16[144,512]{1,0:T(8,128)(2,1)S(1)}, u32[]{:S(2)}, u32[]{:S(2)}) %collective-permute-start.14) | collective-permute-done | bytes 147488 | tf_op jit(solution)/shard_map/ppermute | solution.py:458
  35.1 1.8 %collective-permute-start.15 = (bf16[160,512]{1,0:T(8,128)(2,1)S(1)}, bf16[160,512]{1,0:T(8,128)(2,1)S(1)}, u32[]{:S(2)}, u32[]{:S(2)}) collective-permute-start(bf16[160,512]{1,0:T(8,128)(2,1)S(1)} %inner.5), channel_id=1, source_target_pairs={{0,12},{1,13},{2,14},{3,15},{4,8},{5,9},{6,10},{7,11},{8,4},{9,5},... | collective-permute-start | bytes 491528 | tf_op jit(solution)/shard_map/ppermute | solution.py:458
  38.3 2.3 %collective-permute-done.9.refs_0_ = bf16[144,512]{1,0:T(8,128)(2,1)S(1)} collective-permute-done((bf16[144,512]{1,0:T(8,128)(2,1)S(1)}, bf16[144,512]{1,0:T(8,128)(2,1)S(1)}, u32[]{:S(2)}, u32[]{:S(2)}) %collective-permute-start.9) | collective-permute-done | bytes 147488 | tf_op jit(solution)/shard_map/ppermute | solution.py:458
  40.8 1.5 %collective-permute-start.7 = (bf16[144,512]{1,0:T(8,128)(2,1)S(1)}, bf16[144,512]{1,0:T(8,128)(2,1)S(1)}, u32[]{:S(2)}, u32[]{:S(2)}) collective-permute-start(bf16[144,512]{1,0:T(8,128)(2,1)S(1)} %get-tuple-element.89), channel_id=1, source_target_pairs={{0,2},{1,3},{2,0},{3,1},{4,6},{5,7},{6,4},{7,5},{8,10},{9,11},{10,... | collective-permute-start | bytes 442376 | tf_op jit(solution)/shard_map/ppermute | solution.py:458
  42.3 2.1 %mesh.1 = bf16[256,512]{1,0:T(8,128)(2,1)} custom-call(bf16[256,512]{1,0:T(8,128)(2,1)} %mesh_hbm.5, bf16[512,512]{1,0:T(8,128)(2,1)} %wn2_hbm.3, bf16[256,512]{1,0:T(8,128)(2,1)S(1)} %get-tuple-element.78.node_ref), custom_call_target="tpu_custom_call" | custom-call | flops 1000000000 | bytes 1048576 | tf_op jit(solution)/shard_map/mesh/pallas_call | solution.py:586
  44.4 1.5 %collective-permute-done.7.refs_0_ = bf16[144,512]{1,0:T(8,128)(2,1)S(1)} collective-permute-done((bf16[144,512]{1,0:T(8,128)(2,1)S(1)}, bf16[144,512]{1,0:T(8,128)(2,1)S(1)}, u32[]{:S(2)}, u32[]{:S(2)}) %collective-permute-start.7) | collective-permute-done | bytes 147488 | tf_op jit(solution)/shard_map/ppermute | solution.py:458
  46.0 3.4 %collective-permute-done.13.refs_2_ = bf16[160,512]{1,0:T(8,128)(2,1)S(1)} collective-permute-done((bf16[160,512]{1,0:T(8,128)(2,1)S(1)}, bf16[160,512]{1,0:T(8,128)(2,1)S(1)}, u32[]{:S(2)}, u32[]{:S(2)}) %collective-permute-start.13) | collective-permute-done | bytes 163872 | tf_op jit(solution)/shard_map/ppermute | solution.py:458
  50.6 1.5 %collective-permute-start.20 = (bf16[128,512]{1,0:T(8,128)(2,1)S(1)}, bf16[128,512]{1,0:T(8,128)(2,1)S(1)}, u32[]{:S(2)}, u32[]{:S(2)}) collective-permute-start(bf16[128,512]{1,0:T(8,128)(2,1)S(1)} %get-tuple-element.105.refs_0_), channel_id=1, source_target_pairs={{0,2},{1,3},{2,0},{3,1},{4,6},{5,7},{6,4},{7,5},{8,10},{9,11},{10,... | collective-permute-start | bytes 393224 | tf_op jit(solution)/shard_map/ppermute | solution.py:458
  52.1 2.1 %collective-permute-start.19 = (bf16[128,512]{1,0:T(8,128)(2,1)S(1)}, bf16[128,512]{1,0:T(8,128)(2,1)S(1)}, u32[]{:S(2)}, u32[]{:S(2)}) collective-permute-start(bf16[128,512]{1,0:T(8,128)(2,1)S(1)} %get-tuple-element.105.refs_0_), channel_id=1, source_target_pairs={{0,4},{1,5},{2,6},{3,7},{4,0},{5,1},{6,2},{7,3},{8,12},{9,13},{10,... | collective-permute-start | bytes 393224 | tf_op jit(solution)/shard_map/ppermute | solution.py:458
  54.2 2.4 %put.1 = f32[1024,512]{1,0:T(8,128)} custom-call(s32[1,128]{1,0:T(1,128)} %rows_hbm.3, bf16[32,512]{1,0:T(8,128)(2,1)S(1)} %get-tuple-element.104.refs_0_, bf16[160,512]{1,0:T(8,128)(2,1)S(1)} %collective-permute-done.10.refs_1_, bf16[160,512]{1,0:T(8,128)(2,1)S(1)} %collective-permute-done.13.refs_2_, bf16[160,512]{1,0:T(8,128)(2,1)S(1)} %collective-permute-done.15.refs_3_), custom_call_target="tpu_custom_call" | custom-call | flops 2000000000 | bytes 2097152 | tf_op jit(solution)/shard_map/put/pallas_call | solution.py:641
  56.7 1.4 %collective-permute-done.16.refs_2_ = bf16[128,512]{1,0:T(8,128)(2,1)S(1)} collective-permute-done((bf16[128,512]{1,0:T(8,128)(2,1)S(1)}, bf16[128,512]{1,0:T(8,128)(2,1)S(1)}, u32[]{:S(2)}, u32[]{:S(2)}) %collective-permute-start.16) | collective-permute-done | bytes 131104 | tf_op jit(solution)/shard_map/ppermute | solution.py:458
  61.3 2.2 %collective-permute-done.17.refs_0_ = bf16[128,512]{1,0:T(8,128)(2,1)S(1)} collective-permute-done((bf16[128,512]{1,0:T(8,128)(2,1)S(1)}, bf16[128,512]{1,0:T(8,128)(2,1)S(1)}, u32[]{:S(2)}, u32[]{:S(2)}) %collective-permute-start.17) | collective-permute-done | bytes 131104 | tf_op jit(solution)/shard_map/ppermute | solution.py:458
  66.2 1.5 %collective-permute-done.25.refs_1_ = bf16[128,512]{1,0:T(8,128)(2,1)S(1)} collective-permute-done((bf16[128,512]{1,0:T(8,128)(2,1)S(1)}, bf16[128,512]{1,0:T(8,128)(2,1)S(1)}, u32[]{:S(2)}, u32[]{:S(2)}) %collective-permute-start.25) | collective-permute-done | bytes 131104 | tf_op jit(solution)/shard_map/ppermute | solution.py:458
  68.2 1.5 %collective-permute-done.18.refs_0_ = bf16[128,512]{1,0:T(8,128)(2,1)S(1)} collective-permute-done((bf16[128,512]{1,0:T(8,128)(2,1)S(1)}, bf16[128,512]{1,0:T(8,128)(2,1)S(1)}, u32[]{:S(2)}, u32[]{:S(2)}) %collective-permute-start.18) | collective-permute-done | bytes 131104 | tf_op jit(solution)/shard_map/ppermute | solution.py:458
  (57 shorter events, 16.1 us)
Async XLA Ops:
  3.6 5.7 %collective-permute-start.1 = (bf16[64,512]{1,0:T(8,128)(2,1)S(1)}, bf16[64,512]{1,0:T(8,128)(2,1)S(1)}, u32[]{:S(2)}, u32[]{:S(2)}) collective-permute-start(bf16[64,512]{1,0:T(8,128)(2,1)S(1)} %get-tuple-element.73), channel_id=1, source_target_pairs={{0,2},{1,3},{2,0},{3,1},{4,6},{5,7},{6,4},{7,5},{8,10},{9,11},{10,... | collective-permute-start | bytes 196616 | tf_op jit(solution)/shard_map/ppermute | solution.py:458
  9.4 8.0 %collective-permute-start.2 = (bf16[32,512]{1,0:T(8,128)(2,1)S(1)}, bf16[32,512]{1,0:T(8,128)(2,1)S(1)}, u32[]{:S(2)}, u32[]{:S(2)}) collective-permute-start(bf16[32,512]{1,0:T(8,128)(2,1)S(1)} %get-tuple-element.75), channel_id=1, source_target_pairs={{0,4},{1,5},{2,6},{3,7},{4,0},{5,1},{6,2},{7,3},{8,12},{9,13},{10,... | collective-permute-start | bytes 98312 | tf_op jit(solution)/shard_map/ppermute | solution.py:458
  11.1 6.4 %collective-permute-start.3 = (bf16[32,512]{1,0:T(8,128)(2,1)S(1)}, bf16[32,512]{1,0:T(8,128)(2,1)S(1)}, u32[]{:S(2)}, u32[]{:S(2)}) collective-permute-start(bf16[32,512]{1,0:T(8,128)(2,1)S(1)} %get-tuple-element.76), channel_id=1, source_target_pairs={{0,8},{1,9},{2,10},{3,11},{4,12},{5,13},{6,14},{7,15},{8,0},{9,1},... | collective-permute-start | bytes 98312 | tf_op jit(solution)/shard_map/ppermute | solution.py:458
  13.7 5.7 %collective-permute-start.4 = (bf16[32,512]{1,0:T(8,128)(2,1)S(1)}, bf16[32,512]{1,0:T(8,128)(2,1)S(1)}, u32[]{:S(2)}, u32[]{:S(2)}) collective-permute-start(bf16[32,512]{1,0:T(8,128)(2,1)S(1)} %get-tuple-element.77), channel_id=1, source_target_pairs={{0,12},{1,13},{2,14},{3,15},{4,8},{5,9},{6,10},{7,11},{8,4},{9,5},... | collective-permute-start | bytes 98312 | tf_op jit(solution)/shard_map/ppermute | solution.py:458
  28.0 3.0 %collective-permute-start.8 = (bf16[272,512]{1,0:T(8,128)(2,1)S(1)}, bf16[272,512]{1,0:T(8,128)(2,1)S(1)}, u32[]{:S(2)}, u32[]{:S(2)}) collective-permute-start(bf16[272,512]{1,0:T(8,128)(2,1)S(1)} %get-tuple-element.92), channel_id=1, source_target_pairs={{0,1},{1,0},{2,3},{3,2},{4,5},{5,4},{6,7},{7,6},{8,9},{9,8},{10,11... | collective-permute-start | bytes 835592 | tf_op jit(solution)/shard_map/ppermute | solution.py:458
  28.4 6.7 %collective-permute-start.14 = (bf16[144,512]{1,0:T(8,128)(2,1)S(1)}, bf16[144,512]{1,0:T(8,128)(2,1)S(1)}, u32[]{:S(2)}, u32[]{:S(2)}) collective-permute-start(bf16[144,512]{1,0:T(8,128)(2,1)S(1)} %get-tuple-element.84), channel_id=1, source_target_pairs={{0,2},{1,3},{2,0},{3,1},{4,6},{5,7},{6,4},{7,5},{8,10},{9,11},{10,... | collective-permute-start | bytes 442376 | tf_op jit(solution)/shard_map/ppermute | solution.py:458
  29.8 10.9 %collective-permute-start.6 = (bf16[272,512]{1,0:T(8,128)(2,1)S(1)}, bf16[272,512]{1,0:T(8,128)(2,1)S(1)}, u32[]{:S(2)}, u32[]{:S(2)}) collective-permute-start(bf16[272,512]{1,0:T(8,128)(2,1)S(1)} %get-tuple-element.85), channel_id=1, source_target_pairs={{0,1},{1,0},{2,3},{3,2},{4,5},{5,4},{6,7},{7,6},{8,9},{9,8},{10,11... | collective-permute-start | bytes 835592 | tf_op jit(solution)/shard_map/ppermute | solution.py:458
  29.9 8.4 %collective-permute-start.12 = (bf16[144,512]{1,0:T(8,128)(2,1)S(1)}, bf16[144,512]{1,0:T(8,128)(2,1)S(1)}, u32[]{:S(2)}, u32[]{:S(2)}) collective-permute-start(bf16[144,512]{1,0:T(8,128)(2,1)S(1)} %get-tuple-element.101), channel_id=1, source_target_pairs={{0,2},{1,3},{2,0},{3,1},{4,6},{5,7},{6,4},{7,5},{8,10},{9,11},{10,... | collective-permute-start | bytes 442376 | tf_op jit(solution)/shard_map/ppermute | solution.py:458
  31.0 9.6 %collective-permute-start.9 = (bf16[144,512]{1,0:T(8,128)(2,1)S(1)}, bf16[144,512]{1,0:T(8,128)(2,1)S(1)}, u32[]{:S(2)}, u32[]{:S(2)}) collective-permute-start(bf16[144,512]{1,0:T(8,128)(2,1)S(1)} %get-tuple-element.95), channel_id=1, source_target_pairs={{0,2},{1,3},{2,0},{3,1},{4,6},{5,7},{6,4},{7,5},{8,10},{9,11},{10,... | collective-permute-start | bytes 442376 | tf_op jit(solution)/shard_map/ppermute | solution.py:458
  35.1 9.3 %collective-permute-start.15 = (bf16[160,512]{1,0:T(8,128)(2,1)S(1)}, bf16[160,512]{1,0:T(8,128)(2,1)S(1)}, u32[]{:S(2)}, u32[]{:S(2)}) collective-permute-start(bf16[160,512]{1,0:T(8,128)(2,1)S(1)} %inner.5), channel_id=1, source_target_pairs={{0,12},{1,13},{2,14},{3,15},{4,8},{5,9},{6,10},{7,11},{8,4},{9,5},... | collective-permute-start | bytes 491528 | tf_op jit(solution)/shard_map/ppermute | solution.py:458
  38.2 11.1 %collective-permute-start.13 = (bf16[160,512]{1,0:T(8,128)(2,1)S(1)}, bf16[160,512]{1,0:T(8,128)(2,1)S(1)}, u32[]{:S(2)}, u32[]{:S(2)}) collective-permute-start(bf16[160,512]{1,0:T(8,128)(2,1)S(1)} %inner.4), channel_id=1, source_target_pairs={{0,8},{1,9},{2,10},{3,11},{4,12},{5,13},{6,14},{7,15},{8,0},{9,1},... | collective-permute-start | bytes 491528 | tf_op jit(solution)/shard_map/ppermute | solution.py:458
  40.6 9.8 %collective-permute-start.10 = (bf16[160,512]{1,0:T(8,128)(2,1)S(1)}, bf16[160,512]{1,0:T(8,128)(2,1)S(1)}, u32[]{:S(2)}, u32[]{:S(2)}) collective-permute-start(bf16[160,512]{1,0:T(8,128)(2,1)S(1)} %inner.3), channel_id=1, source_target_pairs={{0,4},{1,5},{2,6},{3,7},{4,0},{5,1},{6,2},{7,3},{8,12},{9,13},{10,... | collective-permute-start | bytes 491528 | tf_op jit(solution)/shard_map/ppermute | solution.py:458
  40.8 5.2 %collective-permute-start.7 = (bf16[144,512]{1,0:T(8,128)(2,1)S(1)}, bf16[144,512]{1,0:T(8,128)(2,1)S(1)}, u32[]{:S(2)}, u32[]{:S(2)}) collective-permute-start(bf16[144,512]{1,0:T(8,128)(2,1)S(1)} %get-tuple-element.89), channel_id=1, source_target_pairs={{0,2},{1,3},{2,0},{3,1},{4,6},{5,7},{6,4},{7,5},{8,10},{9,11},{10,... | collective-permute-start | bytes 442376 | tf_op jit(solution)/shard_map/ppermute | solution.py:458
  50.5 7.6 %collective-permute-start.16 = (bf16[128,512]{1,0:T(8,128)(2,1)S(1)}, bf16[128,512]{1,0:T(8,128)(2,1)S(1)}, u32[]{:S(2)}, u32[]{:S(2)}) collective-permute-start(bf16[128,512]{1,0:T(8,128)(2,1)S(1)} %get-tuple-element.105.refs_0_), channel_id=1, source_target_pairs={{0,8},{1,9},{2,10},{3,11},{4,12},{5,13},{6,14},{7,15},{8,0},{9,1},... | collective-permute-start | bytes 393224 | tf_op jit(solution)/shard_map/ppermute | solution.py:458
  50.5 8.1 %collective-permute-start.21 = (bf16[128,512]{1,0:T(8,128)(2,1)S(1)}, bf16[128,512]{1,0:T(8,128)(2,1)S(1)}, u32[]{:S(2)}, u32[]{:S(2)}) collective-permute-start(bf16[128,512]{1,0:T(8,128)(2,1)S(1)} %get-tuple-element.105.refs_0_), channel_id=1, source_target_pairs={{0,1},{1,0},{2,3},{3,2},{4,5},{5,4},{6,7},{7,6},{8,9},{9,8},{10,11... | collective-permute-start | bytes 393224 | tf_op jit(solution)/shard_map/ppermute | solution.py:458
  50.6 7.5 %collective-permute-start.20 = (bf16[128,512]{1,0:T(8,128)(2,1)S(1)}, bf16[128,512]{1,0:T(8,128)(2,1)S(1)}, u32[]{:S(2)}, u32[]{:S(2)}) collective-permute-start(bf16[128,512]{1,0:T(8,128)(2,1)S(1)} %get-tuple-element.105.refs_0_), channel_id=1, source_target_pairs={{0,2},{1,3},{2,0},{3,1},{4,6},{5,7},{6,4},{7,5},{8,10},{9,11},{10,... | collective-permute-start | bytes 393224 | tf_op jit(solution)/shard_map/ppermute | solution.py:458
  52.1 8.8 %collective-permute-start.19 = (bf16[128,512]{1,0:T(8,128)(2,1)S(1)}, bf16[128,512]{1,0:T(8,128)(2,1)S(1)}, u32[]{:S(2)}, u32[]{:S(2)}) collective-permute-start(bf16[128,512]{1,0:T(8,128)(2,1)S(1)} %get-tuple-element.105.refs_0_), channel_id=1, source_target_pairs={{0,4},{1,5},{2,6},{3,7},{4,0},{5,1},{6,2},{7,3},{8,12},{9,13},{10,... | collective-permute-start | bytes 393224 | tf_op jit(solution)/shard_map/ppermute | solution.py:458
  58.1 5.5 %collective-permute-start.17 = (bf16[128,512]{1,0:T(8,128)(2,1)S(1)}, bf16[128,512]{1,0:T(8,128)(2,1)S(1)}, u32[]{:S(2)}, u32[]{:S(2)}) collective-permute-start(bf16[128,512]{1,0:T(8,128)(2,1)S(1)} %collective-permute-done.16.refs_2_), channel_id=1, source_target_pairs={{0,4},{1,5},{2,6},{3,7},{4,0},{5,1},{6,2},{7,3},{8,12},{9,13},{10,... | collective-permute-start | bytes 393224 | tf_op jit(solution)/shard_map/ppermute | solution.py:458
  58.1 6.7 %collective-permute-start.22 = (bf16[128,512]{1,0:T(8,128)(2,1)S(1)}, bf16[128,512]{1,0:T(8,128)(2,1)S(1)}, u32[]{:S(2)}, u32[]{:S(2)}) collective-permute-start(bf16[128,512]{1,0:T(8,128)(2,1)S(1)} %collective-permute-done.16.refs_2_), channel_id=1, source_target_pairs={{0,1},{1,0},{2,3},{3,2},{4,5},{5,4},{6,7},{7,6},{8,9},{9,8},{10,11... | collective-permute-start | bytes 393224 | tf_op jit(solution)/shard_map/ppermute | solution.py:458
  58.1 6.7 %collective-permute-start.23 = (bf16[128,512]{1,0:T(8,128)(2,1)S(1)}, bf16[128,512]{1,0:T(8,128)(2,1)S(1)}, u32[]{:S(2)}, u32[]{:S(2)}) collective-permute-start(bf16[128,512]{1,0:T(8,128)(2,1)S(1)} %collective-permute-done.20.refs_3_), channel_id=1, source_target_pairs={{0,1},{1,0},{2,3},{3,2},{4,5},{5,4},{6,7},{7,6},{8,9},{9,8},{10,11... | collective-permute-start | bytes 393224 | tf_op jit(solution)/shard_map/ppermute | solution.py:458
  58.6 7.5 %collective-permute-start.26 = (bf16[128,512]{1,0:T(8,128)(2,1)S(1)}, bf16[128,512]{1,0:T(8,128)(2,1)S(1)}, u32[]{:S(2)}, u32[]{:S(2)}) collective-permute-start(bf16[128,512]{1,0:T(8,128)(2,1)S(1)} %collective-permute-done.16.refs_2_), channel_id=1, source_target_pairs={{0,2},{1,3},{2,0},{3,1},{4,6},{5,7},{6,4},{7,5},{8,10},{9,11},{10,... | collective-permute-start | bytes 393224 | tf_op jit(solution)/shard_map/ppermute | solution.py:458
  60.9 6.8 %collective-permute-start.25 = (bf16[128,512]{1,0:T(8,128)(2,1)S(1)}, bf16[128,512]{1,0:T(8,128)(2,1)S(1)}, u32[]{:S(2)}, u32[]{:S(2)}) collective-permute-start(bf16[128,512]{1,0:T(8,128)(2,1)S(1)} %collective-permute-done.19.refs_1_), channel_id=1, source_target_pairs={{0,2},{1,3},{2,0},{3,1},{4,6},{5,7},{6,4},{7,5},{8,10},{9,11},{10,... | collective-permute-start | bytes 393224 | tf_op jit(solution)/shard_map/ppermute | solution.py:458
  63.6 6.2 %collective-permute-start.18 = (bf16[128,512]{1,0:T(8,128)(2,1)S(1)}, bf16[128,512]{1,0:T(8,128)(2,1)S(1)}, u32[]{:S(2)}, u32[]{:S(2)}) collective-permute-start(bf16[128,512]{1,0:T(8,128)(2,1)S(1)} %collective-permute-done.17.refs_0_), channel_id=1, source_target_pairs={{0,2},{1,3},{2,0},{3,1},{4,6},{5,7},{6,4},{7,5},{8,10},{9,11},{10,... | collective-permute-start | bytes 393224 | tf_op jit(solution)/shard_map/ppermute | solution.py:458
  66.1 3.6 %collective-permute-start.30 = (bf16[128,512]{1,0:T(8,128)(2,1)S(1)}, bf16[128,512]{1,0:T(8,128)(2,1)S(1)}, u32[]{:S(2)}, u32[]{:S(2)}) collective-permute-start(bf16[128,512]{1,0:T(8,128)(2,1)S(1)} %collective-permute-done.26.refs_2_), channel_id=1, source_target_pairs={{0,1},{1,0},{2,3},{3,2},{4,5},{5,4},{6,7},{7,6},{8,9},{9,8},{10,11... | collective-permute-start | bytes 393224 | tf_op jit(solution)/shard_map/ppermute | solution.py:458
  (7 other events, 12.0 us)

commit v13 on v11

--- a/solution.py
+++ b/solution.py
@@ -16,10 +16,6 @@
     return jnp.dot(a, b, preferred_element_type=F32)
 
 
-def dot_tn(a, b):
-    return lax.dot_general(a, b, (((0,), (0,)), ((), ())), preferred_element_type=F32)
-
-
 def dot_nt(a, b):
     return lax.dot_general(a, b, (((1,), (1,)), ((), ())), preferred_element_type=F32)
 
@@ -28,6 +24,16 @@
     high = value.astype(BF16)
     low = (value - high.astype(F32)).astype(BF16)
     return high, low
+
+
+def identity():
+    same = lax.broadcasted_iota(jnp.int32, (256, 256), 0) == lax.broadcasted_iota(jnp.int32, (256, 256), 1)
+    return jnp.where(same, 1.0, 0.0).astype(BF16)
+
+
+def turn(eye, value):
+    blocks = [dot_nt(eye, value[:, at : at + 256]).astype(BF16) for at in range(0, value.shape[1], 256)]
+    return jnp.concatenate(blocks, axis=0)
 
 
 def one_hot_rows(index_row, rows):
@@ -153,6 +159,7 @@
     hot_hbm,
     node_hbm,
     cot_out_hbm,
+    mesh_out_hbm,
     moved_ref,
     dst_ref,
     mesh_ref,
@@ -163,6 +170,7 @@
     hot_ref,
     node_ref,
     cot_out_ref,
+    mesh_out_ref,
     sems,
     out_sems,
 ):
@@ -177,15 +185,17 @@
         (wn2_hbm, wn2_ref),
     ]
     copies = load(pairs, sems)
+    pairs = [(hot_ref, hot_hbm), (node_ref, node_hbm), (cot_out_ref, cot_out_hbm), (mesh_out_ref, mesh_out_hbm)]
     outs = [
-        pltpu.make_async_copy(source, target, out_sems.at[at])
-        for at, (source, target) in enumerate([(hot_ref, hot_hbm), (node_ref, node_hbm), (cot_out_ref, cot_out_hbm)])
+        pltpu.make_async_copy(source, target, out_sems.at[at]) for at, (source, target) in enumerate(pairs)
     ]
     copies[0].wait()
     for at in range(hot_ref.shape[0] // tile):
         hot_ref[at * tile : (at + 1) * tile, :] = tile_columns(dst_ref, at, lines, hot_ref.shape[1])
     outs[0].start()
     copies[1].wait()
+    mesh_out_ref[...] = turn(identity(), mesh_ref[...])
+    outs[3].start()
     copies[3].wait()
     node_ref[...] = dot_nn(mesh_ref[...], wn1_ref[...])
     outs[1].start()
@@ -226,8 +236,7 @@
     pairs += [(w1_hbm.at[pl.ds(2 * width, width), :], w1_ref), (hot_hbm, hot_ref)]
     pairs += [(w1_hbm.at[pl.ds(0, width), :], top_ref), (slot_hbm, slot_ref), (dst_hbm, dst_ref)]
     copies = load(pairs, sems)
-    same = lax.broadcasted_iota(jnp.int32, (256, 256), 0) == lax.broadcasted_iota(jnp.int32, (256, 256), 1)
-    eye = jnp.where(same, 1.0, 0.0).astype(BF16)
+    eye = identity()
     outs = []
     for at in range(tiles):
         rows = slice(at * tile, (at + 1) * tile)
@@ -270,8 +279,7 @@
     send_refs, keep_refs, rest = rest[2 : 2 + outer], rest[2 + outer : 2 + 2 * outer], rest[2 + 2 * outer :]
     slope_ref, value_ref, both_ref, grads_ref, slot_grads_ref, ordered_ref = rest[:6]
     mesh_ref, w2_ref, wn1_ref, hot_ref, node_ref, cot_ref, picks_ref, sems = rest[6:]
-    width = mesh_ref.shape[1]
-    mesh_rows = mesh_ref.shape[0]
+    width, mesh_rows = mesh_ref.shape
     slot_rows = ordered_ref.shape[0]
     tile = lines * 128
     tiles = base_ref.shape[0] // tile
@@ -293,6 +301,7 @@
         both_ref[:slot_rows, rows] = tile_rows(slot_ref, at, lines, slot_rows)
         both_ref[slot_rows : slot_rows + mesh_rows, rows] = tile_rows(dst_ref, at, lines, mesh_rows)
 
+    eye = identity()
     slots = slots_value
     slot_pair = jnp.concatenate(split(dot_nn(slots, w1_ref[...])), axis=0)
     for at in range(tiles):
@@ -309,7 +318,6 @@
         copy.wait()
     hidden_sums = dot_nn(both_ref[slot_rows : slot_rows + mesh_rows, :], value_ref[...]).astype(BF16)
     received = dot_nn(hidden_sums, w2_ref[...]).astype(BF16)
-    mesh = mesh_ref[...]
     pre_node = node_ref[...] + dot_nn(received, wn1_ref[...])
     sigma = 0.5 + 0.5 * jnp.tanh(0.5 * pre_node)
     node = pre_node * sigma
@@ -322,15 +330,15 @@
         rows = slice(at * tile, (at + 1) * tile)
         value_ref[rows, :] = (dot_nn(hot_ref[rows, :], spread) * slope_ref[rows, :]).astype(BF16)
 
-    grads_ref[3 * width :, :] = dot_tn(hidden_sums, d_received)
+    grads_ref[3 * width :, :] = dot_nn(turn(eye, hidden_sums), d_received)
     node_out_ref[...] = node.astype(BF16)
     copies[-1].wait()
     product = dot_nn(both_ref[...], value_ref[...])
     sums = product[: slot_rows + mesh_rows].astype(BF16)
     grads_ref[2 * width : 3 * width, :] = product[slot_rows + mesh_rows :]
     slot_grads_ref[...] = dot_nt(sums[:slot_rows], w1_ref[...])
-    grads_ref[:width, :] = dot_tn(slots, sums[:slot_rows])
-    grads_ref[width : 2 * width, :] = dot_tn(mesh, sums[slot_rows:])
+    grads_ref[:width, :] = dot_nn(turn(eye, slots), sums[:slot_rows])
+    grads_ref[width : 2 * width, :] = dot_nn(mesh_ref[...], sums[slot_rows:])
 
     chunk = grads_ref.shape[0] // (2 * outer * inner)
     cap = slot_rows // (2 * outer * inner)
@@ -491,16 +499,17 @@
             name="mix",
         )(*values)
 
-    hot, node, cot, moved = pl.pallas_call(
+    hot, node, cot, mesh_turned, moved = pl.pallas_call(
         functools.partial(ready_kernel, lines),
         out_shape=[
             pltpu.HBM((edges, mesh_rows), BF16),
             pltpu.HBM((mesh_rows, hidden_width), F32),
             pltpu.HBM((mesh_rows, hidden_width), F32),
+            pltpu.HBM((width, mesh_rows), BF16),
             pltpu.VMEM((mesh_rows, hidden_width), BF16),
         ],
         in_specs=specs(pltpu.HBM, 6),
-        out_specs=specs(pltpu.HBM, 3) + specs(pltpu.VMEM, 1),
+        out_specs=specs(pltpu.HBM, 4) + specs(pltpu.VMEM, 1),
         scratch_shapes=[
             pltpu.VMEM(dst_index.shape, jnp.int32),
             pltpu.VMEM(mesh_latent.shape, BF16),
@@ -511,8 +520,9 @@
             pltpu.VMEM((edges, mesh_rows), BF16),
             pltpu.VMEM((mesh_rows, hidden_width), F32),
             pltpu.VMEM((mesh_rows, hidden_width), F32),
+            pltpu.VMEM((width, mesh_rows), BF16),
             pltpu.SemaphoreType.DMA((6,)),
-            pltpu.SemaphoreType.DMA((3,)),
+            pltpu.SemaphoreType.DMA((4,)),
         ],
         compiler_params=params(16),
         cost_estimate=cost(2 * 10**9, 4 * MIB),
@@ -567,7 +577,7 @@
             pltpu.VMEM((grad_rows, hidden_width), F32),
             pltpu.VMEM((slot_rows, width), F32),
             pltpu.VMEM((slot_rows, width), F32),
-            pltpu.VMEM(mesh_latent.shape, BF16),
+            pltpu.VMEM((width, mesh_rows), BF16),
             pltpu.VMEM(w_edge2.shape, BF16),
             pltpu.VMEM((w_node1.shape[0] - width, w_node1.shape[1]), BF16),
             pltpu.VMEM(hot.shape, BF16),
@@ -579,7 +589,7 @@
         compiler_params=params(40),
         name="edges",
     )(
-        *pinned(pltpu.HBM, mesh_latent, w_edge2, w_node1, turned, hot, node, cot),
+        *pinned(pltpu.HBM, mesh_turned, w_edge2, w_node1, turned, hot, node, cot),
         *pinned(pltpu.VMEM, base, *ahead),
         *slot_blocks,
     )

time: 72.1 us -> 72.4 us (level)
  transfers between devices with their start and end apart: 31 -> 31, of which waited for: 12 -> 13; matrix products, arithmetic and copies ran while one was open for 0% -> 0% of each run, Pallas kernels for 19% -> 19%
where the time goes in v13:
time: 72.4 us; the launch traced here: 72.2 us
  starting transfers between devices  25.2 us (35%)
  Pallas kernels  23.3 us (32%)
  waiting for transfers between devices  22.9 us (32%)
  between operations  0.86 us (1%)
    ppermute x31, starting transfers between devices, permute(): return lax.ppermute(value, 'band', pairs)  25.2 us
    ppermute x31, waiting for transfers between devices, permute(): return lax.ppermute(value, 'band', pairs)  22.9 us
    pallas_call x1, Pallas kernels, shards(): pl.pallas_call(functools.partial(main_kernel, lines, sizes), out_shape=[j...  7.05 us
    pallas_call x1, Pallas kernels, shards(): pl.pallas_call(functools.partial(base_kernel, lines), out_shape=[pltpu.VM...  3.55 us
    pallas_call x3, Pallas kernels, shards(): pl.pallas_call(functools.partial(order_kernel, sizes, places, len(grads))...  3.46 us
    pallas_call x1, Pallas kernels, shards(): pl.pallas_call(functools.partial(ready_kernel, lines), out_shape=[pltpu.H...  2.81 us
    pallas_call x1, Pallas kernels, shards(): pl.pallas_call(functools.partial(put_kernel, sizes), out_shape=jax.ShapeD...  2.39 us
    pallas_call x1, Pallas kernels, shards(): pl.pallas_call(mesh_kernel, out_shape=jax.ShapeDtypeStruct((mesh_rows, wi...  2.14 us
  transfers between devices with their start and end apart: 31, of which 13 were waited for; matrix products, arithmetic and copies ran while one was open for 0% of the time, Pallas kernels for 19%

profile of v13, /device:TPU:0, one launch (start us, length us, event | category | flops | bytes accessed | tf_op | source)
XLA Modules:
  0.0 72.2 jit_solution(5982240772374908359)
XLA Ops:
  0.6 1.6 %pick.1 = (bf16[64,512]{1,0:T(8,128)(2,1)S(1)}, bf16[64,512]{1,0:T(8,128)(2,1)S(1)}) custom-call(s32[1,128]{1,0:T(1,128)} %rows_hbm.3, bf16[1024,512]{1,0:T(8,128)(2,1)} %grid_hbm.1), custom_call_target="tpu_custom_call" | custom-call | tf_op jit(solution)/shard_map/pick/pallas_call | solution.py:478
  3.6 2.9 %collective-permute-start.1 = (bf16[64,512]{1,0:T(8,128)(2,1)S(1)}, bf16[64,512]{1,0:T(8,128)(2,1)S(1)}, u32[]{:S(2)}, u32[]{:S(2)}) collective-permute-start(bf16[64,512]{1,0:T(8,128)(2,1)S(1)} %get-tuple-element.72), channel_id=1, source_target_pairs={{0,2},{1,3},{2,0},{3,1},{4,6},{5,7},{6,4},{7,5},{8,10},{9,11},{10,... | collective-permute-start | bytes 196616 | tf_op jit(solution)/shard_map/ppermute | solution.py:466
  6.6 2.8 %ready.1 = (bf16[1536,256]{1,0:T(8,128)(2,1)}, f32[256,512]{1,0:T(8,128)}, f32[256,512]{1,0:T(8,128)}, bf16[512,256]{1,0:T(8,128)(2,1)}, bf16[256,512]{1,0:T(8,128)(2,1)S(1)}) custom-call(s32[12,128]{1,0:T(8,128)} %bitcast.2, bf16[256,512]{1,0:T(8,128)(2,1)} %mesh_hbm.3, bf16[256,512]{1,0:T(8,128)(2,1)} %cot_hbm.1, bf16[1536,512]{1,0:T(8,128)(2,1)} %w1_hbm.3, ...), custom_call_target="tpu_custom_call" | custom-call | flops 2000000000 | bytes 4194304 | tf_op jit(solution)/shard_map/ready/pallas_call | solution.py:502
  9.4 1.6 %collective-permute-start.2 = (bf16[32,512]{1,0:T(8,128)(2,1)S(1)}, bf16[32,512]{1,0:T(8,128)(2,1)S(1)}, u32[]{:S(2)}, u32[]{:S(2)}) collective-permute-start(bf16[32,512]{1,0:T(8,128)(2,1)S(1)} %get-tuple-element.74), channel_id=1, source_target_pairs={{0,4},{1,5},{2,6},{3,7},{4,0},{5,1},{6,2},{7,3},{8,12},{9,13},{10,... | collective-permute-start | bytes 98312 | tf_op jit(solution)/shard_map/ppermute | solution.py:466
  11.1 2.6 %collective-permute-start.3 = (bf16[32,512]{1,0:T(8,128)(2,1)S(1)}, bf16[32,512]{1,0:T(8,128)(2,1)S(1)}, u32[]{:S(2)}, u32[]{:S(2)}) collective-permute-start(bf16[32,512]{1,0:T(8,128)(2,1)S(1)} %get-tuple-element.75), channel_id=1, source_target_pairs={{0,8},{1,9},{2,10},{3,11},{4,12},{5,13},{6,14},{7,15},{8,0},{9,1},... | collective-permute-start | bytes 98312 | tf_op jit(solution)/shard_map/ppermute | solution.py:466
  13.9 3.5 %base.1 = (f32[1536,512]{1,0:T(8,128)S(1)}, s32[12,128]{1,0:T(8,128)S(1)}, s32[12,128]{1,0:T(8,128)S(1)}, bf16[512,512]{1,0:T(8,128)(2,1)S(1)}, bf16[512,1536]{1,0:T(8,128)(2,1)}) custom-call(bf16[1536,256]{1,0:T(8,128)(2,1)} %get-tuple-element.60.hot_hbm, bf16[1536,512]{1,0:T(8,128)(2,1)} %edge_hbm.1, bf16[1536,512]{1,0:T(8,128)(2,1)} %w1_hbm.3, ...), custom_call_target="tpu_custom_call" | custom-call | flops 4000000000 | bytes 4194304 | tf_op jit(solution)/shard_map/base/pallas_call | solution.py:531
  17.5 1.9 %collective-permute-done.4.rest_3_ = bf16[32,512]{1,0:T(8,128)(2,1)S(1)} collective-permute-done((bf16[32,512]{1,0:T(8,128)(2,1)S(1)}, bf16[32,512]{1,0:T(8,128)(2,1)S(1)}, u32[]{:S(2)}, u32[]{:S(2)}) %collective-permute-start.4) | collective-permute-done | bytes 32800 | tf_op jit(solution)/shard_map/ppermute | solution.py:466
  19.4 7.1 %edges.1 = (bf16[256,512]{1,0:T(8,128)(2,1)S(1)}, bf16[64,512]{1,0:T(8,128)(2,1)S(1)}, bf16[272,512]{1,0:T(8,128)(2,1)S(1)}, bf16[272,512]{1,0:T(8,128)(2,1)S(1)...) custom-call(bf16[512,256]{1,0:T(8,128)(2,1)} %get-tuple-element.59.m, ...), custom_call_target="tpu_custom_call" | custom-call | tf_op jit(solution)/shard_map/edges/pallas_call | solution.py:563
  26.5 1.5 %collective-permute-done.5.crossed_ref = bf16[272,512]{1,0:T(8,128)(2,1)S(1)} collective-permute-done((bf16[272,512]{1,0:T(8,128)(2,1)S(1)}, bf16[272,512]{1,0:T(8,128)(2,1)S(1)}, u32[]{:S(2)}, u32[]{:S(2)}) %collective-permute-start.5) | collective-permute-done | bytes 278560 | tf_op jit(solution)/shard_map/ppermute | solution.py:466
  32.4 3.0 %collective-permute-done.14.refs_0_ = bf16[144,512]{1,0:T(8,128)(2,1)S(1)} collective-permute-done((bf16[144,512]{1,0:T(8,128)(2,1)S(1)}, bf16[144,512]{1,0:T(8,128)(2,1)S(1)}, u32[]{:S(2)}, u32[]{:S(2)}) %collective-permute-start.14) | collective-permute-done | bytes 147488 | tf_op jit(solution)/shard_map/ppermute | solution.py:466
  35.4 1.8 %collective-permute-start.15 = (bf16[160,512]{1,0:T(8,128)(2,1)S(1)}, bf16[160,512]{1,0:T(8,128)(2,1)S(1)}, u32[]{:S(2)}, u32[]{:S(2)}) collective-permute-start(bf16[160,512]{1,0:T(8,128)(2,1)S(1)} %inner.5), channel_id=1, source_target_pairs={{0,12},{1,13},{2,14},{3,15},{4,8},{5,9},{6,10},{7,11},{8,4},{9,5},... | collective-permute-start | bytes 491528 | tf_op jit(solution)/shard_map/ppermute | solution.py:466
  38.7 2.3 %collective-permute-done.9.refs_0_ = bf16[144,512]{1,0:T(8,128)(2,1)S(1)} collective-permute-done((bf16[144,512]{1,0:T(8,128)(2,1)S(1)}, bf16[144,512]{1,0:T(8,128)(2,1)S(1)}, u32[]{:S(2)}, u32[]{:S(2)}) %collective-permute-start.9) | collective-permute-done | bytes 147488 | tf_op jit(solution)/shard_map/ppermute | solution.py:466
  41.1 1.5 %collective-permute-start.7 = (bf16[144,512]{1,0:T(8,128)(2,1)S(1)}, bf16[144,512]{1,0:T(8,128)(2,1)S(1)}, u32[]{:S(2)}, u32[]{:S(2)}) collective-permute-start(bf16[144,512]{1,0:T(8,128)(2,1)S(1)} %get-tuple-element.88), channel_id=1, source_target_pairs={{0,2},{1,3},{2,0},{3,1},{4,6},{5,7},{6,4},{7,5},{8,10},{9,11},{10,... | collective-permute-start | bytes 442376 | tf_op jit(solution)/shard_map/ppermute | solution.py:466
  42.6 2.1 %mesh.1 = bf16[256,512]{1,0:T(8,128)(2,1)} custom-call(bf16[256,512]{1,0:T(8,128)(2,1)} %mesh_hbm.3, bf16[512,512]{1,0:T(8,128)(2,1)} %wn2_hbm.3, bf16[256,512]{1,0:T(8,128)(2,1)S(1)} %get-tuple-element.77.node_ref), custom_call_target="tpu_custom_call" | custom-call | flops 1000000000 | bytes 1048576 | tf_op jit(solution)/shard_map/mesh/pallas_call | solution.py:596
  44.7 1.6 %collective-permute-done.7.refs_0_ = bf16[144,512]{1,0:T(8,128)(2,1)S(1)} collective-permute-done((bf16[144,512]{1,0:T(8,128)(2,1)S(1)}, bf16[144,512]{1,0:T(8,128)(2,1)S(1)}, u32[]{:S(2)}, u32[]{:S(2)}) %collective-permute-start.7) | collective-permute-done | bytes 147488 | tf_op jit(solution)/shard_map/ppermute | solution.py:466
  46.3 3.4 %collective-permute-done.13.refs_2_ = bf16[160,512]{1,0:T(8,128)(2,1)S(1)} collective-permute-done((bf16[160,512]{1,0:T(8,128)(2,1)S(1)}, bf16[160,512]{1,0:T(8,128)(2,1)S(1)}, u32[]{:S(2)}, u32[]{:S(2)}) %collective-permute-start.13) | collective-permute-done | bytes 163872 | tf_op jit(solution)/shard_map/ppermute | solution.py:466
  50.9 2.2 %collective-permute-start.19 = (bf16[128,512]{1,0:T(8,128)(2,1)S(1)}, bf16[128,512]{1,0:T(8,128)(2,1)S(1)}, u32[]{:S(2)}, u32[]{:S(2)}) collective-permute-start(bf16[128,512]{1,0:T(8,128)(2,1)S(1)} %get-tuple-element.104.refs_0_), channel_id=1, source_target_pairs={{0,4},{1,5},{2,6},{3,7},{4,0},{5,1},{6,2},{7,3},{8,12},{9,13},{10,... | collective-permute-start | bytes 393224 | tf_op jit(solution)/shard_map/ppermute | solution.py:466
  53.1 1.4 %collective-permute-start.20 = (bf16[128,512]{1,0:T(8,128)(2,1)S(1)}, bf16[128,512]{1,0:T(8,128)(2,1)S(1)}, u32[]{:S(2)}, u32[]{:S(2)}) collective-permute-start(bf16[128,512]{1,0:T(8,128)(2,1)S(1)} %get-tuple-element.104.refs_0_), channel_id=1, source_target_pairs={{0,2},{1,3},{2,0},{3,1},{4,6},{5,7},{6,4},{7,5},{8,10},{9,11},{10,... | collective-permute-start | bytes 393224 | tf_op jit(solution)/shard_map/ppermute | solution.py:466
  54.6 2.4 %put.1 = f32[1024,512]{1,0:T(8,128)} custom-call(s32[1,128]{1,0:T(1,128)} %rows_hbm.3, bf16[32,512]{1,0:T(8,128)(2,1)S(1)} %get-tuple-element.103.refs_0_, bf16[160,512]{1,0:T(8,128)(2,1)S(1)} %collective-permute-done.10.refs_1_, bf16[160,512]{1,0:T(8,128)(2,1)S(1)} %collective-permute-done.13.refs_2_, bf16[160,512]{1,0:T(8,128)(2,1)S(1)} %collective-permute-done.15.refs_3_), custom_call_target="tpu_custom_call" | custom-call | flops 2000000000 | bytes 2097152 | tf_op jit(solution)/shard_map/put/pallas_call | solution.py:651
  57.0 1.5 %collective-permute-done.16.refs_2_ = bf16[128,512]{1,0:T(8,128)(2,1)S(1)} collective-permute-done((bf16[128,512]{1,0:T(8,128)(2,1)S(1)}, bf16[128,512]{1,0:T(8,128)(2,1)S(1)}, u32[]{:S(2)}, u32[]{:S(2)}) %collective-permute-start.16) | collective-permute-done | bytes 131104 | tf_op jit(solution)/shard_map/ppermute | solution.py:466
  58.4 1.4 %collective-permute-start.26 = (bf16[128,512]{1,0:T(8,128)(2,1)S(1)}, bf16[128,512]{1,0:T(8,128)(2,1)S(1)}, u32[]{:S(2)}, u32[]{:S(2)}) collective-permute-start(bf16[128,512]{1,0:T(8,128)(2,1)S(1)} %collective-permute-done.16.refs_2_), channel_id=1, source_target_pairs={{0,2},{1,3},{2,0},{3,1},{4,6},{5,7},{6,4},{7,5},{8,10},{9,11},{10,... | collective-permute-start | bytes 393224 | tf_op jit(solution)/shard_map/ppermute | solution.py:466
  59.9 1.4 %collective-permute-start.21 = (bf16[128,512]{1,0:T(8,128)(2,1)S(1)}, bf16[128,512]{1,0:T(8,128)(2,1)S(1)}, u32[]{:S(2)}, u32[]{:S(2)}) collective-permute-start(bf16[128,512]{1,0:T(8,128)(2,1)S(1)} %collective-permute-done.19.refs_1_), channel_id=1, source_target_pairs={{0,2},{1,3},{2,0},{3,1},{4,6},{5,7},{6,4},{7,5},{8,10},{9,11},{10,... | collective-permute-start | bytes 393224 | tf_op jit(solution)/shard_map/ppermute | solution.py:466
  61.8 1.8 %collective-permute-done.17.refs_0_ = bf16[128,512]{1,0:T(8,128)(2,1)S(1)} collective-permute-done((bf16[128,512]{1,0:T(8,128)(2,1)S(1)}, bf16[128,512]{1,0:T(8,128)(2,1)S(1)}, u32[]{:S(2)}, u32[]{:S(2)}) %collective-permute-start.17) | collective-permute-done | bytes 131104 | tf_op jit(solution)/shard_map/ppermute | solution.py:466
  65.1 2.5 %collective-permute-done.21.refs_4_ = bf16[128,512]{1,0:T(8,128)(2,1)S(1)} collective-permute-done((bf16[128,512]{1,0:T(8,128)(2,1)S(1)}, bf16[128,512]{1,0:T(8,128)(2,1)S(1)}, u32[]{:S(2)}, u32[]{:S(2)}) %collective-permute-start.21) | collective-permute-done | bytes 131104 | tf_op jit(solution)/shard_map/ppermute | solution.py:466
  (57 shorter events, 15.5 us)
Async XLA Ops:
  3.6 5.8 %collective-permute-start.1 = (bf16[64,512]{1,0:T(8,128)(2,1)S(1)}, bf16[64,512]{1,0:T(8,128)(2,1)S(1)}, u32[]{:S(2)}, u32[]{:S(2)}) collective-permute-start(bf16[64,512]{1,0:T(8,128)(2,1)S(1)} %get-tuple-element.72), channel_id=1, source_target_pairs={{0,2},{1,3},{2,0},{3,1},{4,6},{5,7},{6,4},{7,5},{8,10},{9,11},{10,... | collective-permute-start | bytes 196616 | tf_op jit(solution)/shard_map/ppermute | solution.py:466
  9.4 8.0 %collective-permute-start.2 = (bf16[32,512]{1,0:T(8,128)(2,1)S(1)}, bf16[32,512]{1,0:T(8,128)(2,1)S(1)}, u32[]{:S(2)}, u32[]{:S(2)}) collective-permute-start(bf16[32,512]{1,0:T(8,128)(2,1)S(1)} %get-tuple-element.74), channel_id=1, source_target_pairs={{0,4},{1,5},{2,6},{3,7},{4,0},{5,1},{6,2},{7,3},{8,12},{9,13},{10,... | collective-permute-start | bytes 98312 | tf_op jit(solution)/shard_map/ppermute | solution.py:466
  11.1 6.4 %collective-permute-start.3 = (bf16[32,512]{1,0:T(8,128)(2,1)S(1)}, bf16[32,512]{1,0:T(8,128)(2,1)S(1)}, u32[]{:S(2)}, u32[]{:S(2)}) collective-permute-start(bf16[32,512]{1,0:T(8,128)(2,1)S(1)} %get-tuple-element.75), channel_id=1, source_target_pairs={{0,8},{1,9},{2,10},{3,11},{4,12},{5,13},{6,14},{7,15},{8,0},{9,1},... | collective-permute-start | bytes 98312 | tf_op jit(solution)/shard_map/ppermute | solution.py:466
  13.7 5.7 %collective-permute-start.4 = (bf16[32,512]{1,0:T(8,128)(2,1)S(1)}, bf16[32,512]{1,0:T(8,128)(2,1)S(1)}, u32[]{:S(2)}, u32[]{:S(2)}) collective-permute-start(bf16[32,512]{1,0:T(8,128)(2,1)S(1)} %get-tuple-element.76), channel_id=1, source_target_pairs={{0,12},{1,13},{2,14},{3,15},{4,8},{5,9},{6,10},{7,11},{8,4},{9,5},... | collective-permute-start | bytes 98312 | tf_op jit(solution)/shard_map/ppermute | solution.py:466
  28.3 3.0 %collective-permute-start.8 = (bf16[272,512]{1,0:T(8,128)(2,1)S(1)}, bf16[272,512]{1,0:T(8,128)(2,1)S(1)}, u32[]{:S(2)}, u32[]{:S(2)}) collective-permute-start(bf16[272,512]{1,0:T(8,128)(2,1)S(1)} %get-tuple-element.91), channel_id=1, source_target_pairs={{0,1},{1,0},{2,3},{3,2},{4,5},{5,4},{6,7},{7,6},{8,9},{9,8},{10,11... | collective-permute-start | bytes 835592 | tf_op jit(solution)/shard_map/ppermute | solution.py:466
  28.7 6.7 %collective-permute-start.14 = (bf16[144,512]{1,0:T(8,128)(2,1)S(1)}, bf16[144,512]{1,0:T(8,128)(2,1)S(1)}, u32[]{:S(2)}, u32[]{:S(2)}) collective-permute-start(bf16[144,512]{1,0:T(8,128)(2,1)S(1)} %get-tuple-element.83), channel_id=1, source_target_pairs={{0,2},{1,3},{2,0},{3,1},{4,6},{5,7},{6,4},{7,5},{8,10},{9,11},{10,... | collective-permute-start | bytes 442376 | tf_op jit(solution)/shard_map/ppermute | solution.py:466
  30.1 10.9 %collective-permute-start.6 = (bf16[272,512]{1,0:T(8,128)(2,1)S(1)}, bf16[272,512]{1,0:T(8,128)(2,1)S(1)}, u32[]{:S(2)}, u32[]{:S(2)}) collective-permute-start(bf16[272,512]{1,0:T(8,128)(2,1)S(1)} %get-tuple-element.84), channel_id=1, source_target_pairs={{0,1},{1,0},{2,3},{3,2},{4,5},{5,4},{6,7},{7,6},{8,9},{9,8},{10,11... | collective-permute-start | bytes 835592 | tf_op jit(solution)/shard_map/ppermute | solution.py:466
  30.2 8.4 %collective-permute-start.12 = (bf16[144,512]{1,0:T(8,128)(2,1)S(1)}, bf16[144,512]{1,0:T(8,128)(2,1)S(1)}, u32[]{:S(2)}, u32[]{:S(2)}) collective-permute-start(bf16[144,512]{1,0:T(8,128)(2,1)S(1)} %get-tuple-element.100), channel_id=1, source_target_pairs={{0,2},{1,3},{2,0},{3,1},{4,6},{5,7},{6,4},{7,5},{8,10},{9,11},{10,... | collective-permute-start | bytes 442376 | tf_op jit(solution)/shard_map/ppermute | solution.py:466
  31.3 9.6 %collective-permute-start.9 = (bf16[144,512]{1,0:T(8,128)(2,1)S(1)}, bf16[144,512]{1,0:T(8,128)(2,1)S(1)}, u32[]{:S(2)}, u32[]{:S(2)}) collective-permute-start(bf16[144,512]{1,0:T(8,128)(2,1)S(1)} %get-tuple-element.94), channel_id=1, source_target_pairs={{0,2},{1,3},{2,0},{3,1},{4,6},{5,7},{6,4},{7,5},{8,10},{9,11},{10,... | collective-permute-start | bytes 442376 | tf_op jit(solution)/shard_map/ppermute | solution.py:466
  35.4 9.3 %collective-permute-start.15 = (bf16[160,512]{1,0:T(8,128)(2,1)S(1)}, bf16[160,512]{1,0:T(8,128)(2,1)S(1)}, u32[]{:S(2)}, u32[]{:S(2)}) collective-permute-start(bf16[160,512]{1,0:T(8,128)(2,1)S(1)} %inner.5), channel_id=1, source_target_pairs={{0,12},{1,13},{2,14},{3,15},{4,8},{5,9},{6,10},{7,11},{8,4},{9,5},... | collective-permute-start | bytes 491528 | tf_op jit(solution)/shard_map/ppermute | solution.py:466
  38.6 11.1 %collective-permute-start.13 = (bf16[160,512]{1,0:T(8,128)(2,1)S(1)}, bf16[160,512]{1,0:T(8,128)(2,1)S(1)}, u32[]{:S(2)}, u32[]{:S(2)}) collective-permute-start(bf16[160,512]{1,0:T(8,128)(2,1)S(1)} %inner.4), channel_id=1, source_target_pairs={{0,8},{1,9},{2,10},{3,11},{4,12},{5,13},{6,14},{7,15},{8,0},{9,1},... | collective-permute-start | bytes 491528 | tf_op jit(solution)/shard_map/ppermute | solution.py:466
  40.9 9.8 %collective-permute-start.10 = (bf16[160,512]{1,0:T(8,128)(2,1)S(1)}, bf16[160,512]{1,0:T(8,128)(2,1)S(1)}, u32[]{:S(2)}, u32[]{:S(2)}) collective-permute-start(bf16[160,512]{1,0:T(8,128)(2,1)S(1)} %inner.3), channel_id=1, source_target_pairs={{0,4},{1,5},{2,6},{3,7},{4,0},{5,1},{6,2},{7,3},{8,12},{9,13},{10,... | collective-permute-start | bytes 491528 | tf_op jit(solution)/shard_map/ppermute | solution.py:466
  41.1 5.2 %collective-permute-start.7 = (bf16[144,512]{1,0:T(8,128)(2,1)S(1)}, bf16[144,512]{1,0:T(8,128)(2,1)S(1)}, u32[]{:S(2)}, u32[]{:S(2)}) collective-permute-start(bf16[144,512]{1,0:T(8,128)(2,1)S(1)} %get-tuple-element.88), channel_id=1, source_target_pairs={{0,2},{1,3},{2,0},{3,1},{4,6},{5,7},{6,4},{7,5},{8,10},{9,11},{10,... | collective-permute-start | bytes 442376 | tf_op jit(solution)/shard_map/ppermute | solution.py:466
  50.8 7.6 %collective-permute-start.16 = (bf16[128,512]{1,0:T(8,128)(2,1)S(1)}, bf16[128,512]{1,0:T(8,128)(2,1)S(1)}, u32[]{:S(2)}, u32[]{:S(2)}) collective-permute-start(bf16[128,512]{1,0:T(8,128)(2,1)S(1)} %get-tuple-element.104.refs_0_), channel_id=1, source_target_pairs={{0,8},{1,9},{2,10},{3,11},{4,12},{5,13},{6,14},{7,15},{8,0},{9,1},... | collective-permute-start | bytes 393224 | tf_op jit(solution)/shard_map/ppermute | solution.py:466
  50.9 7.6 %collective-permute-start.22 = (bf16[128,512]{1,0:T(8,128)(2,1)S(1)}, bf16[128,512]{1,0:T(8,128)(2,1)S(1)}, u32[]{:S(2)}, u32[]{:S(2)}) collective-permute-start(bf16[128,512]{1,0:T(8,128)(2,1)S(1)} %get-tuple-element.104.refs_0_), channel_id=1, source_target_pairs={{0,1},{1,0},{2,3},{3,2},{4,5},{5,4},{6,7},{7,6},{8,9},{9,8},{10,11... | collective-permute-start | bytes 393224 | tf_op jit(solution)/shard_map/ppermute | solution.py:466
  50.9 9.0 %collective-permute-start.19 = (bf16[128,512]{1,0:T(8,128)(2,1)S(1)}, bf16[128,512]{1,0:T(8,128)(2,1)S(1)}, u32[]{:S(2)}, u32[]{:S(2)}) collective-permute-start(bf16[128,512]{1,0:T(8,128)(2,1)S(1)} %get-tuple-element.104.refs_0_), channel_id=1, source_target_pairs={{0,4},{1,5},{2,6},{3,7},{4,0},{5,1},{6,2},{7,3},{8,12},{9,13},{10,... | collective-permute-start | bytes 393224 | tf_op jit(solution)/shard_map/ppermute | solution.py:466
  53.1 8.2 %collective-permute-start.20 = (bf16[128,512]{1,0:T(8,128)(2,1)S(1)}, bf16[128,512]{1,0:T(8,128)(2,1)S(1)}, u32[]{:S(2)}, u32[]{:S(2)}) collective-permute-start(bf16[128,512]{1,0:T(8,128)(2,1)S(1)} %get-tuple-element.104.refs_0_), channel_id=1, source_target_pairs={{0,2},{1,3},{2,0},{3,1},{4,6},{5,7},{6,4},{7,5},{8,10},{9,11},{10,... | collective-permute-start | bytes 393224 | tf_op jit(solution)/shard_map/ppermute | solution.py:466
  58.4 5.3 %collective-permute-start.17 = (bf16[128,512]{1,0:T(8,128)(2,1)S(1)}, bf16[128,512]{1,0:T(8,128)(2,1)S(1)}, u32[]{:S(2)}, u32[]{:S(2)}) collective-permute-start(bf16[128,512]{1,0:T(8,128)(2,1)S(1)} %collective-permute-done.16.refs_2_), channel_id=1, source_target_pairs={{0,4},{1,5},{2,6},{3,7},{4,0},{5,1},{6,2},{7,3},{8,12},{9,13},{10,... | collective-permute-start | bytes 393224 | tf_op jit(solution)/shard_map/ppermute | solution.py:466
  58.4 6.7 %collective-permute-start.26 = (bf16[128,512]{1,0:T(8,128)(2,1)S(1)}, bf16[128,512]{1,0:T(8,128)(2,1)S(1)}, u32[]{:S(2)}, u32[]{:S(2)}) collective-permute-start(bf16[128,512]{1,0:T(8,128)(2,1)S(1)} %collective-permute-done.16.refs_2_), channel_id=1, source_target_pairs={{0,2},{1,3},{2,0},{3,1},{4,6},{5,7},{6,4},{7,5},{8,10},{9,11},{10,... | collective-permute-start | bytes 393224 | tf_op jit(solution)/shard_map/ppermute | solution.py:466
  59.9 7.7 %collective-permute-start.21 = (bf16[128,512]{1,0:T(8,128)(2,1)S(1)}, bf16[128,512]{1,0:T(8,128)(2,1)S(1)}, u32[]{:S(2)}, u32[]{:S(2)}) collective-permute-start(bf16[128,512]{1,0:T(8,128)(2,1)S(1)} %collective-permute-done.19.refs_1_), channel_id=1, source_target_pairs={{0,2},{1,3},{2,0},{3,1},{4,6},{5,7},{6,4},{7,5},{8,10},{9,11},{10,... | collective-permute-start | bytes 393224 | tf_op jit(solution)/shard_map/ppermute | solution.py:466
  61.3 6.3 %collective-permute-start.23 = (bf16[128,512]{1,0:T(8,128)(2,1)S(1)}, bf16[128,512]{1,0:T(8,128)(2,1)S(1)}, u32[]{:S(2)}, u32[]{:S(2)}) collective-permute-start(bf16[128,512]{1,0:T(8,128)(2,1)S(1)} %collective-permute-done.19.refs_1_), channel_id=1, source_target_pairs={{0,1},{1,0},{2,3},{3,2},{4,5},{5,4},{6,7},{7,6},{8,9},{9,8},{10,11... | collective-permute-start | bytes 393224 | tf_op jit(solution)/shard_map/ppermute | solution.py:466
  61.3 6.8 %collective-permute-start.24 = (bf16[128,512]{1,0:T(8,128)(2,1)S(1)}, bf16[128,512]{1,0:T(8,128)(2,1)S(1)}, u32[]{:S(2)}, u32[]{:S(2)}) collective-permute-start(bf16[128,512]{1,0:T(8,128)(2,1)S(1)} %collective-permute-done.16.refs_2_), channel_id=1, source_target_pairs={{0,1},{1,0},{2,3},{3,2},{4,5},{5,4},{6,7},{7,6},{8,9},{9,8},{10,11... | collective-permute-start | bytes 393224 | tf_op jit(solution)/shard_map/ppermute | solution.py:466
  63.7 5.9 %collective-permute-start.18 = (bf16[128,512]{1,0:T(8,128)(2,1)S(1)}, bf16[128,512]{1,0:T(8,128)(2,1)S(1)}, u32[]{:S(2)}, u32[]{:S(2)}) collective-permute-start(bf16[128,512]{1,0:T(8,128)(2,1)S(1)} %collective-permute-done.17.refs_0_), channel_id=1, source_target_pairs={{0,2},{1,3},{2,0},{3,1},{4,6},{5,7},{6,4},{7,5},{8,10},{9,11},{10,... | collective-permute-start | bytes 393224 | tf_op jit(solution)/shard_map/ppermute | solution.py:466
  65.1 5.0 %collective-permute-start.28 = (bf16[128,512]{1,0:T(8,128)(2,1)S(1)}, bf16[128,512]{1,0:T(8,128)(2,1)S(1)}, u32[]{:S(2)}, u32[]{:S(2)}) collective-permute-start(bf16[128,512]{1,0:T(8,128)(2,1)S(1)} %collective-permute-done.20.refs_3_), channel_id=1, source_target_pairs={{0,1},{1,0},{2,3},{3,2},{4,5},{5,4},{6,7},{7,6},{8,9},{9,8},{10,11... | collective-permute-start | bytes 393224 | tf_op jit(solution)/shard_map/ppermute | solution.py:466
  (7 other events, 13.9 us)

commit v14 on v11

--- a/solution.py
+++ b/solution.py
@@ -142,61 +142,19 @@
             ordered_ref[pl.ds(pl.multiple_of(owner * cap, cap), cap), :] = value[at * cap : (at + 1) * cap]
 
 
-def ready_kernel(
-    lines,
-    dst_hbm,
-    mesh_hbm,
-    cot_hbm,
-    w1_hbm,
-    wn1_hbm,
-    wn2_hbm,
-    hot_hbm,
-    node_hbm,
-    cot_out_hbm,
-    moved_ref,
-    dst_ref,
-    mesh_ref,
-    cot_ref,
-    w1_ref,
-    wn1_ref,
-    wn2_ref,
-    hot_ref,
-    node_ref,
-    cot_out_ref,
-    sems,
-    out_sems,
-):
+def ready_kernel(lines, dst_hbm, mesh_hbm, w1_hbm, hot_hbm, moved_ref, dst_ref, mesh_ref, w1_ref, hot_ref, sems, out_sems):
     width = mesh_ref.shape[1]
     tile = lines * 128
-    pairs = [
-        (dst_hbm, dst_ref),
-        (mesh_hbm, mesh_ref),
-        (w1_hbm.at[pl.ds(width, width), :], w1_ref),
-        (wn1_hbm.at[pl.ds(0, width), :], wn1_ref),
-        (cot_hbm, cot_ref),
-        (wn2_hbm, wn2_ref),
-    ]
+    pairs = [(dst_hbm, dst_ref), (mesh_hbm, mesh_ref), (w1_hbm.at[pl.ds(width, width), :], w1_ref)]
     copies = load(pairs, sems)
-    outs = [
-        pltpu.make_async_copy(source, target, out_sems.at[at])
-        for at, (source, target) in enumerate([(hot_ref, hot_hbm), (node_ref, node_hbm), (cot_out_ref, cot_out_hbm)])
-    ]
     copies[0].wait()
     for at in range(hot_ref.shape[0] // tile):
         hot_ref[at * tile : (at + 1) * tile, :] = tile_columns(dst_ref, at, lines, hot_ref.shape[1])
-    outs[0].start()
+    (out,) = load([(hot_ref, hot_hbm)], out_sems)
     copies[1].wait()
-    copies[3].wait()
-    node_ref[...] = dot_nn(mesh_ref[...], wn1_ref[...])
-    outs[1].start()
-    copies[4].wait()
-    copies[5].wait()
-    cot_out_ref[...] = dot_nt(cot_ref[...], wn2_ref[...])
-    outs[2].start()
     copies[2].wait()
     moved_ref[...] = dot_nn(mesh_ref[...], w1_ref[...]).astype(BF16)
-    for copy in outs:
-        copy.wait()
+    out.wait()
 
 
 def base_kernel(
@@ -206,16 +164,28 @@
     w1_hbm,
     slot_hbm,
     dst_hbm,
+    mesh_hbm,
+    cot_hbm,
+    wn1_hbm,
+    wn2_hbm,
     moved_ref,
     base_ref,
     slot_ref,
     dst_ref,
     top_ref,
     turned_hbm,
+    node_hbm,
+    cot_out_hbm,
     hot_ref,
     edge_ref,
     w1_ref,
     turned_ref,
+    mesh_ref,
+    cot_ref,
+    wn1_ref,
+    wn2_ref,
+    node_ref,
+    cot_out_ref,
     sems,
     out_sems,
 ):
@@ -224,6 +194,7 @@
     tiles = edge_ref.shape[0] // tile
     pairs = [(edge_hbm.at[pl.ds(at * tile, tile), :], edge_ref.at[pl.ds(at * tile, tile), :]) for at in range(tiles)]
     pairs += [(w1_hbm.at[pl.ds(2 * width, width), :], w1_ref), (hot_hbm, hot_ref)]
+    pairs += [(mesh_hbm, mesh_ref), (wn1_hbm.at[pl.ds(0, width), :], wn1_ref), (cot_hbm, cot_ref), (wn2_hbm, wn2_ref)]
     pairs += [(w1_hbm.at[pl.ds(0, width), :], top_ref), (slot_hbm, slot_ref), (dst_hbm, dst_ref)]
     copies = load(pairs, sems)
     same = lax.broadcasted_iota(jnp.int32, (256, 256), 0) == lax.broadcasted_iota(jnp.int32, (256, 256), 1)
@@ -239,12 +210,18 @@
         out = pltpu.make_async_copy(turned_ref.at[:, columns], turned_hbm.at[:, columns], out_sems.at[at])
         out.start()
         outs.append(out)
-    copies[tiles].wait()
-    copies[tiles + 1].wait()
+    for copy in copies[tiles : tiles + 6]:
+        copy.wait()
+    node_ref[...] = dot_nn(mesh_ref[...], wn1_ref[...])
+    cot_out_ref[...] = dot_nt(cot_ref[...], wn2_ref[...])
+    for at, (source, target) in enumerate([(node_ref, node_hbm), (cot_out_ref, cot_out_hbm)]):
+        out = pltpu.make_async_copy(source, target, out_sems.at[tiles + at])
+        out.start()
+        outs.append(out)
     for at in range(tiles):
         rows = slice(at * tile, (at + 1) * tile)
         base_ref[rows, :] = dot_nn(edge_ref[rows, :], w1_ref[...]) + dot_nn(hot_ref[rows, :], moved_ref[...])
-    for out in outs + copies[tiles + 2 :]:
+    for out in outs + copies[tiles + 6 :]:
         out.wait()
 
 
@@ -491,34 +468,28 @@
             name="mix",
         )(*values)
 
-    hot, node, cot, moved = pl.pallas_call(
+    hot, moved = pl.pallas_call(
         functools.partial(ready_kernel, lines),
         out_shape=[
             pltpu.HBM((edges, mesh_rows), BF16),
-            pltpu.HBM((mesh_rows, hidden_width), F32),
-            pltpu.HBM((mesh_rows, hidden_width), F32),
             pltpu.VMEM((mesh_rows, hidden_width), BF16),
         ],
-        in_specs=specs(pltpu.HBM, 6),
-        out_specs=specs(pltpu.HBM, 3) + specs(pltpu.VMEM, 1),
+        in_specs=specs(pltpu.HBM, 3),
+        out_specs=specs(pltpu.HBM, 1) + specs(pltpu.VMEM, 1),
         scratch_shapes=[
             pltpu.VMEM(dst_index.shape, jnp.int32),
             pltpu.VMEM(mesh_latent.shape, BF16),
-            pltpu.VMEM(mesh_cot.shape, BF16),
             pltpu.VMEM((width, hidden_width), BF16),
-            pltpu.VMEM((width, hidden_width), BF16),
-            pltpu.VMEM(w_node2.shape, BF16),
             pltpu.VMEM((edges, mesh_rows), BF16),
-            pltpu.VMEM((mesh_rows, hidden_width), F32),
-            pltpu.VMEM((mesh_rows, hidden_width), F32),
-            pltpu.SemaphoreType.DMA((6,)),
             pltpu.SemaphoreType.DMA((3,)),
+            pltpu.SemaphoreType.DMA((1,)),
         ],
         compiler_params=params(16),
         cost_estimate=cost(2 * 10**9, 4 * MIB),
         name="ready",
-    )(*pinned(pltpu.HBM, dst_index, mesh_latent, mesh_cot, w_edge1, w_node1, w_node2))
-    base, *ahead, turned = pl.pallas_call(
+    )(*pinned(pltpu.HBM, dst_index, mesh_latent, w_edge1))
+    tiles = edges // (128 * lines)
+    base, *ahead, turned, node, cot = pl.pallas_call(
         functools.partial(base_kernel, lines),
         out_shape=[
             pltpu.VMEM((edges, hidden_width), F32),
@@ -526,21 +497,32 @@
             pltpu.VMEM(dst_index.shape, jnp.int32),
             pltpu.VMEM((width, hidden_width), BF16),
             pltpu.HBM((width, edges), BF16),
+            pltpu.HBM((mesh_rows, hidden_width), F32),
+            pltpu.HBM((mesh_rows, hidden_width), F32),
         ],
-        in_specs=specs(pltpu.HBM, 5) + specs(pltpu.VMEM, 1),
-        out_specs=specs(pltpu.VMEM, 4) + specs(pltpu.HBM, 1),
+        in_specs=specs(pltpu.HBM, 9) + specs(pltpu.VMEM, 1),
+        out_specs=specs(pltpu.VMEM, 4) + specs(pltpu.HBM, 3),
         scratch_shapes=[
             pltpu.VMEM((edges, mesh_rows), BF16),
             pltpu.VMEM(edge_latent.shape, BF16),
             pltpu.VMEM((width, hidden_width), BF16),
             pltpu.VMEM((width, edges), BF16),
-            pltpu.SemaphoreType.DMA((5 + edges // (128 * lines),)),
-            pltpu.SemaphoreType.DMA((edges // (128 * lines),)),
+            pltpu.VMEM(mesh_latent.shape, BF16),
+            pltpu.VMEM(mesh_cot.shape, BF16),
+            pltpu.VMEM((width, hidden_width), BF16),
+            pltpu.VMEM(w_node2.shape, BF16),
+            pltpu.VMEM((mesh_rows, hidden_width), F32),
+            pltpu.VMEM((mesh_rows, hidden_width), F32),
+            pltpu.SemaphoreType.DMA((9 + tiles,)),
+            pltpu.SemaphoreType.DMA((2 + tiles,)),
         ],
-        compiler_params=params(16),
+        compiler_params=params(20),
         cost_estimate=cost(4 * 10**9, 4 * MIB),
         name="base",
-    )(*pinned(pltpu.HBM, hot, edge_latent, w_edge1, slot_index, dst_index), *pinned(pltpu.VMEM, moved))
+    )(
+        *pinned(pltpu.HBM, hot, edge_latent, w_edge1, slot_index, dst_index, mesh_latent, mesh_cot, w_node1, w_node2),
+        *pinned(pltpu.VMEM, moved),
+    )
 
     by_inner = mix([kept, to_core(sent)], inner, outer)
     by_inner = [by_inner[0]] + [to_inner(by_inner[k], k) for k in range(1, inner)]
@@ -601,7 +583,7 @@
     small = (2 * cap, width)
     arrived = {}
     first = None
-    for k in [outer - 1, *range(1, outer - 1), 0]:
+    for k in range(outer - 1, -1, -1):
         send = sends[k] if first is None else lax.optimization_barrier((sends[k], first))[0]
         crossed = to_core(send)
         total, mixed, *parts = pl.pallas_call(
@@ -636,7 +618,7 @@
                 ],
                 compiler_params=params(16),
                 name="own",
-            )(total, mixed, *parts, *[arrived[at] for at in range(1, outer)])
+            )(total, mixed, *parts, *[arrived[at] for at in range(outer - 1, 0, -1)])
 
     grid_grad = pl.pallas_call(
         functools.partial(put_kernel, sizes),

time: 72.1 us -> 72.8 us (level)
  starting transfers between devices: 25.2 us -> 27.2 us
  waiting for transfers between devices: 22.8 us -> 21.9 us
    ppermute x31, starting transfers between devices: 25.2 us -> 27.2 us  [permute(): return lax.ppermute(value, 'band', pairs)]
    pallas_call x1, Pallas kernels: 2.8 us -> 1.87 us  [shards(): pl.pallas_call(functools.partial(ready_kernel, lines), out_shape=[pltpu.H...]
    ppermute x31, waiting for transfers between devices: 22.8 us -> 21.9 us  [permute(): return lax.ppermute(value, 'band', pairs)]
  transfers between devices with their start and end apart: 31 -> 31, of which waited for: 12 -> 13; matrix products, arithmetic and copies ran while one was open for 0% -> 0% of each run, Pallas kernels for 19% -> 18%
where the time goes in v14:
time: 72.8 us; the launch traced here: 72.6 us
  starting transfers between devices  27.2 us (37%)
  Pallas kernels  22.6 us (31%)
  waiting for transfers between devices  21.9 us (30%)
  between operations  0.84 us (1%)
    ppermute x31, starting transfers between devices, permute(): return lax.ppermute(value, 'band', pairs)  27.2 us
    ppermute x31, waiting for transfers between devices, permute(): return lax.ppermute(value, 'band', pairs)  21.9 us
    pallas_call x1, Pallas kernels, shards(): pl.pallas_call(functools.partial(main_kernel, lines, sizes), out_shape=[j...  6.73 us
    pallas_call x1, Pallas kernels, shards(): pl.pallas_call(functools.partial(base_kernel, lines), out_shape=[pltpu.VM...  4.05 us
    pallas_call x3, Pallas kernels, shards(): pl.pallas_call(functools.partial(order_kernel, sizes, places, len(grads))...  3.46 us
    pallas_call x1, Pallas kernels, shards(): pl.pallas_call(functools.partial(put_kernel, sizes), out_shape=jax.ShapeD...  2.4 us
    pallas_call x1, Pallas kernels, shards(): pl.pallas_call(mesh_kernel, out_shape=jax.ShapeDtypeStruct((mesh_rows, wi...  2.14 us
    pallas_call x1, Pallas kernels, shards(): pl.pallas_call(functools.partial(ready_kernel, lines), out_shape=[pltpu.H...  1.87 us
  transfers between devices with their start and end apart: 31, of which 13 were waited for; matrix products, arithmetic and copies ran while one was open for 0% of the time, Pallas kernels for 18%

profile of v14, /device:TPU:0, one launch (start us, length us, event | category | flops | bytes accessed | tf_op | source)
XLA Modules:
  0.0 72.6 jit_solution(711812934509402781)
XLA Ops:
  0.6 1.6 %pick.1 = (bf16[64,512]{1,0:T(8,128)(2,1)S(1)}, bf16[64,512]{1,0:T(8,128)(2,1)S(1)}) custom-call(s32[1,128]{1,0:T(1,128)} %rows_hbm.3, bf16[1024,512]{1,0:T(8,128)(2,1)} %grid_hbm.1), custom_call_target="tpu_custom_call" | custom-call | tf_op jit(solution)/shard_map/pick/pallas_call | solution.py:447
  3.6 2.9 %collective-permute-start.1 = (bf16[64,512]{1,0:T(8,128)(2,1)S(1)}, bf16[64,512]{1,0:T(8,128)(2,1)S(1)}, u32[]{:S(2)}, u32[]{:S(2)}) collective-permute-start(bf16[64,512]{1,0:T(8,128)(2,1)S(1)} %get-tuple-element.70), channel_id=1, source_target_pairs={{0,2},{1,3},{2,0},{3,1},{4,6},{5,7},{6,4},{7,5},{8,10},{9,11},{10,... | collective-permute-start | bytes 196616 | tf_op jit(solution)/shard_map/ppermute | solution.py:435
  6.6 1.9 %ready.1 = (bf16[1536,256]{1,0:T(8,128)(2,1)}, bf16[256,512]{1,0:T(8,128)(2,1)S(1)}) custom-call(s32[12,128]{1,0:T(8,128)} %bitcast.2, bf16[256,512]{1,0:T(8,128)(2,1)} %mesh_hbm.7, bf16[1536,512]{1,0:T(8,128)(2,1)} %w1_hbm.3), custom_call_target="tpu_custom_call" | custom-call | flops 2000000000 | bytes 4194304 | tf_op jit(solution)/shard_map/ready/pallas_call | solution.py:471
  9.0 2.0 %collective-permute-start.2 = (bf16[32,512]{1,0:T(8,128)(2,1)S(1)}, bf16[32,512]{1,0:T(8,128)(2,1)S(1)}, u32[]{:S(2)}, u32[]{:S(2)}) collective-permute-start(bf16[32,512]{1,0:T(8,128)(2,1)S(1)} %get-tuple-element.72), channel_id=1, source_target_pairs={{0,4},{1,5},{2,6},{3,7},{4,0},{5,1},{6,2},{7,3},{8,12},{9,13},{10,... | collective-permute-start | bytes 98312 | tf_op jit(solution)/shard_map/ppermute | solution.py:435
  11.0 2.6 %collective-permute-start.3 = (bf16[32,512]{1,0:T(8,128)(2,1)S(1)}, bf16[32,512]{1,0:T(8,128)(2,1)S(1)}, u32[]{:S(2)}, u32[]{:S(2)}) collective-permute-start(bf16[32,512]{1,0:T(8,128)(2,1)S(1)} %get-tuple-element.73), channel_id=1, source_target_pairs={{0,8},{1,9},{2,10},{3,11},{4,12},{5,13},{6,14},{7,15},{8,0},{9,1},... | collective-permute-start | bytes 98312 | tf_op jit(solution)/shard_map/ppermute | solution.py:435
  13.6 4.1 %base.1 = (f32[1536,512]{1,0:T(8,128)S(1)}, s32[12,128]{1,0:T(8,128)S(1)}, s32[12,128]{1,0:T(8,128)S(1)}, bf16[512,512]{1,0:T(8,128)(2,1)S(1)}, bf16[512,1536]{1...) custom-call(bf16[1536,256]{1,0:T(8,128)(2,1)} %get-tuple-element.58.hot_hbm, bf16[1536,512]{1,0:T(8,128)(2,1)} %edge_hbm.1, ...), custom_call_target="tpu_custom_call" | custom-call | flops 4000000000 | bytes 4194304 | tf_op jit(solution)/shard_map/base/pallas_call | solution.py:492
  17.7 1.6 %collective-permute-done.4.rest_3_ = bf16[32,512]{1,0:T(8,128)(2,1)S(1)} collective-permute-done((bf16[32,512]{1,0:T(8,128)(2,1)S(1)}, bf16[32,512]{1,0:T(8,128)(2,1)S(1)}, u32[]{:S(2)}, u32[]{:S(2)}) %collective-permute-start.4) | collective-permute-done | bytes 32800 | tf_op jit(solution)/shard_map/ppermute | solution.py:435
  19.3 6.7 %edges.1 = (bf16[256,512]{1,0:T(8,128)(2,1)S(1)}, bf16[64,512]{1,0:T(8,128)(2,1)S(1)}, bf16[272,512]{1,0:T(8,128)(2,1)S(1)}, bf16[272,512]{1,0:T(8,128)(2,1)S(1)...) custom-call(bf16[256,512]{1,0:T(8,128)(2,1)} %mesh_hbm.7, ...), custom_call_target="tpu_custom_call" | custom-call | tf_op jit(solution)/shard_map/edges/pallas_call | solution.py:535
  26.1 1.5 %collective-permute-done.5.crossed_ref = bf16[272,512]{1,0:T(8,128)(2,1)S(1)} collective-permute-done((bf16[272,512]{1,0:T(8,128)(2,1)S(1)}, bf16[272,512]{1,0:T(8,128)(2,1)S(1)}, u32[]{:S(2)}, u32[]{:S(2)}) %collective-permute-start.5) | collective-permute-done | bytes 278560 | tf_op jit(solution)/shard_map/ppermute | solution.py:435
  28.3 1.5 %collective-permute-start.8 = (bf16[144,512]{1,0:T(8,128)(2,1)S(1)}, bf16[144,512]{1,0:T(8,128)(2,1)S(1)}, u32[]{:S(2)}, u32[]{:S(2)}) collective-permute-start(bf16[144,512]{1,0:T(8,128)(2,1)S(1)} %get-tuple-element.81), channel_id=1, source_target_pairs={{0,2},{1,3},{2,0},{3,1},{4,6},{5,7},{6,4},{7,5},{8,10},{9,11},{10,... | collective-permute-start | bytes 442376 | tf_op jit(solution)/shard_map/ppermute | solution.py:435
  32.1 2.9 %collective-permute-done.8.refs_0_ = bf16[144,512]{1,0:T(8,128)(2,1)S(1)} collective-permute-done((bf16[144,512]{1,0:T(8,128)(2,1)S(1)}, bf16[144,512]{1,0:T(8,128)(2,1)S(1)}, u32[]{:S(2)}, u32[]{:S(2)}) %collective-permute-start.8) | collective-permute-done | bytes 147488 | tf_op jit(solution)/shard_map/ppermute | solution.py:435
  35.0 2.3 %collective-permute-start.9 = (bf16[160,512]{1,0:T(8,128)(2,1)S(1)}, bf16[160,512]{1,0:T(8,128)(2,1)S(1)}, u32[]{:S(2)}, u32[]{:S(2)}) collective-permute-start(bf16[160,512]{1,0:T(8,128)(2,1)S(1)} %inner.3), channel_id=1, source_target_pairs={{0,12},{1,13},{2,14},{3,15},{4,8},{5,9},{6,10},{7,11},{8,4},{9,5},... | collective-permute-start | bytes 491528 | tf_op jit(solution)/shard_map/ppermute | solution.py:435
  38.2 2.3 %collective-permute-done.11.refs_0_ = bf16[144,512]{1,0:T(8,128)(2,1)S(1)} collective-permute-done((bf16[144,512]{1,0:T(8,128)(2,1)S(1)}, bf16[144,512]{1,0:T(8,128)(2,1)S(1)}, u32[]{:S(2)}, u32[]{:S(2)}) %collective-permute-start.11) | collective-permute-done | bytes 147488 | tf_op jit(solution)/shard_map/ppermute | solution.py:435
  41.2 1.6 %collective-permute-start.7 = (bf16[144,512]{1,0:T(8,128)(2,1)S(1)}, bf16[144,512]{1,0:T(8,128)(2,1)S(1)}, u32[]{:S(2)}, u32[]{:S(2)}) collective-permute-start(bf16[144,512]{1,0:T(8,128)(2,1)S(1)} %get-tuple-element.86), channel_id=1, source_target_pairs={{0,2},{1,3},{2,0},{3,1},{4,6},{5,7},{6,4},{7,5},{8,10},{9,11},{10,... | collective-permute-start | bytes 442376 | tf_op jit(solution)/shard_map/ppermute | solution.py:435
  42.7 2.1 %mesh.1 = bf16[256,512]{1,0:T(8,128)(2,1)} custom-call(bf16[256,512]{1,0:T(8,128)(2,1)} %mesh_hbm.7, bf16[512,512]{1,0:T(8,128)(2,1)} %wn2_hbm.3, bf16[256,512]{1,0:T(8,128)(2,1)S(1)} %get-tuple-element.75.node_ref), custom_call_target="tpu_custom_call" | custom-call | flops 1000000000 | bytes 1048576 | tf_op jit(solution)/shard_map/mesh/pallas_call | solution.py:568
  46.7 3.6 %collective-permute-done.12.refs_2_ = bf16[160,512]{1,0:T(8,128)(2,1)S(1)} collective-permute-done((bf16[160,512]{1,0:T(8,128)(2,1)S(1)}, bf16[160,512]{1,0:T(8,128)(2,1)S(1)}, u32[]{:S(2)}, u32[]{:S(2)}) %collective-permute-start.12) | collective-permute-done | bytes 163872 | tf_op jit(solution)/shard_map/ppermute | solution.py:435
  50.6 2.7 %collective-permute-start.19 = (bf16[128,512]{1,0:T(8,128)(2,1)S(1)}, bf16[128,512]{1,0:T(8,128)(2,1)S(1)}, u32[]{:S(2)}, u32[]{:S(2)}) collective-permute-start(bf16[128,512]{1,0:T(8,128)(2,1)S(1)} %get-tuple-element.102.refs_0_), channel_id=1, source_target_pairs={{0,4},{1,5},{2,6},{3,7},{4,0},{5,1},{6,2},{7,3},{8,12},{9,13},{10,... | collective-permute-start | bytes 393224 | tf_op jit(solution)/shard_map/ppermute | solution.py:435
  53.2 1.5 %collective-permute-start.20 = (bf16[128,512]{1,0:T(8,128)(2,1)S(1)}, bf16[128,512]{1,0:T(8,128)(2,1)S(1)}, u32[]{:S(2)}, u32[]{:S(2)}) collective-permute-start(bf16[128,512]{1,0:T(8,128)(2,1)S(1)} %get-tuple-element.102.refs_0_), channel_id=1, source_target_pairs={{0,2},{1,3},{2,0},{3,1},{4,6},{5,7},{6,4},{7,5},{8,10},{9,11},{10,... | collective-permute-start | bytes 393224 | tf_op jit(solution)/shard_map/ppermute | solution.py:435
  54.8 2.4 %put.1 = f32[1024,512]{1,0:T(8,128)} custom-call(s32[1,128]{1,0:T(1,128)} %rows_hbm.3, bf16[32,512]{1,0:T(8,128)(2,1)S(1)} %get-tuple-element.101.refs_0_, bf16[160,512]{1,0:T(8,128)(2,1)S(1)} %collective-permute-done.15.refs_3_.refs_1_, bf16[160,512]{1,0:T(8,128)(2,1)S(1)} %collective-permute-done.12.refs_2_, ...), custom_call_target="tpu_custom_call" | custom-call | flops 2000000000 | bytes 2097152 | tf_op jit(solution)/shard_map/put/pallas_call | solution.py:623
  57.2 1.6 %collective-permute-done.16.refs_2_ = bf16[128,512]{1,0:T(8,128)(2,1)S(1)} collective-permute-done((bf16[128,512]{1,0:T(8,128)(2,1)S(1)}, bf16[128,512]{1,0:T(8,128)(2,1)S(1)}, u32[]{:S(2)}, u32[]{:S(2)}) %collective-permute-start.16) | collective-permute-done | bytes 131104 | tf_op jit(solution)/shard_map/ppermute | solution.py:435
  58.8 1.5 %collective-permute-start.26 = (bf16[128,512]{1,0:T(8,128)(2,1)S(1)}, bf16[128,512]{1,0:T(8,128)(2,1)S(1)}, u32[]{:S(2)}, u32[]{:S(2)}) collective-permute-start(bf16[128,512]{1,0:T(8,128)(2,1)S(1)} %collective-permute-done.16.refs_2_), channel_id=1, source_target_pairs={{0,2},{1,3},{2,0},{3,1},{4,6},{5,7},{6,4},{7,5},{8,10},{9,11},{10,... | collective-permute-start | bytes 393224 | tf_op jit(solution)/shard_map/ppermute | solution.py:435
  62.1 2.0 %collective-permute-done.17.refs_0_ = bf16[128,512]{1,0:T(8,128)(2,1)S(1)} collective-permute-done((bf16[128,512]{1,0:T(8,128)(2,1)S(1)}, bf16[128,512]{1,0:T(8,128)(2,1)S(1)}, u32[]{:S(2)}, u32[]{:S(2)}) %collective-permute-start.17) | collective-permute-done | bytes 131104 | tf_op jit(solution)/shard_map/ppermute | solution.py:435
  64.1 1.5 %collective-permute-start.18 = (bf16[128,512]{1,0:T(8,128)(2,1)S(1)}, bf16[128,512]{1,0:T(8,128)(2,1)S(1)}, u32[]{:S(2)}, u32[]{:S(2)}) collective-permute-start(bf16[128,512]{1,0:T(8,128)(2,1)S(1)} %collective-permute-done.17.refs_0_), channel_id=1, source_target_pairs={{0,2},{1,3},{2,0},{3,1},{4,6},{5,7},{6,4},{7,5},{8,10},{9,11},{10,... | collective-permute-start | bytes 393224 | tf_op jit(solution)/shard_map/ppermute | solution.py:435
  65.7 2.3 %collective-permute-done.21.refs_4_ = bf16[128,512]{1,0:T(8,128)(2,1)S(1)} collective-permute-done((bf16[128,512]{1,0:T(8,128)(2,1)S(1)}, bf16[128,512]{1,0:T(8,128)(2,1)S(1)}, u32[]{:S(2)}, u32[]{:S(2)}) %collective-permute-start.21) | collective-permute-done | bytes 131104 | tf_op jit(solution)/shard_map/ppermute | solution.py:435
  (57 shorter events, 15.0 us)
Async XLA Ops:
  3.6 5.3 %collective-permute-start.1 = (bf16[64,512]{1,0:T(8,128)(2,1)S(1)}, bf16[64,512]{1,0:T(8,128)(2,1)S(1)}, u32[]{:S(2)}, u32[]{:S(2)}) collective-permute-start(bf16[64,512]{1,0:T(8,128)(2,1)S(1)} %get-tuple-element.70), channel_id=1, source_target_pairs={{0,2},{1,3},{2,0},{3,1},{4,6},{5,7},{6,4},{7,5},{8,10},{9,11},{10,... | collective-permute-start | bytes 196616 | tf_op jit(solution)/shard_map/ppermute | solution.py:435
  9.0 8.6 %collective-permute-start.2 = (bf16[32,512]{1,0:T(8,128)(2,1)S(1)}, bf16[32,512]{1,0:T(8,128)(2,1)S(1)}, u32[]{:S(2)}, u32[]{:S(2)}) collective-permute-start(bf16[32,512]{1,0:T(8,128)(2,1)S(1)} %get-tuple-element.72), channel_id=1, source_target_pairs={{0,4},{1,5},{2,6},{3,7},{4,0},{5,1},{6,2},{7,3},{8,12},{9,13},{10,... | collective-permute-start | bytes 98312 | tf_op jit(solution)/shard_map/ppermute | solution.py:435
  11.0 6.7 %collective-permute-start.3 = (bf16[32,512]{1,0:T(8,128)(2,1)S(1)}, bf16[32,512]{1,0:T(8,128)(2,1)S(1)}, u32[]{:S(2)}, u32[]{:S(2)}) collective-permute-start(bf16[32,512]{1,0:T(8,128)(2,1)S(1)} %get-tuple-element.73), channel_id=1, source_target_pairs={{0,8},{1,9},{2,10},{3,11},{4,12},{5,13},{6,14},{7,15},{8,0},{9,1},... | collective-permute-start | bytes 98312 | tf_op jit(solution)/shard_map/ppermute | solution.py:435
  13.6 5.7 %collective-permute-start.4 = (bf16[32,512]{1,0:T(8,128)(2,1)S(1)}, bf16[32,512]{1,0:T(8,128)(2,1)S(1)}, u32[]{:S(2)}, u32[]{:S(2)}) collective-permute-start(bf16[32,512]{1,0:T(8,128)(2,1)S(1)} %get-tuple-element.74), channel_id=1, source_target_pairs={{0,12},{1,13},{2,14},{3,15},{4,8},{5,9},{6,10},{7,11},{8,4},{9,5},... | collective-permute-start | bytes 98312 | tf_op jit(solution)/shard_map/ppermute | solution.py:435
  27.9 3.1 %collective-permute-start.10 = (bf16[272,512]{1,0:T(8,128)(2,1)S(1)}, bf16[272,512]{1,0:T(8,128)(2,1)S(1)}, u32[]{:S(2)}, u32[]{:S(2)}) collective-permute-start(bf16[272,512]{1,0:T(8,128)(2,1)S(1)} %get-tuple-element.91), channel_id=1, source_target_pairs={{0,1},{1,0},{2,3},{3,2},{4,5},{5,4},{6,7},{7,6},{8,9},{9,8},{10,11... | collective-permute-start | bytes 835592 | tf_op jit(solution)/shard_map/ppermute | solution.py:435
  28.3 6.7 %collective-permute-start.8 = (bf16[144,512]{1,0:T(8,128)(2,1)S(1)}, bf16[144,512]{1,0:T(8,128)(2,1)S(1)}, u32[]{:S(2)}, u32[]{:S(2)}) collective-permute-start(bf16[144,512]{1,0:T(8,128)(2,1)S(1)} %get-tuple-element.81), channel_id=1, source_target_pairs={{0,2},{1,3},{2,0},{3,1},{4,6},{5,7},{6,4},{7,5},{8,10},{9,11},{10,... | collective-permute-start | bytes 442376 | tf_op jit(solution)/shard_map/ppermute | solution.py:435
  29.8 11.3 %collective-permute-start.6 = (bf16[272,512]{1,0:T(8,128)(2,1)S(1)}, bf16[272,512]{1,0:T(8,128)(2,1)S(1)}, u32[]{:S(2)}, u32[]{:S(2)}) collective-permute-start(bf16[272,512]{1,0:T(8,128)(2,1)S(1)} %get-tuple-element.82), channel_id=1, source_target_pairs={{0,1},{1,0},{2,3},{3,2},{4,5},{5,4},{6,7},{7,6},{8,9},{9,8},{10,11... | collective-permute-start | bytes 835592 | tf_op jit(solution)/shard_map/ppermute | solution.py:435
  29.9 8.3 %collective-permute-start.14 = (bf16[144,512]{1,0:T(8,128)(2,1)S(1)}, bf16[144,512]{1,0:T(8,128)(2,1)S(1)}, u32[]{:S(2)}, u32[]{:S(2)}) collective-permute-start(bf16[144,512]{1,0:T(8,128)(2,1)S(1)} %get-tuple-element.100), channel_id=1, source_target_pairs={{0,2},{1,3},{2,0},{3,1},{4,6},{5,7},{6,4},{7,5},{8,10},{9,11},{10,... | collective-permute-start | bytes 442376 | tf_op jit(solution)/shard_map/ppermute | solution.py:435
  31.0 9.5 %collective-permute-start.11 = (bf16[144,512]{1,0:T(8,128)(2,1)S(1)}, bf16[144,512]{1,0:T(8,128)(2,1)S(1)}, u32[]{:S(2)}, u32[]{:S(2)}) collective-permute-start(bf16[144,512]{1,0:T(8,128)(2,1)S(1)} %get-tuple-element.94), channel_id=1, source_target_pairs={{0,2},{1,3},{2,0},{3,1},{4,6},{5,7},{6,4},{7,5},{8,10},{9,11},{10,... | collective-permute-start | bytes 442376 | tf_op jit(solution)/shard_map/ppermute | solution.py:435
  35.0 9.9 %collective-permute-start.9 = (bf16[160,512]{1,0:T(8,128)(2,1)S(1)}, bf16[160,512]{1,0:T(8,128)(2,1)S(1)}, u32[]{:S(2)}, u32[]{:S(2)}) collective-permute-start(bf16[160,512]{1,0:T(8,128)(2,1)S(1)} %inner.3), channel_id=1, source_target_pairs={{0,12},{1,13},{2,14},{3,15},{4,8},{5,9},{6,10},{7,11},{8,4},{9,5},... | collective-permute-start | bytes 491528 | tf_op jit(solution)/shard_map/ppermute | solution.py:435
  38.2 8.5 %collective-permute-start.15 = (bf16[160,512]{1,0:T(8,128)(2,1)S(1)}, bf16[160,512]{1,0:T(8,128)(2,1)S(1)}, u32[]{:S(2)}, u32[]{:S(2)}) collective-permute-start(bf16[160,512]{1,0:T(8,128)(2,1)S(1)} %inner.5), channel_id=1, source_target_pairs={{0,4},{1,5},{2,6},{3,7},{4,0},{5,1},{6,2},{7,3},{8,12},{9,13},{10,... | collective-permute-start | bytes 491528 | tf_op jit(solution)/shard_map/ppermute | solution.py:435
  40.5 9.8 %collective-permute-start.12 = (bf16[160,512]{1,0:T(8,128)(2,1)S(1)}, bf16[160,512]{1,0:T(8,128)(2,1)S(1)}, u32[]{:S(2)}, u32[]{:S(2)}) collective-permute-start(bf16[160,512]{1,0:T(8,128)(2,1)S(1)} %inner.4), channel_id=1, source_target_pairs={{0,8},{1,9},{2,10},{3,11},{4,12},{5,13},{6,14},{7,15},{8,0},{9,1},... | collective-permute-start | bytes 491528 | tf_op jit(solution)/shard_map/ppermute | solution.py:435
  41.2 5.2 %collective-permute-start.7 = (bf16[144,512]{1,0:T(8,128)(2,1)S(1)}, bf16[144,512]{1,0:T(8,128)(2,1)S(1)}, u32[]{:S(2)}, u32[]{:S(2)}) collective-permute-start(bf16[144,512]{1,0:T(8,128)(2,1)S(1)} %get-tuple-element.86), channel_id=1, source_target_pairs={{0,2},{1,3},{2,0},{3,1},{4,6},{5,7},{6,4},{7,5},{8,10},{9,11},{10,... | collective-permute-start | bytes 442376 | tf_op jit(solution)/shard_map/ppermute | solution.py:435
  50.4 8.3 %collective-permute-start.16 = (bf16[128,512]{1,0:T(8,128)(2,1)S(1)}, bf16[128,512]{1,0:T(8,128)(2,1)S(1)}, u32[]{:S(2)}, u32[]{:S(2)}) collective-permute-start(bf16[128,512]{1,0:T(8,128)(2,1)S(1)} %get-tuple-element.102.refs_0_), channel_id=1, source_target_pairs={{0,8},{1,9},{2,10},{3,11},{4,12},{5,13},{6,14},{7,15},{8,0},{9,1},... | collective-permute-start | bytes 393224 | tf_op jit(solution)/shard_map/ppermute | solution.py:435
  50.5 8.3 %collective-permute-start.22 = (bf16[128,512]{1,0:T(8,128)(2,1)S(1)}, bf16[128,512]{1,0:T(8,128)(2,1)S(1)}, u32[]{:S(2)}, u32[]{:S(2)}) collective-permute-start(bf16[128,512]{1,0:T(8,128)(2,1)S(1)} %get-tuple-element.102.refs_0_), channel_id=1, source_target_pairs={{0,1},{1,0},{2,3},{3,2},{4,5},{5,4},{6,7},{7,6},{8,9},{9,8},{10,11... | collective-permute-start | bytes 393224 | tf_op jit(solution)/shard_map/ppermute | solution.py:435
  50.6 9.7 %collective-permute-start.19 = (bf16[128,512]{1,0:T(8,128)(2,1)S(1)}, bf16[128,512]{1,0:T(8,128)(2,1)S(1)}, u32[]{:S(2)}, u32[]{:S(2)}) collective-permute-start(bf16[128,512]{1,0:T(8,128)(2,1)S(1)} %get-tuple-element.102.refs_0_), channel_id=1, source_target_pairs={{0,4},{1,5},{2,6},{3,7},{4,0},{5,1},{6,2},{7,3},{8,12},{9,13},{10,... | collective-permute-start | bytes 393224 | tf_op jit(solution)/shard_map/ppermute | solution.py:435
  53.2 8.4 %collective-permute-start.20 = (bf16[128,512]{1,0:T(8,128)(2,1)S(1)}, bf16[128,512]{1,0:T(8,128)(2,1)S(1)}, u32[]{:S(2)}, u32[]{:S(2)}) collective-permute-start(bf16[128,512]{1,0:T(8,128)(2,1)S(1)} %get-tuple-element.102.refs_0_), channel_id=1, source_target_pairs={{0,2},{1,3},{2,0},{3,1},{4,6},{5,7},{6,4},{7,5},{8,10},{9,11},{10,... | collective-permute-start | bytes 393224 | tf_op jit(solution)/shard_map/ppermute | solution.py:435
  58.8 5.4 %collective-permute-start.17 = (bf16[128,512]{1,0:T(8,128)(2,1)S(1)}, bf16[128,512]{1,0:T(8,128)(2,1)S(1)}, u32[]{:S(2)}, u32[]{:S(2)}) collective-permute-start(bf16[128,512]{1,0:T(8,128)(2,1)S(1)} %collective-permute-done.16.refs_2_), channel_id=1, source_target_pairs={{0,4},{1,5},{2,6},{3,7},{4,0},{5,1},{6,2},{7,3},{8,12},{9,13},{10,... | collective-permute-start | bytes 393224 | tf_op jit(solution)/shard_map/ppermute | solution.py:435
  58.8 6.9 %collective-permute-start.26 = (bf16[128,512]{1,0:T(8,128)(2,1)S(1)}, bf16[128,512]{1,0:T(8,128)(2,1)S(1)}, u32[]{:S(2)}, u32[]{:S(2)}) collective-permute-start(bf16[128,512]{1,0:T(8,128)(2,1)S(1)} %collective-permute-done.16.refs_2_), channel_id=1, source_target_pairs={{0,2},{1,3},{2,0},{3,1},{4,6},{5,7},{6,4},{7,5},{8,10},{9,11},{10,... | collective-permute-start | bytes 393224 | tf_op jit(solution)/shard_map/ppermute | solution.py:435
  60.3 7.6 %collective-permute-start.21 = (bf16[128,512]{1,0:T(8,128)(2,1)S(1)}, bf16[128,512]{1,0:T(8,128)(2,1)S(1)}, u32[]{:S(2)}, u32[]{:S(2)}) collective-permute-start(bf16[128,512]{1,0:T(8,128)(2,1)S(1)} %collective-permute-done.19.refs_1_), channel_id=1, source_target_pairs={{0,2},{1,3},{2,0},{3,1},{4,6},{5,7},{6,4},{7,5},{8,10},{9,11},{10,... | collective-permute-start | bytes 393224 | tf_op jit(solution)/shard_map/ppermute | solution.py:435
  61.6 6.3 %collective-permute-start.23 = (bf16[128,512]{1,0:T(8,128)(2,1)S(1)}, bf16[128,512]{1,0:T(8,128)(2,1)S(1)}, u32[]{:S(2)}, u32[]{:S(2)}) collective-permute-start(bf16[128,512]{1,0:T(8,128)(2,1)S(1)} %collective-permute-done.19.refs_1_), channel_id=1, source_target_pairs={{0,1},{1,0},{2,3},{3,2},{4,5},{5,4},{6,7},{7,6},{8,9},{9,8},{10,11... | collective-permute-start | bytes 393224 | tf_op jit(solution)/shard_map/ppermute | solution.py:435
  61.6 6.8 %collective-permute-start.24 = (bf16[128,512]{1,0:T(8,128)(2,1)S(1)}, bf16[128,512]{1,0:T(8,128)(2,1)S(1)}, u32[]{:S(2)}, u32[]{:S(2)}) collective-permute-start(bf16[128,512]{1,0:T(8,128)(2,1)S(1)} %collective-permute-done.16.refs_2_), channel_id=1, source_target_pairs={{0,1},{1,0},{2,3},{3,2},{4,5},{5,4},{6,7},{7,6},{8,9},{9,8},{10,11... | collective-permute-start | bytes 393224 | tf_op jit(solution)/shard_map/ppermute | solution.py:435
  64.1 5.8 %collective-permute-start.18 = (bf16[128,512]{1,0:T(8,128)(2,1)S(1)}, bf16[128,512]{1,0:T(8,128)(2,1)S(1)}, u32[]{:S(2)}, u32[]{:S(2)}) collective-permute-start(bf16[128,512]{1,0:T(8,128)(2,1)S(1)} %collective-permute-done.17.refs_0_), channel_id=1, source_target_pairs={{0,2},{1,3},{2,0},{3,1},{4,6},{5,7},{6,4},{7,5},{8,10},{9,11},{10,... | collective-permute-start | bytes 393224 | tf_op jit(solution)/shard_map/ppermute | solution.py:435
  65.7 4.8 %collective-permute-start.28 = (bf16[128,512]{1,0:T(8,128)(2,1)S(1)}, bf16[128,512]{1,0:T(8,128)(2,1)S(1)}, u32[]{:S(2)}, u32[]{:S(2)}) collective-permute-start(bf16[128,512]{1,0:T(8,128)(2,1)S(1)} %collective-permute-done.20.refs_3_), channel_id=1, source_target_pairs={{0,1},{1,0},{2,3},{3,2},{4,5},{5,4},{6,7},{7,6},{8,9},{9,8},{10,11... | collective-permute-start | bytes 393224 | tf_op jit(solution)/shard_map/ppermute | solution.py:435
  (7 other events, 14.0 us)

commit v15 on v11

--- a/solution.py
+++ b/solution.py
@@ -446,7 +446,7 @@
     edges = edge_latent.shape[0]
     mesh_rows = mesh_latent.shape[0]
     slot_rows = send_rows.shape[1]
-    lines = 4
+    lines = 6
     slot_index = edge_slot.reshape(edges // 128, 128)
     dst_index = edge_dst.reshape(edges // 128, 128)
 

time: 72.1 us -> 72.1 us (level)
  no operation moved by 1% of the time
where the time goes in v15:
time: 72.1 us; the launch traced here: 71.9 us
  starting transfers between devices  24.8 us (34%)
  waiting for transfers between devices  23.4 us (32%)
  Pallas kernels  22.9 us (32%)
  between operations  0.87 us (1%)
    ppermute x31, starting transfers between devices, permute(): return lax.ppermute(value, 'band', pairs)  24.8 us
    ppermute x31, waiting for transfers between devices, permute(): return lax.ppermute(value, 'band', pairs)  23.4 us
    pallas_call x1, Pallas kernels, shards(): pl.pallas_call(functools.partial(main_kernel, lines, sizes), out_shape=[j...  6.74 us
    pallas_call x3, Pallas kernels, shards(): pl.pallas_call(functools.partial(order_kernel, sizes, places, len(grads))...  3.46 us
    pallas_call x1, Pallas kernels, shards(): pl.pallas_call(functools.partial(base_kernel, lines), out_shape=[pltpu.VM...  3.41 us
    pallas_call x1, Pallas kernels, shards(): pl.pallas_call(functools.partial(ready_kernel, lines), out_shape=[pltpu.H...  2.8 us
    pallas_call x1, Pallas kernels, shards(): pl.pallas_call(functools.partial(put_kernel, sizes), out_shape=jax.ShapeD...  2.39 us
    pallas_call x1, Pallas kernels, shards(): pl.pallas_call(mesh_kernel, out_shape=jax.ShapeDtypeStruct((mesh_rows, wi...  2.14 us
  transfers between devices with their start and end apart: 31, of which 12 were waited for; matrix products, arithmetic and copies ran while one was open for 0% of the time, Pallas kernels for 19%

profile of v15, /device:TPU:0, one launch (start us, length us, event | category | flops | bytes accessed | tf_op | source)
XLA Modules:
  0.0 71.9 jit_solution(5694789220033194281)
XLA Ops:
  0.6 1.6 %pick.1 = (bf16[64,512]{1,0:T(8,128)(2,1)S(1)}, bf16[64,512]{1,0:T(8,128)(2,1)S(1)}) custom-call(s32[1,128]{1,0:T(1,128)} %rows_hbm.3, bf16[1024,512]{1,0:T(8,128)(2,1)} %grid_hbm.1), custom_call_target="tpu_custom_call" | custom-call | tf_op jit(solution)/shard_map/pick/pallas_call | solution.py:470
  3.6 2.9 %collective-permute-start.1 = (bf16[64,512]{1,0:T(8,128)(2,1)S(1)}, bf16[64,512]{1,0:T(8,128)(2,1)S(1)}, u32[]{:S(2)}, u32[]{:S(2)}) collective-permute-start(bf16[64,512]{1,0:T(8,128)(2,1)S(1)} %get-tuple-element.70), channel_id=1, source_target_pairs={{0,2},{1,3},{2,0},{3,1},{4,6},{5,7},{6,4},{7,5},{8,10},{9,11},{10,... | collective-permute-start | bytes 196616 | tf_op jit(solution)/shard_map/ppermute | solution.py:458
  6.6 2.8 %ready.1 = (bf16[1536,256]{1,0:T(8,128)(2,1)}, f32[256,512]{1,0:T(8,128)}, f32[256,512]{1,0:T(8,128)}, bf16[256,512]{1,0:T(8,128)(2,1)S(1)}) custom-call(s32[12,128]{1,0:T(8,128)} %bitcast.2, bf16[256,512]{1,0:T(8,128)(2,1)} %mesh_hbm.5, bf16[256,512]{1,0:T(8,128)(2,1)} %cot_hbm.1, bf16[1536,512]{1,0:T(8,128)(2,1)} %w1_hbm.3, bf16[1024,512]{1,0:T(8,128)(2,1)} %wn1_hbm.3, ...), custom_call_target="tpu_custom_call" | custom-call | flops 2000000000 | bytes 4194304 | tf_op jit(solution)/shard_map/ready/pallas_call | solution.py:494
  9.4 1.6 %collective-permute-start.2 = (bf16[32,512]{1,0:T(8,128)(2,1)S(1)}, bf16[32,512]{1,0:T(8,128)(2,1)S(1)}, u32[]{:S(2)}, u32[]{:S(2)}) collective-permute-start(bf16[32,512]{1,0:T(8,128)(2,1)S(1)} %get-tuple-element.72), channel_id=1, source_target_pairs={{0,4},{1,5},{2,6},{3,7},{4,0},{5,1},{6,2},{7,3},{8,12},{9,13},{10,... | collective-permute-start | bytes 98312 | tf_op jit(solution)/shard_map/ppermute | solution.py:458
  11.1 2.6 %collective-permute-start.3 = (bf16[32,512]{1,0:T(8,128)(2,1)S(1)}, bf16[32,512]{1,0:T(8,128)(2,1)S(1)}, u32[]{:S(2)}, u32[]{:S(2)}) collective-permute-start(bf16[32,512]{1,0:T(8,128)(2,1)S(1)} %get-tuple-element.73), channel_id=1, source_target_pairs={{0,8},{1,9},{2,10},{3,11},{4,12},{5,13},{6,14},{7,15},{8,0},{9,1},... | collective-permute-start | bytes 98312 | tf_op jit(solution)/shard_map/ppermute | solution.py:458
  13.9 3.4 %base.1 = (f32[1536,512]{1,0:T(8,128)S(1)}, s32[12,128]{1,0:T(8,128)S(1)}, s32[12,128]{1,0:T(8,128)S(1)}, bf16[512,512]{1,0:T(8,128)(2,1)S(1)}, bf16[512,1536]{1,0:T(8,128)(2,1)}) custom-call(bf16[1536,256]{1,0:T(8,128)(2,1)} %get-tuple-element.58.hot_hbm, bf16[1536,512]{1,0:T(8,128)(2,1)} %edge_hbm.1, bf16[1536,512]{1,0:T(8,128)(2,1)} %w1_hbm.3, ...), custom_call_target="tpu_custom_call" | custom-call | flops 4000000000 | bytes 4194304 | tf_op jit(solution)/shard_map/base/pallas_call | solution.py:521
  17.3 2.1 %collective-permute-done.4.rest_3_ = bf16[32,512]{1,0:T(8,128)(2,1)S(1)} collective-permute-done((bf16[32,512]{1,0:T(8,128)(2,1)S(1)}, bf16[32,512]{1,0:T(8,128)(2,1)S(1)}, u32[]{:S(2)}, u32[]{:S(2)}) %collective-permute-start.4) | collective-permute-done | bytes 32800 | tf_op jit(solution)/shard_map/ppermute | solution.py:458
  19.4 6.7 %edges.1 = (bf16[256,512]{1,0:T(8,128)(2,1)S(1)}, bf16[64,512]{1,0:T(8,128)(2,1)S(1)}, bf16[272,512]{1,0:T(8,128)(2,1)S(1)}, bf16[272,512]{1,0:T(8,128)(2,1)S(1)...) custom-call(bf16[256,512]{1,0:T(8,128)(2,1)} %mesh_hbm.5, ...), custom_call_target="tpu_custom_call" | custom-call | tf_op jit(solution)/shard_map/edges/pallas_call | solution.py:553
  26.2 1.5 %collective-permute-done.5.crossed_ref = bf16[272,512]{1,0:T(8,128)(2,1)S(1)} collective-permute-done((bf16[272,512]{1,0:T(8,128)(2,1)S(1)}, bf16[272,512]{1,0:T(8,128)(2,1)S(1)}, u32[]{:S(2)}, u32[]{:S(2)}) %collective-permute-start.5) | collective-permute-done | bytes 278560 | tf_op jit(solution)/shard_map/ppermute | solution.py:458
  28.4 1.4 %collective-permute-start.14 = (bf16[144,512]{1,0:T(8,128)(2,1)S(1)}, bf16[144,512]{1,0:T(8,128)(2,1)S(1)}, u32[]{:S(2)}, u32[]{:S(2)}) collective-permute-start(bf16[144,512]{1,0:T(8,128)(2,1)S(1)} %get-tuple-element.81), channel_id=1, source_target_pairs={{0,2},{1,3},{2,0},{3,1},{4,6},{5,7},{6,4},{7,5},{8,10},{9,11},{10,... | collective-permute-start | bytes 442376 | tf_op jit(solution)/shard_map/ppermute | solution.py:458
  32.1 3.0 %collective-permute-done.14.refs_0_ = bf16[144,512]{1,0:T(8,128)(2,1)S(1)} collective-permute-done((bf16[144,512]{1,0:T(8,128)(2,1)S(1)}, bf16[144,512]{1,0:T(8,128)(2,1)S(1)}, u32[]{:S(2)}, u32[]{:S(2)}) %collective-permute-start.14) | collective-permute-done | bytes 147488 | tf_op jit(solution)/shard_map/ppermute | solution.py:458
  35.1 1.7 %collective-permute-start.15 = (bf16[160,512]{1,0:T(8,128)(2,1)S(1)}, bf16[160,512]{1,0:T(8,128)(2,1)S(1)}, u32[]{:S(2)}, u32[]{:S(2)}) collective-permute-start(bf16[160,512]{1,0:T(8,128)(2,1)S(1)} %inner.5), channel_id=1, source_target_pairs={{0,12},{1,13},{2,14},{3,15},{4,8},{5,9},{6,10},{7,11},{8,4},{9,5},... | collective-permute-start | bytes 491528 | tf_op jit(solution)/shard_map/ppermute | solution.py:458
  36.8 1.5 %collective-permute-done.12.refs_0_ = bf16[144,512]{1,0:T(8,128)(2,1)S(1)} collective-permute-done((bf16[144,512]{1,0:T(8,128)(2,1)S(1)}, bf16[144,512]{1,0:T(8,128)(2,1)S(1)}, u32[]{:S(2)}, u32[]{:S(2)}) %collective-permute-start.12) | collective-permute-done | bytes 147488 | tf_op jit(solution)/shard_map/ppermute | solution.py:458
  38.3 2.3 %collective-permute-done.9.refs_0_ = bf16[144,512]{1,0:T(8,128)(2,1)S(1)} collective-permute-done((bf16[144,512]{1,0:T(8,128)(2,1)S(1)}, bf16[144,512]{1,0:T(8,128)(2,1)S(1)}, u32[]{:S(2)}, u32[]{:S(2)}) %collective-permute-start.9) | collective-permute-done | bytes 147488 | tf_op jit(solution)/shard_map/ppermute | solution.py:458
  40.8 1.5 %collective-permute-start.7 = (bf16[144,512]{1,0:T(8,128)(2,1)S(1)}, bf16[144,512]{1,0:T(8,128)(2,1)S(1)}, u32[]{:S(2)}, u32[]{:S(2)}) collective-permute-start(bf16[144,512]{1,0:T(8,128)(2,1)S(1)} %get-tuple-element.86), channel_id=1, source_target_pairs={{0,2},{1,3},{2,0},{3,1},{4,6},{5,7},{6,4},{7,5},{8,10},{9,11},{10,... | collective-permute-start | bytes 442376 | tf_op jit(solution)/shard_map/ppermute | solution.py:458
  42.3 2.1 %mesh.1 = bf16[256,512]{1,0:T(8,128)(2,1)} custom-call(bf16[256,512]{1,0:T(8,128)(2,1)} %mesh_hbm.5, bf16[512,512]{1,0:T(8,128)(2,1)} %wn2_hbm.3, bf16[256,512]{1,0:T(8,128)(2,1)S(1)} %get-tuple-element.75.node_ref), custom_call_target="tpu_custom_call" | custom-call | flops 1000000000 | bytes 1048576 | tf_op jit(solution)/shard_map/mesh/pallas_call | solution.py:586
  44.4 1.5 %collective-permute-done.7.refs_0_ = bf16[144,512]{1,0:T(8,128)(2,1)S(1)} collective-permute-done((bf16[144,512]{1,0:T(8,128)(2,1)S(1)}, bf16[144,512]{1,0:T(8,128)(2,1)S(1)}, u32[]{:S(2)}, u32[]{:S(2)}) %collective-permute-start.7) | collective-permute-done | bytes 147488 | tf_op jit(solution)/shard_map/ppermute | solution.py:458
  46.0 3.3 %collective-permute-done.13.refs_2_ = bf16[160,512]{1,0:T(8,128)(2,1)S(1)} collective-permute-done((bf16[160,512]{1,0:T(8,128)(2,1)S(1)}, bf16[160,512]{1,0:T(8,128)(2,1)S(1)}, u32[]{:S(2)}, u32[]{:S(2)}) %collective-permute-start.13) | collective-permute-done | bytes 163872 | tf_op jit(solution)/shard_map/ppermute | solution.py:458
  50.6 2.0 %collective-permute-start.19 = (bf16[128,512]{1,0:T(8,128)(2,1)S(1)}, bf16[128,512]{1,0:T(8,128)(2,1)S(1)}, u32[]{:S(2)}, u32[]{:S(2)}) collective-permute-start(bf16[128,512]{1,0:T(8,128)(2,1)S(1)} %get-tuple-element.102.refs_0_), channel_id=1, source_target_pairs={{0,4},{1,5},{2,6},{3,7},{4,0},{5,1},{6,2},{7,3},{8,12},{9,13},{10,... | collective-permute-start | bytes 393224 | tf_op jit(solution)/shard_map/ppermute | solution.py:458
  54.0 2.4 %put.1 = f32[1024,512]{1,0:T(8,128)} custom-call(s32[1,128]{1,0:T(1,128)} %rows_hbm.3, bf16[32,512]{1,0:T(8,128)(2,1)S(1)} %get-tuple-element.101.refs_0_, bf16[160,512]{1,0:T(8,128)(2,1)S(1)} %collective-permute-done.10.refs_1_, bf16[160,512]{1,0:T(8,128)(2,1)S(1)} %collective-permute-done.13.refs_2_, bf16[160,512]{1,0:T(8,128)(2,1)S(1)} %collective-permute-done.15.refs_3_), custom_call_target="tpu_custom_call" | custom-call | flops 2000000000 | bytes 2097152 | tf_op jit(solution)/shard_map/put/pallas_call | solution.py:641
  56.4 1.7 %collective-permute-done.16.refs_2_ = bf16[128,512]{1,0:T(8,128)(2,1)S(1)} collective-permute-done((bf16[128,512]{1,0:T(8,128)(2,1)S(1)}, bf16[128,512]{1,0:T(8,128)(2,1)S(1)}, u32[]{:S(2)}, u32[]{:S(2)}) %collective-permute-start.16) | collective-permute-done | bytes 131104 | tf_op jit(solution)/shard_map/ppermute | solution.py:458
  58.1 1.4 %collective-permute-start.26 = (bf16[128,512]{1,0:T(8,128)(2,1)S(1)}, bf16[128,512]{1,0:T(8,128)(2,1)S(1)}, u32[]{:S(2)}, u32[]{:S(2)}) collective-permute-start(bf16[128,512]{1,0:T(8,128)(2,1)S(1)} %collective-permute-done.16.refs_2_), channel_id=1, source_target_pairs={{0,2},{1,3},{2,0},{3,1},{4,6},{5,7},{6,4},{7,5},{8,10},{9,11},{10,... | collective-permute-start | bytes 393224 | tf_op jit(solution)/shard_map/ppermute | solution.py:458
  61.3 2.0 %collective-permute-done.17.refs_0_ = bf16[128,512]{1,0:T(8,128)(2,1)S(1)} collective-permute-done((bf16[128,512]{1,0:T(8,128)(2,1)S(1)}, bf16[128,512]{1,0:T(8,128)(2,1)S(1)}, u32[]{:S(2)}, u32[]{:S(2)}) %collective-permute-start.17) | collective-permute-done | bytes 131104 | tf_op jit(solution)/shard_map/ppermute | solution.py:458
  64.8 2.5 %collective-permute-done.21.refs_4_ = bf16[128,512]{1,0:T(8,128)(2,1)S(1)} collective-permute-done((bf16[128,512]{1,0:T(8,128)(2,1)S(1)}, bf16[128,512]{1,0:T(8,128)(2,1)S(1)}, u32[]{:S(2)}, u32[]{:S(2)}) %collective-permute-start.21) | collective-permute-done | bytes 131104 | tf_op jit(solution)/shard_map/ppermute | solution.py:458
  (57 shorter events, 15.5 us)
Async XLA Ops:
  3.6 5.7 %collective-permute-start.1 = (bf16[64,512]{1,0:T(8,128)(2,1)S(1)}, bf16[64,512]{1,0:T(8,128)(2,1)S(1)}, u32[]{:S(2)}, u32[]{:S(2)}) collective-permute-start(bf16[64,512]{1,0:T(8,128)(2,1)S(1)} %get-tuple-element.70), channel_id=1, source_target_pairs={{0,2},{1,3},{2,0},{3,1},{4,6},{5,7},{6,4},{7,5},{8,10},{9,11},{10,... | collective-permute-start | bytes 196616 | tf_op jit(solution)/shard_map/ppermute | solution.py:458
  9.4 7.9 %collective-permute-start.2 = (bf16[32,512]{1,0:T(8,128)(2,1)S(1)}, bf16[32,512]{1,0:T(8,128)(2,1)S(1)}, u32[]{:S(2)}, u32[]{:S(2)}) collective-permute-start(bf16[32,512]{1,0:T(8,128)(2,1)S(1)} %get-tuple-element.72), channel_id=1, source_target_pairs={{0,4},{1,5},{2,6},{3,7},{4,0},{5,1},{6,2},{7,3},{8,12},{9,13},{10,... | collective-permute-start | bytes 98312 | tf_op jit(solution)/shard_map/ppermute | solution.py:458
  11.1 6.2 %collective-permute-start.3 = (bf16[32,512]{1,0:T(8,128)(2,1)S(1)}, bf16[32,512]{1,0:T(8,128)(2,1)S(1)}, u32[]{:S(2)}, u32[]{:S(2)}) collective-permute-start(bf16[32,512]{1,0:T(8,128)(2,1)S(1)} %get-tuple-element.73), channel_id=1, source_target_pairs={{0,8},{1,9},{2,10},{3,11},{4,12},{5,13},{6,14},{7,15},{8,0},{9,1},... | collective-permute-start | bytes 98312 | tf_op jit(solution)/shard_map/ppermute | solution.py:458
  13.7 5.7 %collective-permute-start.4 = (bf16[32,512]{1,0:T(8,128)(2,1)S(1)}, bf16[32,512]{1,0:T(8,128)(2,1)S(1)}, u32[]{:S(2)}, u32[]{:S(2)}) collective-permute-start(bf16[32,512]{1,0:T(8,128)(2,1)S(1)} %get-tuple-element.74), channel_id=1, source_target_pairs={{0,12},{1,13},{2,14},{3,15},{4,8},{5,9},{6,10},{7,11},{8,4},{9,5},... | collective-permute-start | bytes 98312 | tf_op jit(solution)/shard_map/ppermute | solution.py:458
  28.0 3.0 %collective-permute-start.8 = (bf16[272,512]{1,0:T(8,128)(2,1)S(1)}, bf16[272,512]{1,0:T(8,128)(2,1)S(1)}, u32[]{:S(2)}, u32[]{:S(2)}) collective-permute-start(bf16[272,512]{1,0:T(8,128)(2,1)S(1)} %get-tuple-element.89), channel_id=1, source_target_pairs={{0,1},{1,0},{2,3},{3,2},{4,5},{5,4},{6,7},{7,6},{8,9},{9,8},{10,11... | collective-permute-start | bytes 835592 | tf_op jit(solution)/shard_map/ppermute | solution.py:458
  28.4 6.7 %collective-permute-start.14 = (bf16[144,512]{1,0:T(8,128)(2,1)S(1)}, bf16[144,512]{1,0:T(8,128)(2,1)S(1)}, u32[]{:S(2)}, u32[]{:S(2)}) collective-permute-start(bf16[144,512]{1,0:T(8,128)(2,1)S(1)} %get-tuple-element.81), channel_id=1, source_target_pairs={{0,2},{1,3},{2,0},{3,1},{4,6},{5,7},{6,4},{7,5},{8,10},{9,11},{10,... | collective-permute-start | bytes 442376 | tf_op jit(solution)/shard_map/ppermute | solution.py:458
  29.8 10.9 %collective-permute-start.6 = (bf16[272,512]{1,0:T(8,128)(2,1)S(1)}, bf16[272,512]{1,0:T(8,128)(2,1)S(1)}, u32[]{:S(2)}, u32[]{:S(2)}) collective-permute-start(bf16[272,512]{1,0:T(8,128)(2,1)S(1)} %get-tuple-element.82), channel_id=1, source_target_pairs={{0,1},{1,0},{2,3},{3,2},{4,5},{5,4},{6,7},{7,6},{8,9},{9,8},{10,11... | collective-permute-start | bytes 835592 | tf_op jit(solution)/shard_map/ppermute | solution.py:458
  29.9 8.4 %collective-permute-start.12 = (bf16[144,512]{1,0:T(8,128)(2,1)S(1)}, bf16[144,512]{1,0:T(8,128)(2,1)S(1)}, u32[]{:S(2)}, u32[]{:S(2)}) collective-permute-start(bf16[144,512]{1,0:T(8,128)(2,1)S(1)} %get-tuple-element.98), channel_id=1, source_target_pairs={{0,2},{1,3},{2,0},{3,1},{4,6},{5,7},{6,4},{7,5},{8,10},{9,11},{10,... | collective-permute-start | bytes 442376 | tf_op jit(solution)/shard_map/ppermute | solution.py:458
  31.0 9.5 %collective-permute-start.9 = (bf16[144,512]{1,0:T(8,128)(2,1)S(1)}, bf16[144,512]{1,0:T(8,128)(2,1)S(1)}, u32[]{:S(2)}, u32[]{:S(2)}) collective-permute-start(bf16[144,512]{1,0:T(8,128)(2,1)S(1)} %get-tuple-element.92), channel_id=1, source_target_pairs={{0,2},{1,3},{2,0},{3,1},{4,6},{5,7},{6,4},{7,5},{8,10},{9,11},{10,... | collective-permute-start | bytes 442376 | tf_op jit(solution)/shard_map/ppermute | solution.py:458
  35.1 9.3 %collective-permute-start.15 = (bf16[160,512]{1,0:T(8,128)(2,1)S(1)}, bf16[160,512]{1,0:T(8,128)(2,1)S(1)}, u32[]{:S(2)}, u32[]{:S(2)}) collective-permute-start(bf16[160,512]{1,0:T(8,128)(2,1)S(1)} %inner.5), channel_id=1, source_target_pairs={{0,12},{1,13},{2,14},{3,15},{4,8},{5,9},{6,10},{7,11},{8,4},{9,5},... | collective-permute-start | bytes 491528 | tf_op jit(solution)/shard_map/ppermute | solution.py:458
  38.2 11.0 %collective-permute-start.13 = (bf16[160,512]{1,0:T(8,128)(2,1)S(1)}, bf16[160,512]{1,0:T(8,128)(2,1)S(1)}, u32[]{:S(2)}, u32[]{:S(2)}) collective-permute-start(bf16[160,512]{1,0:T(8,128)(2,1)S(1)} %inner.4), channel_id=1, source_target_pairs={{0,8},{1,9},{2,10},{3,11},{4,12},{5,13},{6,14},{7,15},{8,0},{9,1},... | collective-permute-start | bytes 491528 | tf_op jit(solution)/shard_map/ppermute | solution.py:458
  40.6 9.8 %collective-permute-start.10 = (bf16[160,512]{1,0:T(8,128)(2,1)S(1)}, bf16[160,512]{1,0:T(8,128)(2,1)S(1)}, u32[]{:S(2)}, u32[]{:S(2)}) collective-permute-start(bf16[160,512]{1,0:T(8,128)(2,1)S(1)} %inner.3), channel_id=1, source_target_pairs={{0,4},{1,5},{2,6},{3,7},{4,0},{5,1},{6,2},{7,3},{8,12},{9,13},{10,... | collective-permute-start | bytes 491528 | tf_op jit(solution)/shard_map/ppermute | solution.py:458
  40.8 5.2 %collective-permute-start.7 = (bf16[144,512]{1,0:T(8,128)(2,1)S(1)}, bf16[144,512]{1,0:T(8,128)(2,1)S(1)}, u32[]{:S(2)}, u32[]{:S(2)}) collective-permute-start(bf16[144,512]{1,0:T(8,128)(2,1)S(1)} %get-tuple-element.86), channel_id=1, source_target_pairs={{0,2},{1,3},{2,0},{3,1},{4,6},{5,7},{6,4},{7,5},{8,10},{9,11},{10,... | collective-permute-start | bytes 442376 | tf_op jit(solution)/shard_map/ppermute | solution.py:458
  50.5 7.6 %collective-permute-start.16 = (bf16[128,512]{1,0:T(8,128)(2,1)S(1)}, bf16[128,512]{1,0:T(8,128)(2,1)S(1)}, u32[]{:S(2)}, u32[]{:S(2)}) collective-permute-start(bf16[128,512]{1,0:T(8,128)(2,1)S(1)} %get-tuple-element.102.refs_0_), channel_id=1, source_target_pairs={{0,8},{1,9},{2,10},{3,11},{4,12},{5,13},{6,14},{7,15},{8,0},{9,1},... | collective-permute-start | bytes 393224 | tf_op jit(solution)/shard_map/ppermute | solution.py:458
  50.5 7.6 %collective-permute-start.22 = (bf16[128,512]{1,0:T(8,128)(2,1)S(1)}, bf16[128,512]{1,0:T(8,128)(2,1)S(1)}, u32[]{:S(2)}, u32[]{:S(2)}) collective-permute-start(bf16[128,512]{1,0:T(8,128)(2,1)S(1)} %get-tuple-element.102.refs_0_), channel_id=1, source_target_pairs={{0,1},{1,0},{2,3},{3,2},{4,5},{5,4},{6,7},{7,6},{8,9},{9,8},{10,11... | collective-permute-start | bytes 393224 | tf_op jit(solution)/shard_map/ppermute | solution.py:458
  50.6 8.9 %collective-permute-start.19 = (bf16[128,512]{1,0:T(8,128)(2,1)S(1)}, bf16[128,512]{1,0:T(8,128)(2,1)S(1)}, u32[]{:S(2)}, u32[]{:S(2)}) collective-permute-start(bf16[128,512]{1,0:T(8,128)(2,1)S(1)} %get-tuple-element.102.refs_0_), channel_id=1, source_target_pairs={{0,4},{1,5},{2,6},{3,7},{4,0},{5,1},{6,2},{7,3},{8,12},{9,13},{10,... | collective-permute-start | bytes 393224 | tf_op jit(solution)/shard_map/ppermute | solution.py:458
  52.6 8.2 %collective-permute-start.20 = (bf16[128,512]{1,0:T(8,128)(2,1)S(1)}, bf16[128,512]{1,0:T(8,128)(2,1)S(1)}, u32[]{:S(2)}, u32[]{:S(2)}) collective-permute-start(bf16[128,512]{1,0:T(8,128)(2,1)S(1)} %get-tuple-element.102.refs_0_), channel_id=1, source_target_pairs={{0,2},{1,3},{2,0},{3,1},{4,6},{5,7},{6,4},{7,5},{8,10},{9,11},{10,... | collective-permute-start | bytes 393224 | tf_op jit(solution)/shard_map/ppermute | solution.py:458
  58.1 5.3 %collective-permute-start.17 = (bf16[128,512]{1,0:T(8,128)(2,1)S(1)}, bf16[128,512]{1,0:T(8,128)(2,1)S(1)}, u32[]{:S(2)}, u32[]{:S(2)}) collective-permute-start(bf16[128,512]{1,0:T(8,128)(2,1)S(1)} %collective-permute-done.16.refs_2_), channel_id=1, source_target_pairs={{0,4},{1,5},{2,6},{3,7},{4,0},{5,1},{6,2},{7,3},{8,12},{9,13},{10,... | collective-permute-start | bytes 393224 | tf_op jit(solution)/shard_map/ppermute | solution.py:458
  58.1 6.7 %collective-permute-start.26 = (bf16[128,512]{1,0:T(8,128)(2,1)S(1)}, bf16[128,512]{1,0:T(8,128)(2,1)S(1)}, u32[]{:S(2)}, u32[]{:S(2)}) collective-permute-start(bf16[128,512]{1,0:T(8,128)(2,1)S(1)} %collective-permute-done.16.refs_2_), channel_id=1, source_target_pairs={{0,2},{1,3},{2,0},{3,1},{4,6},{5,7},{6,4},{7,5},{8,10},{9,11},{10,... | collective-permute-start | bytes 393224 | tf_op jit(solution)/shard_map/ppermute | solution.py:458
  59.5 7.8 %collective-permute-start.21 = (bf16[128,512]{1,0:T(8,128)(2,1)S(1)}, bf16[128,512]{1,0:T(8,128)(2,1)S(1)}, u32[]{:S(2)}, u32[]{:S(2)}) collective-permute-start(bf16[128,512]{1,0:T(8,128)(2,1)S(1)} %collective-permute-done.19.refs_1_), channel_id=1, source_target_pairs={{0,2},{1,3},{2,0},{3,1},{4,6},{5,7},{6,4},{7,5},{8,10},{9,11},{10,... | collective-permute-start | bytes 393224 | tf_op jit(solution)/shard_map/ppermute | solution.py:458
  60.8 6.5 %collective-permute-start.23 = (bf16[128,512]{1,0:T(8,128)(2,1)S(1)}, bf16[128,512]{1,0:T(8,128)(2,1)S(1)}, u32[]{:S(2)}, u32[]{:S(2)}) collective-permute-start(bf16[128,512]{1,0:T(8,128)(2,1)S(1)} %collective-permute-done.19.refs_1_), channel_id=1, source_target_pairs={{0,1},{1,0},{2,3},{3,2},{4,5},{5,4},{6,7},{7,6},{8,9},{9,8},{10,11... | collective-permute-start | bytes 393224 | tf_op jit(solution)/shard_map/ppermute | solution.py:458
  60.8 7.0 %collective-permute-start.24 = (bf16[128,512]{1,0:T(8,128)(2,1)S(1)}, bf16[128,512]{1,0:T(8,128)(2,1)S(1)}, u32[]{:S(2)}, u32[]{:S(2)}) collective-permute-start(bf16[128,512]{1,0:T(8,128)(2,1)S(1)} %collective-permute-done.16.refs_2_), channel_id=1, source_target_pairs={{0,1},{1,0},{2,3},{3,2},{4,5},{5,4},{6,7},{7,6},{8,9},{9,8},{10,11... | collective-permute-start | bytes 393224 | tf_op jit(solution)/shard_map/ppermute | solution.py:458
  63.4 5.9 %collective-permute-start.18 = (bf16[128,512]{1,0:T(8,128)(2,1)S(1)}, bf16[128,512]{1,0:T(8,128)(2,1)S(1)}, u32[]{:S(2)}, u32[]{:S(2)}) collective-permute-start(bf16[128,512]{1,0:T(8,128)(2,1)S(1)} %collective-permute-done.17.refs_0_), channel_id=1, source_target_pairs={{0,2},{1,3},{2,0},{3,1},{4,6},{5,7},{6,4},{7,5},{8,10},{9,11},{10,... | collective-permute-start | bytes 393224 | tf_op jit(solution)/shard_map/ppermute | solution.py:458
  64.8 5.0 %collective-permute-start.28 = (bf16[128,512]{1,0:T(8,128)(2,1)S(1)}, bf16[128,512]{1,0:T(8,128)(2,1)S(1)}, u32[]{:S(2)}, u32[]{:S(2)}) collective-permute-start(bf16[128,512]{1,0:T(8,128)(2,1)S(1)} %collective-permute-done.20.refs_3_), channel_id=1, source_target_pairs={{0,1},{1,0},{2,3},{3,2},{4,5},{5,4},{6,7},{7,6},{8,9},{9,8},{10,11... | collective-permute-start | bytes 393224 | tf_op jit(solution)/shard_map/ppermute | solution.py:458
  (7 other events, 13.9 us)
